TPU v7x, 32 devices: a whole 2x2x4 slice. The times are simulated.
32 devices in a mesh: seq: 16 (over z, y, core), fsdp: 2 (over x).
Axes of the slice: x: 2, y: 2, z: 4, core: 2. Of those that a mesh axis runs over, the one named last changes fastest.
Arguments:
- tokens: bfloat16 [4096, 1024], P(('seq', 'fsdp')), may hold values from -6 to 6
- norm1_gain: bfloat16 [1024], P('seq'), may hold values from 0.5 to 1.5
- w_qkv: bfloat16 [1024, 3, 1024], P('seq', None, 'fsdp'), may hold values from -0.1875 to 0.1875
- w_attn_out: bfloat16 [1024, 1024], P('fsdp', 'seq'), may hold values from -2 to 2
- norm2_gain: bfloat16 [1024], P('seq'), may hold values from 0.5 to 1.5
- w_in: bfloat16 [1024, 2, 2624], P('seq', None, 'fsdp'), may hold values from -0.1875 to 0.1875
- w_down: bfloat16 [2624, 1024], P('fsdp', 'seq'), may hold values from -0.125 to 0.125
- cotangent: bfloat16 [4096, 1024], P(('seq', 'fsdp')), may hold values from -6 to 6
Outputs:
- output: bfloat16 [4096, 1024], P(('seq', 'fsdp'))
- grad_tokens: bfloat16 [4096, 1024], P(('seq', 'fsdp'))
- grad_norm1_gain: float32 [1024], P('seq')
- grad_w_qkv: float32 [1024, 3, 1024], P('seq', None, 'fsdp')
- grad_w_attn_out: float32 [1024, 1024], P('fsdp', 'seq')
- grad_norm2_gain: float32 [1024], P('seq')
- grad_w_in: float32 [1024, 2, 2624], P('seq', None, 'fsdp')
- grad_w_down: float32 [2624, 1024], P('fsdp', 'seq')
All inputs are finite; a program needn't handle non-finite values.
Results may differ from a plain program's by a relative error of at most 0.019.
Values may be sent and summed in bfloat16 or wider, within the bound.
No kernel may reach another device: no remote copies, remote signals or barrier semaphores. Data moves between devices by JAX's collectives and lax.ppermute only.
A program may use at most 128 MiB of HBM per device.

v0:
```python
import functools
import math

import jax
import jax.numpy as jnp
import numpy as np
from jax import lax
from jax.experimental import pallas as pl
from jax.experimental.pallas import tpu as pltpu
from jax.sharding import PartitionSpec as P

HD = 64
HALF = 64
LANES = 128

EPSILON = 1e-05
THETA = 10000.0
SEQ = "seq"
PAIR = "fsdp"
F32 = jnp.float32
BF16 = jnp.bfloat16


def passed_along(block, axis, distance):
    devices = range(lax.axis_size(axis))
    route = [(i - distance, i) for i in devices if i - distance in devices]
    return lax.ppermute(block, axis, route)


def pair_swap(block):
    return lax.ppermute(block, PAIR, [(0, 1), (1, 0)])


class Ring:
    def __init__(self, width):
        size = lax.axis_size(SEQ)
        self.chips = size // 2
        rows = self.chips // 2
        order = [2 * z for z in range(rows)] + [2 * z + 1 for z in reversed(range(rows))]
        place = np.argsort(np.array(order))
        self.up, self.down = [], []
        for i in range(size):
            chip, core = divmod(i, 2)
            self.up.append((i, order[(place[chip] + 1) % self.chips] * 2 + core))
            self.down.append((i, order[(place[chip] - 1) % self.chips] * 2 + core))
        self.swap = [(i, i ^ 1) for i in range(size)]
        me = lax.axis_index(SEQ)
        self.core = me % 2
        self.place = jnp.asarray(place, jnp.int32)[me // 2]
        self.order = jnp.asarray(order, jnp.int32)
        self.half = self.chips // 2
        self.slots = [self.half]
        for step in range(1, self.half):
            self.slots += [self.half + step, self.half - step]
        self.slots.append(0)
        self.short = width == LANES * self.chips

    def chips_at(self, distances):
        steps = jnp.asarray(distances, jnp.int32)
        return self.order[(self.place + steps + self.chips) % self.chips]

    def go(self, block, route):
        return lax.ppermute(block, SEQ, route)

    def gather(self, block):
        if not self.short:
            return lax.all_gather(block, SEQ, axis=0, tiled=True), []
        rows = block.shape[0]
        middle = rows // 2
        upward = downward = block
        got = {0: block}
        marks = []
        for step in range(1, self.half):
            upward = self.go(upward, self.up)
            downward = self.go(downward, self.down)
            got[-step], got[step] = upward, downward
            marks.append(upward)
        low = self.go(upward[:middle], self.up)
        high = self.go(downward[middle:], self.down)
        got[self.half] = jnp.concatenate([low, high], axis=0)
        distances = sorted(got)
        pieces = [got[d] for d in distances]
        others = [self.go(p, self.swap) for p in pieces]
        chips = self.chips_at(distances)
        starts = jnp.concatenate([chips * 2 + self.core, chips * 2 + 1 - self.core])
        return placed(starts, pieces + others), marks

    def scatter_sum(self, kept, away):
        rows = kept.shape[1]
        middle = rows // 2
        early = 3
        came_first = self.go(away[:early], self.swap)
        came_rest = self.go(away[early:], self.swap)

        def at(slot):
            i = self.slots.index(slot)
            came = came_first[i] if i < early else came_rest[i - early]
            return kept[i].astype(F32) + came.astype(F32)

        far = at(self.half).astype(BF16)
        upward = self.go(far[:middle], self.up)
        downward = self.go(far[middle:], self.down)
        for step in range(1, self.half):
            more_up = upward.astype(F32)
            more_down = downward.astype(F32)
            if step == 1:
                more_up = jnp.pad(more_up, ((0, rows - middle), (0, 0)))
                more_down = jnp.pad(more_down, ((middle, 0), (0, 0)))
            upward = self.go((at(self.half - step) + more_up).astype(BF16), self.up)
            downward = self.go((at(self.half + step) + more_down).astype(BF16), self.down)
        return at(0) + upward.astype(F32) + downward.astype(F32)


def placed_kernel(count, rows, starts, *refs):
    pieces, whole, ready = refs[:count], refs[count], refs[count + 1]
    copies = [
        pltpu.make_async_copy(
            pieces[i],
            whole.at[pl.ds(pl.multiple_of(starts[i] * rows, rows), rows), :],
            ready.at[i],
        )
        for i in range(count)
    ]
    for copy in copies:
        copy.start()
    for copy in copies:
        copy.wait()


def placed(starts, pieces):
    count, (rows, width) = len(pieces), pieces[0].shape
    anywhere = pl.BlockSpec(memory_space=pl.ANY)
    return pl.pallas_call(
        functools.partial(placed_kernel, count, rows),
        grid_spec=pltpu.PrefetchScalarGridSpec(
            num_scalar_prefetch=1,
            grid=(),
            in_specs=[anywhere] * count,
            out_specs=pl.BlockSpec(memory_space=pltpu.VMEM),
            scratch_shapes=[pltpu.SemaphoreType.DMA((count,))],
        ),
        compiler_params=pltpu.CompilerParams(vmem_limit_bytes=24 * 1024 * 1024),
        out_shape=jax.ShapeDtypeStruct((count * rows, width), pieces[0].dtype),
        cost_estimate=pl.CostEstimate(
            flops=0, bytes_accessed=4 * count * rows * width, transcendentals=0
        ),
    )(starts, *pieces)


def weight_kernel(chips, core, left_one, left_two, right_one, right_two, *refs):
    kept, away = refs[-2:]
    lower = core[0] == 0
    depth = kept.shape[1]

    def put(block, start, stop):
        kept[0, :, start:stop] = jnp.where(lower, block[:depth], block[depth:]).astype(BF16)
        away[0, :, start:stop] = jnp.where(lower, block[depth:], block[:depth]).astype(BF16)

    base = 0
    for left, right in ((left_one, right_one), (left_two, right_two)):
        width = right.shape[1]
        turned = left[...].T
        for start in range(0, width, 512):
            stop = min(width, start + 512)
            product = jnp.dot(turned, right[:, start:stop], preferred_element_type=F32)
            put(product, base + start, base + stop)
        base += width
    if len(refs) == 3:
        put(refs[0][...].astype(F32), base, base + refs[0].shape[1])


def weight_terms(ring, left_one, right_one, left_two, right_two, extra=None):
    work_rows, width = left_one.shape
    lanes = width // ring.chips
    depth = lanes // 2
    total = right_one.shape[1] + right_two.shape[1]
    more_args, more_specs = [], []
    if extra is not None:
        total += extra.shape[1]
        more_args.append(extra)
        more_specs.append(
            pl.BlockSpec((lanes, extra.shape[1]), lambda i, chips, core: (chips[i], 0))
        )

    def left_map(i, chips, core):
        return (0, chips[i])

    def whole_map(i, chips, core):
        return (0, 0)

    return pl.pallas_call(
        weight_kernel,
        grid_spec=pltpu.PrefetchScalarGridSpec(
            num_scalar_prefetch=2,
            grid=(ring.chips,),
            in_specs=[
                pl.BlockSpec((work_rows, lanes), left_map),
                pl.BlockSpec((work_rows, lanes), left_map),
                pl.BlockSpec(right_one.shape, whole_map),
                pl.BlockSpec(right_two.shape, whole_map),
                *more_specs,
            ],
            out_specs=[
                pl.BlockSpec((1, depth, total), lambda i, chips, core: (i, 0, 0)),
                pl.BlockSpec((1, depth, total), lambda i, chips, core: (i, 0, 0)),
            ],
        ),
        out_shape=[
            jax.ShapeDtypeStruct((ring.chips, depth, total), BF16),
            jax.ShapeDtypeStruct((ring.chips, depth, total), BF16),
        ],
        compiler_params=pltpu.CompilerParams(vmem_limit_bytes=40 * 1024 * 1024),
        cost_estimate=pl.CostEstimate(
            flops=2 * work_rows * width * total,
            bytes_accessed=2 * (width + work_rows) * total,
            transcendentals=0,
        ),
    )(
        ring.chips_at(ring.slots),
        ring.core.reshape(1),
        left_one,
        left_two,
        right_one,
        right_two,
        *more_args,
    )


def summed_terms(ring, *factors):
    if ring.short:
        return ring.scatter_sum(*weight_terms(ring, *factors))
    left_one, right_one, left_two, right_two, *extra = factors
    terms = [dot(left_one, right_one, (0, 0)), dot(left_two, right_two, (0, 0))]
    terms = jnp.concatenate([t.astype(BF16) for t in terms] + extra, axis=1)
    return lax.psum_scatter(terms, SEQ, scatter_dimension=0, tiled=True).astype(F32)


def norm_rows(values, gain):
    average = jnp.mean(values, axis=-1, keepdims=True)
    centered = values - average
    inverse = lax.rsqrt(jnp.mean(centered * centered, axis=-1, keepdims=True) + EPSILON)
    unit_rows = centered * inverse
    return (unit_rows * gain, unit_rows, inverse)


def norm_back(grad_rows, gain, unit_rows, inverse):
    scaled = grad_rows * gain
    centered_grad = (
        scaled
        - jnp.mean(scaled, axis=-1, keepdims=True)
        - unit_rows * jnp.mean(scaled * unit_rows, axis=-1, keepdims=True)
    )
    return inverse * centered_grad


def rotary_tables(positions, head_size):
    half_size = head_size // 2
    frequency = THETA ** (-(jnp.arange(half_size, dtype=jnp.float32) * 2.0) / head_size)
    angles = positions.astype(jnp.float32)[:, None] * frequency[None, :]
    return (jnp.cos(angles)[:, None, :], jnp.sin(angles)[:, None, :])


def rotate(values, cosine_table, sine_table):
    half_size = values.shape[-1] // 2
    first_half = values[..., :half_size]
    second_half = values[..., half_size:]
    return jnp.concatenate(
        [
            first_half * cosine_table - second_half * sine_table,
            second_half * cosine_table + first_half * sine_table,
        ],
        axis=-1,
    )


def gated(gate_part, up_part):
    return jax.nn.gelu(gate_part, approximate=False) * up_part


def pair_rows(mine):
    other = pair_swap(mine)
    first = lax.axis_index(PAIR) == 0
    return jnp.concatenate([jnp.where(first, mine, other), jnp.where(first, other, mine)], axis=0)


def own_rows(values, row_count):
    return lax.dynamic_slice_in_dim(values, lax.axis_index(PAIR) * row_count, row_count, 0)


def other_rows(values, row_count):
    return lax.dynamic_slice_in_dim(values, (1 - lax.axis_index(PAIR)) * row_count, row_count, 0)


def dot(a, b, over=(1, 0)):
    return lax.dot_general(a, b, (((over[0],), (over[1],)), ((), ())), preferred_element_type=F32)


def padded_to_lanes(values):
    return jnp.pad(values, ((0, 0), (0, -values.shape[1] % LANES)))


def local(tokens, norm1_gain, w_qkv, w_attn_out, norm2_gain, w_in, w_down, cotangent):
    row_count, model_width = tokens.shape
    score_scale = 1.0 / math.sqrt(HD)
    ring = Ring(model_width)
    depth, _, width = w_qkv.shape
    units = w_down.shape[0]
    heads_here = width // HD
    gains = padded_to_lanes(jnp.stack([norm1_gain, norm2_gain], axis=1))
    blob_a = jnp.concatenate([w_qkv.reshape(depth, -1), w_attn_out.T, gains], axis=1)
    whole_a, marks = ring.gather(blob_a)
    qkv_matrix = whole_a[:, : 3 * width]
    attn_matrix = whole_a[:, 3 * width : 4 * width]
    gain_columns = whole_a[:, 4 * width :].astype(F32)
    gain_one = gain_columns[:, 0]
    gain_two = gain_columns[:, 1]
    blob_b = jnp.concatenate(
        [padded_to_lanes(w_in[:, 0]), padded_to_lanes(w_in[:, 1]), padded_to_lanes(w_down.T)], axis=1
    )
    units_pad = blob_b.shape[1] // 3
    whole_b, _ = ring.gather(blob_b)
    in_matrix = whole_b[:, : 2 * units_pad]
    down_matrix = whole_b[:, 2 * units_pad :]

    pair_size = lax.axis_size(PAIR)
    work_rows = row_count * pair_size
    work_start = lax.axis_index(SEQ) * work_rows
    all_rows = work_rows * lax.axis_size(SEQ)
    token_float = pair_rows(tokens).astype(F32)
    cot_work = pair_rows(cotangent)

    normed_one, unit_one, inverse_one = norm_rows(token_float, gain_one)
    work_one = normed_one.astype(BF16)
    query_pos = work_start + jnp.arange(work_rows, dtype=jnp.int32)
    key_pos = work_start - HALF + jnp.arange(work_rows + 2 * HALF, dtype=jnp.int32)
    offset = key_pos[None, :] - query_pos[:, None]
    inside = (jnp.abs(offset) <= HALF) & (key_pos[None, :] >= 0) & (key_pos[None, :] < all_rows)
    cosine_table, sine_table = rotary_tables(query_pos, HD)
    qkv = dot(work_one, qkv_matrix)
    queries = rotate(
        qkv[:, :width].reshape(work_rows, heads_here, HD), cosine_table, sine_table
    ).astype(BF16)
    keys_own = rotate(
        qkv[:, width : 2 * width].reshape(work_rows, heads_here, HD), cosine_table, sine_table
    )
    keys_own = keys_own.reshape(work_rows, width).astype(BF16)
    values_own = qkv[:, 2 * width :].astype(BF16)
    kv_own = jnp.concatenate([keys_own, values_own], axis=1)
    from_before = passed_along(kv_own[work_rows - HALF :], SEQ, 1)
    from_after = passed_along(kv_own[:HALF], SEQ, -1)
    padded = jnp.concatenate([from_before, kv_own, from_after], axis=0)
    keys_all = padded[:, :width].reshape(-1, heads_here, HD)
    values_all = padded[:, width:].reshape(-1, heads_here, HD)
    scores = jnp.einsum("qhd,khd->hqk", queries, keys_all, preferred_element_type=F32) * score_scale
    masked = jnp.where(inside[None], scores, -1e30)
    expo = jnp.exp(masked - jnp.max(masked, axis=-1, keepdims=True))
    softmax_rows = expo / jnp.sum(expo, axis=-1, keepdims=True)
    softmax_low = softmax_rows.astype(BF16)
    context = jnp.einsum("hqk,khd->qhd", softmax_low, values_all, preferred_element_type=F32)
    context = context.reshape(work_rows, width).astype(BF16)
    attn_term = dot(context, attn_matrix, (1, 1)).astype(BF16)
    attn_other = pair_swap(attn_term)
    residual = token_float + (attn_term.astype(F32) + attn_other.astype(F32))

    normed_two, unit_two, inverse_two = norm_rows(residual, gain_two)
    work_two = normed_two.astype(BF16)
    projected = dot(work_two, in_matrix)
    hidden, gate_back = jax.vjp(gated, projected[:, :units_pad], projected[:, units_pad:])
    hidden = hidden.astype(BF16)
    grad_hidden = dot(cot_work, down_matrix)
    grad_gate, grad_up = gate_back(grad_hidden)
    grad_proj = jnp.concatenate([grad_gate, grad_up], axis=1).astype(BF16)
    grad_two = dot(grad_proj, in_matrix, (1, 1)).astype(BF16)
    grad_two_other = pair_swap(grad_two)
    grad_low_two = grad_two.astype(F32) + grad_two_other.astype(F32)

    share_b = summed_terms(ring, work_two, grad_proj, cot_work, hidden)

    down_term = dot(hidden, down_matrix, (1, 1)).astype(BF16)
    down_other = pair_swap(other_rows(down_term, row_count))
    output = (
        own_rows(residual, row_count)
        + (own_rows(down_term, row_count).astype(F32) + down_other.astype(F32))
    ).astype(BF16)

    grad_gain_two = jnp.sum(grad_low_two * unit_two, axis=0)
    grad_residual = cot_work.astype(F32) + norm_back(grad_low_two, gain_two, unit_two, inverse_two)
    grad_res_work = grad_residual.astype(BF16)
    grad_context = dot(grad_res_work, attn_matrix).astype(BF16).reshape(work_rows, heads_here, HD)
    grad_softmax = jnp.einsum(
        "qhd,khd->hqk", grad_context, values_all, preferred_element_type=F32
    )
    grad_scores = softmax_rows * (
        grad_softmax - jnp.sum(grad_softmax * softmax_rows, axis=-1, keepdims=True)
    )
    grad_scores = grad_scores.astype(BF16)
    grad_queries = (
        jnp.einsum("hqk,khd->qhd", grad_scores, keys_all, preferred_element_type=F32) * score_scale
    )
    grad_keys = (
        jnp.einsum("hqk,qhd->khd", grad_scores, queries, preferred_element_type=F32) * score_scale
    )
    grad_values = jnp.einsum("hqk,qhd->khd", softmax_low, grad_context, preferred_element_type=F32)
    grad_padded = jnp.concatenate(
        [grad_keys.reshape(-1, width), grad_values.reshape(-1, width)], axis=1
    )
    from_next = passed_along(grad_padded[:HALF].astype(BF16), SEQ, -1).astype(F32)
    from_prev = passed_along(grad_padded[work_rows + HALF :].astype(BF16), SEQ, 1).astype(F32)
    grad_kv = jnp.concatenate(
        [
            grad_padded[HALF : 2 * HALF] + from_prev,
            grad_padded[2 * HALF : work_rows],
            grad_padded[work_rows : work_rows + HALF] + from_next,
        ],
        axis=0,
    )
    grad_key_rows = rotate(
        grad_kv[:, :width].reshape(work_rows, heads_here, HD), cosine_table, -sine_table
    )
    grad_query_rows = rotate(grad_queries, cosine_table, -sine_table)
    grad_qkv = jnp.concatenate(
        [
            grad_query_rows.reshape(work_rows, width),
            grad_key_rows.reshape(work_rows, width),
            grad_kv[:, width:],
        ],
        axis=1,
    ).astype(BF16)
    grad_one = dot(grad_qkv, qkv_matrix, (1, 1))
    grad_gain_one = jnp.sum(grad_one * unit_one, axis=0)
    gain_terms = jnp.stack([grad_gain_one, grad_gain_two], axis=1)
    gain_high = gain_terms.astype(BF16)
    gain_rest = (gain_terms - gain_high.astype(F32)).astype(BF16)
    gain_columns = padded_to_lanes(jnp.concatenate([gain_high, gain_rest], axis=1))
    share_a = summed_terms(ring, work_one, grad_qkv, grad_res_work, context, gain_columns)

    grad_one = grad_one.astype(BF16)
    one_other = pair_swap(other_rows(grad_one, row_count))
    grad_low_one = own_rows(grad_one, row_count).astype(F32) + one_other.astype(F32)
    grad_tokens = (
        own_rows(grad_residual, row_count)
        + norm_back(
            grad_low_one,
            gain_one,
            own_rows(unit_one, row_count),
            own_rows(inverse_one, row_count),
        )
    ).astype(BF16)

    share_gains = share_a[:, 4 * width : 4 * width + 2] + share_a[:, 4 * width + 2 : 4 * width + 4]
    share_gain_one = share_gains[:, 0]
    share_gain_one = share_gain_one + pair_swap(share_gain_one)
    return (
        output,
        grad_tokens,
        share_gain_one,
        share_a[:, : 3 * width].reshape(depth, 3, width),
        share_a[:, 3 * width : 4 * width].T,
        share_gains[:, 1],
        jnp.stack([share_b[:, :units], share_b[:, units_pad : units_pad + units]], axis=1),
        share_b[:, 2 * units_pad : 2 * units_pad + units].T,
    )


def solution(mesh):
    return jax.shard_map(
        local,
        mesh=mesh,
        in_specs=(
            P((SEQ, PAIR), None),
            P(SEQ),
            P(SEQ, None, PAIR),
            P(PAIR, SEQ),
            P(SEQ),
            P(SEQ, None, PAIR),
            P(PAIR, SEQ),
            P((SEQ, PAIR), None),
        ),
        out_specs=(
            P((SEQ, PAIR), None),
            P((SEQ, PAIR), None),
            P(SEQ),
            P(SEQ, None, PAIR),
            P(PAIR, SEQ),
            P(SEQ),
            P(SEQ, None, PAIR),
            P(PAIR, SEQ),
        ),
        check_vma=False,
    )
```

profile of v0, /device:TPU:0, one launch (start us, length us, event | category | flops | bytes accessed | tf_op | source)
XLA Modules:
  0.0 284.5 jit_solution(8032773835444037753)
XLA Ops:
  3.3 3.1 %collective-permute-start.1 = (bf16[64,2176]{1,0:T(8,128)(2,1)S(1)}, bf16[64,2176]{1,0:T(8,128)(2,1)S(1)}, u32[]{:S(2)}, u32[]{:S(2)}) collective-permute-start(bf16[64,2176]{1,0:T(8,128)(2,1)S(1)} %fusion.69.refs_3_), channel_id=1, source_target_pairs={{0,8},{2,10},{4,0},{6,2},{8,16},{10,18},{12,4},{14,6},{16,24},{18,... | collective-permute-start | bytes 835592 | tf_op jit(solution)/shard_map/ppermute | solution.py:63
  6.4 1.9 collective-permute-start
  9.1 1.6 collective-permute-start.20
  14.3 1.7 collective-permute-start.2
  16.4 14.3 %collective-permute-done.2.refs_1_ = bf16[64,2176]{1,0:T(8,128)(2,1)} collective-permute-done((bf16[64,2176]{1,0:T(8,128)(2,1)S(1)}, bf16[64,2176]{1,0:T(8,128)(2,1)}, u32[]{:S(2)}, u32[]{:S(2)}) %collective-permute-start.2) | collective-permute-done | bytes 278560 | tf_op jit(solution)/shard_map/ppermute | solution.py:63
  30.7 1.8 collective-permute-start.3
  33.5 1.7 collective-permute-start.6
  35.4 3.3 %collective-permute-done.3.refs_0_ = bf16[64,2176]{1,0:T(8,128)(2,1)S(1)} collective-permute-done((bf16[64,2176]{1,0:T(8,128)(2,1)}, bf16[64,2176]{1,0:T(8,128)(2,1)S(1)}, u32[]{:S(2)}, u32[]{:S(2)}) %collective-permute-start.3) | collective-permute-done | bytes 278560 | tf_op jit(solution)/shard_map/ppermute | solution.py:63
  38.8 1.5 collective-permute-start.7
  40.3 11.8 %collective-permute-done.6.refs_6_ = bf16[64,2176]{1,0:T(8,128)(2,1)S(1)} collective-permute-done((bf16[64,2176]{1,0:T(8,128)(2,1)}, bf16[64,2176]{1,0:T(8,128)(2,1)S(1)}, u32[]{:S(2)}, u32[]{:S(2)}) %collective-permute-start.6) | collective-permute-done | bytes 278560 | tf_op jit(solution)/shard_map/ppermute | solution.py:63
  52.7 5.5 %collective-permute-done.8 = bf16[32,2176]{1,0:T(8,128)(2,1)S(1)} collective-permute-done((bf16[32,2176]{1,0:T(8,128)(2,1)S(1)}, bf16[32,2176]{1,0:T(8,128)(2,1)S(1)}, u32[]{:S(2)}, u32[]{:S(2)}) %collective-permute-start.8) | collective-permute-done | bytes 139296 | tf_op jit(solution)/shard_map/ppermute | solution.py:63
  61.2 1.5 collective-permute-start.37
  62.7 1.6 collective-permute-start.21
  65.7 1.9 shard_map.197
  76.1 3.0 %collective-permute-start.17 = (bf16[64,1024]{1,0:T(8,128)(2,1)S(1)}, bf16[64,1024]{1,0:T(8,128)(2,1)S(1)}, u32[]{:S(2)}, u32[]{:S(2)}) collective-permute-start(bf16[64,1024]{1,0:T(8,128)(2,1)S(1)} %get-tuple-element.91), channel_id=1, source_target_pairs={{0,2},{2,4},{4,6},{6,8},{8,10},{10,12},{12,14},{14,16},{16,18},{18... | collective-permute-start | bytes 393224 | tf_op jit(solution)/shard_map/ppermute | solution.py:27
  82.4 1.6 collective-permute-start.22
  86.6 1.9 copy.74
  88.5 3.9 %fusion.96 = (f32[8,256]{1,0:T(8,128)S(1)}, f32[8,256,384]{2,1,0:T(8,128)}) fusion(pred[256,384]{1,0:T(8,128)(4,1)} %fusion.66, bf16[384,8,64]{0,2,1:T(8,128)(2,1)} %bitcast.130, bf16[256,8,32]{0,2,1:T(8,128)(2,1)S(1)} %copy-done.36, bf16[256,8,32]{0,2,1:T(8,128)(2,1)S(1)} %copy-done.34), kind=kOutput, calls=%fused_computation.238 | convolution fusion | flops 104333696 | bytes 3907584 | tf_op jit(solution)/shard_map/sub | solution.py:356
  92.5 1.9 copy.72
  94.4 3.4 %convolution_convert_fusion.1 = bf16[8,64,256]{2,1,0:T(8,128)(2,1)} fusion(bf16[384,8,64]{0,2,1:T(8,128)(2,1)} %bitcast.138, f32[8,256,384]{2,1,0:T(8,128)} %get-tuple-element.109, f32[8,256]{1,0:T(8,128)S(1)} %get-tuple-element.108), kind=kOutput, calls=%fused_computation.66 | convolution fusion | flops 102367232 | bytes 3809280 | tf_op jit(solution)/shard_map/hqk,khd->qhd/dot_general | solution.py:359
  99.0 1.5 collective-permute-start.26
  100.4 1.8 convolution_convert_fusion
  102.3 5.2 %collective-permute-done.26 = bf16[32,4224]{1,0:T(8,128)(2,1)S(1)} collective-permute-done((bf16[32,4224]{1,0:T(8,128)(2,1)S(1)}, bf16[32,4224]{1,0:T(8,128)(2,1)S(1)}, u32[]{:S(2)}, u32[]{:S(2)}) %collective-permute-start.26) | collective-permute-done | bytes 270368 | tf_op jit(solution)/shard_map/ppermute | solution.py:63
  107.6 1.7 collective-permute-start.27
  109.3 6.0 %collective-permute-done.27 = bf16[32,4224]{1,0:T(8,128)(2,1)S(1)} collective-permute-done((bf16[32,4224]{1,0:T(8,128)(2,1)S(1)}, bf16[32,4224]{1,0:T(8,128)(2,1)S(1)}, u32[]{:S(2)}, u32[]{:S(2)}) %collective-permute-start.27) | collective-permute-done | bytes 270368 | tf_op jit(solution)/shard_map/ppermute | solution.py:63
  115.9 11.7 %collective-permute-done.19 = bf16[256,1024]{1,0:T(8,128)(2,1)S(1)} collective-permute-done((bf16[256,1024]{1,0:T(8,128)(2,1)S(1)}, bf16[256,1024]{1,0:T(8,128)(2,1)S(1)}, u32[]{:S(2)}, u32[]{:S(2)}) %collective-permute-start.19) | collective-permute-done | bytes 524320 | tf_op jit(solution)/shard_map/ppermute | solution.py:31
  131.8 2.7 shard_map.198
  134.5 1.7 fusion.3
  136.2 4.0 %add_convert_fusion = (bf16[256,1408]{1,0:T(8,128)(2,1)S(1)}, f32[256,1408]{1,0:T(8,128)S(1)}, f32[256,1408]{1,0:T(8,128)S(1)}) fusion(f32[256,2816]{1,0:T(8,128)S(1)} %fusion.3, bf16[1024,4224]{1,0:T(8,128)(2,1)S(1)} %shard_map.198, bf16[128,1024]{1,0:T(8,128)(2,1)S(1)} %copy-done.23, bf16[128,1024]{1,0:T(8,128)(2,1)S(1)} %copy-done.21), kind=kOutput, calls=%fused_computation.41 | convolution fusion | flops 765558784 | bytes 9895936 | tf_op jit(solution)/shard_map/dot_general | solution.py:295
  140.6 1.7 fusion.27
  143.4 5.0 %shard_map.200 = (bf16[8,64,4224]{2,1,0:T(8,128)(2,1)S(1)}, bf16[8,64,4224]{2,1,0:T(8,128)(2,1)S(1)}) custom-call(s32[8]{0:T(128)S(1)} %gather_fusion.1, s32[1]{0:T(128)} %bitcast.23.core, bf16[256,1024]{1,0:T(8,128)(2,1)S(1)} %multiply_convert_fusion.3.left_one, bf16[256,1024]{1,0:T(8,128)(2,1)S(1)} %copy-done.4, ...), custom_call_target="tpu_custom_call" | custom-call | flops 2214592512 | bytes 10813440 | tf_op jit(solution)/shard_map/pallas_call | solution.py:191
  148.4 2.0 copy-done.1
  151.7 1.7 slice.340
  157.5 1.5 fusion.89
  159.0 1.7 convolution_convert_fusion.2
  160.9 3.0 %multiply_reduce_fusion = (f32[8,256]{1,0:T(8,128)S(1)}, f32[8,256,384]{2,1,0:T(8,128)S(1)}) fusion(f32[8,256,384]{2,1,0:T(8,128)} %get-tuple-element.109, f32[8,256]{1,0:T(8,128)S(1)} %copy-done.52, bf16[256,8,64]{0,2,1:T(8,128)(2,1)S(1)} %bitcast.143, bf16[384,8,64]{0,2,1:T(8,128)(2,1)S(1)} %bitcast.139), kind=kOutput, calls=%fused_computation.8 | convolution fusion | flops 103020544 | bytes 6963200 | tf_op jit(solution)/shard_map/qhd,khd->hqk/dot_general | solution.py:390
  163.9 1.4 fusion.50
  167.9 1.4 copy.79
  169.4 2.1 collective-permute-start.39
  172.8 1.4 fusion.33
  179.7 3.9 %multiply_reduce_fusion.2 = (f32[1024]{0:T(1024)S(1)}, bf16[256,1024]{1,0:T(8,128)(2,1)S(1)}, f32[256,1024]{1,0:T(8,128)}) fusion(f32[256]{0:T(256)S(1)} %copy-done.54, f32[256]{0:T(256)S(1)} %copy-done.50, bf16[128,1024]{1,0:T(8,128)(2,1)S(1)} %copy-done.17, bf16[128,1024]{1,0:T(8,128)(2,1)S(1)} %copy-done.14, bf16[1024,2176]{1,0:T(8,128)(2,1)} %copy-done, ...), kind=kOutput, calls=%fused_computation.92 | convolution fusion | flops 810023936 | bytes 6035456 | tf_op jit(solution)/shard_map/dot_general | solution.py:295
  186.8 3.7 %shard_map.199 = (bf16[8,64,2176]{2,1,0:T(8,128)(2,1)S(1)}, bf16[8,64,2176]{2,1,0:T(8,128)(2,1)S(1)}) custom-call(s32[8]{0:T(128)S(1)} %gather_fusion.1, s32[1]{0:T(128)} %bitcast.23.core, bf16[256,1024]{1,0:T(8,128)(2,1)S(1)} %copy-done.3, bf16[256,1024]{1,0:T(8,128)(2,1)S(1)} %get-tuple-element.49.left_two, ...), custom_call_target="tpu_custom_call" | custom-call | flops 1140850688 | bytes 5570560 | tf_op jit(solution)/shard_map/pallas_call | solution.py:191
  190.6 3.3 %collective-permute-start.43 = (bf16[3,64,2176]{2,1,0:T(8,128)(2,1)S(1)}, bf16[3,64,2176]{2,1,0:T(8,128)(2,1)S(1)}, u32[]{:S(2)}, u32[]{:S(2)}) collective-permute-start(bf16[3,64,2176]{2,1,0:T(8,128)(2,1)S(1)} %slice.319), channel_id=1, source_target_pairs={{0,2},{2,0},{4,6},{6,4},{8,10},{10,8},{12,14},{14,12},{16,18},{18,... | collective-permute-start | bytes 2506760 | tf_op jit(solution)/shard_map/ppermute | solution.py:63
  193.9 1.8 add_convert_fusion.4
  198.2 1.6 collective-permute-start.44
  201.5 2.6 collective-permute-done.44
  205.5 1.6 collective-permute-start.45
  207.8 1.4 collective-permute-start.59
  209.2 5.9 %collective-permute-done.45 = bf16[64,2176]{1,0:T(8,128)(2,1)S(1)} collective-permute-done((bf16[64,2176]{1,0:T(8,128)(2,1)S(1)}, bf16[64,2176]{1,0:T(8,128)(2,1)S(1)}, u32[]{:S(2)}, u32[]{:S(2)}) %collective-permute-start.45) | collective-permute-done | bytes 278560 | tf_op jit(solution)/shard_map/ppermute | solution.py:63
  215.8 1.5 collective-permute-start.46
  217.3 3.6 %collective-permute-done.55 = bf16[32,4224]{1,0:T(8,128)(2,1)S(1)} collective-permute-done((bf16[32,4224]{1,0:T(8,128)(2,1)S(1)}, bf16[32,4224]{1,0:T(8,128)(2,1)S(1)}, u32[]{:S(2)}, u32[]{:S(2)}) %collective-permute-start.55) | collective-permute-done | bytes 270368 | tf_op jit(solution)/shard_map/ppermute | solution.py:63
  220.9 1.6 fusion.37
  222.6 1.6 collective-permute-start.56
  224.7 2.3 collective-permute-done.46
  227.8 1.5 collective-permute-start.47
  229.2 9.3 %collective-permute-done.56 = bf16[64,4224]{1,0:T(8,128)(2,1)S(1)} collective-permute-done((bf16[64,4224]{1,0:T(8,128)(2,1)S(1)}, bf16[64,4224]{1,0:T(8,128)(2,1)S(1)}, u32[]{:S(2)}, u32[]{:S(2)}) %collective-permute-start.56) | collective-permute-done | bytes 540704 | tf_op jit(solution)/shard_map/ppermute | solution.py:63
  238.5 1.3 fusion.38
  239.8 1.6 collective-permute-start.57
  242.1 12.0 %collective-permute-done.57 = bf16[64,4224]{1,0:T(8,128)(2,1)S(1)} collective-permute-done((bf16[64,4224]{1,0:T(8,128)(2,1)S(1)}, bf16[64,4224]{1,0:T(8,128)(2,1)S(1)}, u32[]{:S(2)}, u32[]{:S(2)}) %collective-permute-start.57) | collective-permute-done | bytes 540704 | tf_op jit(solution)/shard_map/ppermute | solution.py:63
  254.1 1.7 fusion.39
  258.0 10.1 %collective-permute-done.61 = bf16[64,4224]{1,0:T(8,128)(2,1)S(1)} collective-permute-done((bf16[64,4224]{1,0:T(8,128)(2,1)S(1)}, bf16[64,4224]{1,0:T(8,128)(2,1)S(1)}, u32[]{:S(2)}, u32[]{:S(2)}) %collective-permute-start.61) | collective-permute-done | bytes 540704 | tf_op jit(solution)/shard_map/ppermute | solution.py:63
  275.4 5.5 %collective-permute-done.62 = bf16[64,4224]{1,0:T(8,128)(2,1)S(1)} collective-permute-done((bf16[64,4224]{1,0:T(8,128)(2,1)S(1)}, bf16[64,4224]{1,0:T(8,128)(2,1)S(1)}, u32[]{:S(2)}, u32[]{:S(2)}) %collective-permute-start.62) | collective-permute-done | bytes 540704 | tf_op jit(solution)/shard_map/ppermute | solution.py:63
  280.9 1.3 fusion.40
  283.1 1.4 copy.86
  (324 shorter events, 72.3 us)
Async XLA Ops:
  3.3 11.0 %collective-permute-start.1 = (bf16[64,2176]{1,0:T(8,128)(2,1)S(1)}, bf16[64,2176]{1,0:T(8,128)(2,1)S(1)}, u32[]{:S(2)}, u32[]{:S(2)}) collective-permute-start(bf16[64,2176]{1,0:T(8,128)(2,1)S(1)} %fusion.69.refs_3_), channel_id=1, source_target_pairs={{0,8},{2,10},{4,0},{6,2},{8,16},{10,18},{12,4},{14,6},{16,24},{18,... | collective-permute-start | bytes 835592 | tf_op jit(solution)/shard_map/ppermute | solution.py:63
  6.4 9.5 %collective-permute-start.4 = (bf16[64,2176]{1,0:T(8,128)(2,1)S(1)}, bf16[64,2176]{1,0:T(8,128)(2,1)S(1)}, u32[]{:S(2)}, u32[]{:S(2)}) collective-permute-start(bf16[64,2176]{1,0:T(8,128)(2,1)S(1)} %fusion.69.refs_3_), channel_id=1, source_target_pairs={{0,4},{2,6},{4,12},{6,14},{8,0},{10,2},{12,20},{14,22},{16,8},{18,... | collective-permute-start | bytes 835592 | tf_op jit(solution)/shard_map/ppermute | solution.py:63
  6.4 51.8 %collective-permute-start.12 = (bf16[64,2176]{1,0:T(8,128)(2,1)S(1)}, bf16[64,2176]{1,0:T(8,128)(2,1)S(1)}, u32[]{:S(2)}, u32[]{:S(2)}) collective-permute-start(bf16[64,2176]{1,0:T(8,128)(2,1)S(1)} %fusion.69.refs_3_), channel_id=1, source_target_pairs={{0,2},{2,0},{4,6},{6,4},{8,10},{10,8},{12,14},{14,12},{16,18},{18,... | collective-permute-start | bytes 835592 | tf_op jit(solution)/shard_map/ppermute | solution.py:63
  6.4 26.8 %collective-permute-start = (bf16[128,1024]{1,0:T(8,128)(2,1)}, bf16[128,1024]{1,0:T(8,128)(2,1)S(1)}, u32[]{:S(2)}, u32[]{:S(2)}) collective-permute-start(bf16[128,1024]{1,0:T(8,128)(2,1)} %param.14), channel_id=1, source_target_pairs={{0,1},{1,0},{2,3},{3,2},{4,5},{5,4},{6,7},{7,6},{8,9},{9,8},{10,11... | collective-permute-start | bytes 786440 | tf_op jit(solution)/shard_map/ppermute | solution.py:31
  9.1 49.8 %collective-permute-start.20 = (bf16[64,4224]{1,0:T(8,128)(2,1)S(1)}, bf16[64,4224]{1,0:T(8,128)(2,1)S(1)}, u32[]{:S(2)}, u32[]{:S(2)}) collective-permute-start(bf16[64,4224]{1,0:T(8,128)(2,1)S(1)} %fusion.62.refs_3_), channel_id=1, source_target_pairs={{0,8},{2,10},{4,0},{6,2},{8,16},{10,18},{12,4},{14,6},{16,24},{18,... | collective-permute-start | bytes 1622024 | tf_op jit(solution)/shard_map/ppermute | solution.py:63
  14.3 16.4 %collective-permute-start.2 = (bf16[64,2176]{1,0:T(8,128)(2,1)S(1)}, bf16[64,2176]{1,0:T(8,128)(2,1)}, u32[]{:S(2)}, u32[]{:S(2)}) collective-permute-start(bf16[64,2176]{1,0:T(8,128)(2,1)S(1)} %collective-permute-done.1.refs_2_), channel_id=1, source_target_pairs={{0,8},{2,10},{4,0},{6,2},{8,16},{10,18},{12,4},{14,6},{16,24},{18,... | collective-permute-start | bytes 835592 | tf_op jit(solution)/shard_map/ppermute | solution.py:63
  16.0 17.5 %collective-permute-start.5 = (bf16[64,2176]{1,0:T(8,128)(2,1)S(1)}, bf16[64,2176]{1,0:T(8,128)(2,1)}, u32[]{:S(2)}, u32[]{:S(2)}) collective-permute-start(bf16[64,2176]{1,0:T(8,128)(2,1)S(1)} %collective-permute-done.4.refs_4_), channel_id=1, source_target_pairs={{0,4},{2,6},{4,12},{6,14},{8,0},{10,2},{12,20},{14,22},{16,8},{18,... | collective-permute-start | bytes 835592 | tf_op jit(solution)/shard_map/ppermute | solution.py:63
  30.7 8.1 %collective-permute-start.3 = (bf16[64,2176]{1,0:T(8,128)(2,1)}, bf16[64,2176]{1,0:T(8,128)(2,1)S(1)}, u32[]{:S(2)}, u32[]{:S(2)}) collective-permute-start(bf16[64,2176]{1,0:T(8,128)(2,1)} %collective-permute-done.2.refs_1_), channel_id=1, source_target_pairs={{0,8},{2,10},{4,0},{6,2},{8,16},{10,18},{12,4},{14,6},{16,24},{18,... | collective-permute-start | bytes 835592 | tf_op jit(solution)/shard_map/ppermute | solution.py:63
  33.2 25.8 %collective-permute-start.23 = (bf16[64,4224]{1,0:T(8,128)(2,1)S(1)}, bf16[64,4224]{1,0:T(8,128)(2,1)S(1)}, u32[]{:S(2)}, u32[]{:S(2)}) collective-permute-start(bf16[64,4224]{1,0:T(8,128)(2,1)S(1)} %fusion.62.refs_3_), channel_id=1, source_target_pairs={{0,4},{2,6},{4,12},{6,14},{8,0},{10,2},{12,20},{14,22},{16,8},{18,... | collective-permute-start | bytes 1622024 | tf_op jit(solution)/shard_map/ppermute | solution.py:63
  33.5 18.6 %collective-permute-start.6 = (bf16[64,2176]{1,0:T(8,128)(2,1)}, bf16[64,2176]{1,0:T(8,128)(2,1)S(1)}, u32[]{:S(2)}, u32[]{:S(2)}) collective-permute-start(bf16[64,2176]{1,0:T(8,128)(2,1)} %collective-permute-done.5.refs_5_), channel_id=1, source_target_pairs={{0,4},{2,6},{4,12},{6,14},{8,0},{10,2},{12,20},{14,22},{16,8},{18,... | collective-permute-start | bytes 835592 | tf_op jit(solution)/shard_map/ppermute | solution.py:63
  35.3 32.8 %copy-start.12 = (bf16[128,1024]{1,0:T(8,128)(2,1)}, bf16[128,1024]{1,0:T(8,128)(2,1)S(1)}, u32[]{:S(2)}) copy-start(bf16[128,1024]{1,0:T(8,128)(2,1)S(1)} %get-tuple-element.93) | copy-start | bytes 786436
  38.8 13.4 %collective-permute-start.7 = (bf16[32,2176]{1,0:T(8,128)(2,1)S(1)}, bf16[32,2176]{1,0:T(8,128)(2,1)S(1)}, u32[]{:S(2)}, u32[]{:S(2)}) collective-permute-start(bf16[32,2176]{1,0:T(8,128)(2,1)S(1)} %slice.368), channel_id=1, source_target_pairs={{0,8},{2,10},{4,0},{6,2},{8,16},{10,18},{12,4},{14,6},{16,24},{18,... | collective-permute-start | bytes 417800 | tf_op jit(solution)/shard_map/ppermute | solution.py:63
  52.1 7.3 %collective-permute-start.11 = (bf16[64,2176]{1,0:T(8,128)(2,1)S(1)}, bf16[64,2176]{1,0:T(8,128)(2,1)S(1)}, u32[]{:S(2)}, u32[]{:S(2)}) collective-permute-start(bf16[64,2176]{1,0:T(8,128)(2,1)S(1)} %collective-permute-done.1.refs_2_), channel_id=1, source_target_pairs={{0,2},{2,0},{4,6},{6,4},{8,10},{10,8},{12,14},{14,12},{16,18},{18,... | collective-permute-start | bytes 835592 | tf_op jit(solution)/shard_map/ppermute | solution.py:63
  52.1 6.1 %collective-permute-start.8 = (bf16[32,2176]{1,0:T(8,128)(2,1)S(1)}, bf16[32,2176]{1,0:T(8,128)(2,1)S(1)}, u32[]{:S(2)}, u32[]{:S(2)}) collective-permute-start(bf16[32,2176]{1,0:T(8,128)(2,1)S(1)} %slice.369), channel_id=1, source_target_pairs={{0,4},{2,6},{4,12},{6,14},{8,0},{10,2},{12,20},{14,22},{16,8},{18,... | collective-permute-start | bytes 417800 | tf_op jit(solution)/shard_map/ppermute | solution.py:63
  58.3 1.6 collective-permute-start.13
  58.3 2.1 collective-permute-start.10
  58.9 2.3 collective-permute-start.14
  59.0 3.8 %collective-permute-start.9 = (bf16[64,2176]{1,0:T(8,128)(2,1)S(1)}, bf16[64,2176]{1,0:T(8,128)(2,1)S(1)}, u32[]{:S(2)}, u32[]{:S(2)}) collective-permute-start(bf16[64,2176]{1,0:T(8,128)(2,1)S(1)} %collective-permute-done.3.refs_0_), channel_id=1, source_target_pairs={{0,2},{2,0},{4,6},{6,4},{8,10},{10,8},{12,14},{14,12},{16,18},{18,... | collective-permute-start | bytes 835592 | tf_op jit(solution)/shard_map/ppermute | solution.py:63
  59.4 4.9 %collective-permute-start.15 = (bf16[64,2176]{1,0:T(8,128)(2,1)S(1)}, bf16[64,2176]{1,0:T(8,128)(2,1)S(1)}, u32[]{:S(2)}, u32[]{:S(2)}) collective-permute-start(bf16[64,2176]{1,0:T(8,128)(2,1)S(1)} %collective-permute-done.6.refs_6_), channel_id=1, source_target_pairs={{0,2},{2,0},{4,6},{6,4},{8,10},{10,8},{12,14},{14,12},{16,18},{18,... | collective-permute-start | bytes 835592 | tf_op jit(solution)/shard_map/ppermute | solution.py:63
  59.8 4.9 %collective-permute-start.16 = (bf16[64,2176]{1,0:T(8,128)(2,1)S(1)}, bf16[64,2176]{1,0:T(8,128)(2,1)S(1)}, u32[]{:S(2)}, u32[]{:S(2)}) collective-permute-start(bf16[64,2176]{1,0:T(8,128)(2,1)S(1)} %constant_dynamic-update-slice_fusion.refs_7_), channel_id=1, source_target_pairs={{0,2},{2,0},{4,6},{6,4},{8,10},{10,8},{12,14},{14,12},{16,18},{18,... | collective-permute-start | bytes 835592 | tf_op jit(solution)/shard_map/ppermute | solution.py:63
  60.4 67.4 %collective-permute-start.31 = (bf16[64,4224]{1,0:T(8,128)(2,1)S(1)}, bf16[64,4224]{1,0:T(8,128)(2,1)S(1)}, u32[]{:S(2)}, u32[]{:S(2)}) collective-permute-start(bf16[64,4224]{1,0:T(8,128)(2,1)S(1)} %fusion.62.refs_3_), channel_id=1, source_target_pairs={{0,2},{2,0},{4,6},{6,4},{8,10},{10,8},{12,14},{14,12},{16,18},{18,... | collective-permute-start | bytes 1622024 | tf_op jit(solution)/shard_map/ppermute | solution.py:63
  61.2 14.9 %collective-permute-start.37 = (bf16[128,1024]{1,0:T(8,128)(2,1)}, bf16[128,1024]{1,0:T(8,128)(2,1)}, u32[]{:S(2)}, u32[]{:S(2)}) collective-permute-start(bf16[128,1024]{1,0:T(8,128)(2,1)} %param.21), channel_id=1, source_target_pairs={{0,1},{1,0},{2,3},{3,2},{4,5},{5,4},{6,7},{7,6},{8,9},{9,8},{10,11... | collective-permute-start | bytes 786440 | tf_op jit(solution)/shard_map/ppermute | solution.py:31
  62.7 19.1 %collective-permute-start.21 = (bf16[64,4224]{1,0:T(8,128)(2,1)S(1)}, bf16[64,4224]{1,0:T(8,128)(2,1)}, u32[]{:S(2)}, u32[]{:S(2)}) collective-permute-start(bf16[64,4224]{1,0:T(8,128)(2,1)S(1)} %collective-permute-done.20.refs_2_), channel_id=1, source_target_pairs={{0,8},{2,10},{4,0},{6,2},{8,16},{10,18},{12,4},{14,6},{16,24},{18,... | collective-permute-start | bytes 1622024 | tf_op jit(solution)/shard_map/ppermute | solution.py:63
  64.3 18.0 %collective-permute-start.24 = (bf16[64,4224]{1,0:T(8,128)(2,1)S(1)}, bf16[64,4224]{1,0:T(8,128)(2,1)}, u32[]{:S(2)}, u32[]{:S(2)}) collective-permute-start(bf16[64,4224]{1,0:T(8,128)(2,1)S(1)} %collective-permute-done.23.refs_4_), channel_id=1, source_target_pairs={{0,4},{2,6},{4,12},{6,14},{8,0},{10,2},{12,20},{14,22},{16,8},{18,... | collective-permute-start | bytes 1622024 | tf_op jit(solution)/shard_map/ppermute | solution.py:63
  74.8 7.6 %collective-permute-start.18 = (bf16[64,1024]{1,0:T(8,128)(2,1)S(1)}, bf16[64,1024]{1,0:T(8,128)(2,1)S(1)}, u32[]{:S(2)}, u32[]{:S(2)}) collective-permute-start(bf16[64,1024]{1,0:T(8,128)(2,1)S(1)} %get-tuple-element.92), channel_id=1, source_target_pairs={{2,0},{4,2},{6,4},{8,6},{10,8},{12,10},{14,12},{16,14},{18,16},{20... | collective-permute-start | bytes 393224 | tf_op jit(solution)/shard_map/ppermute | solution.py:27
  76.1 7.8 %collective-permute-start.17 = (bf16[64,1024]{1,0:T(8,128)(2,1)S(1)}, bf16[64,1024]{1,0:T(8,128)(2,1)S(1)}, u32[]{:S(2)}, u32[]{:S(2)}) collective-permute-start(bf16[64,1024]{1,0:T(8,128)(2,1)S(1)} %get-tuple-element.91), channel_id=1, source_target_pairs={{0,2},{2,4},{4,6},{6,8},{8,10},{10,12},{12,14},{14,16},{16,18},{18... | collective-permute-start | bytes 393224 | tf_op jit(solution)/shard_map/ppermute | solution.py:27
  81.8 46.6 %collective-permute-start.30 = (bf16[64,4224]{1,0:T(8,128)(2,1)S(1)}, bf16[64,4224]{1,0:T(8,128)(2,1)}, u32[]{:S(2)}, u32[]{:S(2)}) collective-permute-start(bf16[64,4224]{1,0:T(8,128)(2,1)S(1)} %collective-permute-done.20.refs_2_), channel_id=1, source_target_pairs={{0,2},{2,0},{4,6},{6,4},{8,10},{10,8},{12,14},{14,12},{16,18},{18,... | collective-permute-start | bytes 1622024 | tf_op jit(solution)/shard_map/ppermute | solution.py:63
  82.3 46.2 %collective-permute-start.32 = (bf16[64,4224]{1,0:T(8,128)(2,1)S(1)}, bf16[64,4224]{1,0:T(8,128)(2,1)}, u32[]{:S(2)}, u32[]{:S(2)}) collective-permute-start(bf16[64,4224]{1,0:T(8,128)(2,1)S(1)} %collective-permute-done.23.refs_4_), channel_id=1, source_target_pairs={{0,2},{2,0},{4,6},{6,4},{8,10},{10,8},{12,14},{14,12},{16,18},{18,... | collective-permute-start | bytes 1622024 | tf_op jit(solution)/shard_map/ppermute | solution.py:63
  82.4 16.5 %collective-permute-start.22 = (bf16[64,4224]{1,0:T(8,128)(2,1)}, bf16[64,4224]{1,0:T(8,128)(2,1)S(1)}, u32[]{:S(2)}, u32[]{:S(2)}) collective-permute-start(bf16[64,4224]{1,0:T(8,128)(2,1)} %collective-permute-done.21.refs_1_), channel_id=1, source_target_pairs={{0,8},{2,10},{4,0},{6,2},{8,16},{10,18},{12,4},{14,6},{16,24},{18,... | collective-permute-start | bytes 1622024 | tf_op jit(solution)/shard_map/ppermute | solution.py:63
  84.0 18.2 %collective-permute-start.25 = (bf16[64,4224]{1,0:T(8,128)(2,1)}, bf16[64,4224]{1,0:T(8,128)(2,1)S(1)}, u32[]{:S(2)}, u32[]{:S(2)}) collective-permute-start(bf16[64,4224]{1,0:T(8,128)(2,1)} %collective-permute-done.24.refs_5_), channel_id=1, source_target_pairs={{0,4},{2,6},{4,12},{6,14},{8,0},{10,2},{12,20},{14,22},{16,8},{18,... | collective-permute-start | bytes 1622024 | tf_op jit(solution)/shard_map/ppermute | solution.py:63
  99.0 8.6 %collective-permute-start.26 = (bf16[32,4224]{1,0:T(8,128)(2,1)S(1)}, bf16[32,4224]{1,0:T(8,128)(2,1)S(1)}, u32[]{:S(2)}, u32[]{:S(2)}) collective-permute-start(bf16[32,4224]{1,0:T(8,128)(2,1)S(1)} %slice.384), channel_id=1, source_target_pairs={{0,8},{2,10},{4,0},{6,2},{8,16},{10,18},{12,4},{14,6},{16,24},{18,... | collective-permute-start | bytes 811016 | tf_op jit(solution)/shard_map/ppermute | solution.py:63
  102.2 27.2 %collective-permute-start.29 = (bf16[64,4224]{1,0:T(8,128)(2,1)}, bf16[64,4224]{1,0:T(8,128)(2,1)S(1)}, u32[]{:S(2)}, u32[]{:S(2)}) collective-permute-start(bf16[64,4224]{1,0:T(8,128)(2,1)} %collective-permute-done.21.refs_1_), channel_id=1, source_target_pairs={{0,2},{2,0},{4,6},{6,4},{8,10},{10,8},{12,14},{14,12},{16,18},{18,... | collective-permute-start | bytes 1622024 | tf_op jit(solution)/shard_map/ppermute | solution.py:63
  107.6 7.7 %collective-permute-start.27 = (bf16[32,4224]{1,0:T(8,128)(2,1)S(1)}, bf16[32,4224]{1,0:T(8,128)(2,1)S(1)}, u32[]{:S(2)}, u32[]{:S(2)}) collective-permute-start(bf16[32,4224]{1,0:T(8,128)(2,1)S(1)} %slice.385), channel_id=1, source_target_pairs={{0,4},{2,6},{4,12},{6,14},{8,0},{10,2},{12,20},{14,22},{16,8},{18,... | collective-permute-start | bytes 811016 | tf_op jit(solution)/shard_map/ppermute | solution.py:63
  115.3 12.2 %collective-permute-start.19 = (bf16[256,1024]{1,0:T(8,128)(2,1)S(1)}, bf16[256,1024]{1,0:T(8,128)(2,1)S(1)}, u32[]{:S(2)}, u32[]{:S(2)}) collective-permute-start(bf16[256,1024]{1,0:T(8,128)(2,1)S(1)} %convolution_convert_fusion), channel_id=1, source_target_pairs={{0,1},{1,0},{2,3},{3,2},{4,5},{5,4},{6,7},{7,6},{8,9},{9,8},{10,11... | collective-permute-start | bytes 1572872 | tf_op jit(solution)/shard_map/ppermute | solution.py:31
  127.5 2.1 collective-permute-start.33
  127.9 2.4 collective-permute-start.28
  128.4 2.6 collective-permute-start.34
  128.5 3.3 %collective-permute-start.35 = (bf16[64,4224]{1,0:T(8,128)(2,1)S(1)}, bf16[64,4224]{1,0:T(8,128)(2,1)S(1)}, u32[]{:S(2)}, u32[]{:S(2)}) collective-permute-start(bf16[64,4224]{1,0:T(8,128)(2,1)S(1)} %constant_dynamic-update-slice_fusion.2.refs_7_), channel_id=1, source_target_pairs={{0,2},{2,0},{4,6},{6,4},{8,10},{10,8},{12,14},{14,12},{16,18},{18,... | collective-permute-start | bytes 1622024 | tf_op jit(solution)/shard_map/ppermute | solution.py:63
  142.4 14.5 %collective-permute-start.38 = (bf16[256,1024]{1,0:T(8,128)(2,1)S(1)}, bf16[256,1024]{1,0:T(8,128)(2,1)S(1)}, u32[]{:S(2)}, u32[]{:S(2)}) collective-permute-start(bf16[256,1024]{1,0:T(8,128)(2,1)S(1)} %fusion.27), channel_id=1, source_target_pairs={{0,1},{1,0},{2,3},{3,2},{4,5},{5,4},{6,7},{7,6},{8,9},{9,8},{10,11... | collective-permute-start | bytes 1572872 | tf_op jit(solution)/shard_map/ppermute | solution.py:31
  155.3 38.7 %collective-permute-start.36 = (bf16[128,1024]{1,0:T(8,128)(2,1)}, bf16[128,1024]{1,0:T(8,128)(2,1)}, u32[]{:S(2)}, u32[]{:S(2)}) collective-permute-start(bf16[128,1024]{1,0:T(8,128)(2,1)} %constant_dynamic-slice_fusion.1), channel_id=1, source_target_pairs={{0,1},{1,0},{2,3},{3,2},{4,5},{5,4},{6,7},{7,6},{8,9},{9,8},{10,11... | collective-permute-start | bytes 786440 | tf_op jit(solution)/shard_map/ppermute | solution.py:31
  156.4 43.8 %collective-permute-start.54 = (bf16[3,64,4224]{2,1,0:T(8,128)(2,1)}, bf16[3,64,4224]{2,1,0:T(8,128)(2,1)}, u32[]{:S(2)}, u32[]{:S(2)}) collective-permute-start(bf16[3,64,4224]{2,1,0:T(8,128)(2,1)} %slice.347), channel_id=1, source_target_pairs={{0,2},{2,0},{4,6},{6,4},{8,10},{10,8},{12,14},{14,12},{16,18},{18,... | collective-permute-start | bytes 4866056 | tf_op jit(solution)/shard_map/ppermute | solution.py:63
  156.4 82.1 %collective-permute-start.53 = (bf16[5,64,4224]{2,1,0:T(8,128)(2,1)}, bf16[5,64,4224]{2,1,0:T(8,128)(2,1)}, u32[]{:S(2)}, u32[]{:S(2)}) collective-permute-start(bf16[5,64,4224]{2,1,0:T(8,128)(2,1)} %slice.340), channel_id=1, source_target_pairs={{0,2},{2,0},{4,6},{6,4},{8,10},{10,8},{12,14},{14,12},{16,18},{18,... | collective-permute-start | bytes 8110088 | tf_op jit(solution)/shard_map/ppermute | solution.py:63
  169.4 4.9 %collective-permute-start.39 = (bf16[64,1024]{1,0:T(8,128)(2,1)S(1)}, bf16[64,1024]{1,0:T(8,128)(2,1)S(1)}, u32[]{:S(2)}, u32[]{:S(2)}) collective-permute-start(bf16[64,1024]{1,0:T(8,128)(2,1)S(1)} %get-tuple-element.74), channel_id=1, source_target_pairs={{0,2},{2,4},{4,6},{6,8},{8,10},{10,12},{12,14},{14,16},{16,18},{18... | collective-permute-start | bytes 393224 | tf_op jit(solution)/shard_map/ppermute | solution.py:27
  171.5 3.9 %collective-permute-start.40 = (bf16[64,1024]{1,0:T(8,128)(2,1)S(1)}, bf16[64,1024]{1,0:T(8,128)(2,1)S(1)}, u32[]{:S(2)}, u32[]{:S(2)}) collective-permute-start(bf16[64,1024]{1,0:T(8,128)(2,1)S(1)} %get-tuple-element.75), channel_id=1, source_target_pairs={{2,0},{4,2},{6,4},{8,6},{10,8},{12,10},{14,12},{16,14},{18,16},{20... | collective-permute-start | bytes 393224 | tf_op jit(solution)/shard_map/ppermute | solution.py:27
  184.4 12.5 %collective-permute-start.41 = (bf16[128,1024]{1,0:T(8,128)(2,1)}, bf16[128,1024]{1,0:T(8,128)(2,1)S(1)}, u32[]{:S(2)}, u32[]{:S(2)}) collective-permute-start(bf16[128,1024]{1,0:T(8,128)(2,1)} %constant_dynamic-slice_fusion), channel_id=1, source_target_pairs={{0,1},{1,0},{2,3},{3,2},{4,5},{5,4},{6,7},{7,6},{8,9},{9,8},{10,11... | collective-permute-start | bytes 786440 | tf_op jit(solution)/shard_map/ppermute | solution.py:31
  190.6 7.5 %collective-permute-start.43 = (bf16[3,64,2176]{2,1,0:T(8,128)(2,1)S(1)}, bf16[3,64,2176]{2,1,0:T(8,128)(2,1)S(1)}, u32[]{:S(2)}, u32[]{:S(2)}) collective-permute-start(bf16[3,64,2176]{2,1,0:T(8,128)(2,1)S(1)} %slice.319), channel_id=1, source_target_pairs={{0,2},{2,0},{4,6},{6,4},{8,10},{10,8},{12,14},{14,12},{16,18},{18,... | collective-permute-start | bytes 2506760 | tf_op jit(solution)/shard_map/ppermute | solution.py:63
  195.8 19.9 %collective-permute-start.42 = (bf16[5,64,2176]{2,1,0:T(8,128)(2,1)S(1)}, bf16[5,64,2176]{2,1,0:T(8,128)(2,1)S(1)}, u32[]{:S(2)}, u32[]{:S(2)}) collective-permute-start(bf16[5,64,2176]{2,1,0:T(8,128)(2,1)S(1)} %slice.312), channel_id=1, source_target_pairs={{0,2},{2,0},{4,6},{6,4},{8,10},{10,8},{12,14},{14,12},{16,18},{18,... | collective-permute-start | bytes 4177928 | tf_op jit(solution)/shard_map/ppermute | solution.py:63
  198.2 5.9 %collective-permute-start.44 = (bf16[32,2176]{1,0:T(8,128)(2,1)S(1)}, bf16[32,2176]{1,0:T(8,128)(2,1)S(1)}, u32[]{:S(2)}, u32[]{:S(2)}) collective-permute-start(bf16[32,2176]{1,0:T(8,128)(2,1)S(1)} %get-tuple-element.97), channel_id=1, source_target_pairs={{0,8},{2,10},{4,0},{6,2},{8,16},{10,18},{12,4},{14,6},{16,24},{18,... | collective-permute-start | bytes 417800 | tf_op jit(solution)/shard_map/ppermute | solution.py:63
  199.8 5.5 %collective-permute-start.48 = (bf16[32,2176]{1,0:T(8,128)(2,1)S(1)}, bf16[32,2176]{1,0:T(8,128)(2,1)S(1)}, u32[]{:S(2)}, u32[]{:S(2)}) collective-permute-start(bf16[32,2176]{1,0:T(8,128)(2,1)S(1)} %get-tuple-element.98), channel_id=1, source_target_pairs={{0,4},{2,6},{4,12},{6,14},{8,0},{10,2},{12,20},{14,22},{16,8},{18,... | collective-permute-start | bytes 417800 | tf_op jit(solution)/shard_map/ppermute | solution.py:63
  205.5 9.6 %collective-permute-start.45 = (bf16[64,2176]{1,0:T(8,128)(2,1)S(1)}, bf16[64,2176]{1,0:T(8,128)(2,1)S(1)}, u32[]{:S(2)}, u32[]{:S(2)}) collective-permute-start(bf16[64,2176]{1,0:T(8,128)(2,1)S(1)} %get-tuple-element.63), channel_id=1, source_target_pairs={{0,8},{2,10},{4,0},{6,2},{8,16},{10,18},{12,4},{14,6},{16,24},{18,... | collective-permute-start | bytes 835592 | tf_op jit(solution)/shard_map/ppermute | solution.py:63
  207.1 13.8 %collective-permute-start.55 = (bf16[32,4224]{1,0:T(8,128)(2,1)S(1)}, bf16[32,4224]{1,0:T(8,128)(2,1)S(1)}, u32[]{:S(2)}, u32[]{:S(2)}) collective-permute-start(bf16[32,4224]{1,0:T(8,128)(2,1)S(1)} %get-tuple-element.86), channel_id=1, source_target_pairs={{0,8},{2,10},{4,0},{6,2},{8,16},{10,18},{12,4},{14,6},{16,24},{18,... | collective-permute-start | bytes 811016 | tf_op jit(solution)/shard_map/ppermute | solution.py:63
  207.8 13.2 %collective-permute-start.59 = (bf16[32,4224]{1,0:T(8,128)(2,1)S(1)}, bf16[32,4224]{1,0:T(8,128)(2,1)S(1)}, u32[]{:S(2)}, u32[]{:S(2)}) collective-permute-start(bf16[32,4224]{1,0:T(8,128)(2,1)S(1)} %get-tuple-element.87), channel_id=1, source_target_pairs={{0,4},{2,6},{4,12},{6,14},{8,0},{10,2},{12,20},{14,22},{16,8},{18,... | collective-permute-start | bytes 811016 | tf_op jit(solution)/shard_map/ppermute | solution.py:63
  215.2 9.5 %collective-permute-start.49 = (bf16[64,2176]{1,0:T(8,128)(2,1)S(1)}, bf16[64,2176]{1,0:T(8,128)(2,1)S(1)}, u32[]{:S(2)}, u32[]{:S(2)}) collective-permute-start(bf16[64,2176]{1,0:T(8,128)(2,1)S(1)} %get-tuple-element.64), channel_id=1, source_target_pairs={{0,4},{2,6},{4,12},{6,14},{8,0},{10,2},{12,20},{14,22},{16,8},{18,... | collective-permute-start | bytes 835592 | tf_op jit(solution)/shard_map/ppermute | solution.py:63
  215.8 11.1 %collective-permute-start.46 = (bf16[64,2176]{1,0:T(8,128)(2,1)S(1)}, bf16[64,2176]{1,0:T(8,128)(2,1)S(1)}, u32[]{:S(2)}, u32[]{:S(2)}) collective-permute-start(bf16[64,2176]{1,0:T(8,128)(2,1)S(1)} %fusion.57), channel_id=1, source_target_pairs={{0,8},{2,10},{4,0},{6,2},{8,16},{10,18},{12,4},{14,6},{16,24},{18,... | collective-permute-start | bytes 835592 | tf_op jit(solution)/shard_map/ppermute | solution.py:63
  222.6 15.9 %collective-permute-start.56 = (bf16[64,4224]{1,0:T(8,128)(2,1)S(1)}, bf16[64,4224]{1,0:T(8,128)(2,1)S(1)}, u32[]{:S(2)}, u32[]{:S(2)}) collective-permute-start(bf16[64,4224]{1,0:T(8,128)(2,1)S(1)} %get-tuple-element.57), channel_id=1, source_target_pairs={{0,8},{2,10},{4,0},{6,2},{8,16},{10,18},{12,4},{14,6},{16,24},{18,... | collective-permute-start | bytes 1622024 | tf_op jit(solution)/shard_map/ppermute | solution.py:63
  224.2 17.9 %collective-permute-start.60 = (bf16[64,4224]{1,0:T(8,128)(2,1)S(1)}, bf16[64,4224]{1,0:T(8,128)(2,1)S(1)}, u32[]{:S(2)}, u32[]{:S(2)}) collective-permute-start(bf16[64,4224]{1,0:T(8,128)(2,1)S(1)} %get-tuple-element.58), channel_id=1, source_target_pairs={{0,4},{2,6},{4,12},{6,14},{8,0},{10,2},{12,20},{14,22},{16,8},{18,... | collective-permute-start | bytes 1622024 | tf_op jit(solution)/shard_map/ppermute | solution.py:63
  227.1 14.3 %collective-permute-start.50 = (bf16[64,2176]{1,0:T(8,128)(2,1)S(1)}, bf16[64,2176]{1,0:T(8,128)(2,1)S(1)}, u32[]{:S(2)}, u32[]{:S(2)}) collective-permute-start(bf16[64,2176]{1,0:T(8,128)(2,1)S(1)} %get-tuple-element.62), channel_id=1, source_target_pairs={{0,4},{2,6},{4,12},{6,14},{8,0},{10,2},{12,20},{14,22},{16,8},{18,... | collective-permute-start | bytes 835592 | tf_op jit(solution)/shard_map/ppermute | solution.py:63
  227.8 28.9 %collective-permute-start.47 = (bf16[64,2176]{1,0:T(8,128)(2,1)S(1)}, bf16[64,2176]{1,0:T(8,128)(2,1)S(1)}, u32[]{:S(2)}, u32[]{:S(2)}) collective-permute-start(bf16[64,2176]{1,0:T(8,128)(2,1)S(1)} %get-tuple-element.61), channel_id=1, source_target_pairs={{0,8},{2,10},{4,0},{6,2},{8,16},{10,18},{12,4},{14,6},{16,24},{18,... | collective-permute-start | bytes 835592 | tf_op jit(solution)/shard_map/ppermute | solution.py:63
  239.8 14.3 %collective-permute-start.57 = (bf16[64,4224]{1,0:T(8,128)(2,1)S(1)}, bf16[64,4224]{1,0:T(8,128)(2,1)S(1)}, u32[]{:S(2)}, u32[]{:S(2)}) collective-permute-start(bf16[64,4224]{1,0:T(8,128)(2,1)S(1)} %fusion.38), channel_id=1, source_target_pairs={{0,8},{2,10},{4,0},{6,2},{8,16},{10,18},{12,4},{14,6},{16,24},{18,... | collective-permute-start | bytes 1622024 | tf_op jit(solution)/shard_map/ppermute | solution.py:63
  241.5 15.2 %collective-permute-start.51 = (bf16[64,2176]{1,0:T(8,128)(2,1)S(1)}, bf16[64,2176]{1,0:T(8,128)(2,1)S(1)}, u32[]{:S(2)}, u32[]{:S(2)}) collective-permute-start(bf16[64,2176]{1,0:T(8,128)(2,1)S(1)} %fusion.55), channel_id=1, source_target_pairs={{0,4},{2,6},{4,12},{6,14},{8,0},{10,2},{12,20},{14,22},{16,8},{18,... | collective-permute-start | bytes 835592 | tf_op jit(solution)/shard_map/ppermute | solution.py:63
  255.8 12.4 %collective-permute-start.61 = (bf16[64,4224]{1,0:T(8,128)(2,1)S(1)}, bf16[64,4224]{1,0:T(8,128)(2,1)S(1)}, u32[]{:S(2)}, u32[]{:S(2)}) collective-permute-start(bf16[64,4224]{1,0:T(8,128)(2,1)S(1)} %get-tuple-element.56), channel_id=1, source_target_pairs={{0,4},{2,6},{4,12},{6,14},{8,0},{10,2},{12,20},{14,22},{16,8},{18,... | collective-permute-start | bytes 1622024 | tf_op jit(solution)/shard_map/ppermute | solution.py:63
  256.8 18.6 %collective-permute-start.58 = (bf16[64,4224]{1,0:T(8,128)(2,1)S(1)}, bf16[64,4224]{1,0:T(8,128)(2,1)S(1)}, u32[]{:S(2)}, u32[]{:S(2)}) collective-permute-start(bf16[64,4224]{1,0:T(8,128)(2,1)S(1)} %get-tuple-element.55), channel_id=1, source_target_pairs={{0,8},{2,10},{4,0},{6,2},{8,16},{10,18},{12,4},{14,6},{16,24},{18,... | collective-permute-start | bytes 1622024 | tf_op jit(solution)/shard_map/ppermute | solution.py:63
  269.4 11.5 %collective-permute-start.62 = (bf16[64,4224]{1,0:T(8,128)(2,1)S(1)}, bf16[64,4224]{1,0:T(8,128)(2,1)S(1)}, u32[]{:S(2)}, u32[]{:S(2)}) collective-permute-start(bf16[64,4224]{1,0:T(8,128)(2,1)S(1)} %fusion.36), channel_id=1, source_target_pairs={{0,4},{2,6},{4,12},{6,14},{8,0},{10,2},{12,20},{14,22},{16,8},{18,... | collective-permute-start | bytes 1622024 | tf_op jit(solution)/shard_map/ppermute | solution.py:63
  271.4 3.5 %collective-permute-start.52 = (f32[64]{0:T(128)S(1)}, f32[64]{0:T(128)S(1)}, u32[]{:S(2)}, u32[]{:S(2)}) collective-permute-start(f32[64]{0:T(128)S(1)} %get-tuple-element.48), channel_id=1, source_target_pairs={{0,1},{1,0},{2,3},{3,2},{4,5},{5,4},{6,7},{7,6},{8,9},{9,8},{10,11... | collective-permute-start | bytes 776 | tf_op jit(solution)/shard_map/ppermute | solution.py:31
  (60 other events, 345.2 us)
where the time goes:
time: 286 us; the launch traced here: 285 us
  waiting for transfers between devices  116 us (41%)
  starting transfers between devices  61.1 us (21%)
  local copies, waits for them, and re-layouts  33.1 us (12%)
  matrix products  30.3 us (11%)
  other arithmetic  29 us (10%)
  Pallas kernels  13.2 us (5%)
    ppermute x52, waiting for transfers between devices, go(): return lax.ppermute(block, SEQ, route)  102 us
    ppermute x52, starting transfers between devices, go(): return lax.ppermute(block, SEQ, route)  45.7 us
    dot_general x8, matrix products, dot(): lax.dot_general(a, b, (((over[0],), (over[1],)), ((), ())), preferred_ele...  16.8 us
    ppermute x7, waiting for transfers between devices, pair_swap(): return lax.ppermute(block, PAIR, [(0, 1), (1, 0)])  12.6 us
    pallas_call x2, Pallas kernels, weight_terms(): pl.pallas_call(weight_kernel, grid_spec=pltpu.PrefetchScalarGridSpec(num_...  8.7 us
    ppermute x7, starting transfers between devices, pair_swap(): return lax.ppermute(block, PAIR, [(0, 1), (1, 0)])  7.74 us
    ppermute x4, starting transfers between devices, passed_along(): return lax.ppermute(block, axis, route)  7.68 us
    unnamed x125, local copies, waits for them, and re-layouts  7.13 us
  transfers between devices with their start and end apart: 63, of which 25 were waited for; matrix products, arithmetic and copies ran while one was open for 26% of the time, Pallas kernels for 4%

commit v1 on v0

v1 whole, which is shorter than its diff:
```python
import functools
import math

import jax
import jax.numpy as jnp
import numpy as np
from jax import lax
from jax.experimental import pallas as pl
from jax.experimental.pallas import tpu as pltpu
from jax.sharding import PartitionSpec as P

HD = 64
HALF = 64
LANES = 128

EPSILON = 1e-05
THETA = 10000.0
SEQ = "seq"
PAIR = "fsdp"
F32 = jnp.float32
BF16 = jnp.bfloat16


def passed_along(block, axis, distance):
    devices = range(lax.axis_size(axis))
    route = [(i - distance, i) for i in devices if i - distance in devices]
    return lax.ppermute(block, axis, route)


def pair_swap(block):
    return lax.ppermute(block, PAIR, [(0, 1), (1, 0)])


class Ring:
    def __init__(self, width):
        size = lax.axis_size(SEQ)
        self.chips = size // 2
        rows = self.chips // 2
        order = [2 * z for z in range(rows)] + [2 * z + 1 for z in reversed(range(rows))]
        place = np.argsort(np.array(order))
        self.up, self.down = [], []
        for i in range(size):
            chip, core = divmod(i, 2)
            self.up.append((i, order[(place[chip] + 1) % self.chips] * 2 + core))
            self.down.append((i, order[(place[chip] - 1) % self.chips] * 2 + core))
        self.swap = [(i, i ^ 1) for i in range(size)]
        me = lax.axis_index(SEQ)
        self.core = me % 2
        self.place = jnp.asarray(place, jnp.int32)[me // 2]
        self.order = jnp.asarray(order, jnp.int32)
        self.half = self.chips // 2
        self.slots = [self.half]
        for step in range(1, self.half):
            self.slots += [self.half + step, self.half - step]
        self.slots.append(0)
        self.short = width == LANES * self.chips

    def chips_at(self, distances):
        steps = jnp.asarray(distances, jnp.int32)
        return self.order[(self.place + steps + self.chips) % self.chips]

    def go(self, block, route, name):
        with jax.named_scope(name):
            return lax.ppermute(block, SEQ, route)

    def gather(self, block, name):
        if not self.short:
            whole = lax.all_gather(block, SEQ, axis=0, tiled=True)
            return [whole], jnp.zeros(1, jnp.int32)
        rows = block.shape[0]
        middle = rows // 2
        upward = downward = block
        got = {0: block}
        for step in range(1, self.half):
            upward = self.go(upward, self.up, f"{name}_up_{step}")
            downward = self.go(downward, self.down, f"{name}_down_{step}")
            upward, downward = yield upward, downward
            got[-step], got[step] = upward, downward
        low = self.go(upward[:middle], self.up, f"{name}_up_{self.half}")
        high = self.go(downward[middle:], self.down, f"{name}_down_{self.half}")
        got[self.half] = jnp.concatenate([low, high], axis=0)
        distances = sorted(got, key=abs)
        pieces = [got[d] for d in distances]
        others = [self.go(p, self.swap, f"{name}_cores_{d}") for d, p in zip(distances, pieces)]
        chips = self.chips_at(distances)
        starts = jnp.concatenate([chips * 2 + self.core, chips * 2 + 1 - self.core]) * rows
        return pieces + others, starts

    def scatter_sum(self, kept, away, name):
        rows = kept.shape[1]
        middle = rows // 2
        away = yield away
        early = 3
        came_first = self.go(away[:early], self.swap, f"{name}_cores_early")
        came_rest = self.go(away[early:], self.swap, f"{name}_cores_rest")

        def at(slot):
            i = self.slots.index(slot)
            came = came_first[i] if i < early else came_rest[i - early]
            return kept[i].astype(F32) + came.astype(F32)

        far = at(self.half).astype(BF16)
        upward, downward = far[:middle], far[middle:]
        for step in range(1, self.half):
            upward, downward = yield upward, downward
            more_up = self.go(upward, self.up, f"{name}_up_{step}").astype(F32)
            more_down = self.go(downward, self.down, f"{name}_down_{step}").astype(F32)
            if step == 1:
                more_up = jnp.pad(more_up, ((0, rows - middle), (0, 0)))
                more_down = jnp.pad(more_down, ((middle, 0), (0, 0)))
            upward = (at(self.half - step) + more_up).astype(BF16)
            downward = (at(self.half + step) + more_down).astype(BF16)
        upward, downward = yield upward, downward
        upward = self.go(upward, self.up, f"{name}_up_{self.half}")
        downward = self.go(downward, self.down, f"{name}_down_{self.half}")
        return at(0) + upward.astype(F32) + downward.astype(F32)


class Stepped:
    def __init__(self, steps):
        self.steps, self.state, self.result = steps, None, None
        self.advance()

    def advance(self):
        try:
            if self.state is not None:
                self.state = lax.optimization_barrier(self.state)
            self.state = self.steps.send(self.state)
        except StopIteration as end:
            self.steps, self.state, self.result = None, None, end.value

    def ride(self, value):
        if self.steps is not None:
            value, self.state = lax.optimization_barrier((value, self.state))
            self.advance()
        return value

    def step(self):
        if self.steps is not None:
            self.advance()

    def beside(self, other):
        if self.steps is not None and other.steps is not None:
            self.state, other.state = lax.optimization_barrier((self.state, other.state))
            self.advance()
            other.advance()

    def finish(self):
        while self.steps is not None:
            self.advance()
        return self.result


VMEM = pl.BlockSpec(memory_space=pltpu.VMEM)
ANY = pl.BlockSpec(memory_space=pl.ANY)
SMEM = pl.BlockSpec(memory_space=pltpu.SMEM)
MIB = 1024 * 1024


def shape_of(rows, columns, kind):
    return jax.ShapeDtypeStruct((rows, columns), kind)


def call(kernel, args, specs, outs, scratch=(), flops=0, moved=0, room=48):
    return pl.pallas_call(
        kernel,
        in_specs=specs,
        out_specs=[VMEM] * len(outs),
        out_shape=outs,
        scratch_shapes=list(scratch),
        compiler_params=pltpu.CompilerParams(vmem_limit_bytes=room * MIB),
        cost_estimate=pl.CostEstimate(flops=flops, bytes_accessed=moved, transcendentals=0),
    )(*args)


def placing(starts, pieces, whole, ready):
    copies = []
    for i, piece in enumerate(pieces):
        rows = piece.shape[0]
        start = pl.multiple_of(starts[i], rows)
        copies.append(
            pltpu.make_async_copy(piece, whole.at[pl.ds(start, rows), :], ready.at[i])
        )
    return copies


def lane_of(rows, width):
    return lax.broadcasted_iota(jnp.int32, (rows, width), 1)


def halves_swapped(values):
    width = values.shape[1]
    lane = lane_of(*values.shape)
    ahead = pltpu.roll(values, width - HD // 2, 1)
    behind = pltpu.roll(values, HD // 2, 1)
    return jnp.where(lane % HD < HD // 2, ahead, behind)


def turned_by(values, cosine, sine):
    copies = values.shape[1] // LANES
    cosine = jnp.concatenate([cosine] * copies, axis=1)
    sine = jnp.concatenate([sine] * copies, axis=1)
    return values * cosine + halves_swapped(values) * sine


def unit_of(values):
    average = jnp.mean(values, axis=-1, keepdims=True)
    centered = values - average
    inverse = lax.rsqrt(jnp.mean(centered * centered, axis=-1, keepdims=True) + EPSILON)
    return centered * inverse, inverse


def first_kernel(count, width, starts, tokens, cosine, sine, *refs):
    pieces = refs[:count]
    whole, matrix, gains, work, queries, keys_values, first, last, ready = refs[count:]
    copies = placing(starts, pieces, whole, ready)
    for copy in copies:
        copy.start()
    unit, _ = unit_of(tokens[...].astype(F32))
    for copy in copies:
        copy.wait()
    matrix[...] = whole[:, 3 * width : 4 * width]
    gains[...] = whole[:, 4 * width :].astype(F32).T[:8]
    work[...] = (unit * gains[0:1, :]).astype(BF16)
    rows = work.shape[0]
    for start in range(0, 3 * width, 256):
        part = dot(work[...], whole[:, start : start + 256])
        if start < 2 * width:
            part = turned_by(part, cosine[...], sine[...])
        part = part.astype(BF16)
        if start < width:
            queries[:, start : start + 256] = part
        else:
            at = slice(start - width, start - width + 256)
            keys_values[:, at] = part
            first[:, at] = part[:HALF]
            last[:, at] = part[rows - HALF :]


def window(seq, tile, tiles):
    row = lax.broadcasted_iota(jnp.int32, (2 * LANES, 2 * LANES), 0) % LANES
    column = lax.broadcasted_iota(jnp.int32, (2 * LANES, 2 * LANES), 1)
    ahead = column - row
    inside = (ahead >= 0) & (ahead <= 2 * HALF)
    if tile == 0:
        inside &= (seq[0] > 0) | (column >= HALF)
    if tile == tiles - 1:
        inside &= (seq[0] < seq[1] - 1) | (column < 2 * LANES - HALF)
    return inside


def heads_apart(pair):
    lane = lane_of(*pair.shape)
    zero = jnp.zeros_like(pair)
    return jnp.concatenate(
        [jnp.where(lane < HD, pair, zero), jnp.where(lane < HD, zero, pair)], axis=0
    )


def heads_joined(apart):
    rows = apart.shape[0] // 2
    return jnp.where(lane_of(rows, apart.shape[1]) < HD, apart[:rows], apart[rows:])


def shares_of(apart, keys, inside):
    scores = dot(apart, keys, (1, 1)) * (1.0 / math.sqrt(HD))
    scores = jnp.where(inside, scores, -1e30)
    expo = jnp.exp(scores - jnp.max(scores, axis=-1, keepdims=True))
    return expo / jnp.sum(expo, axis=-1, keepdims=True)


def joined_rows(before, own, after, whole):
    rows = own.shape[0]
    whole[:HALF] = before[...]
    whole[HALF : HALF + rows] = own[...]
    whole[HALF + rows :] = after[...]


def attend_kernel(seq, queries, own, before, after, matrix, context, term, keys_values):
    rows, width = queries.shape
    joined_rows(before, own, after, keys_values)
    tiles = rows // LANES
    for tile in range(tiles):
        inside = window(seq, tile, tiles)
        at = slice(tile * LANES, tile * LANES + LANES)
        reach = slice(tile * LANES, tile * LANES + 2 * LANES)
        for start in range(0, width, LANES):
            columns = slice(start, start + LANES)
            apart = heads_apart(queries[at, columns])
            shares = shares_of(apart, keys_values[reach, columns], inside)
            values = keys_values[reach, width + start : width + start + LANES]
            context[at, columns] = heads_joined(dot(shares.astype(BF16), values)).astype(BF16)
    term[...] = dot(context[...], matrix[...], (1, 1)).astype(BF16)


def hidden_kernel(count, starts, tokens, term, term_other, gains, cot, *refs):
    pieces = refs[:count]
    residual, work, hidden, grad_proj, grad_two, down, whole, ready = refs[count:]
    copies = placing(starts, pieces, whole, ready)
    for copy in copies:
        copy.start()
    added = term[...].astype(F32) + term_other[...].astype(F32)
    residual[...] = tokens[...].astype(F32) + added
    unit, _ = unit_of(residual[...])
    work[...] = (unit * gains[1:2, :]).astype(BF16)
    for copy in copies:
        copy.wait()
    units = hidden.shape[1]
    for start in range(0, units, 256):
        stop = min(units, start + 256)
        gate = dot(work[...], whole[:, start:stop])
        up = dot(work[...], whole[:, units + start : units + stop])
        back = dot(cot[...], whole[:, 2 * units + start : 2 * units + stop])
        share = 0.5 + 0.5 * lax.erf(gate * (1.0 / math.sqrt(2.0)))
        bell = jnp.exp(-0.5 * gate * gate) * (1.0 / math.sqrt(2.0 * math.pi))
        gelu = gate * share
        hidden[:, start:stop] = (gelu * up).astype(BF16)
        grad_proj[:, start:stop] = (back * up * (share + gate * bell)).astype(BF16)
        grad_proj[:, units + start : units + stop] = (back * gelu).astype(BF16)
    grad_two[...] = dot(grad_proj[...], whole[:, : 2 * units], (1, 1)).astype(BF16)
    down[...] = dot(hidden[...], whole[:, 2 * units :], (1, 1)).astype(BF16)


def attend_back_kernel(
    seq, residual, gains, grad_two, grad_two_other, cot, matrix, queries, own, before, after,
    cosine, sine, grad_residual, grad_low, gain_two, grad_queries, grad_own, to_before, to_after,
    keys_values, grad_all,
):
    rows, width = queries.shape
    joined_rows(before, own, after, keys_values)
    unit, inverse = unit_of(residual[...])
    grad = grad_two[...].astype(F32) + grad_two_other[...].astype(F32)
    gain_two[...] = jnp.broadcast_to(jnp.sum(grad * unit, axis=0, keepdims=True), gain_two.shape)
    scaled = grad * gains[1:2, :]
    middle = jnp.mean(scaled, axis=-1, keepdims=True)
    along = jnp.mean(scaled * unit, axis=-1, keepdims=True)
    total = cot[...].astype(F32) + inverse * (scaled - middle - unit * along)
    grad_residual[...] = total
    grad_low[...] = total.astype(BF16)
    grad_context = dot(grad_low[...], matrix[...]).astype(BF16)
    grad_all[...] = jnp.zeros_like(grad_all)
    scale = 1.0 / math.sqrt(HD)
    tiles = rows // LANES
    for tile in range(tiles):
        inside = window(seq, tile, tiles)
        at = slice(tile * LANES, tile * LANES + LANES)
        reach = slice(tile * LANES, tile * LANES + 2 * LANES)
        for start in range(0, width, LANES):
            columns = slice(start, start + LANES)
            beside = slice(width + start, width + start + LANES)
            apart = heads_apart(queries[at, columns])
            keys = keys_values[reach, columns]
            shares = shares_of(apart, keys, inside)
            grad_apart = heads_apart(grad_context[at, columns])
            grad_shares = dot(grad_apart, keys_values[reach, beside], (1, 1))
            lost = jnp.sum(grad_shares * shares, axis=-1, keepdims=True)
            grad_scores = (shares * (grad_shares - lost)).astype(BF16)
            grad_here = heads_joined(dot(grad_scores, keys)) * scale
            grad_queries[at, columns] = turned_by(grad_here, cosine[at], -sine[at]).astype(BF16)
            grad_all[reach, columns] += dot(grad_scores, apart, (0, 0)) * scale
            grad_all[reach, beside] += dot(shares.astype(BF16), grad_apart, (0, 0))
    to_before[...] = grad_all[:HALF].astype(BF16)
    grad_own[...] = grad_all[HALF : HALF + rows]
    to_after[...] = grad_all[HALF + rows :].astype(BF16)


def last_kernel(
    grad_queries, grad_own, from_before, from_after, cosine, sine, matrix, tokens, gain_two,
    grad_qkv, grad_one, gain_columns, grad_all,
):
    rows, width = grad_queries.shape
    grad_all[...] = grad_own[...]
    grad_all[:HALF] += from_before[...].astype(F32)
    grad_all[rows - HALF :] += from_after[...].astype(F32)
    grad_qkv[:, :width] = grad_queries[...]
    grad_keys = turned_by(grad_all[:, :width], cosine[...], -sine[...])
    grad_qkv[:, width : 2 * width] = grad_keys.astype(BF16)
    grad_qkv[:, 2 * width :] = grad_all[:, width:].astype(BF16)
    grad = dot(grad_qkv[...], matrix[:, : 3 * width], (1, 1))
    grad_one[...] = grad.astype(BF16)
    unit, _ = unit_of(tokens[...].astype(F32))
    gain_one = jnp.sum(grad * unit, axis=0, keepdims=True)
    gain = jnp.concatenate([gain_one, gain_two[0:1, :]], axis=0)
    high = gain.astype(BF16).astype(F32)
    spare = jnp.zeros((LANES - 4, gain.shape[1]), F32)
    gain_columns[...] = jnp.concatenate([high, gain - high, spare], axis=0).T.astype(BF16)


def weight_kernel(chips, core, left_one, left_two, right_one, right_two, *refs):
    kept, away = refs[-2:]
    lower = core[0] == 0
    depth = kept.shape[1]

    def put(block, start, stop):
        kept[0, :, start:stop] = jnp.where(lower, block[:depth], block[depth:]).astype(BF16)
        away[0, :, start:stop] = jnp.where(lower, block[depth:], block[:depth]).astype(BF16)

    base = 0
    for left, right in ((left_one, right_one), (left_two, right_two)):
        width = right.shape[1]
        turned = left[...].T
        for start in range(0, width, 512):
            stop = min(width, start + 512)
            product = jnp.dot(turned, right[:, start:stop], preferred_element_type=F32)
            put(product, base + start, base + stop)
        base += width
    if len(refs) == 3:
        put(refs[0][...].astype(F32), base, base + refs[0].shape[1])


def weight_terms(ring, left_one, right_one, left_two, right_two, extra=None):
    work_rows, width = left_one.shape
    lanes = width // ring.chips
    depth = lanes // 2
    total = right_one.shape[1] + right_two.shape[1]
    more_args, more_specs = [], []
    if extra is not None:
        total += extra.shape[1]
        more_args.append(extra)
        more_specs.append(
            pl.BlockSpec((lanes, extra.shape[1]), lambda i, chips, core: (chips[i], 0))
        )

    def left_map(i, chips, core):
        return (0, chips[i])

    def whole_map(i, chips, core):
        return (0, 0)

    return pl.pallas_call(
        weight_kernel,
        grid_spec=pltpu.PrefetchScalarGridSpec(
            num_scalar_prefetch=2,
            grid=(ring.chips,),
            in_specs=[
                pl.BlockSpec((work_rows, lanes), left_map),
                pl.BlockSpec((work_rows, lanes), left_map),
                pl.BlockSpec(right_one.shape, whole_map),
                pl.BlockSpec(right_two.shape, whole_map),
                *more_specs,
            ],
            out_specs=[
                pl.BlockSpec((1, depth, total), lambda i, chips, core: (i, 0, 0)),
                pl.BlockSpec((1, depth, total), lambda i, chips, core: (i, 0, 0)),
            ],
        ),
        out_shape=[
            jax.ShapeDtypeStruct((ring.chips, depth, total), BF16),
            jax.ShapeDtypeStruct((ring.chips, depth, total), BF16),
        ],
        compiler_params=pltpu.CompilerParams(vmem_limit_bytes=40 * 1024 * 1024),
        cost_estimate=pl.CostEstimate(
            flops=2 * work_rows * width * total,
            bytes_accessed=2 * (width + work_rows) * total,
            transcendentals=0,
        ),
    )(
        ring.chips_at(ring.slots),
        ring.core.reshape(1),
        left_one,
        left_two,
        right_one,
        right_two,
        *more_args,
    )


def summed_terms(ring, name, *factors):
    if ring.short:
        return (yield from ring.scatter_sum(*weight_terms(ring, *factors), name))
    left_one, right_one, left_two, right_two, *extra = factors
    terms = [dot(left_one, right_one, (0, 0)), dot(left_two, right_two, (0, 0))]
    terms = jnp.concatenate([t.astype(BF16) for t in terms] + extra, axis=1)
    return lax.psum_scatter(terms, SEQ, scatter_dimension=0, tiled=True).astype(F32)


def norm_back(grad_rows, gain, unit_rows, inverse):
    scaled = grad_rows * gain
    centered_grad = (
        scaled
        - jnp.mean(scaled, axis=-1, keepdims=True)
        - unit_rows * jnp.mean(scaled * unit_rows, axis=-1, keepdims=True)
    )
    return inverse * centered_grad


def rotary_tables(positions):
    half_size = HD // 2
    frequency = THETA ** (-(jnp.arange(half_size, dtype=F32) * 2.0) / HD)
    angles = positions.astype(F32)[:, None] * frequency[None, :]
    cosine, sine = jnp.cos(angles), jnp.sin(angles)
    copies = LANES // HD
    return jnp.tile(cosine, (1, 2 * copies)), jnp.tile(
        jnp.concatenate([-sine, sine], axis=1), (1, copies)
    )


def pair_rows(mine):
    other = pair_swap(mine)
    first = lax.axis_index(PAIR) == 0
    return jnp.concatenate([jnp.where(first, mine, other), jnp.where(first, other, mine)], axis=0)


def own_rows(values, row_count):
    return lax.dynamic_slice_in_dim(values, lax.axis_index(PAIR) * row_count, row_count, 0)


def other_rows(values, row_count):
    return lax.dynamic_slice_in_dim(values, (1 - lax.axis_index(PAIR)) * row_count, row_count, 0)


def dot(a, b, over=(1, 0)):
    return lax.dot_general(a, b, (((over[0],), (over[1],)), ((), ())), preferred_element_type=F32)


def padded_to_lanes(values):
    return jnp.pad(values, ((0, 0), (0, -values.shape[1] % LANES)))


def local(tokens, norm1_gain, w_qkv, w_attn_out, norm2_gain, w_in, w_down, cotangent):
    row_count, model_width = tokens.shape
    ring = Ring(model_width)
    depth, _, width = w_qkv.shape
    units = w_down.shape[0]
    gains = padded_to_lanes(jnp.stack([norm1_gain, norm2_gain], axis=1))
    blob_a = jnp.concatenate([w_qkv.reshape(depth, -1), w_attn_out.T, gains], axis=1)
    blob_b = jnp.concatenate(
        [padded_to_lanes(w_in[:, 0]), padded_to_lanes(w_in[:, 1]), padded_to_lanes(w_down.T)], axis=1
    )
    units_pad = blob_b.shape[1] // 3
    steps_a = Stepped(ring.gather(blob_a, "gather_a"))
    steps_a.step()
    blob_b = steps_a.ride(blob_b)
    pieces, starts = steps_a.finish()
    steps_b = Stepped(ring.gather(blob_b, "gather_b"))

    work_rows = row_count * lax.axis_size(PAIR)
    tokens_all = pair_rows(tokens)
    cot_all = pair_rows(cotangent)
    seq = jnp.stack([lax.axis_index(SEQ), lax.axis_size(SEQ)]).astype(jnp.int32)
    cosine, sine = rotary_tables(seq[0] * work_rows + jnp.arange(work_rows, dtype=jnp.int32))

    count = len(pieces)
    tokens_all = steps_b.ride(tokens_all)
    whole_a, attn_matrix, gains, work_one, queries, kv_own, kv_first, kv_last = call(
        functools.partial(first_kernel, count, width),
        (starts, tokens_all, cosine, sine, *pieces),
        [SMEM] + [VMEM] * 3 + [ANY] * count,
        [
            shape_of(model_width, blob_a.shape[1], BF16),
            shape_of(model_width, width, BF16),
            shape_of(8, model_width, F32),
            shape_of(work_rows, model_width, BF16),
            shape_of(work_rows, width, BF16),
            shape_of(work_rows, 2 * width, BF16),
            shape_of(HALF, 2 * width, BF16),
            shape_of(HALF, 2 * width, BF16),
        ],
        [pltpu.SemaphoreType.DMA((count,))],
        flops=6 * work_rows * model_width * width,
        moved=16 * MIB,
    )
    from_before = passed_along(kv_last, SEQ, 1)
    from_after = passed_along(kv_first, SEQ, -1)
    reach_rows = work_rows + 2 * HALF
    queries = steps_b.ride(queries)
    context, attn_term = call(
        attend_kernel,
        (seq, queries, kv_own, from_before, from_after, attn_matrix),
        [SMEM] + [VMEM] * 5,
        [shape_of(work_rows, width, BF16), shape_of(work_rows, model_width, BF16)],
        [pltpu.VMEM((reach_rows, 2 * width), BF16)],
        flops=2 * work_rows * model_width * width,
        moved=16 * MIB,
    )
    attn_other = steps_b.ride(pair_swap(attn_term))

    pieces, starts = steps_b.finish()
    count = len(pieces)
    residual, work_two, hidden, grad_proj, grad_two, down_term = call(
        functools.partial(hidden_kernel, count),
        (starts, tokens_all, attn_term, attn_other, gains, cot_all, *pieces),
        [SMEM] + [VMEM] * 5 + [ANY] * count,
        [
            shape_of(work_rows, model_width, F32),
            shape_of(work_rows, model_width, BF16),
            shape_of(work_rows, units_pad, BF16),
            shape_of(work_rows, 2 * units_pad, BF16),
            shape_of(work_rows, model_width, BF16),
            shape_of(work_rows, model_width, BF16),
        ],
        [
            pltpu.VMEM((model_width, blob_b.shape[1]), BF16),
            pltpu.SemaphoreType.DMA((count,)),
        ],
        flops=12 * work_rows * model_width * units_pad,
        moved=32 * MIB,
    )
    grad_two_other = pair_swap(grad_two)
    steps_b = Stepped(summed_terms(ring, "sum_b", work_two, grad_proj, cot_all, hidden))
    steps_b.step()
    grad_two = steps_b.ride(grad_two)
    grad_residual, grad_low, gain_two, grad_queries, grad_own, to_before, to_after = call(
        attend_back_kernel,
        (
            seq, residual, gains, grad_two, grad_two_other, cot_all, attn_matrix,
            queries, kv_own, from_before, from_after, cosine, sine,
        ),
        [SMEM] + [VMEM] * 12,
        [
            shape_of(work_rows, model_width, F32),
            shape_of(work_rows, model_width, BF16),
            shape_of(8, model_width, F32),
            shape_of(work_rows, width, BF16),
            shape_of(work_rows, 2 * width, F32),
            shape_of(HALF, 2 * width, BF16),
            shape_of(HALF, 2 * width, BF16),
        ],
        [
            pltpu.VMEM((reach_rows, 2 * width), BF16),
            pltpu.VMEM((reach_rows, 2 * width), F32),
        ],
        flops=4 * work_rows * model_width * width,
        moved=24 * MIB,
    )
    from_next = passed_along(to_before, SEQ, -1)
    from_prev = passed_along(to_after, SEQ, 1)

    down_other = pair_swap(other_rows(down_term, row_count))
    output = (
        own_rows(residual, row_count)
        + (own_rows(down_term, row_count).astype(F32) + down_other.astype(F32))
    ).astype(BF16)

    grad_queries = steps_b.ride(grad_queries)
    grad_qkv, grad_one, gain_columns = call(
        last_kernel,
        (
            grad_queries, grad_own, from_prev, from_next, cosine, sine, whole_a, tokens_all,
            gain_two,
        ),
        [VMEM] * 9,
        [
            shape_of(work_rows, 3 * width, BF16),
            shape_of(work_rows, model_width, BF16),
            shape_of(model_width, LANES, BF16),
        ],
        [pltpu.VMEM((work_rows, 2 * width), F32)],
        flops=6 * work_rows * model_width * width,
        moved=16 * MIB,
    )
    one_other = pair_swap(other_rows(grad_one, row_count))
    steps_a = Stepped(summed_terms(ring, "sum_a", work_one, grad_qkv, grad_low, context, gain_columns))
    steps_a.beside(steps_b)
    steps_a.step()
    steps_a.beside(steps_b)
    share_b = steps_b.finish()
    share_a = steps_a.finish()

    gain_one = gains[0:1]
    unit_one, inverse_one = unit_of(tokens.astype(F32))
    grad_low_one = own_rows(grad_one, row_count).astype(F32) + one_other.astype(F32)
    grad_tokens = (
        own_rows(grad_residual, row_count)
        + norm_back(grad_low_one, gain_one, unit_one, inverse_one)
    ).astype(BF16)

    share_gains = share_a[:, 4 * width : 4 * width + 2] + share_a[:, 4 * width + 2 : 4 * width + 4]
    share_gain_one = share_gains[:, 0]
    share_gain_one = share_gain_one + pair_swap(share_gain_one)
    return (
        output,
        grad_tokens,
        share_gain_one,
        share_a[:, : 3 * width].reshape(depth, 3, width),
        share_a[:, 3 * width : 4 * width].T,
        share_gains[:, 1],
        jnp.stack([share_b[:, :units], share_b[:, units_pad : units_pad + units]], axis=1),
        share_b[:, 2 * units_pad : 2 * units_pad + units].T,
    )


def solution(mesh):
    return jax.shard_map(
        local,
        mesh=mesh,
        in_specs=(
            P((SEQ, PAIR), None),
            P(SEQ),
            P(SEQ, None, PAIR),
            P(PAIR, SEQ),
            P(SEQ),
            P(SEQ, None, PAIR),
            P(PAIR, SEQ),
            P((SEQ, PAIR), None),
        ),
        out_specs=(
            P((SEQ, PAIR), None),
            P((SEQ, PAIR), None),
            P(SEQ),
            P(SEQ, None, PAIR),
            P(PAIR, SEQ),
            P(SEQ),
            P(SEQ, None, PAIR),
            P(PAIR, SEQ),
        ),
        check_vma=False,
    )
```

time: 286 us -> 250 us (0.87)
  matrix products: 30.3 us -> 0 us
  Pallas kernels: 13.2 us -> 36.6 us
  waiting for transfers between devices: 116 us -> 101 us
  other arithmetic: 29 us -> 22.8 us
  starting transfers between devices: 61.1 us -> 57.4 us
  local copies, waits for them, and re-layouts: 33.1 us -> 29.9 us
    dot_general x13 -> x0, matrix products: 26.4 us -> none  [the longest x8 16.8 us: dot(): lax.dot_general(a, b, (((over[0],), (over[1],)), ((), ())), preferred_ele...]
    ppermute x52, waiting for transfers between devices: 102 us -> 77.5 us  [go(): return lax.ppermute(block, SEQ, route)]
    pallas_call x2 -> x5, Pallas kernels: 4.51 us -> 27.9 us  [call(): pl.pallas_call(kernel, in_specs=specs, out_specs=[VMEM] * len(outs), out_...]
    ppermute x7, waiting for transfers between devices: 12.6 us -> 23.6 us  [pair_swap(): return lax.ppermute(block, PAIR, [(0, 1), (1, 0)])]
    unnamed x125 -> x93, local copies, waits for them, and re-layouts: 7.13 us -> 13.7 us
    slice x22 -> x11, local copies, waits for them, and re-layouts: 13 us -> 7.34 us  [the longest x2 3.24 us: scatter_sum(): came_rest = self.go(away[early:], self.swap, f'{name}_cores_rest')]
    sub x1 -> x0, matrix products: 3.93 us -> none  [local(): expo = jnp.exp(masked - jnp.max(masked, axis=-1, keepdims=True))]
    concatenate x10 -> x1, other arithmetic: 3.68 us -> 0.01 us  [rotary_tables(): jnp.concatenate([-sine, sine], axis=1)]
  transfers between devices with their start and end apart: 63 -> 63, of which waited for: 25 -> 31; matrix products, arithmetic and copies ran while one was open for 26% -> 14% of each run, Pallas kernels for 4% -> 9%
where the time goes in v1:
time: 250 us; the launch traced here: 249 us
  waiting for transfers between devices  101 us (40%)
  starting transfers between devices  57.4 us (23%)
  Pallas kernels  36.6 us (15%)
  local copies, waits for them, and re-layouts  29.9 us (12%)
  other arithmetic  22.8 us (9%)
    ppermute x52, waiting for transfers between devices, go(): return lax.ppermute(block, SEQ, route)  77.5 us
    ppermute x52, starting transfers between devices, go(): return lax.ppermute(block, SEQ, route)  42.2 us
    pallas_call x5, Pallas kernels, call(): pl.pallas_call(kernel, in_specs=specs, out_specs=[VMEM] * len(outs), out_...  27.9 us
    ppermute x7, waiting for transfers between devices, pair_swap(): return lax.ppermute(block, PAIR, [(0, 1), (1, 0)])  23.6 us
    unnamed x93, local copies, waits for them, and re-layouts  13.7 us
    ppermute x7, starting transfers between devices, pair_swap(): return lax.ppermute(block, PAIR, [(0, 1), (1, 0)])  9.67 us
    pallas_call x2, Pallas kernels, weight_terms(): pl.pallas_call(weight_kernel, grid_spec=pltpu.PrefetchScalarGridSpec(num_...  8.72 us
    convert_element_type x6, other arithmetic, scatter_sum(): downward = (at(self.half + step) + more_down).astype(BF16)  8.16 us
  transfers between devices with their start and end apart: 63, of which 31 were waited for; matrix products, arithmetic and copies ran while one was open for 14% of the time, Pallas kernels for 9%

profile of v1, /device:TPU:0, one launch (start us, length us, event | category | flops | bytes accessed | tf_op | source)
XLA Modules:
  0.0 249.2 jit_solution(779818804923995079)
XLA Ops:
  3.8 2.6 %collective-permute-start.2 = (bf16[64,2176]{1,0:T(8,128)(2,1)S(1)}, bf16[64,2176]{1,0:T(8,128)(2,1)S(1)}, u32[]{:S(2)}, u32[]{:S(2)}) collective-permute-start(bf16[64,2176]{1,0:T(8,128)(2,1)S(1)} %fusion.32.refs_0_), channel_id=1, source_target_pairs={{0,4},{2,6},{4,12},{6,14},{8,0},{10,2},{12,20},{14,22},{16,8},{18,... | collective-permute-start | bytes 835592 | tf_op jit(solution)/shard_map/gather_a_down_1/ppermute | solution.py:64
  6.6 1.9 collective-permute-start
  9.1 4.6 %collective-permute-done.2.refs_2_ = bf16[64,2176]{1,0:T(8,128)(2,1)S(1)} collective-permute-done((bf16[64,2176]{1,0:T(8,128)(2,1)S(1)}, bf16[64,2176]{1,0:T(8,128)(2,1)S(1)}, u32[]{:S(2)}, u32[]{:S(2)}) %collective-permute-start.2) | collective-permute-done | bytes 278560 | tf_op jit(solution)/shard_map/gather_a_down_1/ppermute | solution.py:64
  13.7 1.4 collective-permute-done.1.refs_1_
  15.5 1.7 collective-permute-start.4
  18.2 4.9 %collective-permute-done.3.refs_3_ = bf16[64,2176]{1,0:T(8,128)(2,1)S(1)} collective-permute-done((bf16[64,2176]{1,0:T(8,128)(2,1)S(1)}, bf16[64,2176]{1,0:T(8,128)(2,1)S(1)}, u32[]{:S(2)}, u32[]{:S(2)}) %collective-permute-start.3) | collective-permute-done | bytes 278560 | tf_op jit(solution)/shard_map/gather_a_up_2/ppermute | solution.py:64
  23.5 1.6 collective-permute-start.7
  26.9 1.4 collective-permute-start.6
  28.3 2.4 collective-permute-done.7.refs_5_
  30.7 1.4 collective-permute-start.5
  32.1 2.6 %collective-permute-done.8.refs_6_ = bf16[64,2176]{1,0:T(8,128)(2,1)S(1)} collective-permute-done((bf16[64,2176]{1,0:T(8,128)(2,1)S(1)}, bf16[64,2176]{1,0:T(8,128)(2,1)S(1)}, u32[]{:S(2)}, u32[]{:S(2)}) %collective-permute-start.8) | collective-permute-done | bytes 278560 | tf_op jit(solution)/shard_map/gather_a_down_3/ppermute | solution.py:64
  34.7 1.6 collective-permute-start.9
  38.3 7.2 %collective-permute-done.9 = bf16[32,2176]{1,0:T(8,128)(2,1)S(1)} collective-permute-done((bf16[32,2176]{1,0:T(8,128)(2,1)S(1)}, bf16[32,2176]{1,0:T(8,128)(2,1)S(1)}, u32[]{:S(2)}, u32[]{:S(2)}) %collective-permute-start.9) | collective-permute-done | bytes 139296 | tf_op jit(solution)/shard_map/gather_a_up_4/ppermute | solution.py:64
  46.4 4.1 %collective-permute-done.10 = bf16[32,2176]{1,0:T(8,128)(2,1)S(1)} collective-permute-done((bf16[32,2176]{1,0:T(8,128)(2,1)S(1)}, bf16[32,2176]{1,0:T(8,128)(2,1)S(1)}, u32[]{:S(2)}, u32[]{:S(2)}) %collective-permute-start.10) | collective-permute-done | bytes 139296 | tf_op jit(solution)/shard_map/gather_a_down_4/ppermute | solution.py:64
  55.6 5.0 %shard_map.197 = (bf16[1024,2176]{1,0:T(8,128)(2,1)}, bf16[1024,512]{1,0:T(8,128)(2,1)}, f32[8,1024]{1,0:T(8,128)S(1)}, bf16[256,1024]{1,0:T(8,128)(2,1)S(1)}, b...) custom-call(s32[16]{0:T(128)S(1)} %add_multiply_fusion.1.starts, ...), custom_call_target="tpu_custom_call" | custom-call | flops 805306368 | bytes 16777216 | tf_op jit(solution)/shard_map/pallas_call | solution.py:165
  61.3 1.5 collective-permute-start.21
  62.8 1.3 collective-permute-start.22
  64.2 2.7 %collective-permute-done.19.refs_3_ = bf16[64,4224]{1,0:T(8,128)(2,1)} collective-permute-done((bf16[64,4224]{1,0:T(8,128)(2,1)S(1)}, bf16[64,4224]{1,0:T(8,128)(2,1)}, u32[]{:S(2)}, u32[]{:S(2)}) %collective-permute-start.19) | collective-permute-done | bytes 540704 | tf_op jit(solution)/shard_map/gather_b_up_2/ppermute | solution.py:64
  67.9 1.6 collective-permute-start.24
  72.2 2.5 %shard_map.198 = (bf16[256,512]{1,0:T(8,128)(2,1)S(1)}, bf16[256,1024]{1,0:T(8,128)(2,1)S(1)}) custom-call(s32[2]{0:T(128)S(1)} %pad_add_fusion.seq, bf16[256,512]{1,0:T(8,128)(2,1)S(1)} %get-tuple-element.106.queries, bf16[256,1024]{1,0:T(8,128)(2,1)S(1)} %copy-done.4, bf16[64,1024]{1,0:T(8,128)(2,1)S(1)} %collective-permute-done.21.before, ...), custom_call_target="tpu_custom_call" | custom-call | flops 268435456 | bytes 16777216 | tf_op jit(solution)/shard_map/pallas_call | solution.py:165
  75.4 1.5 collective-permute-start.23
  76.9 12.5 %collective-permute-done.23.term_other = bf16[256,1024]{1,0:T(8,128)(2,1)S(1)} collective-permute-done((bf16[256,1024]{1,0:T(8,128)(2,1)S(1)}, bf16[256,1024]{1,0:T(8,128)(2,1)S(1)}, u32[]{:S(2)}, u32[]{:S(2)}) %collective-permute-start.23) | collective-permute-done | bytes 524320 | tf_op jit(solution)/shard_map/ppermute | solution.py:31
  90.6 2.1 collective-permute-start.27
  92.8 1.5 collective-permute-start.26
  95.8 4.0 %collective-permute-done.27 = bf16[32,4224]{1,0:T(8,128)(2,1)S(1)} collective-permute-done((bf16[32,4224]{1,0:T(8,128)(2,1)S(1)}, bf16[32,4224]{1,0:T(8,128)(2,1)S(1)}, u32[]{:S(2)}, u32[]{:S(2)}) %collective-permute-start.27) | collective-permute-done | bytes 270368 | tf_op jit(solution)/shard_map/gather_b_up_4/ppermute | solution.py:64
  101.3 6.8 %collective-permute-done.28 = bf16[32,4224]{1,0:T(8,128)(2,1)S(1)} collective-permute-done((bf16[32,4224]{1,0:T(8,128)(2,1)S(1)}, bf16[32,4224]{1,0:T(8,128)(2,1)S(1)}, u32[]{:S(2)}, u32[]{:S(2)}) %collective-permute-start.28) | collective-permute-done | bytes 270368 | tf_op jit(solution)/shard_map/gather_b_down_4/ppermute | solution.py:64
  115.7 9.5 %shard_map.199 = (f32[256,1024]{1,0:T(8,128)}, bf16[256,1024]{1,0:T(8,128)(2,1)S(1)}, bf16[256,1408]{1,0:T(8,128)(2,1)}, bf16[256,2816]{1,0:T(8,128)(2,1)}, bf16...) custom-call(s32[16]{0:T(128)S(1)} %add_multiply_fusion.1.starts, bf16[256,1024]{1,0:T(8,128)(2,1)S(1)} %copy-done, ...), custom_call_target="tpu_custom_call" | custom-call | flops 4429185024 | bytes 33554432 | tf_op jit(solution)/shard_map/pallas_call | solution.py:165
  125.3 1.4 copy-done.28
  127.7 5.0 %shard_map.200 = (bf16[8,64,4224]{2,1,0:T(8,128)(2,1)S(1)}, bf16[8,64,4224]{2,1,0:T(8,128)(2,1)S(1)}) custom-call(s32[8]{0:T(128)S(1)} %gather_fusion.1, s32[1]{0:T(128)} %bitcast.10.core, bf16[256,1024]{1,0:T(8,128)(2,1)S(1)} %get-tuple-element.125.left_one, bf16[256,1024]{1,0:T(8,128)(2,1)S(1)} %pad_maximum_fusion.2.cot.left_two, ...), custom_call_target="tpu_custom_call" | custom-call | flops 2214592512 | bytes 10813440 | tf_op jit(solution)/shard_map/pallas_call | solution.py:430
  134.0 1.7 slice.250
  135.7 1.3 collective-permute-start.39
  137.4 2.0 collective-permute-start.41
  139.4 10.6 %collective-permute-done.39.grad_two_other = bf16[256,1024]{1,0:T(8,128)(2,1)S(1)} collective-permute-done((bf16[256,1024]{1,0:T(8,128)(2,1)S(1)}, bf16[256,1024]{1,0:T(8,128)(2,1)S(1)}, u32[]{:S(2)}, u32[]{:S(2)}) %collective-permute-start.39) | collective-permute-done | bytes 524320 | tf_op jit(solution)/shard_map/ppermute | solution.py:31
  150.0 7.2 %shard_map.201 = (f32[256,1024]{1,0:T(8,128)S(1)}, bf16[256,1024]{1,0:T(8,128)(2,1)S(1)}, f32[8,1024]{1,0:T(8,128)S(1)}, bf16[256,512]{1,0:T(8,128)(2,1)S(1)}, f...) custom-call(s32[2]{0:T(128)S(1)} %pad_add_fusion.seq, ...), custom_call_target="tpu_custom_call" | custom-call | flops 536870912 | bytes 25165824 | tf_op jit(solution)/shard_map/pallas_call | solution.py:165
  157.2 1.5 collective-permute-start.42
  158.7 1.3 collective-permute-start.43
  160.0 1.3 fusion.5
  161.3 3.3 %collective-permute-start.46 = (bf16[64,4224]{1,0:T(8,128)(2,1)}, bf16[64,4224]{1,0:T(8,128)(2,1)}, u32[]{:S(2)}, u32[]{:S(2)}) collective-permute-start(bf16[64,4224]{1,0:T(8,128)(2,1)} %get-tuple-element.153), channel_id=1, source_target_pairs={{0,8},{2,10},{4,0},{6,2},{8,16},{10,18},{12,4},{14,6},{16,24},{18,... | collective-permute-start | bytes 1622024 | tf_op jit(solution)/shard_map/sum_b_up_2/ppermute | solution.py:64
  168.3 3.7 %shard_map.202 = (bf16[256,1536]{1,0:T(8,128)(2,1)S(1)}, bf16[256,1024]{1,0:T(8,128)(2,1)S(1)}, bf16[1024,128]{1,0:T(8,128)(2,1)S(1)}) custom-call(bf16[256,512]{1,0:T(8,128)(2,1)S(1)} %copy-done.11, f32[256,1024]{1,0:T(8,128)S(1)} %get-tuple-element.138.grad_own, bf16[64,1024]{1,0:T(8,128)(2,1)S(1)} %collective-permute-done.42.from_before, ...), custom_call_target="tpu_custom_call" | custom-call | flops 805306368 | bytes 16777216 | tf_op jit(solution)/shard_map/pallas_call | solution.py:165
  172.7 1.3 collective-permute-start.44
  174.0 3.7 %shard_map.203 = (bf16[8,64,2176]{2,1,0:T(8,128)(2,1)S(1)}, bf16[8,64,2176]{2,1,0:T(8,128)(2,1)S(1)}) custom-call(s32[8]{0:T(128)S(1)} %gather_fusion.1, s32[1]{0:T(128)} %bitcast.10.core, bf16[256,1024]{1,0:T(8,128)(2,1)S(1)} %copy-done.19, bf16[256,1024]{1,0:T(8,128)(2,1)S(1)} %copy-done.25, bf16[256,1536]{1,0:T(8,128)(2,1)S(1)} %get-tuple-element.146.right_one, ...), custom_call_target="tpu_custom_call" | custom-call | flops 1140850688 | bytes 5570560 | tf_op jit(solution)/shard_map/pallas_call | solution.py:430
  178.9 3.2 %fusion.3 = (bf16[64,4224]{1,0:T(8,128)(2,1)}, bf16[64,4224]{1,0:T(8,128)(2,1)}) fusion(bf16[64,4224]{1,0:T(8,128)(2,1)} %collective-permute-done.47, bf16[5,64,4224]{2,1,0:T(8,128)(2,1)} %collective-permute-done.45, bf16[8,64,4224]{2,1,0:T(8,128)(2,1)} %copy-done.1, bf16[64,4224]{1,0:T(8,128)(2,1)} %collective-permute-done.46), kind=kLoop, calls=%fused_computation.13 | loop fusion | flops 3244032 | bytes 4325376 | tf_op jit(solution)/shard_map/convert_element_type | solution.py:112
  183.9 1.9 add_convert_fusion.2
  187.0 1.5 slice.253
  188.6 1.6 collective-permute-start.52
  191.7 1.6 collective-permute-start.50
  193.8 9.9 %collective-permute-done.52 = bf16[64,4224]{1,0:T(8,128)(2,1)S(1)} collective-permute-done((bf16[64,4224]{1,0:T(8,128)(2,1)S(1)}, bf16[64,4224]{1,0:T(8,128)(2,1)S(1)}, u32[]{:S(2)}, u32[]{:S(2)}) %collective-permute-start.52) | collective-permute-done | bytes 540704 | tf_op jit(solution)/shard_map/sum_b_up_3/ppermute | solution.py:64
  203.7 1.6 collective-permute-done.53
  205.3 1.9 fusion.1
  208.8 1.8 collective-permute-start.54
  210.9 1.9 fusion.29
  212.8 1.7 collective-permute-start.61
  214.8 3.6 %collective-permute-done.54 = bf16[64,2176]{1,0:T(8,128)(2,1)S(1)} collective-permute-done((bf16[64,2176]{1,0:T(8,128)(2,1)S(1)}, bf16[64,2176]{1,0:T(8,128)(2,1)S(1)}, u32[]{:S(2)}, u32[]{:S(2)}) %collective-permute-start.54) | collective-permute-done | bytes 278560 | tf_op jit(solution)/shard_map/sum_a_up_2/ppermute | solution.py:64
  218.4 1.7 collective-permute-done.55
  220.4 1.7 collective-permute-start.56
  222.5 7.6 %collective-permute-done.61 = bf16[64,4224]{1,0:T(8,128)(2,1)S(1)} collective-permute-done((bf16[64,4224]{1,0:T(8,128)(2,1)S(1)}, bf16[64,4224]{1,0:T(8,128)(2,1)S(1)}, u32[]{:S(2)}, u32[]{:S(2)}) %collective-permute-start.61) | collective-permute-done | bytes 540704 | tf_op jit(solution)/shard_map/sum_b_up_4/ppermute | solution.py:64
  230.0 1.7 collective-permute-done.62
  231.8 1.5 fusion
  234.3 1.4 collective-permute-done.57
  236.0 1.7 collective-permute-start.58
  238.9 1.4 copy.53
  240.3 2.4 collective-permute-done.58
  242.7 1.5 collective-permute-done.59
  245.1 1.5 collective-permute-start.60
  (232 shorter events, 54.2 us)
Async XLA Ops:
  3.3 47.9 %collective-permute-start.11 = (bf16[64,2176]{1,0:T(8,128)(2,1)S(1)}, bf16[64,2176]{1,0:T(8,128)(2,1)S(1)}, u32[]{:S(2)}, u32[]{:S(2)}) collective-permute-start(bf16[64,2176]{1,0:T(8,128)(2,1)S(1)} %fusion.32.refs_0_), channel_id=1, source_target_pairs={{0,2},{2,0},{4,6},{6,4},{8,10},{10,8},{12,14},{14,12},{16,18},{18,... | collective-permute-start | bytes 835592 | tf_op jit(solution)/shard_map/gather_a_cores_0/ppermute | solution.py:64
  3.8 9.9 %collective-permute-start.2 = (bf16[64,2176]{1,0:T(8,128)(2,1)S(1)}, bf16[64,2176]{1,0:T(8,128)(2,1)S(1)}, u32[]{:S(2)}, u32[]{:S(2)}) collective-permute-start(bf16[64,2176]{1,0:T(8,128)(2,1)S(1)} %fusion.32.refs_0_), channel_id=1, source_target_pairs={{0,4},{2,6},{4,12},{6,14},{8,0},{10,2},{12,20},{14,22},{16,8},{18,... | collective-permute-start | bytes 835592 | tf_op jit(solution)/shard_map/gather_a_down_1/ppermute | solution.py:64
  6.4 8.7 %collective-permute-start.1 = (bf16[64,2176]{1,0:T(8,128)(2,1)S(1)}, bf16[64,2176]{1,0:T(8,128)(2,1)S(1)}, u32[]{:S(2)}, u32[]{:S(2)}) collective-permute-start(bf16[64,2176]{1,0:T(8,128)(2,1)S(1)} %fusion.32.refs_0_), channel_id=1, source_target_pairs={{0,8},{2,10},{4,0},{6,2},{8,16},{10,18},{12,4},{14,6},{16,24},{18,... | collective-permute-start | bytes 835592 | tf_op jit(solution)/shard_map/gather_a_up_1/ppermute | solution.py:64
  6.6 29.8 %collective-permute-start = (bf16[128,1024]{1,0:T(8,128)(2,1)}, bf16[128,1024]{1,0:T(8,128)(2,1)}, u32[]{:S(2)}, u32[]{:S(2)}) collective-permute-start(bf16[128,1024]{1,0:T(8,128)(2,1)} %param.14), channel_id=1, source_target_pairs={{0,1},{1,0},{2,3},{3,2},{4,5},{5,4},{6,7},{7,6},{8,9},{9,8},{10,11... | collective-permute-start | bytes 786440 | tf_op jit(solution)/shard_map/ppermute | solution.py:31
  15.1 8.0 %collective-permute-start.3 = (bf16[64,2176]{1,0:T(8,128)(2,1)S(1)}, bf16[64,2176]{1,0:T(8,128)(2,1)S(1)}, u32[]{:S(2)}, u32[]{:S(2)}) collective-permute-start(bf16[64,2176]{1,0:T(8,128)(2,1)S(1)} %collective-permute-done.1.refs_1_), channel_id=1, source_target_pairs={{0,8},{2,10},{4,0},{6,2},{8,16},{10,18},{12,4},{14,6},{16,24},{18,... | collective-permute-start | bytes 835592 | tf_op jit(solution)/shard_map/gather_a_up_2/ppermute | solution.py:64
  15.5 8.0 %collective-permute-start.4 = (bf16[64,2176]{1,0:T(8,128)(2,1)S(1)}, bf16[64,2176]{1,0:T(8,128)(2,1)S(1)}, u32[]{:S(2)}, u32[]{:S(2)}) collective-permute-start(bf16[64,2176]{1,0:T(8,128)(2,1)S(1)} %collective-permute-done.2.refs_2_), channel_id=1, source_target_pairs={{0,4},{2,6},{4,12},{6,14},{8,0},{10,2},{12,20},{14,22},{16,8},{18,... | collective-permute-start | bytes 835592 | tf_op jit(solution)/shard_map/gather_a_down_2/ppermute | solution.py:64
  23.5 7.1 %collective-permute-start.7 = (bf16[64,2176]{1,0:T(8,128)(2,1)S(1)}, bf16[64,2176]{1,0:T(8,128)(2,1)S(1)}, u32[]{:S(2)}, u32[]{:S(2)}) collective-permute-start(bf16[64,2176]{1,0:T(8,128)(2,1)S(1)} %collective-permute-done.3.refs_3_), channel_id=1, source_target_pairs={{0,8},{2,10},{4,0},{6,2},{8,16},{10,18},{12,4},{14,6},{16,24},{18,... | collective-permute-start | bytes 835592 | tf_op jit(solution)/shard_map/gather_a_up_3/ppermute | solution.py:64
  25.1 9.6 %collective-permute-start.8 = (bf16[64,2176]{1,0:T(8,128)(2,1)S(1)}, bf16[64,2176]{1,0:T(8,128)(2,1)S(1)}, u32[]{:S(2)}, u32[]{:S(2)}) collective-permute-start(bf16[64,2176]{1,0:T(8,128)(2,1)S(1)} %collective-permute-done.4.refs_4_), channel_id=1, source_target_pairs={{0,4},{2,6},{4,12},{6,14},{8,0},{10,2},{12,20},{14,22},{16,8},{18,... | collective-permute-start | bytes 835592 | tf_op jit(solution)/shard_map/gather_a_down_3/ppermute | solution.py:64
  26.9 23.6 %collective-permute-start.6 = (bf16[64,4224]{1,0:T(8,128)(2,1)S(1)}, bf16[64,4224]{1,0:T(8,128)(2,1)S(1)}, u32[]{:S(2)}, u32[]{:S(2)}) collective-permute-start(bf16[64,4224]{1,0:T(8,128)(2,1)S(1)} %fusion.24.refs_0_), channel_id=1, source_target_pairs={{0,4},{2,6},{4,12},{6,14},{8,0},{10,2},{12,20},{14,22},{16,8},{18,... | collective-permute-start | bytes 1622024 | tf_op jit(solution)/shard_map/gather_b_down_1/ppermute | solution.py:64
  30.7 20.4 %collective-permute-start.5 = (bf16[64,4224]{1,0:T(8,128)(2,1)S(1)}, bf16[64,4224]{1,0:T(8,128)(2,1)S(1)}, u32[]{:S(2)}, u32[]{:S(2)}) collective-permute-start(bf16[64,4224]{1,0:T(8,128)(2,1)S(1)} %fusion.24.refs_0_), channel_id=1, source_target_pairs={{0,8},{2,10},{4,0},{6,2},{8,16},{10,18},{12,4},{14,6},{16,24},{18,... | collective-permute-start | bytes 1622024 | tf_op jit(solution)/shard_map/gather_b_up_1/ppermute | solution.py:64
  34.7 10.7 %collective-permute-start.9 = (bf16[32,2176]{1,0:T(8,128)(2,1)S(1)}, bf16[32,2176]{1,0:T(8,128)(2,1)S(1)}, u32[]{:S(2)}, u32[]{:S(2)}) collective-permute-start(bf16[32,2176]{1,0:T(8,128)(2,1)S(1)} %slice.182), channel_id=1, source_target_pairs={{0,8},{2,10},{4,0},{6,2},{8,16},{10,18},{12,4},{14,6},{16,24},{18,... | collective-permute-start | bytes 417800 | tf_op jit(solution)/shard_map/gather_a_up_4/ppermute | solution.py:64
  38.3 13.4 %collective-permute-start.12 = (bf16[64,2176]{1,0:T(8,128)(2,1)S(1)}, bf16[64,2176]{1,0:T(8,128)(2,1)S(1)}, u32[]{:S(2)}, u32[]{:S(2)}) collective-permute-start(bf16[64,2176]{1,0:T(8,128)(2,1)S(1)} %collective-permute-done.1.refs_1_), channel_id=1, source_target_pairs={{0,2},{2,0},{4,6},{6,4},{8,10},{10,8},{12,14},{14,12},{16,18},{18,... | collective-permute-start | bytes 835592 | tf_op jit(solution)/shard_map/gather_a_cores_-1/ppermute | solution.py:64
  45.5 5.1 %collective-permute-start.10 = (bf16[32,2176]{1,0:T(8,128)(2,1)S(1)}, bf16[32,2176]{1,0:T(8,128)(2,1)S(1)}, u32[]{:S(2)}, u32[]{:S(2)}) collective-permute-start(bf16[32,2176]{1,0:T(8,128)(2,1)S(1)} %slice.183), channel_id=1, source_target_pairs={{0,4},{2,6},{4,12},{6,14},{8,0},{10,2},{12,20},{14,22},{16,8},{18,... | collective-permute-start | bytes 417800 | tf_op jit(solution)/shard_map/gather_a_down_4/ppermute | solution.py:64
  50.5 1.6 collective-permute-start.13
  50.5 1.9 collective-permute-start.14
  51.0 2.7 %collective-permute-start.15 = (bf16[64,2176]{1,0:T(8,128)(2,1)S(1)}, bf16[64,2176]{1,0:T(8,128)(2,1)S(1)}, u32[]{:S(2)}, u32[]{:S(2)}) collective-permute-start(bf16[64,2176]{1,0:T(8,128)(2,1)S(1)} %collective-permute-done.4.refs_4_), channel_id=1, source_target_pairs={{0,2},{2,0},{4,6},{6,4},{8,10},{10,8},{12,14},{14,12},{16,18},{18,... | collective-permute-start | bytes 835592 | tf_op jit(solution)/shard_map/gather_a_cores_2/ppermute | solution.py:64
  51.2 3.4 %collective-permute-start.16 = (bf16[64,2176]{1,0:T(8,128)(2,1)S(1)}, bf16[64,2176]{1,0:T(8,128)(2,1)S(1)}, u32[]{:S(2)}, u32[]{:S(2)}) collective-permute-start(bf16[64,2176]{1,0:T(8,128)(2,1)S(1)} %collective-permute-done.7.refs_5_), channel_id=1, source_target_pairs={{0,2},{2,0},{4,6},{6,4},{8,10},{10,8},{12,14},{14,12},{16,18},{18,... | collective-permute-start | bytes 835592 | tf_op jit(solution)/shard_map/gather_a_cores_-3/ppermute | solution.py:64
  51.7 2.9 %collective-permute-start.17 = (bf16[64,2176]{1,0:T(8,128)(2,1)S(1)}, bf16[64,2176]{1,0:T(8,128)(2,1)S(1)}, u32[]{:S(2)}, u32[]{:S(2)}) collective-permute-start(bf16[64,2176]{1,0:T(8,128)(2,1)S(1)} %collective-permute-done.8.refs_6_), channel_id=1, source_target_pairs={{0,2},{2,0},{4,6},{6,4},{8,10},{10,8},{12,14},{14,12},{16,18},{18,... | collective-permute-start | bytes 835592 | tf_op jit(solution)/shard_map/gather_a_cores_3/ppermute | solution.py:64
  52.1 2.5 %collective-permute-start.18 = (bf16[64,2176]{1,0:T(8,128)(2,1)S(1)}, bf16[64,2176]{1,0:T(8,128)(2,1)S(1)}, u32[]{:S(2)}, u32[]{:S(2)}) collective-permute-start(bf16[64,2176]{1,0:T(8,128)(2,1)S(1)} %constant_dynamic-update-slice_fusion.refs_7_), channel_id=1, source_target_pairs={{0,2},{2,0},{4,6},{6,4},{8,10},{10,8},{12,14},{14,12},{16,18},{18,... | collective-permute-start | bytes 835592 | tf_op jit(solution)/shard_map/gather_a_cores_4/ppermute | solution.py:64
  52.5 14.4 %collective-permute-start.19 = (bf16[64,4224]{1,0:T(8,128)(2,1)S(1)}, bf16[64,4224]{1,0:T(8,128)(2,1)}, u32[]{:S(2)}, u32[]{:S(2)}) collective-permute-start(bf16[64,4224]{1,0:T(8,128)(2,1)S(1)} %collective-permute-done.5.refs_1_), channel_id=1, source_target_pairs={{0,8},{2,10},{4,0},{6,2},{8,16},{10,18},{12,4},{14,6},{16,24},{18,... | collective-permute-start | bytes 1622024 | tf_op jit(solution)/shard_map/gather_b_up_2/ppermute | solution.py:64
  53.7 14.1 %collective-permute-start.20 = (bf16[64,4224]{1,0:T(8,128)(2,1)S(1)}, bf16[64,4224]{1,0:T(8,128)(2,1)}, u32[]{:S(2)}, u32[]{:S(2)}) collective-permute-start(bf16[64,4224]{1,0:T(8,128)(2,1)S(1)} %collective-permute-done.6.refs_2_), channel_id=1, source_target_pairs={{0,4},{2,6},{4,12},{6,14},{8,0},{10,2},{12,20},{14,22},{16,8},{18,... | collective-permute-start | bytes 1622024 | tf_op jit(solution)/shard_map/gather_b_down_2/ppermute | solution.py:64
  61.3 52.3 %copy-start.12 = (f32[8,1024]{1,0:T(8,128)}, f32[8,1024]{1,0:T(8,128)S(1)}, u32[]{:S(2)}) copy-start(f32[8,1024]{1,0:T(8,128)S(1)} %get-tuple-element.117.gains) | copy-start | bytes 98308
  61.3 8.6 %collective-permute-start.21 = (bf16[64,1024]{1,0:T(8,128)(2,1)S(1)}, bf16[64,1024]{1,0:T(8,128)(2,1)S(1)}, u32[]{:S(2)}, u32[]{:S(2)}) collective-permute-start(bf16[64,1024]{1,0:T(8,128)(2,1)S(1)} %get-tuple-element.108), channel_id=1, source_target_pairs={{0,2},{2,4},{4,6},{6,8},{8,10},{10,12},{12,14},{14,16},{16,18},{18... | collective-permute-start | bytes 393224 | tf_op jit(solution)/shard_map/ppermute | solution.py:27
  62.8 7.1 %collective-permute-start.22 = (bf16[64,1024]{1,0:T(8,128)(2,1)S(1)}, bf16[64,1024]{1,0:T(8,128)(2,1)S(1)}, u32[]{:S(2)}, u32[]{:S(2)}) collective-permute-start(bf16[64,1024]{1,0:T(8,128)(2,1)S(1)} %get-tuple-element.109), channel_id=1, source_target_pairs={{2,0},{4,2},{6,4},{8,6},{10,8},{12,10},{14,12},{16,14},{18,16},{20... | collective-permute-start | bytes 393224 | tf_op jit(solution)/shard_map/ppermute | solution.py:27
  67.9 21.6 %collective-permute-start.24 = (bf16[64,4224]{1,0:T(8,128)(2,1)}, bf16[64,4224]{1,0:T(8,128)(2,1)}, u32[]{:S(2)}, u32[]{:S(2)}) collective-permute-start(bf16[64,4224]{1,0:T(8,128)(2,1)} %collective-permute-done.19.refs_3_), channel_id=1, source_target_pairs={{0,8},{2,10},{4,0},{6,2},{8,16},{10,18},{12,4},{14,6},{16,24},{18,... | collective-permute-start | bytes 1622024 | tf_op jit(solution)/shard_map/gather_b_up_3/ppermute | solution.py:64
  69.4 20.0 %collective-permute-start.25 = (bf16[64,4224]{1,0:T(8,128)(2,1)}, bf16[64,4224]{1,0:T(8,128)(2,1)}, u32[]{:S(2)}, u32[]{:S(2)}) collective-permute-start(bf16[64,4224]{1,0:T(8,128)(2,1)} %collective-permute-done.20.refs_4_), channel_id=1, source_target_pairs={{0,4},{2,6},{4,12},{6,14},{8,0},{10,2},{12,20},{14,22},{16,8},{18,... | collective-permute-start | bytes 1622024 | tf_op jit(solution)/shard_map/gather_b_down_3/ppermute | solution.py:64
  75.4 14.0 %collective-permute-start.23 = (bf16[256,1024]{1,0:T(8,128)(2,1)S(1)}, bf16[256,1024]{1,0:T(8,128)(2,1)S(1)}, u32[]{:S(2)}, u32[]{:S(2)}) collective-permute-start(bf16[256,1024]{1,0:T(8,128)(2,1)S(1)} %get-tuple-element.111.term), channel_id=1, source_target_pairs={{0,1},{1,0},{2,3},{3,2},{4,5},{5,4},{6,7},{7,6},{8,9},{9,8},{10,11... | collective-permute-start | bytes 1572872 | tf_op jit(solution)/shard_map/ppermute | solution.py:31
  90.6 9.2 %collective-permute-start.27 = (bf16[32,4224]{1,0:T(8,128)(2,1)S(1)}, bf16[32,4224]{1,0:T(8,128)(2,1)S(1)}, u32[]{:S(2)}, u32[]{:S(2)}) collective-permute-start(bf16[32,4224]{1,0:T(8,128)(2,1)S(1)} %slice.184), channel_id=1, source_target_pairs={{0,8},{2,10},{4,0},{6,2},{8,16},{10,18},{12,4},{14,6},{16,24},{18,... | collective-permute-start | bytes 811016 | tf_op jit(solution)/shard_map/gather_b_up_4/ppermute | solution.py:64
  92.8 16.1 %collective-permute-start.26 = (bf16[128,1024]{1,0:T(8,128)(2,1)S(1)}, bf16[128,1024]{1,0:T(8,128)(2,1)S(1)}, u32[]{:S(2)}, u32[]{:S(2)}) collective-permute-start(bf16[128,1024]{1,0:T(8,128)(2,1)S(1)} %copy-done.36), channel_id=1, source_target_pairs={{0,1},{1,0},{2,3},{3,2},{4,5},{5,4},{6,7},{7,6},{8,9},{9,8},{10,11... | collective-permute-start | bytes 786440 | tf_op jit(solution)/shard_map/ppermute | solution.py:31
  94.2 15.2 %collective-permute-start.29 = (bf16[64,4224]{1,0:T(8,128)(2,1)S(1)}, bf16[64,4224]{1,0:T(8,128)(2,1)S(1)}, u32[]{:S(2)}, u32[]{:S(2)}) collective-permute-start(bf16[64,4224]{1,0:T(8,128)(2,1)S(1)} %fusion.24.refs_0_), channel_id=1, source_target_pairs={{0,2},{2,0},{4,6},{6,4},{8,10},{10,8},{12,14},{14,12},{16,18},{18,... | collective-permute-start | bytes 1622024 | tf_op jit(solution)/shard_map/gather_b_cores_0/ppermute | solution.py:64
  94.2 15.3 %collective-permute-start.30 = (bf16[64,4224]{1,0:T(8,128)(2,1)S(1)}, bf16[64,4224]{1,0:T(8,128)(2,1)S(1)}, u32[]{:S(2)}, u32[]{:S(2)}) collective-permute-start(bf16[64,4224]{1,0:T(8,128)(2,1)S(1)} %collective-permute-done.5.refs_1_), channel_id=1, source_target_pairs={{0,2},{2,0},{4,6},{6,4},{8,10},{10,8},{12,14},{14,12},{16,18},{18,... | collective-permute-start | bytes 1622024 | tf_op jit(solution)/shard_map/gather_b_cores_-1/ppermute | solution.py:64
  94.8 15.2 %collective-permute-start.31 = (bf16[64,4224]{1,0:T(8,128)(2,1)S(1)}, bf16[64,4224]{1,0:T(8,128)(2,1)S(1)}, u32[]{:S(2)}, u32[]{:S(2)}) collective-permute-start(bf16[64,4224]{1,0:T(8,128)(2,1)S(1)} %collective-permute-done.6.refs_2_), channel_id=1, source_target_pairs={{0,2},{2,0},{4,6},{6,4},{8,10},{10,8},{12,14},{14,12},{16,18},{18,... | collective-permute-start | bytes 1622024 | tf_op jit(solution)/shard_map/gather_b_cores_1/ppermute | solution.py:64
  99.8 8.3 %collective-permute-start.28 = (bf16[32,4224]{1,0:T(8,128)(2,1)S(1)}, bf16[32,4224]{1,0:T(8,128)(2,1)S(1)}, u32[]{:S(2)}, u32[]{:S(2)}) collective-permute-start(bf16[32,4224]{1,0:T(8,128)(2,1)S(1)} %slice.185), channel_id=1, source_target_pairs={{0,4},{2,6},{4,12},{6,14},{8,0},{10,2},{12,20},{14,22},{16,8},{18,... | collective-permute-start | bytes 811016 | tf_op jit(solution)/shard_map/gather_b_down_4/ppermute | solution.py:64
  108.1 4.5 %collective-permute-start.32 = (bf16[64,4224]{1,0:T(8,128)(2,1)}, bf16[64,4224]{1,0:T(8,128)(2,1)}, u32[]{:S(2)}, u32[]{:S(2)}) collective-permute-start(bf16[64,4224]{1,0:T(8,128)(2,1)} %collective-permute-done.19.refs_3_), channel_id=1, source_target_pairs={{0,2},{2,0},{4,6},{6,4},{8,10},{10,8},{12,14},{14,12},{16,18},{18,... | collective-permute-start | bytes 1622024 | tf_op jit(solution)/shard_map/gather_b_cores_-2/ppermute | solution.py:64
  108.8 3.8 %collective-permute-start.33 = (bf16[64,4224]{1,0:T(8,128)(2,1)}, bf16[64,4224]{1,0:T(8,128)(2,1)}, u32[]{:S(2)}, u32[]{:S(2)}) collective-permute-start(bf16[64,4224]{1,0:T(8,128)(2,1)} %collective-permute-done.20.refs_4_), channel_id=1, source_target_pairs={{0,2},{2,0},{4,6},{6,4},{8,10},{10,8},{12,14},{14,12},{16,18},{18,... | collective-permute-start | bytes 1622024 | tf_op jit(solution)/shard_map/gather_b_cores_2/ppermute | solution.py:64
  109.4 3.2 %collective-permute-start.34 = (bf16[64,4224]{1,0:T(8,128)(2,1)}, bf16[64,4224]{1,0:T(8,128)(2,1)}, u32[]{:S(2)}, u32[]{:S(2)}) collective-permute-start(bf16[64,4224]{1,0:T(8,128)(2,1)} %collective-permute-done.24.refs_5_), channel_id=1, source_target_pairs={{0,2},{2,0},{4,6},{6,4},{8,10},{10,8},{12,14},{14,12},{16,18},{18,... | collective-permute-start | bytes 1622024 | tf_op jit(solution)/shard_map/gather_b_cores_-3/ppermute | solution.py:64
  109.5 3.3 %collective-permute-start.35 = (bf16[64,4224]{1,0:T(8,128)(2,1)}, bf16[64,4224]{1,0:T(8,128)(2,1)}, u32[]{:S(2)}, u32[]{:S(2)}) collective-permute-start(bf16[64,4224]{1,0:T(8,128)(2,1)} %collective-permute-done.25.refs_6_), channel_id=1, source_target_pairs={{0,2},{2,0},{4,6},{6,4},{8,10},{10,8},{12,14},{14,12},{16,18},{18,... | collective-permute-start | bytes 1622024 | tf_op jit(solution)/shard_map/gather_b_cores_3/ppermute | solution.py:64
  109.9 3.7 %collective-permute-start.36 = (bf16[64,4224]{1,0:T(8,128)(2,1)}, bf16[64,4224]{1,0:T(8,128)(2,1)}, u32[]{:S(2)}, u32[]{:S(2)}) collective-permute-start(bf16[64,4224]{1,0:T(8,128)(2,1)} %constant_dynamic-update-slice_fusion.2.refs_7_), channel_id=1, source_target_pairs={{0,2},{2,0},{4,6},{6,4},{8,10},{10,8},{12,14},{14,12},{16,18},{18,... | collective-permute-start | bytes 1622024 | tf_op jit(solution)/shard_map/gather_b_cores_4/ppermute | solution.py:64
  132.9 4.2 %collective-permute-start.38 = (bf16[3,64,4224]{2,1,0:T(8,128)(2,1)S(1)}, bf16[3,64,4224]{2,1,0:T(8,128)(2,1)S(1)}, u32[]{:S(2)}, u32[]{:S(2)}) collective-permute-start(bf16[3,64,4224]{2,1,0:T(8,128)(2,1)S(1)} %slice.244), channel_id=1, source_target_pairs={{0,2},{2,0},{4,6},{6,4},{8,10},{10,8},{12,14},{14,12},{16,18},{18,... | collective-permute-start | bytes 4866056 | tf_op jit(solution)/shard_map/sum_b_cores_early/ppermute | solution.py:64
  135.7 14.2 %collective-permute-start.39 = (bf16[256,1024]{1,0:T(8,128)(2,1)S(1)}, bf16[256,1024]{1,0:T(8,128)(2,1)S(1)}, u32[]{:S(2)}, u32[]{:S(2)}) collective-permute-start(bf16[256,1024]{1,0:T(8,128)(2,1)S(1)} %get-tuple-element.130.grad_two), channel_id=1, source_target_pairs={{0,1},{1,0},{2,3},{3,2},{4,5},{5,4},{6,7},{7,6},{8,9},{9,8},{10,11... | collective-permute-start | bytes 1572872 | tf_op jit(solution)/shard_map/ppermute | solution.py:31
  137.0 41.8 %collective-permute-start.45 = (bf16[5,64,4224]{2,1,0:T(8,128)(2,1)}, bf16[5,64,4224]{2,1,0:T(8,128)(2,1)}, u32[]{:S(2)}, u32[]{:S(2)}) collective-permute-start(bf16[5,64,4224]{2,1,0:T(8,128)(2,1)} %slice.250), channel_id=1, source_target_pairs={{0,2},{2,0},{4,6},{6,4},{8,10},{10,8},{12,14},{14,12},{16,18},{18,... | collective-permute-start | bytes 8110088 | tf_op jit(solution)/shard_map/sum_b_cores_rest/ppermute | solution.py:64
  137.3 22.7 %collective-permute-start.40 = (bf16[32,4224]{1,0:T(8,128)(2,1)S(1)}, bf16[32,4224]{1,0:T(8,128)(2,1)S(1)}, u32[]{:S(2)}, u32[]{:S(2)}) collective-permute-start(bf16[32,4224]{1,0:T(8,128)(2,1)S(1)} %get-tuple-element.135), channel_id=1, source_target_pairs={{0,8},{2,10},{4,0},{6,2},{8,16},{10,18},{12,4},{14,6},{16,24},{18,... | collective-permute-start | bytes 811016 | tf_op jit(solution)/shard_map/sum_b_up_1/ppermute | solution.py:64
  137.4 22.6 %collective-permute-start.41 = (bf16[32,4224]{1,0:T(8,128)(2,1)S(1)}, bf16[32,4224]{1,0:T(8,128)(2,1)S(1)}, u32[]{:S(2)}, u32[]{:S(2)}) collective-permute-start(bf16[32,4224]{1,0:T(8,128)(2,1)S(1)} %get-tuple-element.136), channel_id=1, source_target_pairs={{0,4},{2,6},{4,12},{6,14},{8,0},{10,2},{12,20},{14,22},{16,8},{18,... | collective-permute-start | bytes 811016 | tf_op jit(solution)/shard_map/sum_b_down_1/ppermute | solution.py:64
  157.2 9.4 %collective-permute-start.42 = (bf16[64,1024]{1,0:T(8,128)(2,1)S(1)}, bf16[64,1024]{1,0:T(8,128)(2,1)S(1)}, u32[]{:S(2)}, u32[]{:S(2)}) collective-permute-start(bf16[64,1024]{1,0:T(8,128)(2,1)S(1)} %get-tuple-element.139), channel_id=1, source_target_pairs={{0,2},{2,4},{4,6},{6,8},{8,10},{10,12},{12,14},{14,16},{16,18},{18... | collective-permute-start | bytes 393224 | tf_op jit(solution)/shard_map/ppermute | solution.py:27
  158.7 8.7 %collective-permute-start.43 = (bf16[64,1024]{1,0:T(8,128)(2,1)S(1)}, bf16[64,1024]{1,0:T(8,128)(2,1)S(1)}, u32[]{:S(2)}, u32[]{:S(2)}) collective-permute-start(bf16[64,1024]{1,0:T(8,128)(2,1)S(1)} %get-tuple-element.140), channel_id=1, source_target_pairs={{2,0},{4,2},{6,4},{8,6},{10,8},{12,10},{14,12},{16,14},{18,16},{20... | collective-permute-start | bytes 393224 | tf_op jit(solution)/shard_map/ppermute | solution.py:27
  161.3 17.5 %collective-permute-start.46 = (bf16[64,4224]{1,0:T(8,128)(2,1)}, bf16[64,4224]{1,0:T(8,128)(2,1)}, u32[]{:S(2)}, u32[]{:S(2)}) collective-permute-start(bf16[64,4224]{1,0:T(8,128)(2,1)} %get-tuple-element.153), channel_id=1, source_target_pairs={{0,8},{2,10},{4,0},{6,2},{8,16},{10,18},{12,4},{14,6},{16,24},{18,... | collective-permute-start | bytes 1622024 | tf_op jit(solution)/shard_map/sum_b_up_2/ppermute | solution.py:64
  164.7 14.2 %collective-permute-start.47 = (bf16[64,4224]{1,0:T(8,128)(2,1)}, bf16[64,4224]{1,0:T(8,128)(2,1)}, u32[]{:S(2)}, u32[]{:S(2)}) collective-permute-start(bf16[64,4224]{1,0:T(8,128)(2,1)} %get-tuple-element.154), channel_id=1, source_target_pairs={{0,4},{2,6},{4,12},{6,14},{8,0},{10,2},{12,20},{14,22},{16,8},{18,... | collective-permute-start | bytes 1622024 | tf_op jit(solution)/shard_map/sum_b_down_2/ppermute | solution.py:64
  166.7 17.2 %collective-permute-start.37 = (bf16[128,1024]{1,0:T(8,128)(2,1)}, bf16[128,1024]{1,0:T(8,128)(2,1)}, u32[]{:S(2)}, u32[]{:S(2)}) collective-permute-start(bf16[128,1024]{1,0:T(8,128)(2,1)} %constant_dynamic-slice_fusion.1), channel_id=1, source_target_pairs={{0,1},{1,0},{2,3},{3,2},{4,5},{5,4},{6,7},{7,6},{8,9},{9,8},{10,11... | collective-permute-start | bytes 786440 | tf_op jit(solution)/shard_map/ppermute | solution.py:31
  172.7 13.1 %collective-permute-start.44 = (bf16[128,1024]{1,0:T(8,128)(2,1)}, bf16[128,1024]{1,0:T(8,128)(2,1)}, u32[]{:S(2)}, u32[]{:S(2)}) collective-permute-start(bf16[128,1024]{1,0:T(8,128)(2,1)} %constant_dynamic-slice_fusion), channel_id=1, source_target_pairs={{0,1},{1,0},{2,3},{3,2},{4,5},{5,4},{6,7},{7,6},{8,9},{9,8},{10,11... | collective-permute-start | bytes 786440 | tf_op jit(solution)/shard_map/ppermute | solution.py:31
  183.1 7.6 %collective-permute-start.49 = (bf16[3,64,2176]{2,1,0:T(8,128)(2,1)}, bf16[3,64,2176]{2,1,0:T(8,128)(2,1)}, u32[]{:S(2)}, u32[]{:S(2)}) collective-permute-start(bf16[3,64,2176]{2,1,0:T(8,128)(2,1)} %slice.257), channel_id=1, source_target_pairs={{0,2},{2,0},{4,6},{6,4},{8,10},{10,8},{12,14},{14,12},{16,18},{18,... | collective-permute-start | bytes 2506760 | tf_op jit(solution)/shard_map/sum_a_cores_early/ppermute | solution.py:64
  188.6 15.1 %collective-permute-start.52 = (bf16[64,4224]{1,0:T(8,128)(2,1)S(1)}, bf16[64,4224]{1,0:T(8,128)(2,1)S(1)}, u32[]{:S(2)}, u32[]{:S(2)}) collective-permute-start(bf16[64,4224]{1,0:T(8,128)(2,1)S(1)} %copy-done.35), channel_id=1, source_target_pairs={{0,8},{2,10},{4,0},{6,2},{8,16},{10,18},{12,4},{14,6},{16,24},{18,... | collective-permute-start | bytes 1622024 | tf_op jit(solution)/shard_map/sum_b_up_3/ppermute | solution.py:64
  190.2 15.1 %collective-permute-start.53 = (bf16[64,4224]{1,0:T(8,128)(2,1)S(1)}, bf16[64,4224]{1,0:T(8,128)(2,1)S(1)}, u32[]{:S(2)}, u32[]{:S(2)}) collective-permute-start(bf16[64,4224]{1,0:T(8,128)(2,1)S(1)} %copy-done.34), channel_id=1, source_target_pairs={{0,4},{2,6},{4,12},{6,14},{8,0},{10,2},{12,20},{14,22},{16,8},{18,... | collective-permute-start | bytes 1622024 | tf_op jit(solution)/shard_map/sum_b_down_3/ppermute | solution.py:64
  190.7 29.5 %collective-permute-start.48 = (bf16[5,64,2176]{2,1,0:T(8,128)(2,1)S(1)}, bf16[5,64,2176]{2,1,0:T(8,128)(2,1)S(1)}, u32[]{:S(2)}, u32[]{:S(2)}) collective-permute-start(bf16[5,64,2176]{2,1,0:T(8,128)(2,1)S(1)} %slice.253), channel_id=1, source_target_pairs={{0,2},{2,0},{4,6},{6,4},{8,10},{10,8},{12,14},{14,12},{16,18},{18,... | collective-permute-start | bytes 4177928 | tf_op jit(solution)/shard_map/sum_a_cores_rest/ppermute | solution.py:64
  191.7 15.5 %collective-permute-start.50 = (bf16[32,2176]{1,0:T(8,128)(2,1)S(1)}, bf16[32,2176]{1,0:T(8,128)(2,1)S(1)}, u32[]{:S(2)}, u32[]{:S(2)}) collective-permute-start(bf16[32,2176]{1,0:T(8,128)(2,1)S(1)} %get-tuple-element.156), channel_id=1, source_target_pairs={{0,8},{2,10},{4,0},{6,2},{8,16},{10,18},{12,4},{14,6},{16,24},{18,... | collective-permute-start | bytes 417800 | tf_op jit(solution)/shard_map/sum_a_up_1/ppermute | solution.py:64
  193.3 14.2 %collective-permute-start.51 = (bf16[32,2176]{1,0:T(8,128)(2,1)S(1)}, bf16[32,2176]{1,0:T(8,128)(2,1)S(1)}, u32[]{:S(2)}, u32[]{:S(2)}) collective-permute-start(bf16[32,2176]{1,0:T(8,128)(2,1)S(1)} %get-tuple-element.157), channel_id=1, source_target_pairs={{0,4},{2,6},{4,12},{6,14},{8,0},{10,2},{12,20},{14,22},{16,8},{18,... | collective-permute-start | bytes 417800 | tf_op jit(solution)/shard_map/sum_a_down_1/ppermute | solution.py:64
  208.8 9.6 %collective-permute-start.54 = (bf16[64,2176]{1,0:T(8,128)(2,1)S(1)}, bf16[64,2176]{1,0:T(8,128)(2,1)S(1)}, u32[]{:S(2)}, u32[]{:S(2)}) collective-permute-start(bf16[64,2176]{1,0:T(8,128)(2,1)S(1)} %get-tuple-element.164), channel_id=1, source_target_pairs={{0,8},{2,10},{4,0},{6,2},{8,16},{10,18},{12,4},{14,6},{16,24},{18,... | collective-permute-start | bytes 835592 | tf_op jit(solution)/shard_map/sum_a_up_2/ppermute | solution.py:64
  210.6 9.6 %collective-permute-start.55 = (bf16[64,2176]{1,0:T(8,128)(2,1)S(1)}, bf16[64,2176]{1,0:T(8,128)(2,1)S(1)}, u32[]{:S(2)}, u32[]{:S(2)}) collective-permute-start(bf16[64,2176]{1,0:T(8,128)(2,1)S(1)} %get-tuple-element.165), channel_id=1, source_target_pairs={{0,4},{2,6},{4,12},{6,14},{8,0},{10,2},{12,20},{14,22},{16,8},{18,... | collective-permute-start | bytes 835592 | tf_op jit(solution)/shard_map/sum_a_down_2/ppermute | solution.py:64
  212.8 17.2 %collective-permute-start.61 = (bf16[64,4224]{1,0:T(8,128)(2,1)S(1)}, bf16[64,4224]{1,0:T(8,128)(2,1)S(1)}, u32[]{:S(2)}, u32[]{:S(2)}) collective-permute-start(bf16[64,4224]{1,0:T(8,128)(2,1)S(1)} %get-tuple-element.172), channel_id=1, source_target_pairs={{0,8},{2,10},{4,0},{6,2},{8,16},{10,18},{12,4},{14,6},{16,24},{18,... | collective-permute-start | bytes 1622024 | tf_op jit(solution)/shard_map/sum_b_up_4/ppermute | solution.py:64
  214.5 17.2 %collective-permute-start.62 = (bf16[64,4224]{1,0:T(8,128)(2,1)S(1)}, bf16[64,4224]{1,0:T(8,128)(2,1)S(1)}, u32[]{:S(2)}, u32[]{:S(2)}) collective-permute-start(bf16[64,4224]{1,0:T(8,128)(2,1)S(1)} %get-tuple-element.173), channel_id=1, source_target_pairs={{0,4},{2,6},{4,12},{6,14},{8,0},{10,2},{12,20},{14,22},{16,8},{18,... | collective-permute-start | bytes 1622024 | tf_op jit(solution)/shard_map/sum_b_down_4/ppermute | solution.py:64
  220.4 13.9 %collective-permute-start.56 = (bf16[64,2176]{1,0:T(8,128)(2,1)S(1)}, bf16[64,2176]{1,0:T(8,128)(2,1)S(1)}, u32[]{:S(2)}, u32[]{:S(2)}) collective-permute-start(bf16[64,2176]{1,0:T(8,128)(2,1)S(1)} %get-tuple-element.166), channel_id=1, source_target_pairs={{0,8},{2,10},{4,0},{6,2},{8,16},{10,18},{12,4},{14,6},{16,24},{18,... | collective-permute-start | bytes 835592 | tf_op jit(solution)/shard_map/sum_a_up_3/ppermute | solution.py:64
  222.1 13.6 %collective-permute-start.57 = (bf16[64,2176]{1,0:T(8,128)(2,1)S(1)}, bf16[64,2176]{1,0:T(8,128)(2,1)S(1)}, u32[]{:S(2)}, u32[]{:S(2)}) collective-permute-start(bf16[64,2176]{1,0:T(8,128)(2,1)S(1)} %get-tuple-element.167), channel_id=1, source_target_pairs={{0,4},{2,6},{4,12},{6,14},{8,0},{10,2},{12,20},{14,22},{16,8},{18,... | collective-permute-start | bytes 835592 | tf_op jit(solution)/shard_map/sum_a_down_3/ppermute | solution.py:64
  236.0 6.7 %collective-permute-start.58 = (bf16[64,2176]{1,0:T(8,128)(2,1)S(1)}, bf16[64,2176]{1,0:T(8,128)(2,1)S(1)}, u32[]{:S(2)}, u32[]{:S(2)}) collective-permute-start(bf16[64,2176]{1,0:T(8,128)(2,1)S(1)} %get-tuple-element.168), channel_id=1, source_target_pairs={{0,8},{2,10},{4,0},{6,2},{8,16},{10,18},{12,4},{14,6},{16,24},{18,... | collective-permute-start | bytes 835592 | tf_op jit(solution)/shard_map/sum_a_up_4/ppermute | solution.py:64
  237.7 6.5 %collective-permute-start.59 = (bf16[64,2176]{1,0:T(8,128)(2,1)S(1)}, bf16[64,2176]{1,0:T(8,128)(2,1)S(1)}, u32[]{:S(2)}, u32[]{:S(2)}) collective-permute-start(bf16[64,2176]{1,0:T(8,128)(2,1)S(1)} %get-tuple-element.169), channel_id=1, source_target_pairs={{0,4},{2,6},{4,12},{6,14},{8,0},{10,2},{12,20},{14,22},{16,8},{18,... | collective-permute-start | bytes 835592 | tf_op jit(solution)/shard_map/sum_a_down_4/ppermute | solution.py:64
  245.1 3.5 %collective-permute-start.60 = (f32[64]{0:T(128)S(1)}, f32[64]{0:T(128)S(1)}, u32[]{:S(2)}, u32[]{:S(2)}) collective-permute-start(f32[64]{0:T(128)S(1)} %get-tuple-element.201), channel_id=1, source_target_pairs={{0,1},{1,0},{2,3},{3,2},{4,5},{5,4},{6,7},{7,6},{8,9},{9,8},{10,11... | collective-permute-start | bytes 776 | tf_op jit(solution)/shard_map/ppermute | solution.py:31
  (44 other events, 381.8 us)

commit v2 on v1

--- a/solution.py
+++ b/solution.py
@@ -12,6 +12,7 @@
 HD = 64
 HALF = 64
 LANES = 128
+COST = 1
 
 EPSILON = 1e-05
 THETA = 10000.0
@@ -63,57 +64,64 @@
         with jax.named_scope(name):
             return lax.ppermute(block, SEQ, route)
 
-    def gather(self, block, name):
+    def gather(self, block, name, plan):
         if not self.short:
             whole = lax.all_gather(block, SEQ, axis=0, tiled=True)
             return [whole], jnp.zeros(1, jnp.int32)
         rows = block.shape[0]
         middle = rows // 2
         upward = downward = block
-        got = {0: block}
-        for step in range(1, self.half):
+        held = {0: (block, 0)}
+        swapped = {}
+        for step in range(1, self.half + 1):
+            if step == self.half:
+                upward, downward = upward[:middle], downward[middle:]
             upward = self.go(upward, self.up, f"{name}_up_{step}")
             downward = self.go(downward, self.down, f"{name}_down_{step}")
-            upward, downward = yield upward, downward
-            got[-step], got[step] = upward, downward
-        low = self.go(upward[:middle], self.up, f"{name}_up_{self.half}")
-        high = self.go(downward[middle:], self.down, f"{name}_down_{self.half}")
-        got[self.half] = jnp.concatenate([low, high], axis=0)
-        distances = sorted(got, key=abs)
-        pieces = [got[d] for d in distances]
-        others = [self.go(p, self.swap, f"{name}_cores_{d}") for d, p in zip(distances, pieces)]
-        chips = self.chips_at(distances)
-        starts = jnp.concatenate([chips * 2 + self.core, chips * 2 + 1 - self.core]) * rows
-        return pieces + others, starts
-
-    def scatter_sum(self, kept, away, name):
-        rows = kept.shape[1]
+            meanwhile = [d for d in plan[step - 1] if d in held]
+            came = [self.go(held[d][0], self.swap, f"{name}_cores_{d}") for d in meanwhile]
+            upward, downward, *came = yield upward, downward, *came
+            swapped.update(zip(meanwhile, came))
+            held[-step] = upward, 0
+            held[step] = downward, middle if step == self.half else 0
+        for d in held:
+            if d not in swapped:
+                swapped[d] = self.go(held[d][0], self.swap, f"{name}_cores_{d}")
+        pieces = [held[d][0] for d in held] + [swapped[d] for d in held]
+        places = [(d, 0, held[d][1]) for d in held] + [(d, 1, held[d][1]) for d in held]
+        distances, others, offsets = np.array(places, np.int32).T
+        cores = self.chips_at(distances) * 2 + jnp.where(others == 1, 1 - self.core, self.core)
+        return pieces, cores * rows + offsets
+
+    def scatter_sum(self, early, rest, name):
+        kept_early, away_early = early
+        kept_rest, away_rest = rest
+        count, rows = kept_early.shape[:2]
         middle = rows // 2
-        away = yield away
-        early = 3
-        came_first = self.go(away[:early], self.swap, f"{name}_cores_early")
-        came_rest = self.go(away[early:], self.swap, f"{name}_cores_rest")
+        kept_early, kept_rest = yield kept_early, kept_rest
+        away_early, away_rest = yield away_early, away_rest
+        came_early = self.go(away_early, self.swap, f"{name}_cores_early")
+        came_rest = self.go(away_rest, self.swap, f"{name}_cores_rest")
 
         def at(slot):
             i = self.slots.index(slot)
-            came = came_first[i] if i < early else came_rest[i - early]
-            return kept[i].astype(F32) + came.astype(F32)
+            if i < count:
+                return kept_early[i].astype(F32) + came_early[i].astype(F32)
+            return kept_rest[i - count].astype(F32) + came_rest[i - count].astype(F32)
 
         far = at(self.half).astype(BF16)
         upward, downward = far[:middle], far[middle:]
-        for step in range(1, self.half):
+        for step in range(1, self.half + 1):
             upward, downward = yield upward, downward
-            more_up = self.go(upward, self.up, f"{name}_up_{step}").astype(F32)
-            more_down = self.go(downward, self.down, f"{name}_down_{step}").astype(F32)
+            upward = self.go(upward, self.up, f"{name}_up_{step}").astype(F32)
+            downward = self.go(downward, self.down, f"{name}_down_{step}").astype(F32)
             if step == 1:
-                more_up = jnp.pad(more_up, ((0, rows - middle), (0, 0)))
-                more_down = jnp.pad(more_down, ((middle, 0), (0, 0)))
-            upward = (at(self.half - step) + more_up).astype(BF16)
-            downward = (at(self.half + step) + more_down).astype(BF16)
-        upward, downward = yield upward, downward
-        upward = self.go(upward, self.up, f"{name}_up_{self.half}")
-        downward = self.go(downward, self.down, f"{name}_down_{self.half}")
-        return at(0) + upward.astype(F32) + downward.astype(F32)
+                upward = jnp.pad(upward, ((0, rows - middle), (0, 0)))
+                downward = jnp.pad(downward, ((middle, 0), (0, 0)))
+            if step < self.half:
+                upward = (at(self.half - step) + upward).astype(BF16)
+                downward = (at(self.half + step) + downward).astype(BF16)
+        return at(0) + upward + downward
 
 
 class Stepped:
@@ -135,6 +143,11 @@
             self.advance()
         return value
 
+    def hold(self, value):
+        if self.steps is not None:
+            value, self.state = lax.optimization_barrier((value, self.state))
+        return value
+
     def step(self):
         if self.steps is not None:
             self.advance()
@@ -152,7 +165,7 @@
 
 
 VMEM = pl.BlockSpec(memory_space=pltpu.VMEM)
-ANY = pl.BlockSpec(memory_space=pl.ANY)
+ANY = pl.BlockSpec(memory_space=pltpu.HBM)
 SMEM = pl.BlockSpec(memory_space=pltpu.SMEM)
 MIB = 1024 * 1024
 
@@ -161,7 +174,7 @@
     return jax.ShapeDtypeStruct((rows, columns), kind)
 
 
-def call(kernel, args, specs, outs, scratch=(), flops=0, moved=0, room=48):
+def call(kernel, args, specs, outs, scratch=(), flops=0, moved=0, room=20):
     return pl.pallas_call(
         kernel,
         in_specs=specs,
@@ -169,7 +182,9 @@
         out_shape=outs,
         scratch_shapes=list(scratch),
         compiler_params=pltpu.CompilerParams(vmem_limit_bytes=room * MIB),
-        cost_estimate=pl.CostEstimate(flops=flops, bytes_accessed=moved, transcendentals=0),
+        cost_estimate=pl.CostEstimate(
+            flops=flops // COST, bytes_accessed=moved // COST, transcendentals=0
+        ),
     )(*args)
 
 
@@ -210,31 +225,32 @@
     return centered * inverse, inverse
 
 
-def first_kernel(count, width, starts, tokens, cosine, sine, *refs):
+def first_kernel(count, width, starts, tokens, before, after, cosine, sine, *refs):
     pieces = refs[:count]
-    whole, matrix, gains, work, queries, keys_values, first, last, ready = refs[count:]
+    whole, matrix, gains, work, queries, keys_values, all_rows, ready = refs[count:]
     copies = placing(starts, pieces, whole, ready)
     for copy in copies:
         copy.start()
-    unit, _ = unit_of(tokens[...].astype(F32))
+    joined_rows(before, tokens, after, all_rows)
+    unit, _ = unit_of(all_rows[...].astype(F32))
     for copy in copies:
         copy.wait()
     matrix[...] = whole[:, 3 * width : 4 * width]
     gains[...] = whole[:, 4 * width :].astype(F32).T[:8]
-    work[...] = (unit * gains[0:1, :]).astype(BF16)
+    all_rows[...] = (unit * gains[0:1, :]).astype(BF16)
     rows = work.shape[0]
+    own = slice(HALF, HALF + rows)
+    work[...] = all_rows[own, :]
     for start in range(0, 3 * width, 256):
-        part = dot(work[...], whole[:, start : start + 256])
-        if start < 2 * width:
-            part = turned_by(part, cosine[...], sine[...])
-        part = part.astype(BF16)
+        columns = whole[:, start : start + 256]
         if start < width:
-            queries[:, start : start + 256] = part
+            part = dot(work[...], columns)
+            queries[:, start : start + 256] = turned_by(part, cosine[own], sine[own]).astype(BF16)
         else:
-            at = slice(start - width, start - width + 256)
-            keys_values[:, at] = part
-            first[:, at] = part[:HALF]
-            last[:, at] = part[rows - HALF :]
+            part = dot(all_rows[...], columns)
+            if start < 2 * width:
+                part = turned_by(part, cosine[...], sine[...])
+            keys_values[:, start - width : start - width + 256] = part.astype(BF16)
 
 
 def window(seq, tile, tiles):
@@ -276,9 +292,8 @@
     whole[HALF + rows :] = after[...]
 
 
-def attend_kernel(seq, queries, own, before, after, matrix, context, term, keys_values):
+def attend_kernel(seq, queries, keys_values, matrix, context, term):
     rows, width = queries.shape
-    joined_rows(before, own, after, keys_values)
     tiles = rows // LANES
     for tile in range(tiles):
         inside = window(seq, tile, tiles)
@@ -293,7 +308,7 @@
     term[...] = dot(context[...], matrix[...], (1, 1)).astype(BF16)
 
 
-def hidden_kernel(count, starts, tokens, term, term_other, gains, cot, *refs):
+def hidden_kernel(count, spare, starts, tokens, term, term_other, gains, cot, *refs):
     pieces = refs[:count]
     residual, work, hidden, grad_proj, grad_two, down, whole, ready = refs[count:]
     copies = placing(starts, pieces, whole, ready)
@@ -305,29 +320,44 @@
     work[...] = (unit * gains[1:2, :]).astype(BF16)
     for copy in copies:
         copy.wait()
-    units = hidden.shape[1]
+    units = hidden.shape[1] - LANES
+
+    def grads(gate, up, back):
+        share = 0.5 + 0.5 * lax.erf(gate * (1.0 / math.sqrt(2.0)))
+        bell = jnp.exp(-0.5 * gate * gate) * (1.0 / math.sqrt(2.0 * math.pi))
+        gelu = gate * share
+        return gelu * up, back * up * (share + gate * bell), back * gelu
+
     for start in range(0, units, 256):
         stop = min(units, start + 256)
         gate = dot(work[...], whole[:, start:stop])
         up = dot(work[...], whole[:, units + start : units + stop])
         back = dot(cot[...], whole[:, 2 * units + start : 2 * units + stop])
-        share = 0.5 + 0.5 * lax.erf(gate * (1.0 / math.sqrt(2.0)))
-        bell = jnp.exp(-0.5 * gate * gate) * (1.0 / math.sqrt(2.0 * math.pi))
-        gelu = gate * share
-        hidden[:, start:stop] = (gelu * up).astype(BF16)
-        grad_proj[:, start:stop] = (back * up * (share + gate * bell)).astype(BF16)
-        grad_proj[:, units + start : units + stop] = (back * gelu).astype(BF16)
-    grad_two[...] = dot(grad_proj[...], whole[:, : 2 * units], (1, 1)).astype(BF16)
+        here, grad_gate, grad_up = grads(gate, up, back)
+        hidden[:, start:stop] = here.astype(BF16)
+        grad_proj[:, start:stop] = grad_gate.astype(BF16)
+        grad_proj[:, units + start : units + stop] = grad_up.astype(BF16)
+    tail = whole[:, 3 * units :]
+    both = dot(work[...], tail)
+    back = pltpu.roll(dot(cot[...], tail), LANES - 2 * spare, 1)
+    parts = grads(both, pltpu.roll(both, LANES - spare, 1), back)
+    lane = lane_of(*both.shape)
+    here, grad_gate, grad_up = [jnp.where(lane < spare, part, 0.0) for part in parts]
+    hidden[:, units:] = pltpu.roll(here, 2 * spare, 1).astype(BF16)
+    grad_proj[:, 2 * units :] = (grad_gate + pltpu.roll(grad_up, spare, 1)).astype(BF16)
+    grad_two[...] = (
+        dot(grad_proj[:, : 2 * units], whole[:, : 2 * units], (1, 1))
+        + dot(grad_proj[:, 2 * units :], tail, (1, 1))
+    ).astype(BF16)
     down[...] = dot(hidden[...], whole[:, 2 * units :], (1, 1)).astype(BF16)
 
 
 def attend_back_kernel(
-    seq, residual, gains, grad_two, grad_two_other, cot, matrix, queries, own, before, after,
+    seq, residual, gains, grad_two, grad_two_other, cot, matrix, queries, keys_values,
     cosine, sine, grad_residual, grad_low, gain_two, grad_queries, grad_own, to_before, to_after,
-    keys_values, grad_all,
+    grad_all,
 ):
     rows, width = queries.shape
-    joined_rows(before, own, after, keys_values)
     unit, inverse = unit_of(residual[...])
     grad = grad_two[...].astype(F32) + grad_two_other[...].astype(F32)
     gain_two[...] = jnp.broadcast_to(jnp.sum(grad * unit, axis=0, keepdims=True), gain_two.shape)
@@ -344,6 +374,7 @@
     for tile in range(tiles):
         inside = window(seq, tile, tiles)
         at = slice(tile * LANES, tile * LANES + LANES)
+        own_at = slice(HALF + tile * LANES, HALF + tile * LANES + LANES)
         reach = slice(tile * LANES, tile * LANES + 2 * LANES)
         for start in range(0, width, LANES):
             columns = slice(start, start + LANES)
@@ -356,7 +387,7 @@
             lost = jnp.sum(grad_shares * shares, axis=-1, keepdims=True)
             grad_scores = (shares * (grad_shares - lost)).astype(BF16)
             grad_here = heads_joined(dot(grad_scores, keys)) * scale
-            grad_queries[at, columns] = turned_by(grad_here, cosine[at], -sine[at]).astype(BF16)
+            grad_queries[at, columns] = turned_by(grad_here, cosine[own_at], -sine[own_at]).astype(BF16)
             grad_all[reach, columns] += dot(grad_scores, apart, (0, 0)) * scale
             grad_all[reach, beside] += dot(shares.astype(BF16), grad_apart, (0, 0))
     to_before[...] = grad_all[:HALF].astype(BF16)
@@ -373,7 +404,8 @@
     grad_all[:HALF] += from_before[...].astype(F32)
     grad_all[rows - HALF :] += from_after[...].astype(F32)
     grad_qkv[:, :width] = grad_queries[...]
-    grad_keys = turned_by(grad_all[:, :width], cosine[...], -sine[...])
+    own = slice(HALF, HALF + rows)
+    grad_keys = turned_by(grad_all[:, :width], cosine[own], -sine[own])
     grad_qkv[:, width : 2 * width] = grad_keys.astype(BF16)
     grad_qkv[:, 2 * width :] = grad_all[:, width:].astype(BF16)
     grad = dot(grad_qkv[...], matrix[:, : 3 * width], (1, 1))
@@ -386,7 +418,7 @@
     gain_columns[...] = jnp.concatenate([high, gain - high, spare], axis=0).T.astype(BF16)
 
 
-def weight_kernel(chips, core, left_one, left_two, right_one, right_two, *refs):
+def weight_kernel(tail, chips, core, left_one, left_two, right_one, right_two, *refs):
     kept, away = refs[-2:]
     lower = core[0] == 0
     depth = kept.shape[1]
@@ -396,23 +428,28 @@
         away[0, :, start:stop] = jnp.where(lower, block[depth:], block[:depth]).astype(BF16)
 
     base = 0
+    rest = 0.0
     for left, right in ((left_one, right_one), (left_two, right_two)):
-        width = right.shape[1]
+        width = right.shape[1] - tail
         turned = left[...].T
         for start in range(0, width, 512):
             stop = min(width, start + 512)
             product = jnp.dot(turned, right[:, start:stop], preferred_element_type=F32)
             put(product, base + start, base + stop)
         base += width
+        if tail:
+            rest += jnp.dot(turned, right[:, width:], preferred_element_type=F32)
+    if tail:
+        put(rest, base, base + tail)
     if len(refs) == 3:
         put(refs[0][...].astype(F32), base, base + refs[0].shape[1])
 
 
-def weight_terms(ring, left_one, right_one, left_two, right_two, extra=None):
+def weight_terms(ring, slots, left_one, right_one, left_two, right_two, extra=None, tail=0, room=20):
     work_rows, width = left_one.shape
     lanes = width // ring.chips
     depth = lanes // 2
-    total = right_one.shape[1] + right_two.shape[1]
+    total = right_one.shape[1] + right_two.shape[1] - tail
     more_args, more_specs = [], []
     if extra is not None:
         total += extra.shape[1]
@@ -428,10 +465,10 @@
         return (0, 0)
 
     return pl.pallas_call(
-        weight_kernel,
+        functools.partial(weight_kernel, tail),
         grid_spec=pltpu.PrefetchScalarGridSpec(
             num_scalar_prefetch=2,
-            grid=(ring.chips,),
+            grid=(len(slots),),
             in_specs=[
                 pl.BlockSpec((work_rows, lanes), left_map),
                 pl.BlockSpec((work_rows, lanes), left_map),
@@ -445,17 +482,17 @@
             ],
         ),
         out_shape=[
-            jax.ShapeDtypeStruct((ring.chips, depth, total), BF16),
-            jax.ShapeDtypeStruct((ring.chips, depth, total), BF16),
+            pltpu.HBM((len(slots), depth, total), BF16),
+            pltpu.HBM((len(slots), depth, total), BF16),
         ],
-        compiler_params=pltpu.CompilerParams(vmem_limit_bytes=40 * 1024 * 1024),
+        compiler_params=pltpu.CompilerParams(vmem_limit_bytes=room * MIB),
         cost_estimate=pl.CostEstimate(
-            flops=2 * work_rows * width * total,
-            bytes_accessed=2 * (width + work_rows) * total,
+            flops=2 * work_rows * lanes * len(slots) * total // COST,
+            bytes_accessed=2 * (lanes * len(slots) + work_rows) * total // COST,
             transcendentals=0,
         ),
     )(
-        ring.chips_at(ring.slots),
+        ring.chips_at(slots),
         ring.core.reshape(1),
         left_one,
         left_two,
@@ -465,11 +502,18 @@
     )
 
 
-def summed_terms(ring, name, *factors):
+def summed_terms(ring, name, *factors, tail=0, room=20):
     if ring.short:
-        return (yield from ring.scatter_sum(*weight_terms(ring, *factors), name))
+        early, rest = [
+            weight_terms(ring, slots, *factors, tail=tail, room=room)
+            for slots in (ring.slots[:3], ring.slots[3:])
+        ]
+        return (yield from ring.scatter_sum(early, rest, name))
     left_one, right_one, left_two, right_two, *extra = factors
     terms = [dot(left_one, right_one, (0, 0)), dot(left_two, right_two, (0, 0))]
+    if tail:
+        rest = terms[0][:, -tail:] + terms[1][:, -tail:]
+        terms = [terms[0][:, :-tail], terms[1][:, :-tail], rest]
     terms = jnp.concatenate([t.astype(BF16) for t in terms] + extra, axis=1)
     return lax.psum_scatter(terms, SEQ, scatter_dimension=0, tiled=True).astype(F32)
 
@@ -495,8 +539,14 @@
     )
 
 
-def pair_rows(mine):
-    other = pair_swap(mine)
+def edge_rows(block):
+    blocks = range(lax.axis_size(SEQ))
+    route = [(2 * i, 2 * i - 2) for i in blocks if i > 0]
+    route += [(2 * i + 1, 2 * i + 3) for i in blocks if i + 1 in blocks]
+    return lax.ppermute(block, (SEQ, PAIR), route)
+
+
+def pair_rows(mine, other):
     first = lax.axis_index(PAIR) == 0
     return jnp.concatenate([jnp.where(first, mine, other), jnp.where(first, other, mine)], axis=0)
 
@@ -524,52 +574,63 @@
     units = w_down.shape[0]
     gains = padded_to_lanes(jnp.stack([norm1_gain, norm2_gain], axis=1))
     blob_a = jnp.concatenate([w_qkv.reshape(depth, -1), w_attn_out.T, gains], axis=1)
+    whole_units = units // LANES * LANES
+    spare = units - whole_units
+    parts = [w_in[:, 0], w_in[:, 1], w_down.T]
     blob_b = jnp.concatenate(
-        [padded_to_lanes(w_in[:, 0]), padded_to_lanes(w_in[:, 1]), padded_to_lanes(w_down.T)], axis=1
-    )
-    units_pad = blob_b.shape[1] // 3
-    steps_a = Stepped(ring.gather(blob_a, "gather_a"))
+        [part[:, :whole_units] for part in parts] + [part[:, whole_units:] for part in parts], axis=1
+    )
+    blob_b = jnp.pad(blob_b, ((0, 0), (0, LANES - 3 * spare)))
+    steps_a = Stepped(ring.gather(blob_a, "gather_a", [[0], [-1, 1], [], []]))
+    first = lax.axis_index(PAIR) == 0
+    edge = edge_rows(jnp.where(first, tokens[:HALF], tokens[-HALF:]))
+    edge = steps_a.hold(edge)
+    joined = jnp.concatenate([tokens, edge], axis=0)
+    other = pair_swap(joined)
     steps_a.step()
+    other = steps_a.hold(other)
+    tokens_all = pair_rows(tokens, other[:row_count])
+    tokens_before = jnp.where(first, other[row_count:], edge)
+    tokens_after = jnp.where(first, edge, other[row_count:])
     blob_b = steps_a.ride(blob_b)
+    steps_b = Stepped(ring.gather(blob_b, "gather_b", [[], [0], [-1, 1], [-2, 2]]))
+    steps_a.step()
     pieces, starts = steps_a.finish()
-    steps_b = Stepped(ring.gather(blob_b, "gather_b"))
 
     work_rows = row_count * lax.axis_size(PAIR)
-    tokens_all = pair_rows(tokens)
-    cot_all = pair_rows(cotangent)
+    reach_rows = work_rows + 2 * HALF
     seq = jnp.stack([lax.axis_index(SEQ), lax.axis_size(SEQ)]).astype(jnp.int32)
-    cosine, sine = rotary_tables(seq[0] * work_rows + jnp.arange(work_rows, dtype=jnp.int32))
-
+    cosine, sine = rotary_tables(
+        seq[0] * work_rows - HALF + jnp.arange(reach_rows, dtype=jnp.int32)
+    )
+
+    tokens_all, cot_own = steps_b.ride((tokens_all, cotangent))
+    cot_other = pair_swap(cot_own)
     count = len(pieces)
-    tokens_all = steps_b.ride(tokens_all)
-    whole_a, attn_matrix, gains, work_one, queries, kv_own, kv_first, kv_last = call(
+    whole_a, attn_matrix, gains, work_one, queries, keys_values = call(
         functools.partial(first_kernel, count, width),
-        (starts, tokens_all, cosine, sine, *pieces),
-        [SMEM] + [VMEM] * 3 + [ANY] * count,
+        (starts, tokens_all, tokens_before, tokens_after, cosine, sine, *pieces),
+        [SMEM] + [VMEM] * 5 + [ANY] * count,
         [
             shape_of(model_width, blob_a.shape[1], BF16),
             shape_of(model_width, width, BF16),
             shape_of(8, model_width, F32),
             shape_of(work_rows, model_width, BF16),
             shape_of(work_rows, width, BF16),
-            shape_of(work_rows, 2 * width, BF16),
-            shape_of(HALF, 2 * width, BF16),
-            shape_of(HALF, 2 * width, BF16),
+            shape_of(reach_rows, 2 * width, BF16),
         ],
-        [pltpu.SemaphoreType.DMA((count,))],
+        [pltpu.VMEM((reach_rows, model_width), BF16), pltpu.SemaphoreType.DMA((count,))],
         flops=6 * work_rows * model_width * width,
         moved=16 * MIB,
-    )
-    from_before = passed_along(kv_last, SEQ, 1)
-    from_after = passed_along(kv_first, SEQ, -1)
-    reach_rows = work_rows + 2 * HALF
-    queries = steps_b.ride(queries)
+        room=60,
+    )
+    queries, cot_other = steps_b.ride((queries, cot_other))
+    cot_all = pair_rows(cotangent, cot_other)
     context, attn_term = call(
         attend_kernel,
-        (seq, queries, kv_own, from_before, from_after, attn_matrix),
-        [SMEM] + [VMEM] * 5,
+        (seq, queries, keys_values, attn_matrix),
+        [SMEM] + [VMEM] * 3,
         [shape_of(work_rows, width, BF16), shape_of(work_rows, model_width, BF16)],
-        [pltpu.VMEM((reach_rows, 2 * width), BF16)],
         flops=2 * work_rows * model_width * width,
         moved=16 * MIB,
     )
@@ -578,14 +639,14 @@
     pieces, starts = steps_b.finish()
     count = len(pieces)
     residual, work_two, hidden, grad_proj, grad_two, down_term = call(
-        functools.partial(hidden_kernel, count),
+        functools.partial(hidden_kernel, count, spare),
         (starts, tokens_all, attn_term, attn_other, gains, cot_all, *pieces),
         [SMEM] + [VMEM] * 5 + [ANY] * count,
         [
             shape_of(work_rows, model_width, F32),
             shape_of(work_rows, model_width, BF16),
-            shape_of(work_rows, units_pad, BF16),
-            shape_of(work_rows, 2 * units_pad, BF16),
+            shape_of(work_rows, whole_units + LANES, BF16),
+            shape_of(work_rows, 2 * whole_units + LANES, BF16),
             shape_of(work_rows, model_width, BF16),
             shape_of(work_rows, model_width, BF16),
         ],
@@ -593,20 +654,20 @@
             pltpu.VMEM((model_width, blob_b.shape[1]), BF16),
             pltpu.SemaphoreType.DMA((count,)),
         ],
-        flops=12 * work_rows * model_width * units_pad,
+        flops=12 * work_rows * model_width * units,
         moved=32 * MIB,
+        room=60,
     )
     grad_two_other = pair_swap(grad_two)
-    steps_b = Stepped(summed_terms(ring, "sum_b", work_two, grad_proj, cot_all, hidden))
-    steps_b.step()
+    steps_b = Stepped(summed_terms(ring, "sum_b", work_two, grad_proj, cot_all, hidden, tail=LANES, room=60))
     grad_two = steps_b.ride(grad_two)
     grad_residual, grad_low, gain_two, grad_queries, grad_own, to_before, to_after = call(
         attend_back_kernel,
         (
             seq, residual, gains, grad_two, grad_two_other, cot_all, attn_matrix,
-            queries, kv_own, from_before, from_after, cosine, sine,
+            queries, keys_values, cosine, sine,
         ),
-        [SMEM] + [VMEM] * 12,
+        [SMEM] + [VMEM] * 10,
         [
             shape_of(work_rows, model_width, F32),
             shape_of(work_rows, model_width, BF16),
@@ -616,22 +677,15 @@
             shape_of(HALF, 2 * width, BF16),
             shape_of(HALF, 2 * width, BF16),
         ],
-        [
-            pltpu.VMEM((reach_rows, 2 * width), BF16),
-            pltpu.VMEM((reach_rows, 2 * width), F32),
-        ],
+        [pltpu.VMEM((reach_rows, 2 * width), F32)],
         flops=4 * work_rows * model_width * width,
         moved=24 * MIB,
     )
+    to_before, to_after = steps_b.ride((to_before, to_after))
     from_next = passed_along(to_before, SEQ, -1)
     from_prev = passed_along(to_after, SEQ, 1)
 
     down_other = pair_swap(other_rows(down_term, row_count))
-    output = (
-        own_rows(residual, row_count)
-        + (own_rows(down_term, row_count).astype(F32) + down_other.astype(F32))
-    ).astype(BF16)
-
     grad_queries = steps_b.ride(grad_queries)
     grad_qkv, grad_one, gain_columns = call(
         last_kernel,
@@ -650,12 +704,22 @@
         moved=16 * MIB,
     )
     one_other = pair_swap(other_rows(grad_one, row_count))
+    down_other = steps_b.hold(down_other)
     steps_a = Stepped(summed_terms(ring, "sum_a", work_one, grad_qkv, grad_low, context, gain_columns))
+    steps_a.step()
+    steps_a.beside(steps_b)
+    one_other = steps_a.hold(one_other)
+    steps_a.step()
     steps_a.beside(steps_b)
     steps_a.step()
     steps_a.beside(steps_b)
     share_b = steps_b.finish()
     share_a = steps_a.finish()
+
+    output = (
+        own_rows(residual, row_count)
+        + (own_rows(down_term, row_count).astype(F32) + down_other.astype(F32))
+    ).astype(BF16)
 
     gain_one = gains[0:1]
     unit_one, inverse_one = unit_of(tokens.astype(F32))
@@ -664,6 +728,11 @@
         own_rows(grad_residual, row_count)
         + norm_back(grad_low_one, gain_one, unit_one, inverse_one)
     ).astype(BF16)
+
+    def share_b_part(part):
+        tail = 3 * whole_units + part * spare
+        main = share_b[:, part * whole_units : (part + 1) * whole_units]
+        return jnp.concatenate([main, share_b[:, tail : tail + spare]], axis=1)
 
     share_gains = share_a[:, 4 * width : 4 * width + 2] + share_a[:, 4 * width + 2 : 4 * width + 4]
     share_gain_one = share_gains[:, 0]
@@ -675,8 +744,8 @@
         share_a[:, : 3 * width].reshape(depth, 3, width),
         share_a[:, 3 * width : 4 * width].T,
         share_gains[:, 1],
-        jnp.stack([share_b[:, :units], share_b[:, units_pad : units_pad + units]], axis=1),
-        share_b[:, 2 * units_pad : 2 * units_pad + units].T,
+        jnp.stack([share_b_part(0), share_b_part(1)], axis=1),
+        share_b_part(2).T,
     )
 
 

time: 250 us -> 237 us (0.948)
  waiting for transfers between devices: 101 us -> 87.6 us
  Pallas kernels: 36.6 us -> 48.2 us
  other arithmetic: 22.8 us -> 17.6 us
  local copies, waits for them, and re-layouts: 29.9 us -> 24.9 us
    ppermute x7, waiting for transfers between devices: 23.6 us -> 8.89 us  [pair_swap(): return lax.ppermute(block, PAIR, [(0, 1), (1, 0)])]
    pallas_call x2 -> x4, Pallas kernels: 8.72 us -> 19.9 us  [weight_terms(): pl.pallas_call(functools.partial(weight_kernel, tail), grid_spec=pltpu.Pr...]
    slice x9 -> x13, local copies, waits for them, and re-layouts: 6.98 us -> 0.76 us  [the longest x1 0.5 us: local(): parts = [w_in[:, 0], w_in[:, 1], w_down.T]]
    convert_element_type x6, other arithmetic: 8.16 us -> 3.05 us  [scatter_sum(): downward = (at(self.half + step) + downward).astype(BF16)]
    ppermute x4 -> x2, starting transfers between devices: 5.56 us -> 3.78 us  [passed_along(): return lax.ppermute(block, axis, route)]
    unnamed x93 -> x149, local copies, waits for them, and re-layouts: 13.7 us -> 15.3 us
    ppermute x52 -> x54, waiting for transfers between devices: 77.5 us -> 77.3 us  [go(): return lax.ppermute(block, SEQ, route)]
    ppermute x52 -> x54, starting transfers between devices: 42.2 us -> 42 us  [go(): return lax.ppermute(block, SEQ, route)]
  transfers between devices with their start and end apart: 63 -> 64, of which waited for: 31 -> 31; matrix products, arithmetic and copies ran while one was open for 14% -> 10% of each run, Pallas kernels for 9% -> 13%
where the time goes in v2:
time: 237 us; the launch traced here: 236 us
  waiting for transfers between devices  87.6 us (37%)
  starting transfers between devices  56.4 us (24%)
  Pallas kernels  48.2 us (20%)
  local copies, waits for them, and re-layouts  24.9 us (11%)
  other arithmetic  17.6 us (7%)
    ppermute x54, waiting for transfers between devices, go(): return lax.ppermute(block, SEQ, route)  77.3 us
    ppermute x54, starting transfers between devices, go(): return lax.ppermute(block, SEQ, route)  42 us
    pallas_call x5, Pallas kernels, call(): pl.pallas_call(kernel, in_specs=specs, out_specs=[VMEM] * len(outs), out_...  28.3 us
    pallas_call x4, Pallas kernels, weight_terms(): pl.pallas_call(functools.partial(weight_kernel, tail), grid_spec=pltpu.Pr...  19.9 us
    unnamed x149, local copies, waits for them, and re-layouts  15.3 us
    ppermute x7, starting transfers between devices, pair_swap(): return lax.ppermute(block, PAIR, [(0, 1), (1, 0)])  9.33 us
    ppermute x7, waiting for transfers between devices, pair_swap(): return lax.ppermute(block, PAIR, [(0, 1), (1, 0)])  8.89 us
  transfers between devices with their start and end apart: 64, of which 31 were waited for; matrix products, arithmetic and copies ran while one was open for 10% of the time, Pallas kernels for 13%

profile of v2, /device:TPU:0, one launch (start us, length us, event | category | flops | bytes accessed | tf_op | source)
XLA Modules:
  0.0 236.4 jit_solution(14293972064595251100)
XLA Ops:
  3.3 3.1 %collective-permute-start.1 = (bf16[64,2176]{1,0:T(8,128)(2,1)S(1)}, bf16[64,2176]{1,0:T(8,128)(2,1)S(1)}, u32[]{:S(2)}, u32[]{:S(2)}) collective-permute-start(bf16[64,2176]{1,0:T(8,128)(2,1)S(1)} %fusion.26.refs_0_), channel_id=1, source_target_pairs={{0,8},{2,10},{4,0},{6,2},{8,16},{10,18},{12,4},{14,6},{16,24},{18,... | collective-permute-start | bytes 835592 | tf_op jit(solution)/shard_map/gather_a_up_1/ppermute | solution.py:65
  7.4 1.3 collective-permute-start
  9.2 1.4 collective-permute-done
  10.7 2.3 collective-permute-done.1.refs_1_
  13.0 1.5 collective-permute-done.2.refs_2_
  14.5 1.6 collective-permute-start.5
  16.2 1.2 collective-permute-start.6
  17.4 2.1 collective-permute-start.4
  20.0 4.2 %collective-permute-done.5.refs_3_ = bf16[64,2176]{1,0:T(8,128)(2,1)} collective-permute-done((bf16[64,2176]{1,0:T(8,128)(2,1)S(1)}, bf16[64,2176]{1,0:T(8,128)(2,1)}, u32[]{:S(2)}, u32[]{:S(2)}) %collective-permute-start.5) | collective-permute-done | bytes 278560 | tf_op jit(solution)/shard_map/gather_a_up_2/ppermute | solution.py:65
  24.2 1.1 collective-permute-done.6.refs_4_
  25.3 3.7 %collective-permute-done.4 = bf16[192,1024]{1,0:T(8,128)(2,1)S(1)} collective-permute-done((bf16[192,1024]{1,0:T(8,128)(2,1)S(1)}, bf16[192,1024]{1,0:T(8,128)(2,1)S(1)}, u32[]{:S(2)}, u32[]{:S(2)}) %collective-permute-start.4) | collective-permute-done | bytes 393248 | tf_op jit(solution)/shard_map/ppermute | solution.py:32
  29.0 1.8 collective-permute-start.11
  31.9 5.6 %collective-permute-done.11.refs_5_ = bf16[64,2176]{1,0:T(8,128)(2,1)S(1)} collective-permute-done((bf16[64,2176]{1,0:T(8,128)(2,1)}, bf16[64,2176]{1,0:T(8,128)(2,1)S(1)}, u32[]{:S(2)}, u32[]{:S(2)}) %collective-permute-start.11) | collective-permute-done | bytes 278560 | tf_op jit(solution)/shard_map/gather_a_up_3/ppermute | solution.py:65
  37.5 1.6 collective-permute-done.12.refs_6_
  39.1 1.6 collective-permute-start.13
  42.8 1.4 collective-permute-done.13.refs_7_
  44.3 1.6 collective-permute-start.9
  48.0 8.9 %collective-permute-done.10.refs_2_ = bf16[64,3968]{1,0:T(8,128)(2,1)} collective-permute-done((bf16[64,3968]{1,0:T(8,128)(2,1)S(1)}, bf16[64,3968]{1,0:T(8,128)(2,1)}, u32[]{:S(2)}, u32[]{:S(2)}) %collective-permute-start.10) | collective-permute-done | bytes 507936 | tf_op jit(solution)/shard_map/gather_b_down_1/ppermute | solution.py:65
  58.3 1.7 collective-permute-start.22
  63.0 1.4 collective-permute-start.21
  65.1 6.8 %shard_map.251 = (bf16[1024,2176]{1,0:T(8,128)(2,1)}, bf16[1024,512]{1,0:T(8,128)(2,1)}, f32[8,1024]{1,0:T(8,128)}, bf16[256,1024]{1,0:T(8,128)(2,1)}, bf16[256,...) custom-call(s32[18]{0:T(128)} %multiply_add_fusion.starts, bf16[256,1024]{1,0:T(8,128)(2,1)} %pad_maximum_fusion.1.tokens, ...), custom_call_target="tpu_custom_call" | custom-call | flops 805306368 | bytes 16777216 | tf_op jit(solution)/shard_map/pallas_call | solution.py:178
  72.0 2.3 collective-permute-done.23.refs_4_
  74.3 1.2 copy-done.3
  77.6 2.5 %shard_map.252 = (bf16[256,512]{1,0:T(8,128)(2,1)S(1)}, bf16[256,1024]{1,0:T(8,128)(2,1)S(1)}) custom-call(s32[2]{0:T(128)S(1)} %pad_add_fusion.seq, bf16[256,512]{1,0:T(8,128)(2,1)S(1)} %copy-done.12, bf16[384,1024]{1,0:T(8,128)(2,1)S(1)} %copy-done.7, bf16[1024,512]{1,0:T(8,128)(2,1)S(1)} %copy-done.3), custom_call_target="tpu_custom_call" | custom-call | flops 268435456 | bytes 16777216 | tf_op jit(solution)/shard_map/pallas_call | solution.py:178
  80.8 1.4 collective-permute-start.25
  83.1 1.1 collective-permute-start.27
  84.8 10.5 %collective-permute-done.26.refs_5_ = bf16[64,3968]{1,0:T(8,128)(2,1)S(1)} collective-permute-done((bf16[64,3968]{1,0:T(8,128)(2,1)}, bf16[64,3968]{1,0:T(8,128)(2,1)S(1)}, u32[]{:S(2)}, u32[]{:S(2)}) %collective-permute-start.26) | collective-permute-done | bytes 507936 | tf_op jit(solution)/shard_map/gather_b_up_3/ppermute | solution.py:65
  99.3 1.2 gather_fusion.2
  100.5 4.2 %collective-permute-done.30.refs_7_ = bf16[32,3968]{1,0:T(8,128)(2,1)S(1)} collective-permute-done((bf16[32,3968]{1,0:T(8,128)(2,1)S(1)}, bf16[32,3968]{1,0:T(8,128)(2,1)S(1)}, u32[]{:S(2)}, u32[]{:S(2)}) %collective-permute-start.30) | collective-permute-done | bytes 253984 | tf_op jit(solution)/shard_map/gather_b_up_4/ppermute | solution.py:65
  108.1 11.0 %shard_map.253 = (f32[256,1024]{1,0:T(8,128)}, bf16[256,1024]{1,0:T(8,128)(2,1)}, bf16[256,1408]{1,0:T(8,128)(2,1)}, bf16[256,2688]{1,0:T(8,128)(2,1)}, bf16[256...) custom-call(s32[18]{0:T(128)} %multiply_add_fusion.starts, bf16[256,1024]{1,0:T(8,128)(2,1)} %pad_maximum_fusion.1.tokens, ...), custom_call_target="tpu_custom_call" | custom-call | flops 4127195136 | bytes 33554432 | tf_op jit(solution)/shard_map/pallas_call | solution.py:178
  120.4 1.1 gather_fusion.1
  121.6 5.4 %shard_map.254 = (bf16[3,64,3968]{2,1,0:T(8,128)(2,1)}, bf16[3,64,3968]{2,1,0:T(8,128)(2,1)}) custom-call(s32[3]{0:T(128)} %gather_fusion.1, s32[1]{0:T(128)} %bitcast.10.core, bf16[256,1024]{1,0:T(8,128)(2,1)} %get-tuple-element.204.left_one, bf16[256,1024]{1,0:T(8,128)(2,1)} %pad_maximum_fusion.2.cot.left_two, ...), custom_call_target="tpu_custom_call" | custom-call | flops 780140544 | bytes 5079040 | tf_op jit(solution)/shard_map/pallas_call | solution.py:467
  127.0 7.4 %shard_map.255 = (bf16[5,64,3968]{2,1,0:T(8,128)(2,1)}, bf16[5,64,3968]{2,1,0:T(8,128)(2,1)}) custom-call(s32[5]{0:T(128)} %gather_fusion.2, s32[1]{0:T(128)} %bitcast.10.core, bf16[256,1024]{1,0:T(8,128)(2,1)} %get-tuple-element.204.left_one, bf16[256,1024]{1,0:T(8,128)(2,1)} %pad_maximum_fusion.2.cot.left_two, ...), custom_call_target="tpu_custom_call" | custom-call | flops 1300234240 | bytes 7110656 | tf_op jit(solution)/shard_map/pallas_call | solution.py:467
  136.1 6.7 %shard_map.256 = (f32[256,1024]{1,0:T(8,128)S(1)}, bf16[256,1024]{1,0:T(8,128)(2,1)S(1)}, f32[8,1024]{1,0:T(8,128)S(1)}, bf16[256,512]{1,0:T(8,128)(2,1)S(1)}, f...) custom-call(s32[2]{0:T(128)S(1)} %copy-done.27, f32[256,1024]{1,0:T(8,128)S(1)} %copy-done.9, ...), custom_call_target="tpu_custom_call" | custom-call | flops 536870912 | bytes 25165824 | tf_op jit(solution)/shard_map/pallas_call | solution.py:178
  148.8 2.5 %collective-permute-start.43 = (bf16[64,1024]{1,0:T(8,128)(2,1)}, bf16[64,1024]{1,0:T(8,128)(2,1)S(1)}, u32[]{:S(2)}, u32[]{:S(2)}) collective-permute-start(bf16[64,1024]{1,0:T(8,128)(2,1)} %copy-done.31), channel_id=1, source_target_pairs={{0,2},{2,4},{4,6},{6,8},{8,10},{10,12},{12,14},{14,16},{16,18},{18... | collective-permute-start | bytes 393224 | tf_op jit(solution)/shard_map/ppermute | solution.py:28
  151.3 1.3 collective-permute-start.44
  152.6 1.3 add_convert_fusion
  153.9 3.6 %collective-permute-start.41 = (bf16[32,3968]{1,0:T(8,128)(2,1)S(1)}, bf16[32,3968]{1,0:T(8,128)(2,1)S(1)}, u32[]{:S(2)}, u32[]{:S(2)}) collective-permute-start(bf16[32,3968]{1,0:T(8,128)(2,1)S(1)} %get-tuple-element.223), channel_id=1, source_target_pairs={{0,8},{2,10},{4,0},{6,2},{8,16},{10,18},{12,4},{14,6},{16,24},{18,... | collective-permute-start | bytes 761864 | tf_op jit(solution)/shard_map/sum_b_up_1/ppermute | solution.py:65
  157.6 1.5 collective-permute-start.38
  159.1 2.3 copy-done.2
  161.4 1.3 shard_map.257
  162.7 3.0 %shard_map.258 = (bf16[3,64,2176]{2,1,0:T(8,128)(2,1)}, bf16[3,64,2176]{2,1,0:T(8,128)(2,1)}) custom-call(s32[3]{0:T(128)S(1)} %copy-done.25, s32[1]{0:T(128)} %bitcast.10.core, bf16[256,1024]{1,0:T(8,128)(2,1)S(1)} %copy-done.14, bf16[256,1024]{1,0:T(8,128)(2,1)S(1)} %copy-done.16, bf16[256,1536]{1,0:T(8,128)(2,1)S(1)} %get-tuple-element.236.right_one, ...), custom_call_target="tpu_custom_call" | custom-call | flops 427819008 | bytes 2785280 | tf_op jit(solution)/shard_map/pallas_call | solution.py:467
  165.7 4.2 %shard_map.259 = (bf16[5,64,2176]{2,1,0:T(8,128)(2,1)}, bf16[5,64,2176]{2,1,0:T(8,128)(2,1)}) custom-call(s32[5]{0:T(128)S(1)} %copy-done.28, s32[1]{0:T(128)} %bitcast.10.core, bf16[256,1024]{1,0:T(8,128)(2,1)S(1)} %copy-done.14, bf16[256,1024]{1,0:T(8,128)(2,1)S(1)} %copy-done.16, bf16[256,1536]{1,0:T(8,128)(2,1)S(1)} %get-tuple-element.236.right_one, ...), custom_call_target="tpu_custom_call" | custom-call | flops 713031680 | bytes 3899392 | tf_op jit(solution)/shard_map/pallas_call | solution.py:467
  169.9 1.7 fusion.5
  173.3 1.9 collective-permute-start.51
  176.2 4.5 %collective-permute-done.45 = bf16[128,1024]{1,0:T(8,128)(2,1)S(1)} collective-permute-done((bf16[128,1024]{1,0:T(8,128)(2,1)S(1)}, bf16[128,1024]{1,0:T(8,128)(2,1)S(1)}, u32[]{:S(2)}, u32[]{:S(2)}) %collective-permute-start.45) | collective-permute-done | bytes 262176 | tf_op jit(solution)/shard_map/ppermute | solution.py:32
  180.8 2.0 collective-permute-start.48
  182.8 5.0 %collective-permute-done.51 = bf16[64,3968]{1,0:T(8,128)(2,1)S(1)} collective-permute-done((bf16[64,3968]{1,0:T(8,128)(2,1)S(1)}, bf16[64,3968]{1,0:T(8,128)(2,1)S(1)}, u32[]{:S(2)}, u32[]{:S(2)}) %collective-permute-start.51) | collective-permute-done | bytes 507936 | tf_op jit(solution)/shard_map/sum_b_up_2/ppermute | solution.py:65
  187.8 1.5 collective-permute-start.49
  189.7 3.2 %collective-permute-done.49 = bf16[32,2176]{1,0:T(8,128)(2,1)S(1)} collective-permute-done((bf16[32,2176]{1,0:T(8,128)(2,1)S(1)}, bf16[32,2176]{1,0:T(8,128)(2,1)S(1)}, u32[]{:S(2)}, u32[]{:S(2)}) %collective-permute-start.49) | collective-permute-done | bytes 139296 | tf_op jit(solution)/shard_map/sum_a_down_1/ppermute | solution.py:65
  193.0 1.9 collective-permute-start.53
  195.4 1.9 collective-permute-start.57
  197.4 5.2 %collective-permute-done.53 = bf16[64,2176]{1,0:T(8,128)(2,1)S(1)} collective-permute-done((bf16[64,2176]{1,0:T(8,128)(2,1)S(1)}, bf16[64,2176]{1,0:T(8,128)(2,1)S(1)}, u32[]{:S(2)}, u32[]{:S(2)}) %collective-permute-start.53) | collective-permute-done | bytes 278560 | tf_op jit(solution)/shard_map/sum_a_up_2/ppermute | solution.py:65
  202.7 1.9 collective-permute-done.54
  204.8 1.3 collective-permute-start.55
  206.9 5.4 %collective-permute-done.57 = bf16[64,3968]{1,0:T(8,128)(2,1)S(1)} collective-permute-done((bf16[64,3968]{1,0:T(8,128)(2,1)S(1)}, bf16[64,3968]{1,0:T(8,128)(2,1)S(1)}, u32[]{:S(2)}, u32[]{:S(2)}) %collective-permute-start.57) | collective-permute-done | bytes 507936 | tf_op jit(solution)/shard_map/sum_b_up_3/ppermute | solution.py:65
  212.3 1.6 collective-permute-done.58
  215.4 2.2 collective-permute-done.56
  217.8 1.8 collective-permute-start.59
  220.9 1.7 collective-permute-start.62
  222.9 3.8 %collective-permute-done.59 = bf16[64,2176]{1,0:T(8,128)(2,1)S(1)} collective-permute-done((bf16[64,2176]{1,0:T(8,128)(2,1)S(1)}, bf16[64,2176]{1,0:T(8,128)(2,1)S(1)}, u32[]{:S(2)}, u32[]{:S(2)}) %collective-permute-start.59) | collective-permute-done | bytes 278560 | tf_op jit(solution)/shard_map/sum_a_up_4/ppermute | solution.py:65
  226.7 1.6 collective-permute-done.60
  229.2 1.4 collective-permute-start.61
  234.2 1.4 copy.59
  (303 shorter events, 48.7 us)
Async XLA Ops:
  3.3 9.7 %collective-permute-start.1 = (bf16[64,2176]{1,0:T(8,128)(2,1)S(1)}, bf16[64,2176]{1,0:T(8,128)(2,1)S(1)}, u32[]{:S(2)}, u32[]{:S(2)}) collective-permute-start(bf16[64,2176]{1,0:T(8,128)(2,1)S(1)} %fusion.26.refs_0_), channel_id=1, source_target_pairs={{0,8},{2,10},{4,0},{6,2},{8,16},{10,18},{12,4},{14,6},{16,24},{18,... | collective-permute-start | bytes 835592 | tf_op jit(solution)/shard_map/gather_a_up_1/ppermute | solution.py:65
  6.4 8.1 %collective-permute-start.2 = (bf16[64,2176]{1,0:T(8,128)(2,1)S(1)}, bf16[64,2176]{1,0:T(8,128)(2,1)S(1)}, u32[]{:S(2)}, u32[]{:S(2)}) collective-permute-start(bf16[64,2176]{1,0:T(8,128)(2,1)S(1)} %fusion.26.refs_0_), channel_id=1, source_target_pairs={{0,4},{2,6},{4,12},{6,14},{8,0},{10,2},{12,20},{14,22},{16,8},{18,... | collective-permute-start | bytes 835592 | tf_op jit(solution)/shard_map/gather_a_down_1/ppermute | solution.py:65
  6.4 8.1 %collective-permute-start.3 = (bf16[64,2176]{1,0:T(8,128)(2,1)S(1)}, bf16[64,2176]{1,0:T(8,128)(2,1)S(1)}, u32[]{:S(2)}, u32[]{:S(2)}) collective-permute-start(bf16[64,2176]{1,0:T(8,128)(2,1)S(1)} %fusion.26.refs_0_), channel_id=1, source_target_pairs={{0,2},{2,0},{4,6},{6,4},{8,10},{10,8},{12,14},{14,12},{16,18},{18,... | collective-permute-start | bytes 835592 | tf_op jit(solution)/shard_map/gather_a_cores_0/ppermute | solution.py:65
  7.4 3.3 %collective-permute-start = (bf16[64,1024]{1,0:T(8,128)(2,1)S(1)}, bf16[64,1024]{1,0:T(8,128)(2,1)S(1)}, u32[]{:S(2)}, u32[]{:S(2)}) collective-permute-start(bf16[64,1024]{1,0:T(8,128)(2,1)S(1)} %slice_select_fusion), channel_id=1, source_target_pairs={{2,0},{4,2},{6,4},{8,6},{10,8},{12,10},{14,12},{16,14},{18,16},{20... | collective-permute-start | bytes 393224 | tf_op jit(solution)/shard_map/ppermute | solution.py:546
  14.5 9.7 %collective-permute-start.5 = (bf16[64,2176]{1,0:T(8,128)(2,1)S(1)}, bf16[64,2176]{1,0:T(8,128)(2,1)}, u32[]{:S(2)}, u32[]{:S(2)}) collective-permute-start(bf16[64,2176]{1,0:T(8,128)(2,1)S(1)} %collective-permute-done.1.refs_1_), channel_id=1, source_target_pairs={{0,8},{2,10},{4,0},{6,2},{8,16},{10,18},{12,4},{14,6},{16,24},{18,... | collective-permute-start | bytes 835592 | tf_op jit(solution)/shard_map/gather_a_up_2/ppermute | solution.py:65
  16.2 9.2 %collective-permute-start.7 = (bf16[64,2176]{1,0:T(8,128)(2,1)S(1)}, bf16[64,2176]{1,0:T(8,128)(2,1)}, u32[]{:S(2)}, u32[]{:S(2)}) collective-permute-start(bf16[64,2176]{1,0:T(8,128)(2,1)S(1)} %collective-permute-done.1.refs_1_), channel_id=1, source_target_pairs={{0,2},{2,0},{4,6},{6,4},{8,10},{10,8},{12,14},{14,12},{16,18},{18,... | collective-permute-start | bytes 835592 | tf_op jit(solution)/shard_map/gather_a_cores_-1/ppermute | solution.py:65
  16.2 9.2 %collective-permute-start.6 = (bf16[64,2176]{1,0:T(8,128)(2,1)S(1)}, bf16[64,2176]{1,0:T(8,128)(2,1)}, u32[]{:S(2)}, u32[]{:S(2)}) collective-permute-start(bf16[64,2176]{1,0:T(8,128)(2,1)S(1)} %collective-permute-done.2.refs_2_), channel_id=1, source_target_pairs={{0,4},{2,6},{4,12},{6,14},{8,0},{10,2},{12,20},{14,22},{16,8},{18,... | collective-permute-start | bytes 835592 | tf_op jit(solution)/shard_map/gather_a_down_2/ppermute | solution.py:65
  17.4 8.0 %collective-permute-start.8 = (bf16[64,2176]{1,0:T(8,128)(2,1)S(1)}, bf16[64,2176]{1,0:T(8,128)(2,1)}, u32[]{:S(2)}, u32[]{:S(2)}) collective-permute-start(bf16[64,2176]{1,0:T(8,128)(2,1)S(1)} %collective-permute-done.2.refs_2_), channel_id=1, source_target_pairs={{0,2},{2,0},{4,6},{6,4},{8,10},{10,8},{12,14},{14,12},{16,18},{18,... | collective-permute-start | bytes 835592 | tf_op jit(solution)/shard_map/gather_a_cores_1/ppermute | solution.py:65
  17.4 11.6 %collective-permute-start.4 = (bf16[192,1024]{1,0:T(8,128)(2,1)S(1)}, bf16[192,1024]{1,0:T(8,128)(2,1)S(1)}, u32[]{:S(2)}, u32[]{:S(2)}) collective-permute-start(bf16[192,1024]{1,0:T(8,128)(2,1)S(1)} %pad_maximum_fusion.3), channel_id=1, source_target_pairs={{0,1},{1,0},{2,3},{3,2},{4,5},{5,4},{6,7},{7,6},{8,9},{9,8},{10,11... | collective-permute-start | bytes 1179656 | tf_op jit(solution)/shard_map/ppermute | solution.py:32
  29.0 8.5 %collective-permute-start.11 = (bf16[64,2176]{1,0:T(8,128)(2,1)}, bf16[64,2176]{1,0:T(8,128)(2,1)S(1)}, u32[]{:S(2)}, u32[]{:S(2)}) collective-permute-start(bf16[64,2176]{1,0:T(8,128)(2,1)} %collective-permute-done.5.refs_3_), channel_id=1, source_target_pairs={{0,8},{2,10},{4,0},{6,2},{8,16},{10,18},{12,4},{14,6},{16,24},{18,... | collective-permute-start | bytes 835592 | tf_op jit(solution)/shard_map/gather_a_up_3/ppermute | solution.py:65
  30.8 8.3 %collective-permute-start.12 = (bf16[64,2176]{1,0:T(8,128)(2,1)}, bf16[64,2176]{1,0:T(8,128)(2,1)S(1)}, u32[]{:S(2)}, u32[]{:S(2)}) collective-permute-start(bf16[64,2176]{1,0:T(8,128)(2,1)} %collective-permute-done.6.refs_4_), channel_id=1, source_target_pairs={{0,4},{2,6},{4,12},{6,14},{8,0},{10,2},{12,20},{14,22},{16,8},{18,... | collective-permute-start | bytes 835592 | tf_op jit(solution)/shard_map/gather_a_down_3/ppermute | solution.py:65
  39.1 5.1 %collective-permute-start.13 = (bf16[32,2176]{1,0:T(8,128)(2,1)S(1)}, bf16[32,2176]{1,0:T(8,128)(2,1)S(1)}, u32[]{:S(2)}, u32[]{:S(2)}) collective-permute-start(bf16[32,2176]{1,0:T(8,128)(2,1)S(1)} %slice.220), channel_id=1, source_target_pairs={{0,8},{2,10},{4,0},{6,2},{8,16},{10,18},{12,4},{14,6},{16,24},{18,... | collective-permute-start | bytes 417800 | tf_op jit(solution)/shard_map/gather_a_up_4/ppermute | solution.py:65
  40.8 5.9 %collective-permute-start.14 = (bf16[32,2176]{1,0:T(8,128)(2,1)S(1)}, bf16[32,2176]{1,0:T(8,128)(2,1)}, u32[]{:S(2)}, u32[]{:S(2)}) collective-permute-start(bf16[32,2176]{1,0:T(8,128)(2,1)S(1)} %slice.221), channel_id=1, source_target_pairs={{0,4},{2,6},{4,12},{6,14},{8,0},{10,2},{12,20},{14,22},{16,8},{18,... | collective-permute-start | bytes 417800 | tf_op jit(solution)/shard_map/gather_a_down_4/ppermute | solution.py:65
  42.0 5.4 %collective-permute-start.15 = (bf16[64,2176]{1,0:T(8,128)(2,1)}, bf16[64,2176]{1,0:T(8,128)(2,1)S(1)}, u32[]{:S(2)}, u32[]{:S(2)}) collective-permute-start(bf16[64,2176]{1,0:T(8,128)(2,1)} %collective-permute-done.5.refs_3_), channel_id=1, source_target_pairs={{0,2},{2,0},{4,6},{6,4},{8,10},{10,8},{12,14},{14,12},{16,18},{18,... | collective-permute-start | bytes 835592 | tf_op jit(solution)/shard_map/gather_a_cores_-2/ppermute | solution.py:65
  42.0 5.8 %collective-permute-start.16 = (bf16[64,2176]{1,0:T(8,128)(2,1)}, bf16[64,2176]{1,0:T(8,128)(2,1)S(1)}, u32[]{:S(2)}, u32[]{:S(2)}) collective-permute-start(bf16[64,2176]{1,0:T(8,128)(2,1)} %collective-permute-done.6.refs_4_), channel_id=1, source_target_pairs={{0,2},{2,0},{4,6},{6,4},{8,10},{10,8},{12,14},{14,12},{16,18},{18,... | collective-permute-start | bytes 835592 | tf_op jit(solution)/shard_map/gather_a_cores_2/ppermute | solution.py:65
  42.5 14.4 %collective-permute-start.10 = (bf16[64,3968]{1,0:T(8,128)(2,1)S(1)}, bf16[64,3968]{1,0:T(8,128)(2,1)}, u32[]{:S(2)}, u32[]{:S(2)}) collective-permute-start(bf16[64,3968]{1,0:T(8,128)(2,1)S(1)} %pad.37.refs_0_), channel_id=1, source_target_pairs={{0,4},{2,6},{4,12},{6,14},{8,0},{10,2},{12,20},{14,22},{16,8},{18,... | collective-permute-start | bytes 1523720 | tf_op jit(solution)/shard_map/gather_b_down_1/ppermute | solution.py:65
  44.3 12.6 %collective-permute-start.9 = (bf16[64,3968]{1,0:T(8,128)(2,1)S(1)}, bf16[64,3968]{1,0:T(8,128)(2,1)}, u32[]{:S(2)}, u32[]{:S(2)}) collective-permute-start(bf16[64,3968]{1,0:T(8,128)(2,1)S(1)} %pad.37.refs_0_), channel_id=1, source_target_pairs={{0,8},{2,10},{4,0},{6,2},{8,16},{10,18},{12,4},{14,6},{16,24},{18,... | collective-permute-start | bytes 1523720 | tf_op jit(solution)/shard_map/gather_b_up_1/ppermute | solution.py:65
  46.7 11.5 %collective-permute-start.24 = (bf16[64,3968]{1,0:T(8,128)(2,1)S(1)}, bf16[64,3968]{1,0:T(8,128)(2,1)S(1)}, u32[]{:S(2)}, u32[]{:S(2)}) collective-permute-start(bf16[64,3968]{1,0:T(8,128)(2,1)S(1)} %pad.37.refs_0_), channel_id=1, source_target_pairs={{0,2},{2,0},{4,6},{6,4},{8,10},{10,8},{12,14},{14,12},{16,18},{18,... | collective-permute-start | bytes 1523720 | tf_op jit(solution)/shard_map/gather_b_cores_0/ppermute | solution.py:65
  47.3 12.7 %collective-permute-start.19 = (bf16[32,2176]{1,0:T(8,128)(2,1)S(1)}, bf16[32,2176]{1,0:T(8,128)(2,1)S(1)}, u32[]{:S(2)}, u32[]{:S(2)}) collective-permute-start(bf16[32,2176]{1,0:T(8,128)(2,1)S(1)} %collective-permute-done.13.refs_7_), channel_id=1, source_target_pairs={{0,2},{2,0},{4,6},{6,4},{8,10},{10,8},{12,14},{14,12},{16,18},{18,... | collective-permute-start | bytes 417800 | tf_op jit(solution)/shard_map/gather_a_cores_-4/ppermute | solution.py:65
  47.8 12.2 %collective-permute-start.20 = (bf16[32,2176]{1,0:T(8,128)(2,1)}, bf16[32,2176]{1,0:T(8,128)(2,1)S(1)}, u32[]{:S(2)}, u32[]{:S(2)}) collective-permute-start(bf16[32,2176]{1,0:T(8,128)(2,1)} %collective-permute-done.14.refs_8_), channel_id=1, source_target_pairs={{0,2},{2,0},{4,6},{6,4},{8,10},{10,8},{12,14},{14,12},{16,18},{18,... | collective-permute-start | bytes 417800 | tf_op jit(solution)/shard_map/gather_a_cores_4/ppermute | solution.py:65
  56.9 5.6 %collective-permute-start.17 = (bf16[64,2176]{1,0:T(8,128)(2,1)S(1)}, bf16[64,2176]{1,0:T(8,128)(2,1)S(1)}, u32[]{:S(2)}, u32[]{:S(2)}) collective-permute-start(bf16[64,2176]{1,0:T(8,128)(2,1)S(1)} %collective-permute-done.11.refs_5_), channel_id=1, source_target_pairs={{0,2},{2,0},{4,6},{6,4},{8,10},{10,8},{12,14},{14,12},{16,18},{18,... | collective-permute-start | bytes 835592 | tf_op jit(solution)/shard_map/gather_a_cores_-3/ppermute | solution.py:65
  56.9 6.1 %collective-permute-start.18 = (bf16[64,2176]{1,0:T(8,128)(2,1)S(1)}, bf16[64,2176]{1,0:T(8,128)(2,1)}, u32[]{:S(2)}, u32[]{:S(2)}) collective-permute-start(bf16[64,2176]{1,0:T(8,128)(2,1)S(1)} %collective-permute-done.12.refs_6_), channel_id=1, source_target_pairs={{0,2},{2,0},{4,6},{6,4},{8,10},{10,8},{12,14},{14,12},{16,18},{18,... | collective-permute-start | bytes 835592 | tf_op jit(solution)/shard_map/gather_a_cores_3/ppermute | solution.py:65
  58.3 13.7 %collective-permute-start.22 = (bf16[64,3968]{1,0:T(8,128)(2,1)}, bf16[64,3968]{1,0:T(8,128)(2,1)S(1)}, u32[]{:S(2)}, u32[]{:S(2)}) collective-permute-start(bf16[64,3968]{1,0:T(8,128)(2,1)} %collective-permute-done.9.refs_1_), channel_id=1, source_target_pairs={{0,8},{2,10},{4,0},{6,2},{8,16},{10,18},{12,4},{14,6},{16,24},{18,... | collective-permute-start | bytes 1523720 | tf_op jit(solution)/shard_map/gather_b_up_2/ppermute | solution.py:65
  60.0 24.3 %collective-permute-start.28 = (bf16[64,3968]{1,0:T(8,128)(2,1)}, bf16[64,3968]{1,0:T(8,128)(2,1)}, u32[]{:S(2)}, u32[]{:S(2)}) collective-permute-start(bf16[64,3968]{1,0:T(8,128)(2,1)} %collective-permute-done.9.refs_1_), channel_id=1, source_target_pairs={{0,2},{2,0},{4,6},{6,4},{8,10},{10,8},{12,14},{14,12},{16,18},{18,... | collective-permute-start | bytes 1523720 | tf_op jit(solution)/shard_map/gather_b_cores_-1/ppermute | solution.py:65
  60.0 14.3 %collective-permute-start.23 = (bf16[64,3968]{1,0:T(8,128)(2,1)}, bf16[64,3968]{1,0:T(8,128)(2,1)}, u32[]{:S(2)}, u32[]{:S(2)}) collective-permute-start(bf16[64,3968]{1,0:T(8,128)(2,1)} %collective-permute-done.10.refs_2_), channel_id=1, source_target_pairs={{0,4},{2,6},{4,12},{6,14},{8,0},{10,2},{12,20},{14,22},{16,8},{18,... | collective-permute-start | bytes 1523720 | tf_op jit(solution)/shard_map/gather_b_down_2/ppermute | solution.py:65
  62.4 21.8 %collective-permute-start.29 = (bf16[64,3968]{1,0:T(8,128)(2,1)}, bf16[64,3968]{1,0:T(8,128)(2,1)S(1)}, u32[]{:S(2)}, u32[]{:S(2)}) collective-permute-start(bf16[64,3968]{1,0:T(8,128)(2,1)} %collective-permute-done.10.refs_2_), channel_id=1, source_target_pairs={{0,2},{2,0},{4,6},{6,4},{8,10},{10,8},{12,14},{14,12},{16,18},{18,... | collective-permute-start | bytes 1523720 | tf_op jit(solution)/shard_map/gather_b_cores_1/ppermute | solution.py:65
  63.0 9.0 %collective-permute-start.21 = (bf16[128,1024]{1,0:T(8,128)(2,1)}, bf16[128,1024]{1,0:T(8,128)(2,1)S(1)}, u32[]{:S(2)}, u32[]{:S(2)}) collective-permute-start(bf16[128,1024]{1,0:T(8,128)(2,1)} %param.27), channel_id=1, source_target_pairs={{0,1},{1,0},{2,3},{3,2},{4,5},{5,4},{6,7},{7,6},{8,9},{9,8},{10,11... | collective-permute-start | bytes 786440 | tf_op jit(solution)/shard_map/ppermute | solution.py:32
  80.8 15.1 %collective-permute-start.25 = (bf16[256,1024]{1,0:T(8,128)(2,1)S(1)}, bf16[256,1024]{1,0:T(8,128)(2,1)}, u32[]{:S(2)}, u32[]{:S(2)}) collective-permute-start(bf16[256,1024]{1,0:T(8,128)(2,1)S(1)} %get-tuple-element.179.term), channel_id=1, source_target_pairs={{0,1},{1,0},{2,3},{3,2},{4,5},{5,4},{6,7},{7,6},{8,9},{9,8},{10,11... | collective-permute-start | bytes 1572872 | tf_op jit(solution)/shard_map/ppermute | solution.py:32
  82.3 13.1 %collective-permute-start.26 = (bf16[64,3968]{1,0:T(8,128)(2,1)}, bf16[64,3968]{1,0:T(8,128)(2,1)S(1)}, u32[]{:S(2)}, u32[]{:S(2)}) collective-permute-start(bf16[64,3968]{1,0:T(8,128)(2,1)} %copy-done.63), channel_id=1, source_target_pairs={{0,8},{2,10},{4,0},{6,2},{8,16},{10,18},{12,4},{14,6},{16,24},{18,... | collective-permute-start | bytes 1523720 | tf_op jit(solution)/shard_map/gather_b_up_3/ppermute | solution.py:65
  83.1 12.8 %collective-permute-start.27 = (bf16[64,3968]{1,0:T(8,128)(2,1)}, bf16[64,3968]{1,0:T(8,128)(2,1)S(1)}, u32[]{:S(2)}, u32[]{:S(2)}) collective-permute-start(bf16[64,3968]{1,0:T(8,128)(2,1)} %collective-permute-done.23.refs_4_), channel_id=1, source_target_pairs={{0,4},{2,6},{4,12},{6,14},{8,0},{10,2},{12,20},{14,22},{16,8},{18,... | collective-permute-start | bytes 1523720 | tf_op jit(solution)/shard_map/gather_b_down_3/ppermute | solution.py:65
  84.3 13.4 %collective-permute-start.32 = (bf16[64,3968]{1,0:T(8,128)(2,1)}, bf16[64,3968]{1,0:T(8,128)(2,1)S(1)}, u32[]{:S(2)}, u32[]{:S(2)}) collective-permute-start(bf16[64,3968]{1,0:T(8,128)(2,1)} %copy-done.63), channel_id=1, source_target_pairs={{0,2},{2,0},{4,6},{6,4},{8,10},{10,8},{12,14},{14,12},{16,18},{18,... | collective-permute-start | bytes 1523720 | tf_op jit(solution)/shard_map/gather_b_cores_-2/ppermute | solution.py:65
  84.3 16.2 %collective-permute-start.33 = (bf16[64,3968]{1,0:T(8,128)(2,1)}, bf16[64,3968]{1,0:T(8,128)(2,1)}, u32[]{:S(2)}, u32[]{:S(2)}) collective-permute-start(bf16[64,3968]{1,0:T(8,128)(2,1)} %collective-permute-done.23.refs_4_), channel_id=1, source_target_pairs={{0,2},{2,0},{4,6},{6,4},{8,10},{10,8},{12,14},{14,12},{16,18},{18,... | collective-permute-start | bytes 1523720 | tf_op jit(solution)/shard_map/gather_b_cores_2/ppermute | solution.py:65
  96.0 11.4 %collective-permute-start.34 = (bf16[64,3968]{1,0:T(8,128)(2,1)S(1)}, bf16[64,3968]{1,0:T(8,128)(2,1)}, u32[]{:S(2)}, u32[]{:S(2)}) collective-permute-start(bf16[64,3968]{1,0:T(8,128)(2,1)S(1)} %collective-permute-done.26.refs_5_), channel_id=1, source_target_pairs={{0,2},{2,0},{4,6},{6,4},{8,10},{10,8},{12,14},{14,12},{16,18},{18,... | collective-permute-start | bytes 1523720 | tf_op jit(solution)/shard_map/gather_b_cores_-3/ppermute | solution.py:65
  96.1 11.3 %collective-permute-start.35 = (bf16[64,3968]{1,0:T(8,128)(2,1)S(1)}, bf16[64,3968]{1,0:T(8,128)(2,1)}, u32[]{:S(2)}, u32[]{:S(2)}) collective-permute-start(bf16[64,3968]{1,0:T(8,128)(2,1)S(1)} %collective-permute-done.27.refs_6_), channel_id=1, source_target_pairs={{0,2},{2,0},{4,6},{6,4},{8,10},{10,8},{12,14},{14,12},{16,18},{18,... | collective-permute-start | bytes 1523720 | tf_op jit(solution)/shard_map/gather_b_cores_3/ppermute | solution.py:65
  96.6 8.1 %collective-permute-start.30 = (bf16[32,3968]{1,0:T(8,128)(2,1)S(1)}, bf16[32,3968]{1,0:T(8,128)(2,1)S(1)}, u32[]{:S(2)}, u32[]{:S(2)}) collective-permute-start(bf16[32,3968]{1,0:T(8,128)(2,1)S(1)} %slice.222), channel_id=1, source_target_pairs={{0,8},{2,10},{4,0},{6,2},{8,16},{10,18},{12,4},{14,6},{16,24},{18,... | collective-permute-start | bytes 761864 | tf_op jit(solution)/shard_map/gather_b_up_4/ppermute | solution.py:65
  97.7 7.8 %collective-permute-start.31 = (bf16[32,3968]{1,0:T(8,128)(2,1)S(1)}, bf16[32,3968]{1,0:T(8,128)(2,1)S(1)}, u32[]{:S(2)}, u32[]{:S(2)}) collective-permute-start(bf16[32,3968]{1,0:T(8,128)(2,1)S(1)} %slice.223), channel_id=1, source_target_pairs={{0,4},{2,6},{4,12},{6,14},{8,0},{10,2},{12,20},{14,22},{16,8},{18,... | collective-permute-start | bytes 761864 | tf_op jit(solution)/shard_map/gather_b_down_4/ppermute | solution.py:65
  105.5 1.5 collective-permute-start.36
  105.5 1.9 collective-permute-start.37
  119.1 15.3 %collective-permute-start.39 = (bf16[256,1024]{1,0:T(8,128)(2,1)}, bf16[256,1024]{1,0:T(8,128)(2,1)}, u32[]{:S(2)}, u32[]{:S(2)}) collective-permute-start(bf16[256,1024]{1,0:T(8,128)(2,1)} %get-tuple-element.212.grad_two), channel_id=1, source_target_pairs={{0,1},{1,0},{2,3},{3,2},{4,5},{5,4},{6,7},{7,6},{8,9},{9,8},{10,11... | collective-permute-start | bytes 1572872 | tf_op jit(solution)/shard_map/ppermute | solution.py:32
  147.6 5.0 %collective-permute-start.40 = (bf16[3,64,3968]{2,1,0:T(8,128)(2,1)}, bf16[3,64,3968]{2,1,0:T(8,128)(2,1)}, u32[]{:S(2)}, u32[]{:S(2)}) collective-permute-start(bf16[3,64,3968]{2,1,0:T(8,128)(2,1)} %get-tuple-element.219), channel_id=1, source_target_pairs={{0,2},{2,0},{4,6},{6,4},{8,10},{10,8},{12,14},{14,12},{16,18},{18,... | collective-permute-start | bytes 4571144 | tf_op jit(solution)/shard_map/sum_b_cores_early/ppermute | solution.py:65
  148.8 10.3 %collective-permute-start.43 = (bf16[64,1024]{1,0:T(8,128)(2,1)}, bf16[64,1024]{1,0:T(8,128)(2,1)S(1)}, u32[]{:S(2)}, u32[]{:S(2)}) collective-permute-start(bf16[64,1024]{1,0:T(8,128)(2,1)} %copy-done.31), channel_id=1, source_target_pairs={{0,2},{2,4},{4,6},{6,8},{8,10},{10,12},{12,14},{14,16},{16,18},{18... | collective-permute-start | bytes 393224 | tf_op jit(solution)/shard_map/ppermute | solution.py:28
  151.3 7.8 %collective-permute-start.44 = (bf16[64,1024]{1,0:T(8,128)(2,1)}, bf16[64,1024]{1,0:T(8,128)(2,1)S(1)}, u32[]{:S(2)}, u32[]{:S(2)}) collective-permute-start(bf16[64,1024]{1,0:T(8,128)(2,1)} %copy-done.30), channel_id=1, source_target_pairs={{2,0},{4,2},{6,4},{8,6},{10,8},{12,10},{14,12},{16,14},{18,16},{20... | collective-permute-start | bytes 393224 | tf_op jit(solution)/shard_map/ppermute | solution.py:28
  153.9 16.0 %collective-permute-start.41 = (bf16[32,3968]{1,0:T(8,128)(2,1)S(1)}, bf16[32,3968]{1,0:T(8,128)(2,1)S(1)}, u32[]{:S(2)}, u32[]{:S(2)}) collective-permute-start(bf16[32,3968]{1,0:T(8,128)(2,1)S(1)} %get-tuple-element.223), channel_id=1, source_target_pairs={{0,8},{2,10},{4,0},{6,2},{8,16},{10,18},{12,4},{14,6},{16,24},{18,... | collective-permute-start | bytes 761864 | tf_op jit(solution)/shard_map/sum_b_up_1/ppermute | solution.py:65
  157.6 12.3 %collective-permute-start.42 = (bf16[32,3968]{1,0:T(8,128)(2,1)S(1)}, bf16[32,3968]{1,0:T(8,128)(2,1)S(1)}, u32[]{:S(2)}, u32[]{:S(2)}) collective-permute-start(bf16[32,3968]{1,0:T(8,128)(2,1)S(1)} %get-tuple-element.224), channel_id=1, source_target_pairs={{0,4},{2,6},{4,12},{6,14},{8,0},{10,2},{12,20},{14,22},{16,8},{18,... | collective-permute-start | bytes 761864 | tf_op jit(solution)/shard_map/sum_b_down_1/ppermute | solution.py:65
  157.6 14.0 %collective-permute-start.38 = (bf16[128,1024]{1,0:T(8,128)(2,1)S(1)}, bf16[128,1024]{1,0:T(8,128)(2,1)S(1)}, u32[]{:S(2)}, u32[]{:S(2)}) collective-permute-start(bf16[128,1024]{1,0:T(8,128)(2,1)S(1)} %constant_dynamic-slice_fusion.1), channel_id=1, source_target_pairs={{0,1},{1,0},{2,3},{3,2},{4,5},{5,4},{6,7},{7,6},{8,9},{9,8},{10,11... | collective-permute-start | bytes 786440 | tf_op jit(solution)/shard_map/ppermute | solution.py:32
  159.1 30.2 %collective-permute-start.50 = (bf16[5,64,3968]{2,1,0:T(8,128)(2,1)}, bf16[5,64,3968]{2,1,0:T(8,128)(2,1)S(1)}, u32[]{:S(2)}, u32[]{:S(2)}) collective-permute-start(bf16[5,64,3968]{2,1,0:T(8,128)(2,1)} %get-tuple-element.257), channel_id=1, source_target_pairs={{0,2},{2,0},{4,6},{6,4},{8,10},{10,8},{12,14},{14,12},{16,18},{18,... | collective-permute-start | bytes 7618568 | tf_op jit(solution)/shard_map/sum_b_cores_rest/ppermute | solution.py:65
  171.6 4.5 %collective-permute-start.46 = (bf16[3,64,2176]{2,1,0:T(8,128)(2,1)S(1)}, bf16[3,64,2176]{2,1,0:T(8,128)(2,1)S(1)}, u32[]{:S(2)}, u32[]{:S(2)}) collective-permute-start(bf16[3,64,2176]{2,1,0:T(8,128)(2,1)S(1)} %copy-done.61), channel_id=1, source_target_pairs={{0,2},{2,0},{4,6},{6,4},{8,10},{10,8},{12,14},{14,12},{16,18},{18,... | collective-permute-start | bytes 2506760 | tf_op jit(solution)/shard_map/sum_a_cores_early/ppermute | solution.py:65
  172.5 8.3 %collective-permute-start.45 = (bf16[128,1024]{1,0:T(8,128)(2,1)S(1)}, bf16[128,1024]{1,0:T(8,128)(2,1)S(1)}, u32[]{:S(2)}, u32[]{:S(2)}) collective-permute-start(bf16[128,1024]{1,0:T(8,128)(2,1)S(1)} %constant_dynamic-slice_fusion), channel_id=1, source_target_pairs={{0,1},{1,0},{2,3},{3,2},{4,5},{5,4},{6,7},{7,6},{8,9},{9,8},{10,11... | collective-permute-start | bytes 786440 | tf_op jit(solution)/shard_map/ppermute | solution.py:32
  173.3 14.5 %collective-permute-start.51 = (bf16[64,3968]{1,0:T(8,128)(2,1)S(1)}, bf16[64,3968]{1,0:T(8,128)(2,1)S(1)}, u32[]{:S(2)}, u32[]{:S(2)}) collective-permute-start(bf16[64,3968]{1,0:T(8,128)(2,1)S(1)} %get-tuple-element.260), channel_id=1, source_target_pairs={{0,8},{2,10},{4,0},{6,2},{8,16},{10,18},{12,4},{14,6},{16,24},{18,... | collective-permute-start | bytes 1523720 | tf_op jit(solution)/shard_map/sum_b_up_2/ppermute | solution.py:65
  175.2 14.1 %collective-permute-start.52 = (bf16[64,3968]{1,0:T(8,128)(2,1)S(1)}, bf16[64,3968]{1,0:T(8,128)(2,1)S(1)}, u32[]{:S(2)}, u32[]{:S(2)}) collective-permute-start(bf16[64,3968]{1,0:T(8,128)(2,1)S(1)} %get-tuple-element.261), channel_id=1, source_target_pairs={{0,4},{2,6},{4,12},{6,14},{8,0},{10,2},{12,20},{14,22},{16,8},{18,... | collective-permute-start | bytes 1523720 | tf_op jit(solution)/shard_map/sum_b_down_2/ppermute | solution.py:65
  176.1 28.4 %collective-permute-start.47 = (bf16[5,64,2176]{2,1,0:T(8,128)(2,1)S(1)}, bf16[5,64,2176]{2,1,0:T(8,128)(2,1)S(1)}, u32[]{:S(2)}, u32[]{:S(2)}) collective-permute-start(bf16[5,64,2176]{2,1,0:T(8,128)(2,1)S(1)} %copy-done.60), channel_id=1, source_target_pairs={{0,2},{2,0},{4,6},{6,4},{8,10},{10,8},{12,14},{14,12},{16,18},{18,... | collective-permute-start | bytes 4177928 | tf_op jit(solution)/shard_map/sum_a_cores_rest/ppermute | solution.py:65
  180.8 8.9 %collective-permute-start.48 = (bf16[32,2176]{1,0:T(8,128)(2,1)S(1)}, bf16[32,2176]{1,0:T(8,128)(2,1)S(1)}, u32[]{:S(2)}, u32[]{:S(2)}) collective-permute-start(bf16[32,2176]{1,0:T(8,128)(2,1)S(1)} %get-tuple-element.254), channel_id=1, source_target_pairs={{0,8},{2,10},{4,0},{6,2},{8,16},{10,18},{12,4},{14,6},{16,24},{18,... | collective-permute-start | bytes 417800 | tf_op jit(solution)/shard_map/sum_a_up_1/ppermute | solution.py:65
  187.8 5.1 %collective-permute-start.49 = (bf16[32,2176]{1,0:T(8,128)(2,1)S(1)}, bf16[32,2176]{1,0:T(8,128)(2,1)S(1)}, u32[]{:S(2)}, u32[]{:S(2)}) collective-permute-start(bf16[32,2176]{1,0:T(8,128)(2,1)S(1)} %get-tuple-element.255), channel_id=1, source_target_pairs={{0,4},{2,6},{4,12},{6,14},{8,0},{10,2},{12,20},{14,22},{16,8},{18,... | collective-permute-start | bytes 417800 | tf_op jit(solution)/shard_map/sum_a_down_1/ppermute | solution.py:65
  193.0 9.6 %collective-permute-start.53 = (bf16[64,2176]{1,0:T(8,128)(2,1)S(1)}, bf16[64,2176]{1,0:T(8,128)(2,1)S(1)}, u32[]{:S(2)}, u32[]{:S(2)}) collective-permute-start(bf16[64,2176]{1,0:T(8,128)(2,1)S(1)} %get-tuple-element.264), channel_id=1, source_target_pairs={{0,8},{2,10},{4,0},{6,2},{8,16},{10,18},{12,4},{14,6},{16,24},{18,... | collective-permute-start | bytes 835592 | tf_op jit(solution)/shard_map/sum_a_up_2/ppermute | solution.py:65
  195.0 9.6 %collective-permute-start.54 = (bf16[64,2176]{1,0:T(8,128)(2,1)S(1)}, bf16[64,2176]{1,0:T(8,128)(2,1)S(1)}, u32[]{:S(2)}, u32[]{:S(2)}) collective-permute-start(bf16[64,2176]{1,0:T(8,128)(2,1)S(1)} %get-tuple-element.265), channel_id=1, source_target_pairs={{0,4},{2,6},{4,12},{6,14},{8,0},{10,2},{12,20},{14,22},{16,8},{18,... | collective-permute-start | bytes 835592 | tf_op jit(solution)/shard_map/sum_a_down_2/ppermute | solution.py:65
  195.4 16.9 %collective-permute-start.57 = (bf16[64,3968]{1,0:T(8,128)(2,1)S(1)}, bf16[64,3968]{1,0:T(8,128)(2,1)S(1)}, u32[]{:S(2)}, u32[]{:S(2)}) collective-permute-start(bf16[64,3968]{1,0:T(8,128)(2,1)S(1)} %get-tuple-element.270), channel_id=1, source_target_pairs={{0,8},{2,10},{4,0},{6,2},{8,16},{10,18},{12,4},{14,6},{16,24},{18,... | collective-permute-start | bytes 1523720 | tf_op jit(solution)/shard_map/sum_b_up_3/ppermute | solution.py:65
  197.3 16.6 %collective-permute-start.58 = (bf16[64,3968]{1,0:T(8,128)(2,1)S(1)}, bf16[64,3968]{1,0:T(8,128)(2,1)S(1)}, u32[]{:S(2)}, u32[]{:S(2)}) collective-permute-start(bf16[64,3968]{1,0:T(8,128)(2,1)S(1)} %get-tuple-element.271), channel_id=1, source_target_pairs={{0,4},{2,6},{4,12},{6,14},{8,0},{10,2},{12,20},{14,22},{16,8},{18,... | collective-permute-start | bytes 1523720 | tf_op jit(solution)/shard_map/sum_b_down_3/ppermute | solution.py:65
  204.8 10.6 %collective-permute-start.55 = (bf16[64,2176]{1,0:T(8,128)(2,1)S(1)}, bf16[64,2176]{1,0:T(8,128)(2,1)S(1)}, u32[]{:S(2)}, u32[]{:S(2)}) collective-permute-start(bf16[64,2176]{1,0:T(8,128)(2,1)S(1)} %get-tuple-element.266), channel_id=1, source_target_pairs={{0,8},{2,10},{4,0},{6,2},{8,16},{10,18},{12,4},{14,6},{16,24},{18,... | collective-permute-start | bytes 835592 | tf_op jit(solution)/shard_map/sum_a_up_3/ppermute | solution.py:65
  206.1 11.5 %collective-permute-start.56 = (bf16[64,2176]{1,0:T(8,128)(2,1)S(1)}, bf16[64,2176]{1,0:T(8,128)(2,1)S(1)}, u32[]{:S(2)}, u32[]{:S(2)}) collective-permute-start(bf16[64,2176]{1,0:T(8,128)(2,1)S(1)} %get-tuple-element.267), channel_id=1, source_target_pairs={{0,4},{2,6},{4,12},{6,14},{8,0},{10,2},{12,20},{14,22},{16,8},{18,... | collective-permute-start | bytes 835592 | tf_op jit(solution)/shard_map/sum_a_down_3/ppermute | solution.py:65
  217.8 8.9 %collective-permute-start.59 = (bf16[64,2176]{1,0:T(8,128)(2,1)S(1)}, bf16[64,2176]{1,0:T(8,128)(2,1)S(1)}, u32[]{:S(2)}, u32[]{:S(2)}) collective-permute-start(bf16[64,2176]{1,0:T(8,128)(2,1)S(1)} %get-tuple-element.274), channel_id=1, source_target_pairs={{0,8},{2,10},{4,0},{6,2},{8,16},{10,18},{12,4},{14,6},{16,24},{18,... | collective-permute-start | bytes 835592 | tf_op jit(solution)/shard_map/sum_a_up_4/ppermute | solution.py:65
  219.6 8.7 %collective-permute-start.60 = (bf16[64,2176]{1,0:T(8,128)(2,1)S(1)}, bf16[64,2176]{1,0:T(8,128)(2,1)S(1)}, u32[]{:S(2)}, u32[]{:S(2)}) collective-permute-start(bf16[64,2176]{1,0:T(8,128)(2,1)S(1)} %get-tuple-element.275), channel_id=1, source_target_pairs={{0,4},{2,6},{4,12},{6,14},{8,0},{10,2},{12,20},{14,22},{16,8},{18,... | collective-permute-start | bytes 835592 | tf_op jit(solution)/shard_map/sum_a_down_4/ppermute | solution.py:65
  220.9 12.4 %collective-permute-start.62 = (bf16[64,3968]{1,0:T(8,128)(2,1)S(1)}, bf16[64,3968]{1,0:T(8,128)(2,1)S(1)}, u32[]{:S(2)}, u32[]{:S(2)}) collective-permute-start(bf16[64,3968]{1,0:T(8,128)(2,1)S(1)} %get-tuple-element.278), channel_id=1, source_target_pairs={{0,8},{2,10},{4,0},{6,2},{8,16},{10,18},{12,4},{14,6},{16,24},{18,... | collective-permute-start | bytes 1523720 | tf_op jit(solution)/shard_map/sum_b_up_4/ppermute | solution.py:65
  222.6 11.1 %collective-permute-start.63 = (bf16[64,3968]{1,0:T(8,128)(2,1)S(1)}, bf16[64,3968]{1,0:T(8,128)(2,1)S(1)}, u32[]{:S(2)}, u32[]{:S(2)}) collective-permute-start(bf16[64,3968]{1,0:T(8,128)(2,1)S(1)} %get-tuple-element.279), channel_id=1, source_target_pairs={{0,4},{2,6},{4,12},{6,14},{8,0},{10,2},{12,20},{14,22},{16,8},{18,... | collective-permute-start | bytes 1523720 | tf_op jit(solution)/shard_map/sum_b_down_4/ppermute | solution.py:65
  229.2 3.5 %collective-permute-start.61 = (f32[64]{0:T(128)S(1)}, f32[64]{0:T(128)S(1)}, u32[]{:S(2)}, u32[]{:S(2)}) collective-permute-start(f32[64]{0:T(128)S(1)} %get-tuple-element.307), channel_id=1, source_target_pairs={{0,1},{1,0},{2,3},{3,2},{4,5},{5,4},{6,7},{7,6},{8,9},{9,8},{10,11... | collective-permute-start | bytes 776 | tf_op jit(solution)/shard_map/ppermute | solution.py:32
  (74 other events, 640.9 us)

commit v3 on v2

--- a/solution.py
+++ b/solution.py
@@ -71,6 +71,14 @@
         rows = block.shape[0]
         middle = rows // 2
         upward = downward = block
+        order = [0]
+        for step in range(1, self.half + 1):
+            order += [-step, step]
+        places = [(d, 0, middle if d == self.half else 0) for d in order]
+        places += [(d, 1, offset) for d, _, offset in places]
+        distances, others, offsets = np.array(places, np.int32).T
+        cores = self.chips_at(distances) * 2 + jnp.where(others == 1, 1 - self.core, self.core)
+        starts = cores * rows + offsets
         held = {0: (block, 0)}
         swapped = {}
         for step in range(1, self.half + 1):
@@ -80,7 +88,7 @@
             downward = self.go(downward, self.down, f"{name}_down_{step}")
             meanwhile = [d for d in plan[step - 1] if d in held]
             came = [self.go(held[d][0], self.swap, f"{name}_cores_{d}") for d in meanwhile]
-            upward, downward, *came = yield upward, downward, *came
+            upward, downward, starts, *came = yield upward, downward, starts, *came
             swapped.update(zip(meanwhile, came))
             held[-step] = upward, 0
             held[step] = downward, middle if step == self.half else 0
@@ -88,18 +96,13 @@
             if d not in swapped:
                 swapped[d] = self.go(held[d][0], self.swap, f"{name}_cores_{d}")
         pieces = [held[d][0] for d in held] + [swapped[d] for d in held]
-        places = [(d, 0, held[d][1]) for d in held] + [(d, 1, held[d][1]) for d in held]
-        distances, others, offsets = np.array(places, np.int32).T
-        cores = self.chips_at(distances) * 2 + jnp.where(others == 1, 1 - self.core, self.core)
-        return pieces, cores * rows + offsets
+        return pieces, starts
 
     def scatter_sum(self, early, rest, name):
         kept_early, away_early = early
         kept_rest, away_rest = rest
         count, rows = kept_early.shape[:2]
         middle = rows // 2
-        kept_early, kept_rest = yield kept_early, kept_rest
-        away_early, away_rest = yield away_early, away_rest
         came_early = self.go(away_early, self.swap, f"{name}_cores_early")
         came_rest = self.go(away_rest, self.swap, f"{name}_cores_rest")
 
@@ -113,8 +116,10 @@
         upward, downward = far[:middle], far[middle:]
         for step in range(1, self.half + 1):
             upward, downward = yield upward, downward
-            upward = self.go(upward, self.up, f"{name}_up_{step}").astype(F32)
-            downward = self.go(downward, self.down, f"{name}_down_{step}").astype(F32)
+            upward = self.go(upward, self.up, f"{name}_up_{step}")
+            downward = self.go(downward, self.down, f"{name}_down_{step}")
+            upward, downward = yield upward, downward
+            upward, downward = upward.astype(F32), downward.astype(F32)
             if step == 1:
                 upward = jnp.pad(upward, ((0, rows - middle), (0, 0)))
                 downward = jnp.pad(downward, ((middle, 0), (0, 0)))
@@ -227,11 +232,14 @@
 
 def first_kernel(count, width, starts, tokens, before, after, cosine, sine, *refs):
     pieces = refs[:count]
-    whole, matrix, gains, work, queries, keys_values, all_rows, ready = refs[count:]
+    whole, matrix, gains, work, queries, keys_values, wide_cosine, wide_sine = refs[count:-2]
+    all_rows, ready = refs[-2:]
     copies = placing(starts, pieces, whole, ready)
     for copy in copies:
         copy.start()
     joined_rows(before, tokens, after, all_rows)
+    wide_cosine[...] = jnp.concatenate([cosine[...]] * 4, axis=1)
+    wide_sine[...] = jnp.concatenate([-sine[...], sine[...]] * 2, axis=1)
     unit, _ = unit_of(all_rows[...].astype(F32))
     for copy in copies:
         copy.wait()
@@ -245,11 +253,11 @@
         columns = whole[:, start : start + 256]
         if start < width:
             part = dot(work[...], columns)
-            queries[:, start : start + 256] = turned_by(part, cosine[own], sine[own]).astype(BF16)
+            queries[:, start : start + 256] = turned_by(part, wide_cosine[own], wide_sine[own]).astype(BF16)
         else:
             part = dot(all_rows[...], columns)
             if start < 2 * width:
-                part = turned_by(part, cosine[...], sine[...])
+                part = turned_by(part, wide_cosine[...], wide_sine[...])
             keys_values[:, start - width : start - width + 256] = part.astype(BF16)
 
 
@@ -308,9 +316,9 @@
     term[...] = dot(context[...], matrix[...], (1, 1)).astype(BF16)
 
 
-def hidden_kernel(count, spare, starts, tokens, term, term_other, gains, cot, *refs):
+def hidden_kernel(count, spare, early, starts, chips, core, tokens, term, term_other, gains, cot, *refs):
     pieces = refs[:count]
-    residual, work, hidden, grad_proj, grad_two, down, whole, ready = refs[count:]
+    residual, work, hidden, grad_proj, grad_two, down, *terms, whole, ready = refs[count:]
     copies = placing(starts, pieces, whole, ready)
     for copy in copies:
         copy.start()
@@ -350,6 +358,8 @@
         + dot(grad_proj[:, 2 * units :], tail, (1, 1))
     ).astype(BF16)
     down[...] = dot(hidden[...], whole[:, 2 * units :], (1, 1)).astype(BF16)
+    if early:
+        early_rows(early, chips, core, LANES, [(work, grad_proj), (cot, hidden)], None, *terms)
 
 
 def attend_back_kernel(
@@ -396,10 +406,13 @@
 
 
 def last_kernel(
-    grad_queries, grad_own, from_before, from_after, cosine, sine, matrix, tokens, gain_two,
-    grad_qkv, grad_one, gain_columns, grad_all,
+    early, chips, core, grad_queries, grad_own, from_before, from_after, cosine, sine, tokens,
+    gain_two, work, grad_low, context, matrix_whole, grad_qkv, grad_one, gain_columns, *refs,
 ):
+    *parts, grad_all, matrix, ready = refs
     rows, width = grad_queries.shape
+    fetch = pltpu.make_async_copy(matrix_whole.at[:, : 3 * width], matrix, ready)
+    fetch.start()
     grad_all[...] = grad_own[...]
     grad_all[:HALF] += from_before[...].astype(F32)
     grad_all[rows - HALF :] += from_after[...].astype(F32)
@@ -408,7 +421,8 @@
     grad_keys = turned_by(grad_all[:, :width], cosine[own], -sine[own])
     grad_qkv[:, width : 2 * width] = grad_keys.astype(BF16)
     grad_qkv[:, 2 * width :] = grad_all[:, width:].astype(BF16)
-    grad = dot(grad_qkv[...], matrix[:, : 3 * width], (1, 1))
+    fetch.wait()
+    grad = dot(grad_qkv[...], matrix[...], (1, 1))
     grad_one[...] = grad.astype(BF16)
     unit, _ = unit_of(tokens[...].astype(F32))
     gain_one = jnp.sum(grad * unit, axis=0, keepdims=True)
@@ -416,22 +430,23 @@
     high = gain.astype(BF16).astype(F32)
     spare = jnp.zeros((LANES - 4, gain.shape[1]), F32)
     gain_columns[...] = jnp.concatenate([high, gain - high, spare], axis=0).T.astype(BF16)
-
-
-def weight_kernel(tail, chips, core, left_one, left_two, right_one, right_two, *refs):
-    kept, away = refs[-2:]
-    lower = core[0] == 0
+    if early:
+        pairs = [(work, grad_qkv), (grad_low, context)]
+        early_rows(early, chips, core, 0, pairs, gain_columns, *parts)
+
+
+def weight_rows(i, tail, lower, pairs, extra, kept, away):
     depth = kept.shape[1]
 
     def put(block, start, stop):
-        kept[0, :, start:stop] = jnp.where(lower, block[:depth], block[depth:]).astype(BF16)
-        away[0, :, start:stop] = jnp.where(lower, block[depth:], block[:depth]).astype(BF16)
+        kept[i, :, start:stop] = jnp.where(lower, block[:depth], block[depth:]).astype(BF16)
+        away[i, :, start:stop] = jnp.where(lower, block[depth:], block[:depth]).astype(BF16)
 
     base = 0
     rest = 0.0
-    for left, right in ((left_one, right_one), (left_two, right_two)):
+    for left, right in pairs:
         width = right.shape[1] - tail
-        turned = left[...].T
+        turned = left.T
         for start in range(0, width, 512):
             stop = min(width, start + 512)
             product = jnp.dot(turned, right[:, start:stop], preferred_element_type=F32)
@@ -441,11 +456,26 @@
             rest += jnp.dot(turned, right[:, width:], preferred_element_type=F32)
     if tail:
         put(rest, base, base + tail)
-    if len(refs) == 3:
-        put(refs[0][...].astype(F32), base, base + refs[0].shape[1])
-
-
-def weight_terms(ring, slots, left_one, right_one, left_two, right_two, extra=None, tail=0, room=20):
+    if extra is not None:
+        put(extra.astype(F32), base, base + extra.shape[1])
+
+
+def early_rows(count, chips, core, tail, pairs, extra, kept, away):
+    lower = core[0] == 0
+    for i in range(count):
+        lanes = pl.ds(pl.multiple_of(chips[i] * LANES, LANES), LANES)
+        blocks = [(left[:, lanes], right) for left, right in pairs]
+        more = None if extra is None else extra[lanes, :]
+        weight_rows(i, tail, lower, blocks, more, kept, away)
+
+
+def weight_kernel(tail, chips, core, left_one, left_two, right_one, right_two, *refs):
+    pairs = [(left_one[...], right_one), (left_two[...], right_two)]
+    extra = refs[0][...] if len(refs) == 3 else None
+    weight_rows(0, tail, core[0] == 0, pairs, extra, *refs[-2:])
+
+
+def weight_terms(ring, chips, core, skip, left_one, right_one, left_two, right_two, extra=None, tail=0, room=20):
     work_rows, width = left_one.shape
     lanes = width // ring.chips
     depth = lanes // 2
@@ -455,11 +485,13 @@
         total += extra.shape[1]
         more_args.append(extra)
         more_specs.append(
-            pl.BlockSpec((lanes, extra.shape[1]), lambda i, chips, core: (chips[i], 0))
+            pl.BlockSpec((lanes, extra.shape[1]), lambda i, chips, core: (chips[i + skip], 0))
         )
 
+    count = ring.chips - skip
+
     def left_map(i, chips, core):
-        return (0, chips[i])
+        return (0, chips[i + skip])
 
     def whole_map(i, chips, core):
         return (0, 0)
@@ -468,7 +500,7 @@
         functools.partial(weight_kernel, tail),
         grid_spec=pltpu.PrefetchScalarGridSpec(
             num_scalar_prefetch=2,
-            grid=(len(slots),),
+            grid=(count,),
             in_specs=[
                 pl.BlockSpec((work_rows, lanes), left_map),
                 pl.BlockSpec((work_rows, lanes), left_map),
@@ -482,18 +514,18 @@
             ],
         ),
         out_shape=[
-            pltpu.HBM((len(slots), depth, total), BF16),
-            pltpu.HBM((len(slots), depth, total), BF16),
+            pltpu.HBM((count, depth, total), BF16),
+            pltpu.HBM((count, depth, total), BF16),
         ],
         compiler_params=pltpu.CompilerParams(vmem_limit_bytes=room * MIB),
         cost_estimate=pl.CostEstimate(
-            flops=2 * work_rows * lanes * len(slots) * total // COST,
-            bytes_accessed=2 * (lanes * len(slots) + work_rows) * total // COST,
+            flops=2 * work_rows * lanes * count * total // COST,
+            bytes_accessed=2 * (lanes * count + work_rows) * total // COST,
             transcendentals=0,
         ),
     )(
-        ring.chips_at(slots),
-        ring.core.reshape(1),
+        chips,
+        core,
         left_one,
         left_two,
         right_one,
@@ -502,19 +534,14 @@
     )
 
 
-def summed_terms(ring, name, *factors, tail=0, room=20):
-    if ring.short:
-        early, rest = [
-            weight_terms(ring, slots, *factors, tail=tail, room=room)
-            for slots in (ring.slots[:3], ring.slots[3:])
-        ]
-        return (yield from ring.scatter_sum(early, rest, name))
-    left_one, right_one, left_two, right_two, *extra = factors
+def summed_terms(left_one, right_one, left_two, right_two, extra=None, tail=0):
+    yield from ()
     terms = [dot(left_one, right_one, (0, 0)), dot(left_two, right_two, (0, 0))]
     if tail:
         rest = terms[0][:, -tail:] + terms[1][:, -tail:]
         terms = [terms[0][:, :-tail], terms[1][:, :-tail], rest]
-    terms = jnp.concatenate([t.astype(BF16) for t in terms] + extra, axis=1)
+    terms = [t.astype(BF16) for t in terms] + ([] if extra is None else [extra])
+    terms = jnp.concatenate(terms, axis=1)
     return lax.psum_scatter(terms, SEQ, scatter_dimension=0, tiled=True).astype(F32)
 
 
@@ -532,11 +559,7 @@
     half_size = HD // 2
     frequency = THETA ** (-(jnp.arange(half_size, dtype=F32) * 2.0) / HD)
     angles = positions.astype(F32)[:, None] * frequency[None, :]
-    cosine, sine = jnp.cos(angles), jnp.sin(angles)
-    copies = LANES // HD
-    return jnp.tile(cosine, (1, 2 * copies)), jnp.tile(
-        jnp.concatenate([-sine, sine], axis=1), (1, copies)
-    )
+    return jnp.cos(angles), jnp.sin(angles)
 
 
 def edge_rows(block):
@@ -570,6 +593,8 @@
 def local(tokens, norm1_gain, w_qkv, w_attn_out, norm2_gain, w_in, w_down, cotangent):
     row_count, model_width = tokens.shape
     ring = Ring(model_width)
+    early = 3 if ring.short else 0
+    chips, core = ring.chips_at(ring.slots), ring.core.reshape(1)
     depth, _, width = w_qkv.shape
     units = w_down.shape[0]
     gains = padded_to_lanes(jnp.stack([norm1_gain, norm2_gain], axis=1))
@@ -581,21 +606,21 @@
         [part[:, :whole_units] for part in parts] + [part[:, whole_units:] for part in parts], axis=1
     )
     blob_b = jnp.pad(blob_b, ((0, 0), (0, LANES - 3 * spare)))
-    steps_a = Stepped(ring.gather(blob_a, "gather_a", [[0], [-1, 1], [], []]))
+    steps_a = Stepped(ring.gather(blob_a, "gather_a", [[0], [-1, 1], [], [-2]]))
     first = lax.axis_index(PAIR) == 0
     edge = edge_rows(jnp.where(first, tokens[:HALF], tokens[-HALF:]))
     edge = steps_a.hold(edge)
-    joined = jnp.concatenate([tokens, edge], axis=0)
+    joined = jnp.concatenate([tokens, edge, cotangent], axis=0)
     other = pair_swap(joined)
     steps_a.step()
+    blob_b = steps_a.ride(blob_b)
+    steps_b = Stepped(ring.gather(blob_b, "gather_b", [[], [], [0, -1, 1], [-2, 2]]))
     other = steps_a.hold(other)
     tokens_all = pair_rows(tokens, other[:row_count])
-    tokens_before = jnp.where(first, other[row_count:], edge)
-    tokens_after = jnp.where(first, edge, other[row_count:])
-    blob_b = steps_a.ride(blob_b)
-    steps_b = Stepped(ring.gather(blob_b, "gather_b", [[], [0], [-1, 1], [-2, 2]]))
-    steps_a.step()
-    pieces, starts = steps_a.finish()
+    beside = other[row_count : row_count + HALF]
+    tokens_before = jnp.where(first, beside, edge)
+    tokens_after = jnp.where(first, edge, beside)
+    cot_all = pair_rows(cotangent, other[row_count + HALF :])
 
     work_rows = row_count * lax.axis_size(PAIR)
     reach_rows = work_rows + 2 * HALF
@@ -603,11 +628,13 @@
     cosine, sine = rotary_tables(
         seq[0] * work_rows - HALF + jnp.arange(reach_rows, dtype=jnp.int32)
     )
-
-    tokens_all, cot_own = steps_b.ride((tokens_all, cotangent))
-    cot_other = pair_swap(cot_own)
+    inputs = tokens_all, tokens_before, tokens_after, cot_all, seq, cosine, sine, chips, core
+    inputs = steps_a.hold(inputs)
+    tokens_all, tokens_before, tokens_after, cot_all, seq, cosine, sine, chips, core = inputs
+    steps_a.beside(steps_b)
+    pieces, starts = steps_a.finish()
     count = len(pieces)
-    whole_a, attn_matrix, gains, work_one, queries, keys_values = call(
+    whole_a, attn_matrix, gains, work_one, queries, keys_values, cosine, sine = call(
         functools.partial(first_kernel, count, width),
         (starts, tokens_all, tokens_before, tokens_after, cosine, sine, *pieces),
         [SMEM] + [VMEM] * 5 + [ANY] * count,
@@ -618,30 +645,32 @@
             shape_of(work_rows, model_width, BF16),
             shape_of(work_rows, width, BF16),
             shape_of(reach_rows, 2 * width, BF16),
+            shape_of(reach_rows, LANES, F32),
+            shape_of(reach_rows, LANES, F32),
         ],
         [pltpu.VMEM((reach_rows, model_width), BF16), pltpu.SemaphoreType.DMA((count,))],
         flops=6 * work_rows * model_width * width,
         moved=16 * MIB,
         room=60,
     )
-    queries, cot_other = steps_b.ride((queries, cot_other))
-    cot_all = pair_rows(cotangent, cot_other)
+    queries = steps_b.ride(queries)
     context, attn_term = call(
         attend_kernel,
         (seq, queries, keys_values, attn_matrix),
         [SMEM] + [VMEM] * 3,
-        [shape_of(work_rows, width, BF16), shape_of(work_rows, model_width, BF16)],
+        [pltpu.HBM((work_rows, width), BF16), pltpu.HBM((work_rows, model_width), BF16)],
         flops=2 * work_rows * model_width * width,
         moved=16 * MIB,
+        room=60,
     )
     attn_other = steps_b.ride(pair_swap(attn_term))
 
     pieces, starts = steps_b.finish()
     count = len(pieces)
-    residual, work_two, hidden, grad_proj, grad_two, down_term = call(
-        functools.partial(hidden_kernel, count, spare),
-        (starts, tokens_all, attn_term, attn_other, gains, cot_all, *pieces),
-        [SMEM] + [VMEM] * 5 + [ANY] * count,
+    residual, work_two, hidden, grad_proj, grad_two, down_term, *early_b = call(
+        functools.partial(hidden_kernel, count, spare, early),
+        (starts, chips, core, tokens_all, attn_term, attn_other, gains, cot_all, *pieces),
+        [SMEM] * 3 + [VMEM] * 5 + [ANY] * count,
         [
             shape_of(work_rows, model_width, F32),
             shape_of(work_rows, model_width, BF16),
@@ -649,7 +678,8 @@
             shape_of(work_rows, 2 * whole_units + LANES, BF16),
             shape_of(work_rows, model_width, BF16),
             shape_of(work_rows, model_width, BF16),
-        ],
+        ]
+        + [pltpu.HBM((early, depth, blob_b.shape[1]), BF16)] * (2 if early else 0),
         [
             pltpu.VMEM((model_width, blob_b.shape[1]), BF16),
             pltpu.SemaphoreType.DMA((count,)),
@@ -659,8 +689,14 @@
         room=60,
     )
     grad_two_other = pair_swap(grad_two)
-    steps_b = Stepped(summed_terms(ring, "sum_b", work_two, grad_proj, cot_all, hidden, tail=LANES, room=60))
-    grad_two = steps_b.ride(grad_two)
+    factors = work_two, grad_proj, cot_all, hidden
+    if early:
+        rest_b = weight_terms(ring, chips, core, early, *factors, tail=LANES, room=60)
+        steps_b = Stepped(ring.scatter_sum(early_b, rest_b, "sum_b"))
+    else:
+        rest_b = ()
+        steps_b = Stepped(summed_terms(*factors, tail=LANES))
+    grad_two, rest_b = steps_b.ride((grad_two, rest_b))
     grad_residual, grad_low, gain_two, grad_queries, grad_own, to_before, to_after = call(
         attend_back_kernel,
         (
@@ -669,13 +705,13 @@
         ),
         [SMEM] + [VMEM] * 10,
         [
-            shape_of(work_rows, model_width, F32),
-            shape_of(work_rows, model_width, BF16),
+            pltpu.HBM((work_rows, model_width), F32),
+            pltpu.HBM((work_rows, model_width), BF16),
             shape_of(8, model_width, F32),
             shape_of(work_rows, width, BF16),
             shape_of(work_rows, 2 * width, F32),
-            shape_of(HALF, 2 * width, BF16),
-            shape_of(HALF, 2 * width, BF16),
+            pltpu.HBM((HALF, 2 * width), BF16),
+            pltpu.HBM((HALF, 2 * width), BF16),
         ],
         [pltpu.VMEM((reach_rows, 2 * width), F32)],
         flops=4 * work_rows * model_width * width,
@@ -687,30 +723,46 @@
 
     down_other = pair_swap(other_rows(down_term, row_count))
     grad_queries = steps_b.ride(grad_queries)
-    grad_qkv, grad_one, gain_columns = call(
-        last_kernel,
+    last = call(
+        functools.partial(last_kernel, early),
         (
-            grad_queries, grad_own, from_prev, from_next, cosine, sine, whole_a, tokens_all,
-            gain_two,
+            chips, core, grad_queries, grad_own, from_prev, from_next, cosine, sine, tokens_all,
+            gain_two, work_one, grad_low, context, whole_a,
         ),
-        [VMEM] * 9,
+        [SMEM] * 2 + [VMEM] * 11 + [ANY],
         [
             shape_of(work_rows, 3 * width, BF16),
             shape_of(work_rows, model_width, BF16),
             shape_of(model_width, LANES, BF16),
+        ]
+        + [pltpu.HBM((early, depth, blob_a.shape[1]), BF16)] * (2 if early else 0),
+        [
+            pltpu.VMEM((work_rows, 2 * width), F32),
+            pltpu.VMEM((model_width, 3 * width), BF16),
+            pltpu.SemaphoreType.DMA,
         ],
-        [pltpu.VMEM((work_rows, 2 * width), F32)],
         flops=6 * work_rows * model_width * width,
         moved=16 * MIB,
-    )
+        room=60,
+    )
+    grad_qkv, grad_one, gain_columns, *early_a = steps_b.ride(tuple(last))
     one_other = pair_swap(other_rows(grad_one, row_count))
-    down_other = steps_b.hold(down_other)
-    steps_a = Stepped(summed_terms(ring, "sum_a", work_one, grad_qkv, grad_low, context, gain_columns))
+    grad_qkv = steps_b.ride(grad_qkv)
+    factors = work_one, grad_qkv, grad_low, context, gain_columns
+    if early:
+        rest_a = weight_terms(ring, chips, core, early, *factors)
+        steps_a = Stepped(ring.scatter_sum(early_a, rest_a, "sum_a"))
+    else:
+        steps_a = Stepped(summed_terms(*factors))
     steps_a.step()
-    steps_a.beside(steps_b)
+    steps_a.step()
     one_other = steps_a.hold(one_other)
     steps_a.step()
+    steps_a.step()
+    steps_b.step()
+    down_other = steps_a.hold(down_other)
     steps_a.beside(steps_b)
+    steps_a.step()
     steps_a.step()
     steps_a.beside(steps_b)
     share_b = steps_b.finish()

time: 237 us -> 223 us (0.941)
  local copies, waits for them, and re-layouts: 24.9 us -> 11.2 us
  waiting for transfers between devices: 87.6 us -> 80.6 us
  other arithmetic: 17.6 us -> 22.8 us
    unnamed x149 -> x125, local copies, waits for them, and re-layouts: 15.3 us -> 3.82 us
    pallas_call x5, Pallas kernels: 28.3 us -> 37.9 us  [call(): pl.pallas_call(kernel, in_specs=specs, out_specs=[VMEM] * len(outs), out_...]
    pallas_call x4 -> x2, Pallas kernels: 19.9 us -> 11.2 us  [weight_terms(): pl.pallas_call(functools.partial(weight_kernel, tail), grid_spec=pltpu.Pr...]
    ppermute x54, waiting for transfers between devices: 77.3 us -> 71.5 us  [go(): return lax.ppermute(block, SEQ, route)]
    ppermute x54, starting transfers between devices: 42 us -> 47.2 us  [go(): return lax.ppermute(block, SEQ, route)]
    ppermute x7 -> x6, starting transfers between devices: 9.33 us -> 5.96 us  [pair_swap(): return lax.ppermute(block, PAIR, [(0, 1), (1, 0)])]
    convert_element_type x6, other arithmetic: 3.05 us -> 6.3 us  [scatter_sum(): downward = (at(self.half + step) + downward).astype(BF16)]
    ppermute x7 -> x6, waiting for transfers between devices: 8.89 us -> 7.01 us  [pair_swap(): return lax.ppermute(block, PAIR, [(0, 1), (1, 0)])]
  transfers between devices with their start and end apart: 64 -> 63, of which waited for: 31 -> 32; matrix products, arithmetic and copies ran while one was open for 10% -> 12% of each run, Pallas kernels for 13% -> 16%
where the time goes in v3:
time: 223 us; the launch traced here: 222 us
  waiting for transfers between devices  80.6 us (36%)
  starting transfers between devices  57.1 us (26%)
  Pallas kernels  49.1 us (22%)
  other arithmetic  22.8 us (10%)
  local copies, waits for them, and re-layouts  11.2 us (5%)
    ppermute x54, waiting for transfers between devices, go(): return lax.ppermute(block, SEQ, route)  71.5 us
    ppermute x54, starting transfers between devices, go(): return lax.ppermute(block, SEQ, route)  47.2 us
    pallas_call x5, Pallas kernels, call(): pl.pallas_call(kernel, in_specs=specs, out_specs=[VMEM] * len(outs), out_...  37.9 us
    pallas_call x2, Pallas kernels, weight_terms(): pl.pallas_call(functools.partial(weight_kernel, tail), grid_spec=pltpu.Pr...  11.2 us
    ppermute x6, waiting for transfers between devices, pair_swap(): return lax.ppermute(block, PAIR, [(0, 1), (1, 0)])  7.01 us
    convert_element_type x6, other arithmetic, scatter_sum(): downward = (at(self.half + step) + downward).astype(BF16)  6.3 us
    ppermute x6, starting transfers between devices, pair_swap(): return lax.ppermute(block, PAIR, [(0, 1), (1, 0)])  5.96 us
  transfers between devices with their start and end apart: 63, of which 32 were waited for; matrix products, arithmetic and copies ran while one was open for 12% of the time, Pallas kernels for 16%

profile of v3, /device:TPU:0, one launch (start us, length us, event | category | flops | bytes accessed | tf_op | source)
XLA Modules:
  0.0 222.5 jit_solution(9441277211284815177)
XLA Ops:
  3.3 3.1 %collective-permute-start.1 = (bf16[64,2176]{1,0:T(8,128)(2,1)S(1)}, bf16[64,2176]{1,0:T(8,128)(2,1)}, u32[]{:S(2)}, u32[]{:S(2)}) collective-permute-start(bf16[64,2176]{1,0:T(8,128)(2,1)S(1)} %fusion.26.refs_0_), channel_id=1, source_target_pairs={{0,8},{2,10},{4,0},{6,2},{8,16},{10,18},{12,4},{14,6},{16,24},{18,... | collective-permute-start | bytes 835592 | tf_op jit(solution)/shard_map/gather_a_up_1/ppermute | solution.py:65
  7.4 1.3 collective-permute-start
  8.7 1.2 dynamic_slice.21
  10.0 1.3 compare_select_fusion.1
  14.6 3.5 %collective-permute-start.5 = (bf16[64,2176]{1,0:T(8,128)(2,1)}, bf16[64,2176]{1,0:T(8,128)(2,1)}, u32[]{:S(2)}, u32[]{:S(2)}) collective-permute-start(bf16[64,2176]{1,0:T(8,128)(2,1)} %collective-permute-done.1.refs_1_), channel_id=1, source_target_pairs={{0,8},{2,10},{4,0},{6,2},{8,16},{10,18},{12,4},{14,6},{16,24},{18,... | collective-permute-start | bytes 835592 | tf_op jit(solution)/shard_map/gather_a_up_2/ppermute | solution.py:65
  18.7 1.3 collective-permute-start.4
  20.3 4.1 %collective-permute-done.5.refs_3_ = bf16[64,2176]{1,0:T(8,128)(2,1)} collective-permute-done((bf16[64,2176]{1,0:T(8,128)(2,1)}, bf16[64,2176]{1,0:T(8,128)(2,1)}, u32[]{:S(2)}, u32[]{:S(2)}) %collective-permute-start.5) | collective-permute-done | bytes 278560 | tf_op jit(solution)/shard_map/gather_a_up_2/ppermute | solution.py:65
  24.4 3.1 %collective-permute-done.6.refs_4_ = bf16[64,2176]{1,0:T(8,128)(2,1)} collective-permute-done((bf16[64,2176]{1,0:T(8,128)(2,1)}, bf16[64,2176]{1,0:T(8,128)(2,1)}, u32[]{:S(2)}, u32[]{:S(2)}) %collective-permute-start.6) | collective-permute-done | bytes 278560 | tf_op jit(solution)/shard_map/gather_a_down_2/ppermute | solution.py:65
  27.8 1.7 collective-permute-start.9
  30.1 1.2 gather_fusion.1
  31.2 1.5 multiply_sine_fusion
  32.8 1.6 collective-permute-start.11
  34.8 1.3 collective-permute-done.10.refs_6_
  36.1 1.5 collective-permute-done.9.refs_5_
  40.1 7.1 %collective-permute-done.11.refs_1_ = bf16[64,3968]{1,0:T(8,128)(2,1)} collective-permute-done((bf16[64,3968]{1,0:T(8,128)(2,1)S(1)}, bf16[64,3968]{1,0:T(8,128)(2,1)}, u32[]{:S(2)}, u32[]{:S(2)}) %collective-permute-start.11) | collective-permute-done | bytes 507936 | tf_op jit(solution)/shard_map/gather_b_up_1/ppermute | solution.py:65
  47.2 1.6 collective-permute-start.13
  49.4 2.9 %collective-permute-done.13.refs_7_ = bf16[32,2176]{1,0:T(8,128)(2,1)S(1)} collective-permute-done((bf16[32,2176]{1,0:T(8,128)(2,1)S(1)}, bf16[32,2176]{1,0:T(8,128)(2,1)S(1)}, u32[]{:S(2)}, u32[]{:S(2)}) %collective-permute-start.13) | collective-permute-done | bytes 139296 | tf_op jit(solution)/shard_map/gather_a_up_4/ppermute | solution.py:65
  52.3 1.6 collective-permute-done.14.refs_8_
  54.4 1.6 collective-permute-start.21
  58.8 6.9 %shard_map.224 = (bf16[1024,2176]{1,0:T(8,128)(2,1)}, bf16[1024,512]{1,0:T(8,128)(2,1)}, f32[8,1024]{1,0:T(8,128)}, bf16[256,1024]{1,0:T(8,128)(2,1)}, bf16[256,...) custom-call(s32[18]{0:T(128)} %multiply_add_fusion.starts, ...), custom_call_target="tpu_custom_call" | custom-call | flops 805306368 | bytes 16777216 | tf_op jit(solution)/shard_map/pallas_call | solution.py:183
  65.7 2.4 %collective-permute-done.21.refs_3_ = bf16[64,3968]{1,0:T(8,128)(2,1)S(1)} collective-permute-done((bf16[64,3968]{1,0:T(8,128)(2,1)}, bf16[64,3968]{1,0:T(8,128)(2,1)S(1)}, u32[]{:S(2)}, u32[]{:S(2)}) %collective-permute-start.21) | collective-permute-done | bytes 507936 | tf_op jit(solution)/shard_map/gather_b_up_2/ppermute | solution.py:65
  68.1 1.3 collective-permute-done.22.refs_4_
  69.4 4.5 %shard_map.225 = (bf16[256,512]{1,0:T(8,128)(2,1)}, bf16[256,1024]{1,0:T(8,128)(2,1)}) custom-call(s32[2]{0:T(128)} %pad_add_fusion.seq, bf16[256,512]{1,0:T(8,128)(2,1)} %get-tuple-element.235.queries, bf16[384,1024]{1,0:T(8,128)(2,1)} %get-tuple-element.236.keys_values, bf16[1024,512]{1,0:T(8,128)(2,1)} %get-tuple-element.237.matrix), custom_call_target="tpu_custom_call" | custom-call | flops 268435456 | bytes 16777216 | tf_op jit(solution)/shard_map/pallas_call | solution.py:183
  74.4 1.7 collective-permute-start.24
  76.9 9.5 %collective-permute-done.24.refs_5_ = bf16[64,3968]{1,0:T(8,128)(2,1)S(1)} collective-permute-done((bf16[64,3968]{1,0:T(8,128)(2,1)S(1)}, bf16[64,3968]{1,0:T(8,128)(2,1)S(1)}, u32[]{:S(2)}, u32[]{:S(2)}) %collective-permute-start.24) | collective-permute-done | bytes 507936 | tf_op jit(solution)/shard_map/gather_b_up_3/ppermute | solution.py:65
  86.4 1.4 collective-permute-done.25.refs_6_
  87.8 1.5 collective-permute-start.29
  90.7 3.5 %collective-permute-done.29.refs_7_ = bf16[32,3968]{1,0:T(8,128)(2,1)S(1)} collective-permute-done((bf16[32,3968]{1,0:T(8,128)(2,1)S(1)}, bf16[32,3968]{1,0:T(8,128)(2,1)S(1)}, u32[]{:S(2)}, u32[]{:S(2)}) %collective-permute-start.29) | collective-permute-done | bytes 253984 | tf_op jit(solution)/shard_map/gather_b_up_4/ppermute | solution.py:65
  94.2 1.7 collective-permute-done.30.refs_8_
  96.4 1.0 collective-permute-done.35.refs_16_
  99.5 12.8 %shard_map.226 = (f32[256,1024]{1,0:T(8,128)}, bf16[256,1024]{1,0:T(8,128)(2,1)}, bf16[256,1408]{1,0:T(8,128)(2,1)}, bf16[256,2688]{1,0:T(8,128)(2,1)}, bf16[256...) custom-call(s32[18]{0:T(128)} %multiply_add_fusion.starts, ...), custom_call_target="tpu_custom_call" | custom-call | flops 4127195136 | bytes 33554432 | tf_op jit(solution)/shard_map/pallas_call | solution.py:183
  113.5 7.0 %shard_map.227 = (bf16[5,64,3968]{2,1,0:T(8,128)(2,1)}, bf16[5,64,3968]{2,1,0:T(8,128)(2,1)}) custom-call(s32[8]{0:T(128)} %gather_fusion.1, s32[1]{0:T(128)} %bitcast.8.core, bf16[256,1024]{1,0:T(8,128)(2,1)} %get-tuple-element.271.left_one, bf16[256,1024]{1,0:T(8,128)(2,1)} %pad_maximum_fusion.3.cot.left_two, ...), custom_call_target="tpu_custom_call" | custom-call | flops 1300234240 | bytes 7110656 | tf_op jit(solution)/shard_map/pallas_call | solution.py:499
  120.7 1.4 add_convert_fusion
  122.8 1.4 collective-permute-start.41
  124.2 2.8 %collective-permute-done.39.grad_two_other = bf16[256,1024]{1,0:T(8,128)(2,1)S(1)} collective-permute-done((bf16[256,1024]{1,0:T(8,128)(2,1)}, bf16[256,1024]{1,0:T(8,128)(2,1)S(1)}, u32[]{:S(2)}, u32[]{:S(2)}) %collective-permute-start.39) | collective-permute-done | bytes 524320 | tf_op jit(solution)/shard_map/ppermute | solution.py:32
  127.1 7.0 %shard_map.228 = (f32[256,1024]{1,0:T(8,128)}, bf16[256,1024]{1,0:T(8,128)(2,1)}, f32[8,1024]{1,0:T(8,128)S(1)}, bf16[256,512]{1,0:T(8,128)(2,1)S(1)}, f32[256,1...) custom-call(s32[2]{0:T(128)S(1)} %copy-done.16, f32[256,1024]{1,0:T(8,128)S(1)} %copy-done.2, ...), custom_call_target="tpu_custom_call" | custom-call | flops 536870912 | bytes 25165824 | tf_op jit(solution)/shard_map/pallas_call | solution.py:183
  134.2 2.0 fusion.5
  137.0 1.2 collective-permute-start.45
  138.5 1.3 collective-permute-start.42
  139.8 1.3 collective-permute-start.43
  142.0 2.1 collective-permute-done.43.from_after
  144.2 6.8 %shard_map.229 = (bf16[256,1536]{1,0:T(8,128)(2,1)}, bf16[256,1024]{1,0:T(8,128)(2,1)}, bf16[1024,128]{1,0:T(8,128)(2,1)}, bf16[3,64,2176]{2,1,0:T(8,128)(2,1)}, bf16[3,64,2176]{2,1,0:T(8,128)(2,1)}) custom-call(s32[8]{0:T(128)} %gather_fusion.1, s32[1]{0:T(128)} %bitcast.8.core, bf16[256,512]{1,0:T(8,128)(2,1)} %copy-done.12, f32[256,1024]{1,0:T(8,128)} %copy-done.4, ...), custom_call_target="tpu_custom_call" | custom-call | flops 805306368 | bytes 16777216 | tf_op jit(solution)/shard_map/pallas_call | solution.py:183
  151.3 7.3 %collective-permute-start.49 = (bf16[3,64,2176]{2,1,0:T(8,128)(2,1)}, bf16[3,64,2176]{2,1,0:T(8,128)(2,1)S(1)}, u32[]{:S(2)}, u32[]{:S(2)}) collective-permute-start(bf16[3,64,2176]{2,1,0:T(8,128)(2,1)} %get-tuple-element.320), channel_id=1, source_target_pairs={{0,2},{2,0},{4,6},{6,4},{8,10},{10,8},{12,14},{14,12},{16,18},{18,... | collective-permute-start | bytes 2506760 | tf_op jit(solution)/shard_map/sum_a_cores_early/ppermute | solution.py:65
  158.6 2.1 fusion.3
  160.8 1.9 collective-permute-start.54
  163.6 1.3 collective-permute-start.50
  165.8 4.1 %shard_map.230 = (bf16[5,64,2176]{2,1,0:T(8,128)(2,1)}, bf16[5,64,2176]{2,1,0:T(8,128)(2,1)}) custom-call(s32[8]{0:T(128)S(1)} %copy-done.15, s32[1]{0:T(128)} %bitcast.8.core, bf16[256,1024]{1,0:T(8,128)(2,1)S(1)} %copy-done.8, bf16[256,1024]{1,0:T(8,128)(2,1)S(1)} %copy-done.9, bf16[256,1536]{1,0:T(8,128)(2,1)S(1)} %copy-done.17, ...), custom_call_target="tpu_custom_call" | custom-call | flops 713031680 | bytes 3899392 | tf_op jit(solution)/shard_map/pallas_call | solution.py:499
  169.9 5.9 %collective-permute-done.54 = bf16[64,3968]{1,0:T(8,128)(2,1)S(1)} collective-permute-done((bf16[64,3968]{1,0:T(8,128)(2,1)S(1)}, bf16[64,3968]{1,0:T(8,128)(2,1)S(1)}, u32[]{:S(2)}, u32[]{:S(2)}) %collective-permute-start.54) | collective-permute-done | bytes 507936 | tf_op jit(solution)/shard_map/sum_b_up_3/ppermute | solution.py:65
  175.9 1.2 collective-permute-start.48
  177.1 1.5 collective-permute-done.50
  179.5 4.2 %collective-permute-done.48 = bf16[128,1024]{1,0:T(8,128)(2,1)S(1)} collective-permute-done((bf16[128,1024]{1,0:T(8,128)(2,1)S(1)}, bf16[128,1024]{1,0:T(8,128)(2,1)S(1)}, u32[]{:S(2)}, u32[]{:S(2)}) %collective-permute-start.48) | collective-permute-done | bytes 262176 | tf_op jit(solution)/shard_map/ppermute | solution.py:32
  184.5 1.2 collective-permute-start.53
  185.7 1.6 fusion.1
  187.6 3.4 %collective-permute-done.52 = bf16[64,2176]{1,0:T(8,128)(2,1)S(1)} collective-permute-done((bf16[64,2176]{1,0:T(8,128)(2,1)S(1)}, bf16[64,2176]{1,0:T(8,128)(2,1)S(1)}, u32[]{:S(2)}, u32[]{:S(2)}) %collective-permute-start.52) | collective-permute-done | bytes 278560 | tf_op jit(solution)/shard_map/sum_a_up_2/ppermute | solution.py:65
  191.8 1.6 collective-permute-start.57
  193.8 1.6 collective-permute-start.61
  195.4 5.5 %collective-permute-done.56 = bf16[64,2176]{1,0:T(8,128)(2,1)S(1)} collective-permute-done((bf16[64,2176]{1,0:T(8,128)(2,1)S(1)}, bf16[64,2176]{1,0:T(8,128)(2,1)S(1)}, u32[]{:S(2)}, u32[]{:S(2)}) %collective-permute-start.56) | collective-permute-done | bytes 278560 | tf_op jit(solution)/shard_map/sum_a_up_3/ppermute | solution.py:65
  202.1 1.6 collective-permute-start.59
  203.7 1.0 fusion.23
  205.5 6.0 %collective-permute-done.60 = bf16[64,3968]{1,0:T(8,128)(2,1)S(1)} collective-permute-done((bf16[64,3968]{1,0:T(8,128)(2,1)S(1)}, bf16[64,3968]{1,0:T(8,128)(2,1)S(1)}, u32[]{:S(2)}, u32[]{:S(2)}) %collective-permute-start.60) | collective-permute-done | bytes 507936 | tf_op jit(solution)/shard_map/sum_b_up_4/ppermute | solution.py:65
  211.6 2.9 %collective-permute-done.58 = bf16[64,2176]{1,0:T(8,128)(2,1)S(1)} collective-permute-done((bf16[64,2176]{1,0:T(8,128)(2,1)S(1)}, bf16[64,2176]{1,0:T(8,128)(2,1)S(1)}, u32[]{:S(2)}, u32[]{:S(2)}) %collective-permute-start.58) | collective-permute-done | bytes 278560 | tf_op jit(solution)/shard_map/sum_a_up_4/ppermute | solution.py:65
  214.6 1.3 fusion
  217.0 1.2 collective-permute-start.62
  219.8 1.4 copy.44
  (267 shorter events, 36.1 us)
Async XLA Ops:
  3.3 10.5 %collective-permute-start.1 = (bf16[64,2176]{1,0:T(8,128)(2,1)S(1)}, bf16[64,2176]{1,0:T(8,128)(2,1)}, u32[]{:S(2)}, u32[]{:S(2)}) collective-permute-start(bf16[64,2176]{1,0:T(8,128)(2,1)S(1)} %fusion.26.refs_0_), channel_id=1, source_target_pairs={{0,8},{2,10},{4,0},{6,2},{8,16},{10,18},{12,4},{14,6},{16,24},{18,... | collective-permute-start | bytes 835592 | tf_op jit(solution)/shard_map/gather_a_up_1/ppermute | solution.py:65
  6.4 8.2 %collective-permute-start.2 = (bf16[64,2176]{1,0:T(8,128)(2,1)S(1)}, bf16[64,2176]{1,0:T(8,128)(2,1)}, u32[]{:S(2)}, u32[]{:S(2)}) collective-permute-start(bf16[64,2176]{1,0:T(8,128)(2,1)S(1)} %fusion.26.refs_0_), channel_id=1, source_target_pairs={{0,4},{2,6},{4,12},{6,14},{8,0},{10,2},{12,20},{14,22},{16,8},{18,... | collective-permute-start | bytes 835592 | tf_op jit(solution)/shard_map/gather_a_down_1/ppermute | solution.py:65
  6.4 8.2 %collective-permute-start.3 = (bf16[64,2176]{1,0:T(8,128)(2,1)S(1)}, bf16[64,2176]{1,0:T(8,128)(2,1)S(1)}, u32[]{:S(2)}, u32[]{:S(2)}) collective-permute-start(bf16[64,2176]{1,0:T(8,128)(2,1)S(1)} %fusion.26.refs_0_), channel_id=1, source_target_pairs={{0,2},{2,0},{4,6},{6,4},{8,10},{10,8},{12,14},{14,12},{16,18},{18,... | collective-permute-start | bytes 835592 | tf_op jit(solution)/shard_map/gather_a_cores_0/ppermute | solution.py:65
  7.4 6.4 %collective-permute-start = (bf16[64,1024]{1,0:T(8,128)(2,1)S(1)}, bf16[64,1024]{1,0:T(8,128)(2,1)S(1)}, u32[]{:S(2)}, u32[]{:S(2)}) collective-permute-start(bf16[64,1024]{1,0:T(8,128)(2,1)S(1)} %slice_select_fusion), channel_id=1, source_target_pairs={{2,0},{4,2},{6,4},{8,6},{10,8},{12,10},{14,12},{16,14},{18,16},{20... | collective-permute-start | bytes 393224 | tf_op jit(solution)/shard_map/ppermute | solution.py:569
  14.6 9.8 %collective-permute-start.5 = (bf16[64,2176]{1,0:T(8,128)(2,1)}, bf16[64,2176]{1,0:T(8,128)(2,1)}, u32[]{:S(2)}, u32[]{:S(2)}) collective-permute-start(bf16[64,2176]{1,0:T(8,128)(2,1)} %collective-permute-done.1.refs_1_), channel_id=1, source_target_pairs={{0,8},{2,10},{4,0},{6,2},{8,16},{10,18},{12,4},{14,6},{16,24},{18,... | collective-permute-start | bytes 835592 | tf_op jit(solution)/shard_map/gather_a_up_2/ppermute | solution.py:65
  18.1 9.4 %collective-permute-start.7 = (bf16[64,2176]{1,0:T(8,128)(2,1)}, bf16[64,2176]{1,0:T(8,128)(2,1)}, u32[]{:S(2)}, u32[]{:S(2)}) collective-permute-start(bf16[64,2176]{1,0:T(8,128)(2,1)} %collective-permute-done.1.refs_1_), channel_id=1, source_target_pairs={{0,2},{2,0},{4,6},{6,4},{8,10},{10,8},{12,14},{14,12},{16,18},{18,... | collective-permute-start | bytes 835592 | tf_op jit(solution)/shard_map/gather_a_cores_-1/ppermute | solution.py:65
  18.1 9.4 %collective-permute-start.6 = (bf16[64,2176]{1,0:T(8,128)(2,1)}, bf16[64,2176]{1,0:T(8,128)(2,1)}, u32[]{:S(2)}, u32[]{:S(2)}) collective-permute-start(bf16[64,2176]{1,0:T(8,128)(2,1)} %collective-permute-done.2.refs_2_), channel_id=1, source_target_pairs={{0,4},{2,6},{4,12},{6,14},{8,0},{10,2},{12,20},{14,22},{16,8},{18,... | collective-permute-start | bytes 835592 | tf_op jit(solution)/shard_map/gather_a_down_2/ppermute | solution.py:65
  18.1 9.4 %collective-permute-start.8 = (bf16[64,2176]{1,0:T(8,128)(2,1)}, bf16[64,2176]{1,0:T(8,128)(2,1)}, u32[]{:S(2)}, u32[]{:S(2)}) collective-permute-start(bf16[64,2176]{1,0:T(8,128)(2,1)} %collective-permute-done.2.refs_2_), channel_id=1, source_target_pairs={{0,2},{2,0},{4,6},{6,4},{8,10},{10,8},{12,14},{14,12},{16,18},{18,... | collective-permute-start | bytes 835592 | tf_op jit(solution)/shard_map/gather_a_cores_1/ppermute | solution.py:65
  18.7 18.9 %collective-permute-start.4 = (bf16[320,1024]{1,0:T(8,128)(2,1)S(1)}, bf16[320,1024]{1,0:T(8,128)(2,1)S(1)}, u32[]{:S(2)}, u32[]{:S(2)}) collective-permute-start(bf16[320,1024]{1,0:T(8,128)(2,1)S(1)} %pad_maximum_fusion.1), channel_id=1, source_target_pairs={{0,1},{1,0},{2,3},{3,2},{4,5},{5,4},{6,7},{7,6},{8,9},{9,8},{10,11... | collective-permute-start | bytes 1966088 | tf_op jit(solution)/shard_map/ppermute | solution.py:32
  20.3 36.3 %copy-start.33 = (bf16[64,3968]{1,0:T(8,128)(2,1)}, bf16[64,3968]{1,0:T(8,128)(2,1)S(1)}, u32[]{:S(2)}) copy-start(bf16[64,3968]{1,0:T(8,128)(2,1)S(1)} %pad.37.refs_0_) | copy-start | bytes 1523716
  27.5 8.6 %collective-permute-start.10 = (bf16[64,2176]{1,0:T(8,128)(2,1)}, bf16[64,2176]{1,0:T(8,128)(2,1)S(1)}, u32[]{:S(2)}, u32[]{:S(2)}) collective-permute-start(bf16[64,2176]{1,0:T(8,128)(2,1)} %collective-permute-done.6.refs_4_), channel_id=1, source_target_pairs={{0,4},{2,6},{4,12},{6,14},{8,0},{10,2},{12,20},{14,22},{16,8},{18,... | collective-permute-start | bytes 835592 | tf_op jit(solution)/shard_map/gather_a_down_3/ppermute | solution.py:65
  27.8 9.8 %collective-permute-start.9 = (bf16[64,2176]{1,0:T(8,128)(2,1)}, bf16[64,2176]{1,0:T(8,128)(2,1)S(1)}, u32[]{:S(2)}, u32[]{:S(2)}) collective-permute-start(bf16[64,2176]{1,0:T(8,128)(2,1)} %collective-permute-done.5.refs_3_), channel_id=1, source_target_pairs={{0,8},{2,10},{4,0},{6,2},{8,16},{10,18},{12,4},{14,6},{16,24},{18,... | collective-permute-start | bytes 835592 | tf_op jit(solution)/shard_map/gather_a_up_3/ppermute | solution.py:65
  32.8 14.4 %collective-permute-start.11 = (bf16[64,3968]{1,0:T(8,128)(2,1)S(1)}, bf16[64,3968]{1,0:T(8,128)(2,1)}, u32[]{:S(2)}, u32[]{:S(2)}) collective-permute-start(bf16[64,3968]{1,0:T(8,128)(2,1)S(1)} %pad.37.refs_0_), channel_id=1, source_target_pairs={{0,8},{2,10},{4,0},{6,2},{8,16},{10,18},{12,4},{14,6},{16,24},{18,... | collective-permute-start | bytes 1523720 | tf_op jit(solution)/shard_map/gather_b_up_1/ppermute | solution.py:65
  34.3 12.8 %collective-permute-start.12 = (bf16[64,3968]{1,0:T(8,128)(2,1)S(1)}, bf16[64,3968]{1,0:T(8,128)(2,1)}, u32[]{:S(2)}, u32[]{:S(2)}) collective-permute-start(bf16[64,3968]{1,0:T(8,128)(2,1)S(1)} %pad.37.refs_0_), channel_id=1, source_target_pairs={{0,4},{2,6},{4,12},{6,14},{8,0},{10,2},{12,20},{14,22},{16,8},{18,... | collective-permute-start | bytes 1523720 | tf_op jit(solution)/shard_map/gather_b_down_1/ppermute | solution.py:65
  36.1 13.3 %collective-permute-start.15 = (bf16[64,2176]{1,0:T(8,128)(2,1)}, bf16[64,2176]{1,0:T(8,128)(2,1)S(1)}, u32[]{:S(2)}, u32[]{:S(2)}) collective-permute-start(bf16[64,2176]{1,0:T(8,128)(2,1)} %collective-permute-done.5.refs_3_), channel_id=1, source_target_pairs={{0,2},{2,0},{4,6},{6,4},{8,10},{10,8},{12,14},{14,12},{16,18},{18,... | collective-permute-start | bytes 835592 | tf_op jit(solution)/shard_map/gather_a_cores_-2/ppermute | solution.py:65
  37.6 18.5 %collective-permute-start.16 = (bf16[64,2176]{1,0:T(8,128)(2,1)}, bf16[64,2176]{1,0:T(8,128)(2,1)S(1)}, u32[]{:S(2)}, u32[]{:S(2)}) collective-permute-start(bf16[64,2176]{1,0:T(8,128)(2,1)} %collective-permute-done.6.refs_4_), channel_id=1, source_target_pairs={{0,2},{2,0},{4,6},{6,4},{8,10},{10,8},{12,14},{14,12},{16,18},{18,... | collective-permute-start | bytes 835592 | tf_op jit(solution)/shard_map/gather_a_cores_2/ppermute | solution.py:65
  47.2 5.1 %collective-permute-start.13 = (bf16[32,2176]{1,0:T(8,128)(2,1)S(1)}, bf16[32,2176]{1,0:T(8,128)(2,1)S(1)}, u32[]{:S(2)}, u32[]{:S(2)}) collective-permute-start(bf16[32,2176]{1,0:T(8,128)(2,1)S(1)} %slice.223), channel_id=1, source_target_pairs={{0,8},{2,10},{4,0},{6,2},{8,16},{10,18},{12,4},{14,6},{16,24},{18,... | collective-permute-start | bytes 417800 | tf_op jit(solution)/shard_map/gather_a_up_4/ppermute | solution.py:65
  48.8 5.1 %collective-permute-start.14 = (bf16[32,2176]{1,0:T(8,128)(2,1)S(1)}, bf16[32,2176]{1,0:T(8,128)(2,1)S(1)}, u32[]{:S(2)}, u32[]{:S(2)}) collective-permute-start(bf16[32,2176]{1,0:T(8,128)(2,1)S(1)} %slice.224), channel_id=1, source_target_pairs={{0,4},{2,6},{4,12},{6,14},{8,0},{10,2},{12,20},{14,22},{16,8},{18,... | collective-permute-start | bytes 417800 | tf_op jit(solution)/shard_map/gather_a_down_4/ppermute | solution.py:65
  49.3 7.8 %collective-permute-start.17 = (bf16[64,2176]{1,0:T(8,128)(2,1)S(1)}, bf16[64,2176]{1,0:T(8,128)(2,1)S(1)}, u32[]{:S(2)}, u32[]{:S(2)}) collective-permute-start(bf16[64,2176]{1,0:T(8,128)(2,1)S(1)} %collective-permute-done.9.refs_5_), channel_id=1, source_target_pairs={{0,2},{2,0},{4,6},{6,4},{8,10},{10,8},{12,14},{14,12},{16,18},{18,... | collective-permute-start | bytes 835592 | tf_op jit(solution)/shard_map/gather_a_cores_-3/ppermute | solution.py:65
  53.9 2.5 %collective-permute-start.19 = (bf16[32,2176]{1,0:T(8,128)(2,1)S(1)}, bf16[32,2176]{1,0:T(8,128)(2,1)S(1)}, u32[]{:S(2)}, u32[]{:S(2)}) collective-permute-start(bf16[32,2176]{1,0:T(8,128)(2,1)S(1)} %collective-permute-done.13.refs_7_), channel_id=1, source_target_pairs={{0,2},{2,0},{4,6},{6,4},{8,10},{10,8},{12,14},{14,12},{16,18},{18,... | collective-permute-start | bytes 417800 | tf_op jit(solution)/shard_map/gather_a_cores_-4/ppermute | solution.py:65
  53.9 2.6 %collective-permute-start.20 = (bf16[32,2176]{1,0:T(8,128)(2,1)S(1)}, bf16[32,2176]{1,0:T(8,128)(2,1)S(1)}, u32[]{:S(2)}, u32[]{:S(2)}) collective-permute-start(bf16[32,2176]{1,0:T(8,128)(2,1)S(1)} %collective-permute-done.14.refs_8_), channel_id=1, source_target_pairs={{0,2},{2,0},{4,6},{6,4},{8,10},{10,8},{12,14},{14,12},{16,18},{18,... | collective-permute-start | bytes 417800 | tf_op jit(solution)/shard_map/gather_a_cores_4/ppermute | solution.py:65
  54.4 13.7 %collective-permute-start.21 = (bf16[64,3968]{1,0:T(8,128)(2,1)}, bf16[64,3968]{1,0:T(8,128)(2,1)S(1)}, u32[]{:S(2)}, u32[]{:S(2)}) collective-permute-start(bf16[64,3968]{1,0:T(8,128)(2,1)} %collective-permute-done.11.refs_1_), channel_id=1, source_target_pairs={{0,8},{2,10},{4,0},{6,2},{8,16},{10,18},{12,4},{14,6},{16,24},{18,... | collective-permute-start | bytes 1523720 | tf_op jit(solution)/shard_map/gather_b_up_2/ppermute | solution.py:65
  56.0 13.4 %collective-permute-start.22 = (bf16[64,3968]{1,0:T(8,128)(2,1)}, bf16[64,3968]{1,0:T(8,128)(2,1)S(1)}, u32[]{:S(2)}, u32[]{:S(2)}) collective-permute-start(bf16[64,3968]{1,0:T(8,128)(2,1)} %collective-permute-done.12.refs_2_), channel_id=1, source_target_pairs={{0,4},{2,6},{4,12},{6,14},{8,0},{10,2},{12,20},{14,22},{16,8},{18,... | collective-permute-start | bytes 1523720 | tf_op jit(solution)/shard_map/gather_b_down_2/ppermute | solution.py:65
  56.5 1.6 collective-permute-start.18
  56.6 19.5 %collective-permute-start.26 = (bf16[64,3968]{1,0:T(8,128)(2,1)S(1)}, bf16[64,3968]{1,0:T(8,128)(2,1)}, u32[]{:S(2)}, u32[]{:S(2)}) collective-permute-start(bf16[64,3968]{1,0:T(8,128)(2,1)S(1)} %pad.37.refs_0_), channel_id=1, source_target_pairs={{0,2},{2,0},{4,6},{6,4},{8,10},{10,8},{12,14},{14,12},{16,18},{18,... | collective-permute-start | bytes 1523720 | tf_op jit(solution)/shard_map/gather_b_cores_0/ppermute | solution.py:65
  57.1 19.3 %collective-permute-start.27 = (bf16[64,3968]{1,0:T(8,128)(2,1)}, bf16[64,3968]{1,0:T(8,128)(2,1)}, u32[]{:S(2)}, u32[]{:S(2)}) collective-permute-start(bf16[64,3968]{1,0:T(8,128)(2,1)} %collective-permute-done.11.refs_1_), channel_id=1, source_target_pairs={{0,2},{2,0},{4,6},{6,4},{8,10},{10,8},{12,14},{14,12},{16,18},{18,... | collective-permute-start | bytes 1523720 | tf_op jit(solution)/shard_map/gather_b_cores_-1/ppermute | solution.py:65
  58.1 18.3 %collective-permute-start.28 = (bf16[64,3968]{1,0:T(8,128)(2,1)}, bf16[64,3968]{1,0:T(8,128)(2,1)}, u32[]{:S(2)}, u32[]{:S(2)}) collective-permute-start(bf16[64,3968]{1,0:T(8,128)(2,1)} %collective-permute-done.12.refs_2_), channel_id=1, source_target_pairs={{0,2},{2,0},{4,6},{6,4},{8,10},{10,8},{12,14},{14,12},{16,18},{18,... | collective-permute-start | bytes 1523720 | tf_op jit(solution)/shard_map/gather_b_cores_1/ppermute | solution.py:65
  73.9 13.9 %collective-permute-start.23 = (bf16[256,1024]{1,0:T(8,128)(2,1)}, bf16[256,1024]{1,0:T(8,128)(2,1)S(1)}, u32[]{:S(2)}, u32[]{:S(2)}) collective-permute-start(bf16[256,1024]{1,0:T(8,128)(2,1)} %get-tuple-element.238.term), channel_id=1, source_target_pairs={{0,1},{1,0},{2,3},{3,2},{4,5},{5,4},{6,7},{7,6},{8,9},{9,8},{10,11... | collective-permute-start | bytes 1572872 | tf_op jit(solution)/shard_map/ppermute | solution.py:32
  74.4 12.0 %collective-permute-start.24 = (bf16[64,3968]{1,0:T(8,128)(2,1)S(1)}, bf16[64,3968]{1,0:T(8,128)(2,1)S(1)}, u32[]{:S(2)}, u32[]{:S(2)}) collective-permute-start(bf16[64,3968]{1,0:T(8,128)(2,1)S(1)} %collective-permute-done.21.refs_3_), channel_id=1, source_target_pairs={{0,8},{2,10},{4,0},{6,2},{8,16},{10,18},{12,4},{14,6},{16,24},{18,... | collective-permute-start | bytes 1523720 | tf_op jit(solution)/shard_map/gather_b_up_3/ppermute | solution.py:65
  76.0 11.8 %collective-permute-start.25 = (bf16[64,3968]{1,0:T(8,128)(2,1)S(1)}, bf16[64,3968]{1,0:T(8,128)(2,1)S(1)}, u32[]{:S(2)}, u32[]{:S(2)}) collective-permute-start(bf16[64,3968]{1,0:T(8,128)(2,1)S(1)} %collective-permute-done.22.refs_4_), channel_id=1, source_target_pairs={{0,4},{2,6},{4,12},{6,14},{8,0},{10,2},{12,20},{14,22},{16,8},{18,... | collective-permute-start | bytes 1523720 | tf_op jit(solution)/shard_map/gather_b_down_3/ppermute | solution.py:65
  76.4 13.8 %collective-permute-start.31 = (bf16[64,3968]{1,0:T(8,128)(2,1)S(1)}, bf16[64,3968]{1,0:T(8,128)(2,1)S(1)}, u32[]{:S(2)}, u32[]{:S(2)}) collective-permute-start(bf16[64,3968]{1,0:T(8,128)(2,1)S(1)} %collective-permute-done.21.refs_3_), channel_id=1, source_target_pairs={{0,2},{2,0},{4,6},{6,4},{8,10},{10,8},{12,14},{14,12},{16,18},{18,... | collective-permute-start | bytes 1523720 | tf_op jit(solution)/shard_map/gather_b_cores_-2/ppermute | solution.py:65
  76.4 14.3 %collective-permute-start.32 = (bf16[64,3968]{1,0:T(8,128)(2,1)S(1)}, bf16[64,3968]{1,0:T(8,128)(2,1)S(1)}, u32[]{:S(2)}, u32[]{:S(2)}) collective-permute-start(bf16[64,3968]{1,0:T(8,128)(2,1)S(1)} %collective-permute-done.22.refs_4_), channel_id=1, source_target_pairs={{0,2},{2,0},{4,6},{6,4},{8,10},{10,8},{12,14},{14,12},{16,18},{18,... | collective-permute-start | bytes 1523720 | tf_op jit(solution)/shard_map/gather_b_cores_2/ppermute | solution.py:65
  87.8 6.3 %collective-permute-start.29 = (bf16[32,3968]{1,0:T(8,128)(2,1)S(1)}, bf16[32,3968]{1,0:T(8,128)(2,1)S(1)}, u32[]{:S(2)}, u32[]{:S(2)}) collective-permute-start(bf16[32,3968]{1,0:T(8,128)(2,1)S(1)} %slice.225), channel_id=1, source_target_pairs={{0,8},{2,10},{4,0},{6,2},{8,16},{10,18},{12,4},{14,6},{16,24},{18,... | collective-permute-start | bytes 761864 | tf_op jit(solution)/shard_map/gather_b_up_4/ppermute | solution.py:65
  89.4 6.5 %collective-permute-start.30 = (bf16[32,3968]{1,0:T(8,128)(2,1)S(1)}, bf16[32,3968]{1,0:T(8,128)(2,1)S(1)}, u32[]{:S(2)}, u32[]{:S(2)}) collective-permute-start(bf16[32,3968]{1,0:T(8,128)(2,1)S(1)} %slice.226), channel_id=1, source_target_pairs={{0,4},{2,6},{4,12},{6,14},{8,0},{10,2},{12,20},{14,22},{16,8},{18,... | collective-permute-start | bytes 761864 | tf_op jit(solution)/shard_map/gather_b_down_4/ppermute | solution.py:65
  90.2 7.6 %collective-permute-start.33 = (bf16[64,3968]{1,0:T(8,128)(2,1)S(1)}, bf16[64,3968]{1,0:T(8,128)(2,1)S(1)}, u32[]{:S(2)}, u32[]{:S(2)}) collective-permute-start(bf16[64,3968]{1,0:T(8,128)(2,1)S(1)} %collective-permute-done.24.refs_5_), channel_id=1, source_target_pairs={{0,2},{2,0},{4,6},{6,4},{8,10},{10,8},{12,14},{14,12},{16,18},{18,... | collective-permute-start | bytes 1523720 | tf_op jit(solution)/shard_map/gather_b_cores_-3/ppermute | solution.py:65
  90.2 7.6 %collective-permute-start.34 = (bf16[64,3968]{1,0:T(8,128)(2,1)S(1)}, bf16[64,3968]{1,0:T(8,128)(2,1)S(1)}, u32[]{:S(2)}, u32[]{:S(2)}) collective-permute-start(bf16[64,3968]{1,0:T(8,128)(2,1)S(1)} %collective-permute-done.25.refs_6_), channel_id=1, source_target_pairs={{0,2},{2,0},{4,6},{6,4},{8,10},{10,8},{12,14},{14,12},{16,18},{18,... | collective-permute-start | bytes 1523720 | tf_op jit(solution)/shard_map/gather_b_cores_3/ppermute | solution.py:65
  95.9 1.5 collective-permute-start.35
  95.9 1.9 collective-permute-start.36
  112.3 8.4 %collective-permute-start.38 = (bf16[3,64,3968]{2,1,0:T(8,128)(2,1)}, bf16[3,64,3968]{2,1,0:T(8,128)(2,1)}, u32[]{:S(2)}, u32[]{:S(2)}) collective-permute-start(bf16[3,64,3968]{2,1,0:T(8,128)(2,1)} %get-tuple-element.277), channel_id=1, source_target_pairs={{0,2},{2,0},{4,6},{6,4},{8,10},{10,8},{12,14},{14,12},{16,18},{18,... | collective-permute-start | bytes 4571144 | tf_op jit(solution)/shard_map/sum_b_cores_early/ppermute | solution.py:65
  112.6 14.5 %collective-permute-start.39 = (bf16[256,1024]{1,0:T(8,128)(2,1)}, bf16[256,1024]{1,0:T(8,128)(2,1)S(1)}, u32[]{:S(2)}, u32[]{:S(2)}) collective-permute-start(bf16[256,1024]{1,0:T(8,128)(2,1)} %get-tuple-element.278.grad_two), channel_id=1, source_target_pairs={{0,1},{1,0},{2,3},{3,2},{4,5},{5,4},{6,7},{7,6},{8,9},{9,8},{10,11... | collective-permute-start | bytes 1572872 | tf_op jit(solution)/shard_map/ppermute | solution.py:32
  120.5 38.1 %collective-permute-start.46 = (bf16[5,64,3968]{2,1,0:T(8,128)(2,1)}, bf16[5,64,3968]{2,1,0:T(8,128)(2,1)}, u32[]{:S(2)}, u32[]{:S(2)}) collective-permute-start(bf16[5,64,3968]{2,1,0:T(8,128)(2,1)} %get-tuple-element.275), channel_id=1, source_target_pairs={{0,2},{2,0},{4,6},{6,4},{8,10},{10,8},{12,14},{14,12},{16,18},{18,... | collective-permute-start | bytes 7618568 | tf_op jit(solution)/shard_map/sum_b_cores_rest/ppermute | solution.py:65
  122.2 12.0 %collective-permute-start.40 = (bf16[32,3968]{1,0:T(8,128)(2,1)S(1)}, bf16[32,3968]{1,0:T(8,128)(2,1)S(1)}, u32[]{:S(2)}, u32[]{:S(2)}) collective-permute-start(bf16[32,3968]{1,0:T(8,128)(2,1)S(1)} %get-tuple-element.287), channel_id=1, source_target_pairs={{0,8},{2,10},{4,0},{6,2},{8,16},{10,18},{12,4},{14,6},{16,24},{18,... | collective-permute-start | bytes 761864 | tf_op jit(solution)/shard_map/sum_b_up_1/ppermute | solution.py:65
  122.8 11.3 %collective-permute-start.41 = (bf16[32,3968]{1,0:T(8,128)(2,1)S(1)}, bf16[32,3968]{1,0:T(8,128)(2,1)S(1)}, u32[]{:S(2)}, u32[]{:S(2)}) collective-permute-start(bf16[32,3968]{1,0:T(8,128)(2,1)S(1)} %get-tuple-element.288), channel_id=1, source_target_pairs={{0,4},{2,6},{4,12},{6,14},{8,0},{10,2},{12,20},{14,22},{16,8},{18,... | collective-permute-start | bytes 761864 | tf_op jit(solution)/shard_map/sum_b_down_1/ppermute | solution.py:65
  136.2 14.8 %collective-permute-start.44 = (bf16[64,3968]{1,0:T(8,128)(2,1)S(1)}, bf16[64,3968]{1,0:T(8,128)(2,1)S(1)}, u32[]{:S(2)}, u32[]{:S(2)}) collective-permute-start(bf16[64,3968]{1,0:T(8,128)(2,1)S(1)} %get-tuple-element.307), channel_id=1, source_target_pairs={{0,8},{2,10},{4,0},{6,2},{8,16},{10,18},{12,4},{14,6},{16,24},{18,... | collective-permute-start | bytes 1523720 | tf_op jit(solution)/shard_map/sum_b_up_2/ppermute | solution.py:65
  137.0 14.3 %collective-permute-start.45 = (bf16[64,3968]{1,0:T(8,128)(2,1)S(1)}, bf16[64,3968]{1,0:T(8,128)(2,1)}, u32[]{:S(2)}, u32[]{:S(2)}) collective-permute-start(bf16[64,3968]{1,0:T(8,128)(2,1)S(1)} %get-tuple-element.308), channel_id=1, source_target_pairs={{0,4},{2,6},{4,12},{6,14},{8,0},{10,2},{12,20},{14,22},{16,8},{18,... | collective-permute-start | bytes 1523720 | tf_op jit(solution)/shard_map/sum_b_down_2/ppermute | solution.py:65
  138.5 2.7 %collective-permute-start.42 = (bf16[64,1024]{1,0:T(8,128)(2,1)}, bf16[64,1024]{1,0:T(8,128)(2,1)S(1)}, u32[]{:S(2)}, u32[]{:S(2)}) collective-permute-start(bf16[64,1024]{1,0:T(8,128)(2,1)} %get-tuple-element.295), channel_id=1, source_target_pairs={{0,2},{2,4},{4,6},{6,8},{8,10},{10,12},{12,14},{14,16},{16,18},{18... | collective-permute-start | bytes 393224 | tf_op jit(solution)/shard_map/ppermute | solution.py:28
  139.8 4.4 %collective-permute-start.43 = (bf16[64,1024]{1,0:T(8,128)(2,1)}, bf16[64,1024]{1,0:T(8,128)(2,1)}, u32[]{:S(2)}, u32[]{:S(2)}) collective-permute-start(bf16[64,1024]{1,0:T(8,128)(2,1)} %get-tuple-element.296), channel_id=1, source_target_pairs={{2,0},{4,2},{6,4},{8,6},{10,8},{12,10},{14,12},{16,14},{18,16},{20... | collective-permute-start | bytes 393224 | tf_op jit(solution)/shard_map/ppermute | solution.py:28
  141.2 50.1 %collective-permute-start.37 = (bf16[128,1024]{1,0:T(8,128)(2,1)S(1)}, bf16[128,1024]{1,0:T(8,128)(2,1)S(1)}, u32[]{:S(2)}, u32[]{:S(2)}) collective-permute-start(bf16[128,1024]{1,0:T(8,128)(2,1)S(1)} %constant_dynamic-slice_fusion.1), channel_id=1, source_target_pairs={{0,1},{1,0},{2,3},{3,2},{4,5},{5,4},{6,7},{7,6},{8,9},{9,8},{10,11... | collective-permute-start | bytes 786440 | tf_op jit(solution)/shard_map/ppermute | solution.py:32
  151.3 12.2 %collective-permute-start.49 = (bf16[3,64,2176]{2,1,0:T(8,128)(2,1)}, bf16[3,64,2176]{2,1,0:T(8,128)(2,1)S(1)}, u32[]{:S(2)}, u32[]{:S(2)}) collective-permute-start(bf16[3,64,2176]{2,1,0:T(8,128)(2,1)} %get-tuple-element.320), channel_id=1, source_target_pairs={{0,2},{2,0},{4,6},{6,4},{8,10},{10,8},{12,14},{14,12},{16,18},{18,... | collective-permute-start | bytes 2506760 | tf_op jit(solution)/shard_map/sum_a_cores_early/ppermute | solution.py:65
  160.8 15.1 %collective-permute-start.54 = (bf16[64,3968]{1,0:T(8,128)(2,1)S(1)}, bf16[64,3968]{1,0:T(8,128)(2,1)S(1)}, u32[]{:S(2)}, u32[]{:S(2)}) collective-permute-start(bf16[64,3968]{1,0:T(8,128)(2,1)S(1)} %get-tuple-element.338), channel_id=1, source_target_pairs={{0,8},{2,10},{4,0},{6,2},{8,16},{10,18},{12,4},{14,6},{16,24},{18,... | collective-permute-start | bytes 1523720 | tf_op jit(solution)/shard_map/sum_b_up_3/ppermute | solution.py:65
  162.7 14.4 %collective-permute-start.55 = (bf16[64,3968]{1,0:T(8,128)(2,1)S(1)}, bf16[64,3968]{1,0:T(8,128)(2,1)S(1)}, u32[]{:S(2)}, u32[]{:S(2)}) collective-permute-start(bf16[64,3968]{1,0:T(8,128)(2,1)S(1)} %get-tuple-element.339), channel_id=1, source_target_pairs={{0,4},{2,6},{4,12},{6,14},{8,0},{10,2},{12,20},{14,22},{16,8},{18,... | collective-permute-start | bytes 1523720 | tf_op jit(solution)/shard_map/sum_b_down_3/ppermute | solution.py:65
  163.6 15.0 %collective-permute-start.50 = (bf16[32,2176]{1,0:T(8,128)(2,1)S(1)}, bf16[32,2176]{1,0:T(8,128)(2,1)S(1)}, u32[]{:S(2)}, u32[]{:S(2)}) collective-permute-start(bf16[32,2176]{1,0:T(8,128)(2,1)S(1)} %get-tuple-element.321), channel_id=1, source_target_pairs={{0,8},{2,10},{4,0},{6,2},{8,16},{10,18},{12,4},{14,6},{16,24},{18,... | collective-permute-start | bytes 417800 | tf_op jit(solution)/shard_map/sum_a_up_1/ppermute | solution.py:65
  164.9 14.4 %collective-permute-start.51 = (bf16[32,2176]{1,0:T(8,128)(2,1)S(1)}, bf16[32,2176]{1,0:T(8,128)(2,1)S(1)}, u32[]{:S(2)}, u32[]{:S(2)}) collective-permute-start(bf16[32,2176]{1,0:T(8,128)(2,1)S(1)} %get-tuple-element.322), channel_id=1, source_target_pairs={{0,4},{2,6},{4,12},{6,14},{8,0},{10,2},{12,20},{14,22},{16,8},{18,... | collective-permute-start | bytes 417800 | tf_op jit(solution)/shard_map/sum_a_down_1/ppermute | solution.py:65
  175.9 7.8 %collective-permute-start.48 = (bf16[128,1024]{1,0:T(8,128)(2,1)S(1)}, bf16[128,1024]{1,0:T(8,128)(2,1)S(1)}, u32[]{:S(2)}, u32[]{:S(2)}) collective-permute-start(bf16[128,1024]{1,0:T(8,128)(2,1)S(1)} %constant_dynamic-slice_fusion), channel_id=1, source_target_pairs={{0,1},{1,0},{2,3},{3,2},{4,5},{5,4},{6,7},{7,6},{8,9},{9,8},{10,11... | collective-permute-start | bytes 786440 | tf_op jit(solution)/shard_map/ppermute | solution.py:32
  177.1 14.0 %collective-permute-start.47 = (bf16[5,64,2176]{2,1,0:T(8,128)(2,1)}, bf16[5,64,2176]{2,1,0:T(8,128)(2,1)S(1)}, u32[]{:S(2)}, u32[]{:S(2)}) collective-permute-start(bf16[5,64,2176]{2,1,0:T(8,128)(2,1)} %get-tuple-element.317), channel_id=1, source_target_pairs={{0,2},{2,0},{4,6},{6,4},{8,10},{10,8},{12,14},{14,12},{16,18},{18,... | collective-permute-start | bytes 4177928 | tf_op jit(solution)/shard_map/sum_a_cores_rest/ppermute | solution.py:65
  183.7 7.3 %collective-permute-start.52 = (bf16[64,2176]{1,0:T(8,128)(2,1)S(1)}, bf16[64,2176]{1,0:T(8,128)(2,1)S(1)}, u32[]{:S(2)}, u32[]{:S(2)}) collective-permute-start(bf16[64,2176]{1,0:T(8,128)(2,1)S(1)} %get-tuple-element.327), channel_id=1, source_target_pairs={{0,8},{2,10},{4,0},{6,2},{8,16},{10,18},{12,4},{14,6},{16,24},{18,... | collective-permute-start | bytes 835592 | tf_op jit(solution)/shard_map/sum_a_up_2/ppermute | solution.py:65
  184.5 6.6 %collective-permute-start.53 = (bf16[64,2176]{1,0:T(8,128)(2,1)S(1)}, bf16[64,2176]{1,0:T(8,128)(2,1)S(1)}, u32[]{:S(2)}, u32[]{:S(2)}) collective-permute-start(bf16[64,2176]{1,0:T(8,128)(2,1)S(1)} %get-tuple-element.328), channel_id=1, source_target_pairs={{0,4},{2,6},{4,12},{6,14},{8,0},{10,2},{12,20},{14,22},{16,8},{18,... | collective-permute-start | bytes 835592 | tf_op jit(solution)/shard_map/sum_a_down_2/ppermute | solution.py:65
  191.3 9.6 %collective-permute-start.56 = (bf16[64,2176]{1,0:T(8,128)(2,1)S(1)}, bf16[64,2176]{1,0:T(8,128)(2,1)S(1)}, u32[]{:S(2)}, u32[]{:S(2)}) collective-permute-start(bf16[64,2176]{1,0:T(8,128)(2,1)S(1)} %get-tuple-element.344), channel_id=1, source_target_pairs={{0,8},{2,10},{4,0},{6,2},{8,16},{10,18},{12,4},{14,6},{16,24},{18,... | collective-permute-start | bytes 835592 | tf_op jit(solution)/shard_map/sum_a_up_3/ppermute | solution.py:65
  191.8 9.6 %collective-permute-start.57 = (bf16[64,2176]{1,0:T(8,128)(2,1)S(1)}, bf16[64,2176]{1,0:T(8,128)(2,1)S(1)}, u32[]{:S(2)}, u32[]{:S(2)}) collective-permute-start(bf16[64,2176]{1,0:T(8,128)(2,1)S(1)} %get-tuple-element.345), channel_id=1, source_target_pairs={{0,4},{2,6},{4,12},{6,14},{8,0},{10,2},{12,20},{14,22},{16,8},{18,... | collective-permute-start | bytes 835592 | tf_op jit(solution)/shard_map/sum_a_down_3/ppermute | solution.py:65
  193.4 18.1 %collective-permute-start.60 = (bf16[64,3968]{1,0:T(8,128)(2,1)S(1)}, bf16[64,3968]{1,0:T(8,128)(2,1)S(1)}, u32[]{:S(2)}, u32[]{:S(2)}) collective-permute-start(bf16[64,3968]{1,0:T(8,128)(2,1)S(1)} %get-tuple-element.352), channel_id=1, source_target_pairs={{0,8},{2,10},{4,0},{6,2},{8,16},{10,18},{12,4},{14,6},{16,24},{18,... | collective-permute-start | bytes 1523720 | tf_op jit(solution)/shard_map/sum_b_up_4/ppermute | solution.py:65
  193.8 17.7 %collective-permute-start.61 = (bf16[64,3968]{1,0:T(8,128)(2,1)S(1)}, bf16[64,3968]{1,0:T(8,128)(2,1)S(1)}, u32[]{:S(2)}, u32[]{:S(2)}) collective-permute-start(bf16[64,3968]{1,0:T(8,128)(2,1)S(1)} %get-tuple-element.353), channel_id=1, source_target_pairs={{0,4},{2,6},{4,12},{6,14},{8,0},{10,2},{12,20},{14,22},{16,8},{18,... | collective-permute-start | bytes 1523720 | tf_op jit(solution)/shard_map/sum_b_down_4/ppermute | solution.py:65
  201.6 12.9 %collective-permute-start.58 = (bf16[64,2176]{1,0:T(8,128)(2,1)S(1)}, bf16[64,2176]{1,0:T(8,128)(2,1)S(1)}, u32[]{:S(2)}, u32[]{:S(2)}) collective-permute-start(bf16[64,2176]{1,0:T(8,128)(2,1)S(1)} %get-tuple-element.348), channel_id=1, source_target_pairs={{0,8},{2,10},{4,0},{6,2},{8,16},{10,18},{12,4},{14,6},{16,24},{18,... | collective-permute-start | bytes 835592 | tf_op jit(solution)/shard_map/sum_a_up_4/ppermute | solution.py:65
  202.1 12.4 %collective-permute-start.59 = (bf16[64,2176]{1,0:T(8,128)(2,1)S(1)}, bf16[64,2176]{1,0:T(8,128)(2,1)S(1)}, u32[]{:S(2)}, u32[]{:S(2)}) collective-permute-start(bf16[64,2176]{1,0:T(8,128)(2,1)S(1)} %get-tuple-element.349), channel_id=1, source_target_pairs={{0,4},{2,6},{4,12},{6,14},{8,0},{10,2},{12,20},{14,22},{16,8},{18,... | collective-permute-start | bytes 835592 | tf_op jit(solution)/shard_map/sum_a_down_4/ppermute | solution.py:65
  217.0 5.0 %collective-permute-start.62 = (f32[64]{0:T(128)S(1)}, f32[64]{0:T(128)S(1)}, u32[]{:S(2)}, u32[]{:S(2)}) collective-permute-start(f32[64]{0:T(128)S(1)} %get-tuple-element.389), channel_id=1, source_target_pairs={{0,1},{1,0},{2,3},{3,2},{4,5},{5,4},{6,7},{7,6},{8,9},{9,8},{10,11... | collective-permute-start | bytes 776 | tf_op jit(solution)/shard_map/ppermute | solution.py:32
  (62 other events, 441.6 us)

commit v4 on v3

--- a/solution.py
+++ b/solution.py
@@ -230,9 +230,10 @@
     return centered * inverse, inverse
 
 
-def first_kernel(count, width, starts, tokens, before, after, cosine, sine, *refs):
+def first_kernel(count, width, starts, seq, tokens, before, after, cosine, sine, *refs):
     pieces = refs[:count]
-    whole, matrix, gains, work, queries, keys_values, wide_cosine, wide_sine = refs[count:-2]
+    whole, matrix, gains, work, queries, keys_values, wide_cosine, wide_sine = refs[count:-4]
+    context, term = refs[-4:-2]
     all_rows, ready = refs[-2:]
     copies = placing(starts, pieces, whole, ready)
     for copy in copies:
@@ -259,6 +260,7 @@
             if start < 2 * width:
                 part = turned_by(part, wide_cosine[...], wide_sine[...])
             keys_values[:, start - width : start - width + 256] = part.astype(BF16)
+    attend(seq, queries, keys_values, matrix, context, term)
 
 
 def window(seq, tile, tiles):
@@ -300,7 +302,7 @@
     whole[HALF + rows :] = after[...]
 
 
-def attend_kernel(seq, queries, keys_values, matrix, context, term):
+def attend(seq, queries, keys_values, matrix, context, term):
     rows, width = queries.shape
     tiles = rows // LANES
     for tile in range(tiles):
@@ -634,10 +636,10 @@
     steps_a.beside(steps_b)
     pieces, starts = steps_a.finish()
     count = len(pieces)
-    whole_a, attn_matrix, gains, work_one, queries, keys_values, cosine, sine = call(
+    whole_a, attn_matrix, gains, work_one, queries, keys_values, *later = call(
         functools.partial(first_kernel, count, width),
-        (starts, tokens_all, tokens_before, tokens_after, cosine, sine, *pieces),
-        [SMEM] + [VMEM] * 5 + [ANY] * count,
+        (starts, seq, tokens_all, tokens_before, tokens_after, cosine, sine, *pieces),
+        [SMEM] * 2 + [VMEM] * 5 + [ANY] * count,
         [
             shape_of(model_width, blob_a.shape[1], BF16),
             shape_of(model_width, width, BF16),
@@ -647,22 +649,16 @@
             shape_of(reach_rows, 2 * width, BF16),
             shape_of(reach_rows, LANES, F32),
             shape_of(reach_rows, LANES, F32),
+            shape_of(work_rows, width, BF16),
+            shape_of(work_rows, model_width, BF16),
         ],
         [pltpu.VMEM((reach_rows, model_width), BF16), pltpu.SemaphoreType.DMA((count,))],
         flops=6 * work_rows * model_width * width,
         moved=16 * MIB,
         room=60,
     )
-    queries = steps_b.ride(queries)
-    context, attn_term = call(
-        attend_kernel,
-        (seq, queries, keys_values, attn_matrix),
-        [SMEM] + [VMEM] * 3,
-        [pltpu.HBM((work_rows, width), BF16), pltpu.HBM((work_rows, model_width), BF16)],
-        flops=2 * work_rows * model_width * width,
-        moved=16 * MIB,
-        room=60,
-    )
+    cosine, sine, context, attn_term = later
+    attn_term = steps_b.ride(attn_term)
     attn_other = steps_b.ride(pair_swap(attn_term))
 
     pieces, starts = steps_b.finish()
@@ -722,7 +718,7 @@
     from_prev = passed_along(to_after, SEQ, 1)
 
     down_other = pair_swap(other_rows(down_term, row_count))
-    grad_queries = steps_b.ride(grad_queries)
+    from_prev, from_next = steps_b.ride((from_prev, from_next))
     last = call(
         functools.partial(last_kernel, early),
         (
@@ -756,13 +752,13 @@
         steps_a = Stepped(summed_terms(*factors))
     steps_a.step()
     steps_a.step()
-    one_other = steps_a.hold(one_other)
     steps_a.step()
     steps_a.step()
     steps_b.step()
-    down_other = steps_a.hold(down_other)
+    one_other = steps_a.hold(one_other)
     steps_a.beside(steps_b)
     steps_a.step()
+    down_other = steps_a.hold(down_other)
     steps_a.step()
     steps_a.beside(steps_b)
     share_b = steps_b.finish()

time: 223 us -> 217 us (0.973)
  starting transfers between devices: 57.1 us -> 53 us
  Pallas kernels: 49.1 us -> 46.2 us
  waiting for transfers between devices: 80.6 us -> 78 us
    ppermute x54, starting transfers between devices: 47.2 us -> 42.5 us  [go(): return lax.ppermute(block, SEQ, route)]
    ppermute x6, waiting for transfers between devices: 7.01 us -> 2.85 us  [pair_swap(): return lax.ppermute(block, PAIR, [(0, 1), (1, 0)])]
    ppermute x54, waiting for transfers between devices: 71.5 us -> 75 us  [go(): return lax.ppermute(block, SEQ, route)]
    pallas_call x5 -> x4, Pallas kernels: 37.9 us -> 35 us  [call(): pl.pallas_call(kernel, in_specs=specs, out_specs=[VMEM] * len(outs), out_...]
  transfers between devices with their start and end apart: 63 -> 63, of which waited for: 32 -> 29; matrix products, arithmetic and copies ran while one was open for 12% -> 13% of each run, Pallas kernels for 16% -> 15%
where the time goes in v4:
time: 217 us; the launch traced here: 216 us
  waiting for transfers between devices  78 us (36%)
  starting transfers between devices  53 us (24%)
  Pallas kernels  46.2 us (21%)
  other arithmetic  24.2 us (11%)
  local copies, waits for them, and re-layouts  12.8 us (6%)
    ppermute x54, waiting for transfers between devices, go(): return lax.ppermute(block, SEQ, route)  75 us
    ppermute x54, starting transfers between devices, go(): return lax.ppermute(block, SEQ, route)  42.5 us
    pallas_call x4, Pallas kernels, call(): pl.pallas_call(kernel, in_specs=specs, out_specs=[VMEM] * len(outs), out_...  35 us
    pallas_call x2, Pallas kernels, weight_terms(): pl.pallas_call(functools.partial(weight_kernel, tail), grid_spec=pltpu.Pr...  11.2 us
    convert_element_type x6, other arithmetic, scatter_sum(): downward = (at(self.half + step) + downward).astype(BF16)  6.69 us
    ppermute x6, starting transfers between devices, pair_swap(): return lax.ppermute(block, PAIR, [(0, 1), (1, 0)])  6.36 us
  transfers between devices with their start and end apart: 63, of which 29 were waited for; matrix products, arithmetic and copies ran while one was open for 13% of the time, Pallas kernels for 15%

profile of v4, /device:TPU:0, one launch (start us, length us, event | category | flops | bytes accessed | tf_op | source)
XLA Modules:
  0.0 215.8 jit_solution(1613912833267083179)
XLA Ops:
  0.7 1.0 copy.48
  3.3 3.1 %collective-permute-start.1 = (bf16[64,2176]{1,0:T(8,128)(2,1)S(1)}, bf16[64,2176]{1,0:T(8,128)(2,1)S(1)}, u32[]{:S(2)}, u32[]{:S(2)}) collective-permute-start(bf16[64,2176]{1,0:T(8,128)(2,1)S(1)} %fusion.26.refs_0_), channel_id=1, source_target_pairs={{0,8},{2,10},{4,0},{6,2},{8,16},{10,18},{12,4},{14,6},{16,24},{18,... | collective-permute-start | bytes 835592 | tf_op jit(solution)/shard_map/gather_a_up_1/ppermute | solution.py:65
  6.4 1.0 slice_select_fusion
  7.4 1.3 collective-permute-start
  8.7 1.2 dynamic_slice.21
  10.0 1.3 compare_select_fusion.1
  14.6 3.5 %collective-permute-start.5 = (bf16[64,2176]{1,0:T(8,128)(2,1)S(1)}, bf16[64,2176]{1,0:T(8,128)(2,1)}, u32[]{:S(2)}, u32[]{:S(2)}) collective-permute-start(bf16[64,2176]{1,0:T(8,128)(2,1)S(1)} %collective-permute-done.1.refs_1_), channel_id=1, source_target_pairs={{0,8},{2,10},{4,0},{6,2},{8,16},{10,18},{12,4},{14,6},{16,24},{18,... | collective-permute-start | bytes 835592 | tf_op jit(solution)/shard_map/gather_a_up_2/ppermute | solution.py:65
  18.7 1.3 collective-permute-start.4
  21.2 3.0 %collective-permute-done.5.refs_3_ = bf16[64,2176]{1,0:T(8,128)(2,1)} collective-permute-done((bf16[64,2176]{1,0:T(8,128)(2,1)S(1)}, bf16[64,2176]{1,0:T(8,128)(2,1)}, u32[]{:S(2)}, u32[]{:S(2)}) %collective-permute-start.5) | collective-permute-done | bytes 278560 | tf_op jit(solution)/shard_map/gather_a_up_2/ppermute | solution.py:65
  24.2 3.3 %collective-permute-done.6.refs_4_ = bf16[64,2176]{1,0:T(8,128)(2,1)} collective-permute-done((bf16[64,2176]{1,0:T(8,128)(2,1)}, bf16[64,2176]{1,0:T(8,128)(2,1)}, u32[]{:S(2)}, u32[]{:S(2)}) %collective-permute-start.6) | collective-permute-done | bytes 278560 | tf_op jit(solution)/shard_map/gather_a_down_2/ppermute | solution.py:65
  27.8 1.7 collective-permute-start.9
  30.2 1.2 gather_fusion.1
  31.3 1.5 multiply_sine_fusion
  32.8 1.6 collective-permute-start.11
  34.8 1.2 collective-permute-done.10.refs_6_
  36.1 1.6 collective-permute-done.9.refs_5_
  40.2 7.0 %collective-permute-done.11.refs_1_ = bf16[64,3968]{1,0:T(8,128)(2,1)} collective-permute-done((bf16[64,3968]{1,0:T(8,128)(2,1)}, bf16[64,3968]{1,0:T(8,128)(2,1)}, u32[]{:S(2)}, u32[]{:S(2)}) %collective-permute-start.11) | collective-permute-done | bytes 507936 | tf_op jit(solution)/shard_map/gather_b_up_1/ppermute | solution.py:65
  47.3 1.6 collective-permute-start.13
  49.9 2.4 %collective-permute-done.13.refs_7_ = bf16[32,2176]{1,0:T(8,128)(2,1)S(1)} collective-permute-done((bf16[32,2176]{1,0:T(8,128)(2,1)S(1)}, bf16[32,2176]{1,0:T(8,128)(2,1)S(1)}, u32[]{:S(2)}, u32[]{:S(2)}) %collective-permute-start.13) | collective-permute-done | bytes 139296 | tf_op jit(solution)/shard_map/gather_a_up_4/ppermute | solution.py:65
  52.4 1.6 collective-permute-done.14.refs_8_
  54.5 1.6 collective-permute-start.21
  57.9 8.3 %shard_map.224 = (bf16[1024,2176]{1,0:T(8,128)(2,1)}, bf16[1024,512]{1,0:T(8,128)(2,1)}, f32[8,1024]{1,0:T(8,128)}, bf16[256,1024]{1,0:T(8,128)(2,1)}, bf16[256,...) custom-call(s32[18]{0:T(128)} %multiply_add_fusion.starts, ...), custom_call_target="tpu_custom_call" | custom-call | flops 805306368 | bytes 16777216 | tf_op jit(solution)/shard_map/pallas_call | solution.py:183
  66.2 2.5 %collective-permute-done.21.refs_3_ = bf16[64,3968]{1,0:T(8,128)(2,1)S(1)} collective-permute-done((bf16[64,3968]{1,0:T(8,128)(2,1)}, bf16[64,3968]{1,0:T(8,128)(2,1)S(1)}, u32[]{:S(2)}, u32[]{:S(2)}) %collective-permute-start.21) | collective-permute-done | bytes 507936 | tf_op jit(solution)/shard_map/gather_b_up_2/ppermute | solution.py:65
  68.7 1.3 collective-permute-done.22.refs_4_
  70.3 1.7 collective-permute-start.24
  72.8 10.0 %collective-permute-done.24.refs_5_ = bf16[64,3968]{1,0:T(8,128)(2,1)S(1)} collective-permute-done((bf16[64,3968]{1,0:T(8,128)(2,1)S(1)}, bf16[64,3968]{1,0:T(8,128)(2,1)S(1)}, u32[]{:S(2)}, u32[]{:S(2)}) %collective-permute-start.24) | collective-permute-done | bytes 507936 | tf_op jit(solution)/shard_map/gather_b_up_3/ppermute | solution.py:65
  82.8 1.4 collective-permute-done.25.refs_6_
  84.3 1.7 collective-permute-start.29
  87.1 3.5 %collective-permute-done.29.refs_7_ = bf16[32,3968]{1,0:T(8,128)(2,1)S(1)} collective-permute-done((bf16[32,3968]{1,0:T(8,128)(2,1)S(1)}, bf16[32,3968]{1,0:T(8,128)(2,1)S(1)}, u32[]{:S(2)}, u32[]{:S(2)}) %collective-permute-start.29) | collective-permute-done | bytes 253984 | tf_op jit(solution)/shard_map/gather_b_up_4/ppermute | solution.py:65
  90.6 1.9 collective-permute-done.30.refs_8_
  93.0 1.0 collective-permute-done.35.refs_16_
  96.2 12.8 %shard_map.225 = (f32[256,1024]{1,0:T(8,128)}, bf16[256,1024]{1,0:T(8,128)(2,1)}, bf16[256,1408]{1,0:T(8,128)(2,1)}, bf16[256,2688]{1,0:T(8,128)(2,1)}, bf16[256...) custom-call(s32[18]{0:T(128)} %multiply_add_fusion.starts, ...), custom_call_target="tpu_custom_call" | custom-call | flops 4127195136 | bytes 33554432 | tf_op jit(solution)/shard_map/pallas_call | solution.py:183
  110.1 7.0 %shard_map.226 = (bf16[5,64,3968]{2,1,0:T(8,128)(2,1)}, bf16[5,64,3968]{2,1,0:T(8,128)(2,1)}) custom-call(s32[8]{0:T(128)} %gather_fusion.1, s32[1]{0:T(128)} %bitcast.8.core, bf16[256,1024]{1,0:T(8,128)(2,1)} %get-tuple-element.269.left_one, bf16[256,1024]{1,0:T(8,128)(2,1)} %pad_maximum_fusion.3.cot.left_two, ...), custom_call_target="tpu_custom_call" | custom-call | flops 1300234240 | bytes 7110656 | tf_op jit(solution)/shard_map/pallas_call | solution.py:501
  117.3 1.4 add_convert_fusion
  119.5 1.4 collective-permute-start.41
  120.9 2.8 %collective-permute-done.39.grad_two_other = bf16[256,1024]{1,0:T(8,128)(2,1)S(1)} collective-permute-done((bf16[256,1024]{1,0:T(8,128)(2,1)}, bf16[256,1024]{1,0:T(8,128)(2,1)S(1)}, u32[]{:S(2)}, u32[]{:S(2)}) %collective-permute-start.39) | collective-permute-done | bytes 524320 | tf_op jit(solution)/shard_map/ppermute | solution.py:32
  123.8 7.0 %shard_map.227 = (f32[256,1024]{1,0:T(8,128)}, bf16[256,1024]{1,0:T(8,128)(2,1)}, f32[8,1024]{1,0:T(8,128)S(1)}, bf16[256,512]{1,0:T(8,128)(2,1)S(1)}, f32[256,1...) custom-call(s32[2]{0:T(128)S(1)} %copy-done.16, f32[256,1024]{1,0:T(8,128)S(1)} %copy-done, ...), custom_call_target="tpu_custom_call" | custom-call | flops 536870912 | bytes 25165824 | tf_op jit(solution)/shard_map/pallas_call | solution.py:183
  130.9 1.6 collective-permute-start.42
  132.5 1.3 collective-permute-start.43
  133.8 2.5 %fusion.5 = (bf16[64,3968]{1,0:T(8,128)(2,1)}, bf16[64,3968]{1,0:T(8,128)(2,1)}) fusion(bf16[3,64,3968]{2,1,0:T(8,128)(2,1)} %collective-permute-done.38, bf16[32,3968]{1,0:T(8,128)(2,1)S(1)} %collective-permute-done.41, bf16[3,64,3968]{2,1,0:T(8,128)(2,1)S(1)} %copy-done.23, bf16[32,3968]{1,0:T(8,128)(2,1)S(1)} %collective-permute-done.40), kind=kLoop, calls=%fused_computation.13 | loop fusion | flops 3047424 | bytes 3555328 | tf_op jit(solution)/shard_map/convert_element_type | solution.py:128
  136.4 4.6 %collective-permute-start.44 = (bf16[64,3968]{1,0:T(8,128)(2,1)}, bf16[64,3968]{1,0:T(8,128)(2,1)}, u32[]{:S(2)}, u32[]{:S(2)}) collective-permute-start(bf16[64,3968]{1,0:T(8,128)(2,1)} %get-tuple-element.309), channel_id=1, source_target_pairs={{0,8},{2,10},{4,0},{6,2},{8,16},{10,18},{12,4},{14,6},{16,24},{18,... | collective-permute-start | bytes 1523720 | tf_op jit(solution)/shard_map/sum_b_up_2/ppermute | solution.py:65
  142.7 6.9 %shard_map.228 = (bf16[256,1536]{1,0:T(8,128)(2,1)}, bf16[256,1024]{1,0:T(8,128)(2,1)}, bf16[1024,128]{1,0:T(8,128)(2,1)}, bf16[3,64,2176]{2,1,0:T(8,128)(2,1)}, bf16[3,64,2176]{2,1,0:T(8,128)(2,1)}) custom-call(s32[8]{0:T(128)} %gather_fusion.1, s32[1]{0:T(128)} %bitcast.8.core, bf16[256,512]{1,0:T(8,128)(2,1)} %copy-done.11, f32[256,1024]{1,0:T(8,128)} %copy-done.2, ...), custom_call_target="tpu_custom_call" | custom-call | flops 805306368 | bytes 16777216 | tf_op jit(solution)/shard_map/pallas_call | solution.py:183
  149.6 2.1 collective-permute-done.44
  151.7 2.2 %collective-permute-done.45 = bf16[64,3968]{1,0:T(8,128)(2,1)} collective-permute-done((bf16[64,3968]{1,0:T(8,128)(2,1)}, bf16[64,3968]{1,0:T(8,128)(2,1)}, u32[]{:S(2)}, u32[]{:S(2)}) %collective-permute-start.45) | collective-permute-done | bytes 507936 | tf_op jit(solution)/shard_map/sum_b_down_2/ppermute | solution.py:65
  153.9 2.0 fusion.3
  156.4 1.6 collective-permute-start.55
  158.6 1.6 collective-permute-start.51
  160.3 4.2 %shard_map.229 = (bf16[5,64,2176]{2,1,0:T(8,128)(2,1)}, bf16[5,64,2176]{2,1,0:T(8,128)(2,1)}) custom-call(s32[8]{0:T(128)S(1)} %copy-done.15, s32[1]{0:T(128)} %bitcast.8.core, bf16[256,1024]{1,0:T(8,128)(2,1)S(1)} %copy-done.7, bf16[256,1024]{1,0:T(8,128)(2,1)S(1)} %copy-done.8, bf16[256,1536]{1,0:T(8,128)(2,1)S(1)} %copy-done.17, ...), custom_call_target="tpu_custom_call" | custom-call | flops 713031680 | bytes 3899392 | tf_op jit(solution)/shard_map/pallas_call | solution.py:501
  164.5 5.9 %collective-permute-done.54 = bf16[64,3968]{1,0:T(8,128)(2,1)S(1)} collective-permute-done((bf16[64,3968]{1,0:T(8,128)(2,1)S(1)}, bf16[64,3968]{1,0:T(8,128)(2,1)S(1)}, u32[]{:S(2)}, u32[]{:S(2)}) %collective-permute-start.54) | collective-permute-done | bytes 507936 | tf_op jit(solution)/shard_map/sum_b_up_3/ppermute | solution.py:65
  170.4 1.7 collective-permute-start.48
  173.2 1.1 collective-permute-start.52
  174.4 0.9 collective-permute-start.53
  175.3 1.6 fusion.1
  176.9 4.5 %collective-permute-done.52 = bf16[64,2176]{1,0:T(8,128)(2,1)S(1)} collective-permute-done((bf16[64,2176]{1,0:T(8,128)(2,1)S(1)}, bf16[64,2176]{1,0:T(8,128)(2,1)S(1)}, u32[]{:S(2)}, u32[]{:S(2)}) %collective-permute-start.52) | collective-permute-done | bytes 278560 | tf_op jit(solution)/shard_map/sum_a_up_2/ppermute | solution.py:65
  183.0 1.3 collective-permute-start.61
  185.0 1.3 collective-permute-start.57
  186.6 13.2 %collective-permute-done.56 = bf16[64,2176]{1,0:T(8,128)(2,1)S(1)} collective-permute-done((bf16[64,2176]{1,0:T(8,128)(2,1)S(1)}, bf16[64,2176]{1,0:T(8,128)(2,1)S(1)}, u32[]{:S(2)}, u32[]{:S(2)}) %collective-permute-start.56) | collective-permute-done | bytes 278560 | tf_op jit(solution)/shard_map/sum_a_up_3/ppermute | solution.py:65
  201.0 1.4 collective-permute-start.59
  202.5 1.0 fusion.23
  203.5 1.8 add_convert_fusion.2
  205.2 1.8 collective-permute-done.58
  207.6 1.3 fusion
  210.0 1.5 collective-permute-start.62
  213.1 1.4 copy.44
  (274 shorter events, 32.9 us)
Async XLA Ops:
  3.3 10.6 %collective-permute-start.1 = (bf16[64,2176]{1,0:T(8,128)(2,1)S(1)}, bf16[64,2176]{1,0:T(8,128)(2,1)S(1)}, u32[]{:S(2)}, u32[]{:S(2)}) collective-permute-start(bf16[64,2176]{1,0:T(8,128)(2,1)S(1)} %fusion.26.refs_0_), channel_id=1, source_target_pairs={{0,8},{2,10},{4,0},{6,2},{8,16},{10,18},{12,4},{14,6},{16,24},{18,... | collective-permute-start | bytes 835592 | tf_op jit(solution)/shard_map/gather_a_up_1/ppermute | solution.py:65
  6.4 8.2 %collective-permute-start.2 = (bf16[64,2176]{1,0:T(8,128)(2,1)S(1)}, bf16[64,2176]{1,0:T(8,128)(2,1)}, u32[]{:S(2)}, u32[]{:S(2)}) collective-permute-start(bf16[64,2176]{1,0:T(8,128)(2,1)S(1)} %fusion.26.refs_0_), channel_id=1, source_target_pairs={{0,4},{2,6},{4,12},{6,14},{8,0},{10,2},{12,20},{14,22},{16,8},{18,... | collective-permute-start | bytes 835592 | tf_op jit(solution)/shard_map/gather_a_down_1/ppermute | solution.py:65
  6.4 8.2 %collective-permute-start.3 = (bf16[64,2176]{1,0:T(8,128)(2,1)S(1)}, bf16[64,2176]{1,0:T(8,128)(2,1)S(1)}, u32[]{:S(2)}, u32[]{:S(2)}) collective-permute-start(bf16[64,2176]{1,0:T(8,128)(2,1)S(1)} %fusion.26.refs_0_), channel_id=1, source_target_pairs={{0,2},{2,0},{4,6},{6,4},{8,10},{10,8},{12,14},{14,12},{16,18},{18,... | collective-permute-start | bytes 835592 | tf_op jit(solution)/shard_map/gather_a_cores_0/ppermute | solution.py:65
  7.4 6.5 %collective-permute-start = (bf16[64,1024]{1,0:T(8,128)(2,1)S(1)}, bf16[64,1024]{1,0:T(8,128)(2,1)S(1)}, u32[]{:S(2)}, u32[]{:S(2)}) collective-permute-start(bf16[64,1024]{1,0:T(8,128)(2,1)S(1)} %slice_select_fusion), channel_id=1, source_target_pairs={{2,0},{4,2},{6,4},{8,6},{10,8},{12,10},{14,12},{16,14},{18,16},{20... | collective-permute-start | bytes 393224 | tf_op jit(solution)/shard_map/ppermute | solution.py:571
  14.6 9.6 %collective-permute-start.5 = (bf16[64,2176]{1,0:T(8,128)(2,1)S(1)}, bf16[64,2176]{1,0:T(8,128)(2,1)}, u32[]{:S(2)}, u32[]{:S(2)}) collective-permute-start(bf16[64,2176]{1,0:T(8,128)(2,1)S(1)} %collective-permute-done.1.refs_1_), channel_id=1, source_target_pairs={{0,8},{2,10},{4,0},{6,2},{8,16},{10,18},{12,4},{14,6},{16,24},{18,... | collective-permute-start | bytes 835592 | tf_op jit(solution)/shard_map/gather_a_up_2/ppermute | solution.py:65
  18.2 9.4 %collective-permute-start.7 = (bf16[64,2176]{1,0:T(8,128)(2,1)S(1)}, bf16[64,2176]{1,0:T(8,128)(2,1)}, u32[]{:S(2)}, u32[]{:S(2)}) collective-permute-start(bf16[64,2176]{1,0:T(8,128)(2,1)S(1)} %collective-permute-done.1.refs_1_), channel_id=1, source_target_pairs={{0,2},{2,0},{4,6},{6,4},{8,10},{10,8},{12,14},{14,12},{16,18},{18,... | collective-permute-start | bytes 835592 | tf_op jit(solution)/shard_map/gather_a_cores_-1/ppermute | solution.py:65
  18.2 9.4 %collective-permute-start.6 = (bf16[64,2176]{1,0:T(8,128)(2,1)}, bf16[64,2176]{1,0:T(8,128)(2,1)}, u32[]{:S(2)}, u32[]{:S(2)}) collective-permute-start(bf16[64,2176]{1,0:T(8,128)(2,1)} %collective-permute-done.2.refs_2_), channel_id=1, source_target_pairs={{0,4},{2,6},{4,12},{6,14},{8,0},{10,2},{12,20},{14,22},{16,8},{18,... | collective-permute-start | bytes 835592 | tf_op jit(solution)/shard_map/gather_a_down_2/ppermute | solution.py:65
  18.2 9.4 %collective-permute-start.8 = (bf16[64,2176]{1,0:T(8,128)(2,1)}, bf16[64,2176]{1,0:T(8,128)(2,1)}, u32[]{:S(2)}, u32[]{:S(2)}) collective-permute-start(bf16[64,2176]{1,0:T(8,128)(2,1)} %collective-permute-done.2.refs_2_), channel_id=1, source_target_pairs={{0,2},{2,0},{4,6},{6,4},{8,10},{10,8},{12,14},{14,12},{16,18},{18,... | collective-permute-start | bytes 835592 | tf_op jit(solution)/shard_map/gather_a_cores_1/ppermute | solution.py:65
  18.7 18.9 %collective-permute-start.4 = (bf16[320,1024]{1,0:T(8,128)(2,1)S(1)}, bf16[320,1024]{1,0:T(8,128)(2,1)S(1)}, u32[]{:S(2)}, u32[]{:S(2)}) collective-permute-start(bf16[320,1024]{1,0:T(8,128)(2,1)S(1)} %pad_maximum_fusion.1), channel_id=1, source_target_pairs={{0,1},{1,0},{2,3},{3,2},{4,5},{5,4},{6,7},{7,6},{8,9},{9,8},{10,11... | collective-permute-start | bytes 1966088 | tf_op jit(solution)/shard_map/ppermute | solution.py:32
  27.6 8.5 %collective-permute-start.10 = (bf16[64,2176]{1,0:T(8,128)(2,1)}, bf16[64,2176]{1,0:T(8,128)(2,1)S(1)}, u32[]{:S(2)}, u32[]{:S(2)}) collective-permute-start(bf16[64,2176]{1,0:T(8,128)(2,1)} %collective-permute-done.6.refs_4_), channel_id=1, source_target_pairs={{0,4},{2,6},{4,12},{6,14},{8,0},{10,2},{12,20},{14,22},{16,8},{18,... | collective-permute-start | bytes 835592 | tf_op jit(solution)/shard_map/gather_a_down_3/ppermute | solution.py:65
  27.8 9.8 %collective-permute-start.9 = (bf16[64,2176]{1,0:T(8,128)(2,1)}, bf16[64,2176]{1,0:T(8,128)(2,1)S(1)}, u32[]{:S(2)}, u32[]{:S(2)}) collective-permute-start(bf16[64,2176]{1,0:T(8,128)(2,1)} %collective-permute-done.5.refs_3_), channel_id=1, source_target_pairs={{0,8},{2,10},{4,0},{6,2},{8,16},{10,18},{12,4},{14,6},{16,24},{18,... | collective-permute-start | bytes 835592 | tf_op jit(solution)/shard_map/gather_a_up_3/ppermute | solution.py:65
  32.8 14.4 %collective-permute-start.11 = (bf16[64,3968]{1,0:T(8,128)(2,1)}, bf16[64,3968]{1,0:T(8,128)(2,1)}, u32[]{:S(2)}, u32[]{:S(2)}) collective-permute-start(bf16[64,3968]{1,0:T(8,128)(2,1)} %pad.37.refs_0_), channel_id=1, source_target_pairs={{0,8},{2,10},{4,0},{6,2},{8,16},{10,18},{12,4},{14,6},{16,24},{18,... | collective-permute-start | bytes 1523720 | tf_op jit(solution)/shard_map/gather_b_up_1/ppermute | solution.py:65
  34.4 12.9 %collective-permute-start.12 = (bf16[64,3968]{1,0:T(8,128)(2,1)}, bf16[64,3968]{1,0:T(8,128)(2,1)}, u32[]{:S(2)}, u32[]{:S(2)}) collective-permute-start(bf16[64,3968]{1,0:T(8,128)(2,1)} %pad.37.refs_0_), channel_id=1, source_target_pairs={{0,4},{2,6},{4,12},{6,14},{8,0},{10,2},{12,20},{14,22},{16,8},{18,... | collective-permute-start | bytes 1523720 | tf_op jit(solution)/shard_map/gather_b_down_1/ppermute | solution.py:65
  36.1 13.9 %collective-permute-start.15 = (bf16[64,2176]{1,0:T(8,128)(2,1)}, bf16[64,2176]{1,0:T(8,128)(2,1)S(1)}, u32[]{:S(2)}, u32[]{:S(2)}) collective-permute-start(bf16[64,2176]{1,0:T(8,128)(2,1)} %collective-permute-done.5.refs_3_), channel_id=1, source_target_pairs={{0,2},{2,0},{4,6},{6,4},{8,10},{10,8},{12,14},{14,12},{16,18},{18,... | collective-permute-start | bytes 835592 | tf_op jit(solution)/shard_map/gather_a_cores_-2/ppermute | solution.py:65
  47.3 5.1 %collective-permute-start.13 = (bf16[32,2176]{1,0:T(8,128)(2,1)S(1)}, bf16[32,2176]{1,0:T(8,128)(2,1)S(1)}, u32[]{:S(2)}, u32[]{:S(2)}) collective-permute-start(bf16[32,2176]{1,0:T(8,128)(2,1)S(1)} %slice.223), channel_id=1, source_target_pairs={{0,8},{2,10},{4,0},{6,2},{8,16},{10,18},{12,4},{14,6},{16,24},{18,... | collective-permute-start | bytes 417800 | tf_op jit(solution)/shard_map/gather_a_up_4/ppermute | solution.py:65
  48.9 5.1 %collective-permute-start.14 = (bf16[32,2176]{1,0:T(8,128)(2,1)S(1)}, bf16[32,2176]{1,0:T(8,128)(2,1)S(1)}, u32[]{:S(2)}, u32[]{:S(2)}) collective-permute-start(bf16[32,2176]{1,0:T(8,128)(2,1)S(1)} %slice.224), channel_id=1, source_target_pairs={{0,4},{2,6},{4,12},{6,14},{8,0},{10,2},{12,20},{14,22},{16,8},{18,... | collective-permute-start | bytes 417800 | tf_op jit(solution)/shard_map/gather_a_down_4/ppermute | solution.py:65
  49.4 5.1 %collective-permute-start.16 = (bf16[64,2176]{1,0:T(8,128)(2,1)}, bf16[64,2176]{1,0:T(8,128)(2,1)S(1)}, u32[]{:S(2)}, u32[]{:S(2)}) collective-permute-start(bf16[64,2176]{1,0:T(8,128)(2,1)} %collective-permute-done.6.refs_4_), channel_id=1, source_target_pairs={{0,2},{2,0},{4,6},{6,4},{8,10},{10,8},{12,14},{14,12},{16,18},{18,... | collective-permute-start | bytes 835592 | tf_op jit(solution)/shard_map/gather_a_cores_2/ppermute | solution.py:65
  49.4 7.3 %collective-permute-start.17 = (bf16[64,2176]{1,0:T(8,128)(2,1)S(1)}, bf16[64,2176]{1,0:T(8,128)(2,1)S(1)}, u32[]{:S(2)}, u32[]{:S(2)}) collective-permute-start(bf16[64,2176]{1,0:T(8,128)(2,1)S(1)} %collective-permute-done.9.refs_5_), channel_id=1, source_target_pairs={{0,2},{2,0},{4,6},{6,4},{8,10},{10,8},{12,14},{14,12},{16,18},{18,... | collective-permute-start | bytes 835592 | tf_op jit(solution)/shard_map/gather_a_cores_-3/ppermute | solution.py:65
  54.0 2.2 %collective-permute-start.19 = (bf16[32,2176]{1,0:T(8,128)(2,1)S(1)}, bf16[32,2176]{1,0:T(8,128)(2,1)S(1)}, u32[]{:S(2)}, u32[]{:S(2)}) collective-permute-start(bf16[32,2176]{1,0:T(8,128)(2,1)S(1)} %collective-permute-done.13.refs_7_), channel_id=1, source_target_pairs={{0,2},{2,0},{4,6},{6,4},{8,10},{10,8},{12,14},{14,12},{16,18},{18,... | collective-permute-start | bytes 417800 | tf_op jit(solution)/shard_map/gather_a_cores_-4/ppermute | solution.py:65
  54.0 2.6 %collective-permute-start.20 = (bf16[32,2176]{1,0:T(8,128)(2,1)S(1)}, bf16[32,2176]{1,0:T(8,128)(2,1)S(1)}, u32[]{:S(2)}, u32[]{:S(2)}) collective-permute-start(bf16[32,2176]{1,0:T(8,128)(2,1)S(1)} %collective-permute-done.14.refs_8_), channel_id=1, source_target_pairs={{0,2},{2,0},{4,6},{6,4},{8,10},{10,8},{12,14},{14,12},{16,18},{18,... | collective-permute-start | bytes 417800 | tf_op jit(solution)/shard_map/gather_a_cores_4/ppermute | solution.py:65
  54.5 2.7 %collective-permute-start.18 = (bf16[64,2176]{1,0:T(8,128)(2,1)S(1)}, bf16[64,2176]{1,0:T(8,128)(2,1)S(1)}, u32[]{:S(2)}, u32[]{:S(2)}) collective-permute-start(bf16[64,2176]{1,0:T(8,128)(2,1)S(1)} %collective-permute-done.10.refs_6_), channel_id=1, source_target_pairs={{0,2},{2,0},{4,6},{6,4},{8,10},{10,8},{12,14},{14,12},{16,18},{18,... | collective-permute-start | bytes 835592 | tf_op jit(solution)/shard_map/gather_a_cores_3/ppermute | solution.py:65
  54.5 14.2 %collective-permute-start.21 = (bf16[64,3968]{1,0:T(8,128)(2,1)}, bf16[64,3968]{1,0:T(8,128)(2,1)S(1)}, u32[]{:S(2)}, u32[]{:S(2)}) collective-permute-start(bf16[64,3968]{1,0:T(8,128)(2,1)} %collective-permute-done.11.refs_1_), channel_id=1, source_target_pairs={{0,8},{2,10},{4,0},{6,2},{8,16},{10,18},{12,4},{14,6},{16,24},{18,... | collective-permute-start | bytes 1523720 | tf_op jit(solution)/shard_map/gather_b_up_2/ppermute | solution.py:65
  56.2 13.9 %collective-permute-start.22 = (bf16[64,3968]{1,0:T(8,128)(2,1)}, bf16[64,3968]{1,0:T(8,128)(2,1)S(1)}, u32[]{:S(2)}, u32[]{:S(2)}) collective-permute-start(bf16[64,3968]{1,0:T(8,128)(2,1)} %collective-permute-done.12.refs_2_), channel_id=1, source_target_pairs={{0,4},{2,6},{4,12},{6,14},{8,0},{10,2},{12,20},{14,22},{16,8},{18,... | collective-permute-start | bytes 1523720 | tf_op jit(solution)/shard_map/gather_b_down_2/ppermute | solution.py:65
  56.6 15.4 %collective-permute-start.26 = (bf16[64,3968]{1,0:T(8,128)(2,1)S(1)}, bf16[64,3968]{1,0:T(8,128)(2,1)}, u32[]{:S(2)}, u32[]{:S(2)}) collective-permute-start(bf16[64,3968]{1,0:T(8,128)(2,1)S(1)} %copy-done.34), channel_id=1, source_target_pairs={{0,2},{2,0},{4,6},{6,4},{8,10},{10,8},{12,14},{14,12},{16,18},{18,... | collective-permute-start | bytes 1523720 | tf_op jit(solution)/shard_map/gather_b_cores_0/ppermute | solution.py:65
  56.7 15.6 %collective-permute-start.27 = (bf16[64,3968]{1,0:T(8,128)(2,1)}, bf16[64,3968]{1,0:T(8,128)(2,1)S(1)}, u32[]{:S(2)}, u32[]{:S(2)}) collective-permute-start(bf16[64,3968]{1,0:T(8,128)(2,1)} %collective-permute-done.11.refs_1_), channel_id=1, source_target_pairs={{0,2},{2,0},{4,6},{6,4},{8,10},{10,8},{12,14},{14,12},{16,18},{18,... | collective-permute-start | bytes 1523720 | tf_op jit(solution)/shard_map/gather_b_cores_-1/ppermute | solution.py:65
  57.2 15.1 %collective-permute-start.28 = (bf16[64,3968]{1,0:T(8,128)(2,1)}, bf16[64,3968]{1,0:T(8,128)(2,1)}, u32[]{:S(2)}, u32[]{:S(2)}) collective-permute-start(bf16[64,3968]{1,0:T(8,128)(2,1)} %collective-permute-done.12.refs_2_), channel_id=1, source_target_pairs={{0,2},{2,0},{4,6},{6,4},{8,10},{10,8},{12,14},{14,12},{16,18},{18,... | collective-permute-start | bytes 1523720 | tf_op jit(solution)/shard_map/gather_b_cores_1/ppermute | solution.py:65
  68.7 27.4 %copy-start.54 = (bf16[64,3968]{1,0:T(8,128)(2,1)}, bf16[64,3968]{1,0:T(8,128)(2,1)S(1)}, u32[]{:S(2)}) copy-start(bf16[64,3968]{1,0:T(8,128)(2,1)S(1)} %collective-permute-done.21.refs_3_) | copy-start | bytes 1523716
  70.0 14.2 %collective-permute-start.23 = (bf16[256,1024]{1,0:T(8,128)(2,1)}, bf16[256,1024]{1,0:T(8,128)(2,1)S(1)}, u32[]{:S(2)}, u32[]{:S(2)}) collective-permute-start(bf16[256,1024]{1,0:T(8,128)(2,1)} %get-tuple-element.236.term), channel_id=1, source_target_pairs={{0,1},{1,0},{2,3},{3,2},{4,5},{5,4},{6,7},{7,6},{8,9},{9,8},{10,11... | collective-permute-start | bytes 1572872 | tf_op jit(solution)/shard_map/ppermute | solution.py:32
  70.3 12.5 %collective-permute-start.24 = (bf16[64,3968]{1,0:T(8,128)(2,1)S(1)}, bf16[64,3968]{1,0:T(8,128)(2,1)S(1)}, u32[]{:S(2)}, u32[]{:S(2)}) collective-permute-start(bf16[64,3968]{1,0:T(8,128)(2,1)S(1)} %collective-permute-done.21.refs_3_), channel_id=1, source_target_pairs={{0,8},{2,10},{4,0},{6,2},{8,16},{10,18},{12,4},{14,6},{16,24},{18,... | collective-permute-start | bytes 1523720 | tf_op jit(solution)/shard_map/gather_b_up_3/ppermute | solution.py:65
  72.0 12.3 %collective-permute-start.25 = (bf16[64,3968]{1,0:T(8,128)(2,1)S(1)}, bf16[64,3968]{1,0:T(8,128)(2,1)S(1)}, u32[]{:S(2)}, u32[]{:S(2)}) collective-permute-start(bf16[64,3968]{1,0:T(8,128)(2,1)S(1)} %collective-permute-done.22.refs_4_), channel_id=1, source_target_pairs={{0,4},{2,6},{4,12},{6,14},{8,0},{10,2},{12,20},{14,22},{16,8},{18,... | collective-permute-start | bytes 1523720 | tf_op jit(solution)/shard_map/gather_b_down_3/ppermute | solution.py:65
  72.3 14.3 %collective-permute-start.31 = (bf16[64,3968]{1,0:T(8,128)(2,1)S(1)}, bf16[64,3968]{1,0:T(8,128)(2,1)S(1)}, u32[]{:S(2)}, u32[]{:S(2)}) collective-permute-start(bf16[64,3968]{1,0:T(8,128)(2,1)S(1)} %collective-permute-done.21.refs_3_), channel_id=1, source_target_pairs={{0,2},{2,0},{4,6},{6,4},{8,10},{10,8},{12,14},{14,12},{16,18},{18,... | collective-permute-start | bytes 1523720 | tf_op jit(solution)/shard_map/gather_b_cores_-2/ppermute | solution.py:65
  72.3 14.8 %collective-permute-start.32 = (bf16[64,3968]{1,0:T(8,128)(2,1)S(1)}, bf16[64,3968]{1,0:T(8,128)(2,1)S(1)}, u32[]{:S(2)}, u32[]{:S(2)}) collective-permute-start(bf16[64,3968]{1,0:T(8,128)(2,1)S(1)} %collective-permute-done.22.refs_4_), channel_id=1, source_target_pairs={{0,2},{2,0},{4,6},{6,4},{8,10},{10,8},{12,14},{14,12},{16,18},{18,... | collective-permute-start | bytes 1523720 | tf_op jit(solution)/shard_map/gather_b_cores_2/ppermute | solution.py:65
  84.3 6.3 %collective-permute-start.29 = (bf16[32,3968]{1,0:T(8,128)(2,1)S(1)}, bf16[32,3968]{1,0:T(8,128)(2,1)S(1)}, u32[]{:S(2)}, u32[]{:S(2)}) collective-permute-start(bf16[32,3968]{1,0:T(8,128)(2,1)S(1)} %slice.225), channel_id=1, source_target_pairs={{0,8},{2,10},{4,0},{6,2},{8,16},{10,18},{12,4},{14,6},{16,24},{18,... | collective-permute-start | bytes 761864 | tf_op jit(solution)/shard_map/gather_b_up_4/ppermute | solution.py:65
  86.0 6.5 %collective-permute-start.30 = (bf16[32,3968]{1,0:T(8,128)(2,1)S(1)}, bf16[32,3968]{1,0:T(8,128)(2,1)S(1)}, u32[]{:S(2)}, u32[]{:S(2)}) collective-permute-start(bf16[32,3968]{1,0:T(8,128)(2,1)S(1)} %slice.226), channel_id=1, source_target_pairs={{0,4},{2,6},{4,12},{6,14},{8,0},{10,2},{12,20},{14,22},{16,8},{18,... | collective-permute-start | bytes 761864 | tf_op jit(solution)/shard_map/gather_b_down_4/ppermute | solution.py:65
  86.6 7.8 %collective-permute-start.33 = (bf16[64,3968]{1,0:T(8,128)(2,1)S(1)}, bf16[64,3968]{1,0:T(8,128)(2,1)S(1)}, u32[]{:S(2)}, u32[]{:S(2)}) collective-permute-start(bf16[64,3968]{1,0:T(8,128)(2,1)S(1)} %collective-permute-done.24.refs_5_), channel_id=1, source_target_pairs={{0,2},{2,0},{4,6},{6,4},{8,10},{10,8},{12,14},{14,12},{16,18},{18,... | collective-permute-start | bytes 1523720 | tf_op jit(solution)/shard_map/gather_b_cores_-3/ppermute | solution.py:65
  86.6 7.8 %collective-permute-start.34 = (bf16[64,3968]{1,0:T(8,128)(2,1)S(1)}, bf16[64,3968]{1,0:T(8,128)(2,1)S(1)}, u32[]{:S(2)}, u32[]{:S(2)}) collective-permute-start(bf16[64,3968]{1,0:T(8,128)(2,1)S(1)} %collective-permute-done.25.refs_6_), channel_id=1, source_target_pairs={{0,2},{2,0},{4,6},{6,4},{8,10},{10,8},{12,14},{14,12},{16,18},{18,... | collective-permute-start | bytes 1523720 | tf_op jit(solution)/shard_map/gather_b_cores_3/ppermute | solution.py:65
  92.5 1.5 collective-permute-start.35
  92.5 1.9 collective-permute-start.36
  108.9 8.4 %collective-permute-start.38 = (bf16[3,64,3968]{2,1,0:T(8,128)(2,1)}, bf16[3,64,3968]{2,1,0:T(8,128)(2,1)}, u32[]{:S(2)}, u32[]{:S(2)}) collective-permute-start(bf16[3,64,3968]{2,1,0:T(8,128)(2,1)} %get-tuple-element.275), channel_id=1, source_target_pairs={{0,2},{2,0},{4,6},{6,4},{8,10},{10,8},{12,14},{14,12},{16,18},{18,... | collective-permute-start | bytes 4571144 | tf_op jit(solution)/shard_map/sum_b_cores_early/ppermute | solution.py:65
  109.3 14.5 %collective-permute-start.39 = (bf16[256,1024]{1,0:T(8,128)(2,1)}, bf16[256,1024]{1,0:T(8,128)(2,1)S(1)}, u32[]{:S(2)}, u32[]{:S(2)}) collective-permute-start(bf16[256,1024]{1,0:T(8,128)(2,1)} %get-tuple-element.276.grad_two), channel_id=1, source_target_pairs={{0,1},{1,0},{2,3},{3,2},{4,5},{5,4},{6,7},{7,6},{8,9},{9,8},{10,11... | collective-permute-start | bytes 1572872 | tf_op jit(solution)/shard_map/ppermute | solution.py:32
  117.2 36.7 %collective-permute-start.46 = (bf16[5,64,3968]{2,1,0:T(8,128)(2,1)}, bf16[5,64,3968]{2,1,0:T(8,128)(2,1)}, u32[]{:S(2)}, u32[]{:S(2)}) collective-permute-start(bf16[5,64,3968]{2,1,0:T(8,128)(2,1)} %get-tuple-element.273), channel_id=1, source_target_pairs={{0,2},{2,0},{4,6},{6,4},{8,10},{10,8},{12,14},{14,12},{16,18},{18,... | collective-permute-start | bytes 7618568 | tf_op jit(solution)/shard_map/sum_b_cores_rest/ppermute | solution.py:65
  118.8 12.0 %collective-permute-start.40 = (bf16[32,3968]{1,0:T(8,128)(2,1)S(1)}, bf16[32,3968]{1,0:T(8,128)(2,1)S(1)}, u32[]{:S(2)}, u32[]{:S(2)}) collective-permute-start(bf16[32,3968]{1,0:T(8,128)(2,1)S(1)} %get-tuple-element.289), channel_id=1, source_target_pairs={{0,8},{2,10},{4,0},{6,2},{8,16},{10,18},{12,4},{14,6},{16,24},{18,... | collective-permute-start | bytes 761864 | tf_op jit(solution)/shard_map/sum_b_up_1/ppermute | solution.py:65
  119.5 11.4 %collective-permute-start.41 = (bf16[32,3968]{1,0:T(8,128)(2,1)S(1)}, bf16[32,3968]{1,0:T(8,128)(2,1)S(1)}, u32[]{:S(2)}, u32[]{:S(2)}) collective-permute-start(bf16[32,3968]{1,0:T(8,128)(2,1)S(1)} %get-tuple-element.290), channel_id=1, source_target_pairs={{0,4},{2,6},{4,12},{6,14},{8,0},{10,2},{12,20},{14,22},{16,8},{18,... | collective-permute-start | bytes 761864 | tf_op jit(solution)/shard_map/sum_b_down_1/ppermute | solution.py:65
  130.9 5.4 %collective-permute-start.42 = (bf16[64,1024]{1,0:T(8,128)(2,1)}, bf16[64,1024]{1,0:T(8,128)(2,1)S(1)}, u32[]{:S(2)}, u32[]{:S(2)}) collective-permute-start(bf16[64,1024]{1,0:T(8,128)(2,1)} %get-tuple-element.291), channel_id=1, source_target_pairs={{0,2},{2,4},{4,6},{6,8},{8,10},{10,12},{12,14},{14,16},{16,18},{18... | collective-permute-start | bytes 393224 | tf_op jit(solution)/shard_map/ppermute | solution.py:28
  132.5 3.9 %collective-permute-start.43 = (bf16[64,1024]{1,0:T(8,128)(2,1)}, bf16[64,1024]{1,0:T(8,128)(2,1)S(1)}, u32[]{:S(2)}, u32[]{:S(2)}) collective-permute-start(bf16[64,1024]{1,0:T(8,128)(2,1)} %get-tuple-element.292), channel_id=1, source_target_pairs={{2,0},{4,2},{6,4},{8,6},{10,8},{12,10},{14,12},{16,14},{18,16},{20... | collective-permute-start | bytes 393224 | tf_op jit(solution)/shard_map/ppermute | solution.py:28
  136.4 15.3 %collective-permute-start.44 = (bf16[64,3968]{1,0:T(8,128)(2,1)}, bf16[64,3968]{1,0:T(8,128)(2,1)}, u32[]{:S(2)}, u32[]{:S(2)}) collective-permute-start(bf16[64,3968]{1,0:T(8,128)(2,1)} %get-tuple-element.309), channel_id=1, source_target_pairs={{0,8},{2,10},{4,0},{6,2},{8,16},{10,18},{12,4},{14,6},{16,24},{18,... | collective-permute-start | bytes 1523720 | tf_op jit(solution)/shard_map/sum_b_up_2/ppermute | solution.py:65
  141.0 12.8 %collective-permute-start.45 = (bf16[64,3968]{1,0:T(8,128)(2,1)}, bf16[64,3968]{1,0:T(8,128)(2,1)}, u32[]{:S(2)}, u32[]{:S(2)}) collective-permute-start(bf16[64,3968]{1,0:T(8,128)(2,1)} %get-tuple-element.310), channel_id=1, source_target_pairs={{0,4},{2,6},{4,12},{6,14},{8,0},{10,2},{12,20},{14,22},{16,8},{18,... | collective-permute-start | bytes 1523720 | tf_op jit(solution)/shard_map/sum_b_down_2/ppermute | solution.py:65
  142.0 58.4 %collective-permute-start.37 = (bf16[128,1024]{1,0:T(8,128)(2,1)}, bf16[128,1024]{1,0:T(8,128)(2,1)}, u32[]{:S(2)}, u32[]{:S(2)}) collective-permute-start(bf16[128,1024]{1,0:T(8,128)(2,1)} %constant_dynamic-slice_fusion.1), channel_id=1, source_target_pairs={{0,1},{1,0},{2,3},{3,2},{4,5},{5,4},{6,7},{7,6},{8,9},{9,8},{10,11... | collective-permute-start | bytes 786440 | tf_op jit(solution)/shard_map/ppermute | solution.py:32
  153.9 4.2 %collective-permute-start.49 = (bf16[3,64,2176]{2,1,0:T(8,128)(2,1)}, bf16[3,64,2176]{2,1,0:T(8,128)(2,1)S(1)}, u32[]{:S(2)}, u32[]{:S(2)}) collective-permute-start(bf16[3,64,2176]{2,1,0:T(8,128)(2,1)} %get-tuple-element.322), channel_id=1, source_target_pairs={{0,2},{2,0},{4,6},{6,4},{8,10},{10,8},{12,14},{14,12},{16,18},{18,... | collective-permute-start | bytes 2506760 | tf_op jit(solution)/shard_map/sum_a_cores_early/ppermute | solution.py:65
  156.0 14.4 %collective-permute-start.54 = (bf16[64,3968]{1,0:T(8,128)(2,1)S(1)}, bf16[64,3968]{1,0:T(8,128)(2,1)S(1)}, u32[]{:S(2)}, u32[]{:S(2)}) collective-permute-start(bf16[64,3968]{1,0:T(8,128)(2,1)S(1)} %get-tuple-element.335), channel_id=1, source_target_pairs={{0,8},{2,10},{4,0},{6,2},{8,16},{10,18},{12,4},{14,6},{16,24},{18,... | collective-permute-start | bytes 1523720 | tf_op jit(solution)/shard_map/sum_b_up_3/ppermute | solution.py:65
  156.4 15.7 %collective-permute-start.55 = (bf16[64,3968]{1,0:T(8,128)(2,1)S(1)}, bf16[64,3968]{1,0:T(8,128)(2,1)S(1)}, u32[]{:S(2)}, u32[]{:S(2)}) collective-permute-start(bf16[64,3968]{1,0:T(8,128)(2,1)S(1)} %get-tuple-element.336), channel_id=1, source_target_pairs={{0,4},{2,6},{4,12},{6,14},{8,0},{10,2},{12,20},{14,22},{16,8},{18,... | collective-permute-start | bytes 1523720 | tf_op jit(solution)/shard_map/sum_b_down_3/ppermute | solution.py:65
  158.2 14.8 %collective-permute-start.50 = (bf16[32,2176]{1,0:T(8,128)(2,1)S(1)}, bf16[32,2176]{1,0:T(8,128)(2,1)S(1)}, u32[]{:S(2)}, u32[]{:S(2)}) collective-permute-start(bf16[32,2176]{1,0:T(8,128)(2,1)S(1)} %get-tuple-element.323), channel_id=1, source_target_pairs={{0,8},{2,10},{4,0},{6,2},{8,16},{10,18},{12,4},{14,6},{16,24},{18,... | collective-permute-start | bytes 417800 | tf_op jit(solution)/shard_map/sum_a_up_1/ppermute | solution.py:65
  158.6 14.4 %collective-permute-start.51 = (bf16[32,2176]{1,0:T(8,128)(2,1)S(1)}, bf16[32,2176]{1,0:T(8,128)(2,1)S(1)}, u32[]{:S(2)}, u32[]{:S(2)}) collective-permute-start(bf16[32,2176]{1,0:T(8,128)(2,1)S(1)} %get-tuple-element.324), channel_id=1, source_target_pairs={{0,4},{2,6},{4,12},{6,14},{8,0},{10,2},{12,20},{14,22},{16,8},{18,... | collective-permute-start | bytes 417800 | tf_op jit(solution)/shard_map/sum_a_down_1/ppermute | solution.py:65
  170.4 11.8 %collective-permute-start.48 = (bf16[128,1024]{1,0:T(8,128)(2,1)S(1)}, bf16[128,1024]{1,0:T(8,128)(2,1)S(1)}, u32[]{:S(2)}, u32[]{:S(2)}) collective-permute-start(bf16[128,1024]{1,0:T(8,128)(2,1)S(1)} %constant_dynamic-slice_fusion), channel_id=1, source_target_pairs={{0,1},{1,0},{2,3},{3,2},{4,5},{5,4},{6,7},{7,6},{8,9},{9,8},{10,11... | collective-permute-start | bytes 786440 | tf_op jit(solution)/shard_map/ppermute | solution.py:32
  172.1 9.9 %collective-permute-start.47 = (bf16[5,64,2176]{2,1,0:T(8,128)(2,1)}, bf16[5,64,2176]{2,1,0:T(8,128)(2,1)S(1)}, u32[]{:S(2)}, u32[]{:S(2)}) collective-permute-start(bf16[5,64,2176]{2,1,0:T(8,128)(2,1)} %get-tuple-element.319), channel_id=1, source_target_pairs={{0,2},{2,0},{4,6},{6,4},{8,10},{10,8},{12,14},{14,12},{16,18},{18,... | collective-permute-start | bytes 4177928 | tf_op jit(solution)/shard_map/sum_a_cores_rest/ppermute | solution.py:65
  173.2 8.2 %collective-permute-start.52 = (bf16[64,2176]{1,0:T(8,128)(2,1)S(1)}, bf16[64,2176]{1,0:T(8,128)(2,1)S(1)}, u32[]{:S(2)}, u32[]{:S(2)}) collective-permute-start(bf16[64,2176]{1,0:T(8,128)(2,1)S(1)} %get-tuple-element.327), channel_id=1, source_target_pairs={{0,8},{2,10},{4,0},{6,2},{8,16},{10,18},{12,4},{14,6},{16,24},{18,... | collective-permute-start | bytes 835592 | tf_op jit(solution)/shard_map/sum_a_up_2/ppermute | solution.py:65
  174.4 7.6 %collective-permute-start.53 = (bf16[64,2176]{1,0:T(8,128)(2,1)S(1)}, bf16[64,2176]{1,0:T(8,128)(2,1)S(1)}, u32[]{:S(2)}, u32[]{:S(2)}) collective-permute-start(bf16[64,2176]{1,0:T(8,128)(2,1)S(1)} %get-tuple-element.328), channel_id=1, source_target_pairs={{0,4},{2,6},{4,12},{6,14},{8,0},{10,2},{12,20},{14,22},{16,8},{18,... | collective-permute-start | bytes 835592 | tf_op jit(solution)/shard_map/sum_a_down_2/ppermute | solution.py:65
  182.2 23.0 %collective-permute-start.60 = (bf16[64,3968]{1,0:T(8,128)(2,1)S(1)}, bf16[64,3968]{1,0:T(8,128)(2,1)S(1)}, u32[]{:S(2)}, u32[]{:S(2)}) collective-permute-start(bf16[64,3968]{1,0:T(8,128)(2,1)S(1)} %get-tuple-element.354), channel_id=1, source_target_pairs={{0,8},{2,10},{4,0},{6,2},{8,16},{10,18},{12,4},{14,6},{16,24},{18,... | collective-permute-start | bytes 1523720 | tf_op jit(solution)/shard_map/sum_b_up_4/ppermute | solution.py:65
  183.0 22.2 %collective-permute-start.61 = (bf16[64,3968]{1,0:T(8,128)(2,1)S(1)}, bf16[64,3968]{1,0:T(8,128)(2,1)S(1)}, u32[]{:S(2)}, u32[]{:S(2)}) collective-permute-start(bf16[64,3968]{1,0:T(8,128)(2,1)S(1)} %get-tuple-element.355), channel_id=1, source_target_pairs={{0,4},{2,6},{4,12},{6,14},{8,0},{10,2},{12,20},{14,22},{16,8},{18,... | collective-permute-start | bytes 1523720 | tf_op jit(solution)/shard_map/sum_b_down_4/ppermute | solution.py:65
  184.3 15.5 %collective-permute-start.56 = (bf16[64,2176]{1,0:T(8,128)(2,1)S(1)}, bf16[64,2176]{1,0:T(8,128)(2,1)S(1)}, u32[]{:S(2)}, u32[]{:S(2)}) collective-permute-start(bf16[64,2176]{1,0:T(8,128)(2,1)S(1)} %get-tuple-element.341), channel_id=1, source_target_pairs={{0,8},{2,10},{4,0},{6,2},{8,16},{10,18},{12,4},{14,6},{16,24},{18,... | collective-permute-start | bytes 835592 | tf_op jit(solution)/shard_map/sum_a_up_3/ppermute | solution.py:65
  185.0 15.1 %collective-permute-start.57 = (bf16[64,2176]{1,0:T(8,128)(2,1)S(1)}, bf16[64,2176]{1,0:T(8,128)(2,1)S(1)}, u32[]{:S(2)}, u32[]{:S(2)}) collective-permute-start(bf16[64,2176]{1,0:T(8,128)(2,1)S(1)} %get-tuple-element.342), channel_id=1, source_target_pairs={{0,4},{2,6},{4,12},{6,14},{8,0},{10,2},{12,20},{14,22},{16,8},{18,... | collective-permute-start | bytes 835592 | tf_op jit(solution)/shard_map/sum_a_down_3/ppermute | solution.py:65
  200.4 6.6 %collective-permute-start.58 = (bf16[64,2176]{1,0:T(8,128)(2,1)S(1)}, bf16[64,2176]{1,0:T(8,128)(2,1)S(1)}, u32[]{:S(2)}, u32[]{:S(2)}) collective-permute-start(bf16[64,2176]{1,0:T(8,128)(2,1)S(1)} %get-tuple-element.350), channel_id=1, source_target_pairs={{0,8},{2,10},{4,0},{6,2},{8,16},{10,18},{12,4},{14,6},{16,24},{18,... | collective-permute-start | bytes 835592 | tf_op jit(solution)/shard_map/sum_a_up_4/ppermute | solution.py:65
  201.0 6.5 %collective-permute-start.59 = (bf16[64,2176]{1,0:T(8,128)(2,1)S(1)}, bf16[64,2176]{1,0:T(8,128)(2,1)S(1)}, u32[]{:S(2)}, u32[]{:S(2)}) collective-permute-start(bf16[64,2176]{1,0:T(8,128)(2,1)S(1)} %get-tuple-element.351), channel_id=1, source_target_pairs={{0,4},{2,6},{4,12},{6,14},{8,0},{10,2},{12,20},{14,22},{16,8},{18,... | collective-permute-start | bytes 835592 | tf_op jit(solution)/shard_map/sum_a_down_4/ppermute | solution.py:65
  210.0 5.3 %collective-permute-start.62 = (f32[64]{0:T(128)S(1)}, f32[64]{0:T(128)S(1)}, u32[]{:S(2)}, u32[]{:S(2)}) collective-permute-start(f32[64]{0:T(128)S(1)} %get-tuple-element.391), channel_id=1, source_target_pairs={{0,1},{1,0},{2,3},{3,2},{4,5},{5,4},{6,7},{7,6},{8,9},{9,8},{10,11... | collective-permute-start | bytes 776 | tf_op jit(solution)/shard_map/ppermute | solution.py:32
  (66 other events, 504.3 us)

commit v5 on v4

--- a/solution.py
+++ b/solution.py
@@ -633,6 +633,7 @@
     inputs = tokens_all, tokens_before, tokens_after, cot_all, seq, cosine, sine, chips, core
     inputs = steps_a.hold(inputs)
     tokens_all, tokens_before, tokens_after, cot_all, seq, cosine, sine, chips, core = inputs
+    steps_a.step()
     steps_a.beside(steps_b)
     pieces, starts = steps_a.finish()
     count = len(pieces)
@@ -741,7 +742,8 @@
         moved=16 * MIB,
         room=60,
     )
-    grad_qkv, grad_one, gain_columns, *early_a = steps_b.ride(tuple(last))
+    last, down_other = steps_b.ride((tuple(last), down_other))
+    grad_qkv, grad_one, gain_columns, *early_a = last
     one_other = pair_swap(other_rows(grad_one, row_count))
     grad_qkv = steps_b.ride(grad_qkv)
     factors = work_one, grad_qkv, grad_low, context, gain_columns
@@ -751,14 +753,12 @@
     else:
         steps_a = Stepped(summed_terms(*factors))
     steps_a.step()
+    steps_a.beside(steps_b)
+    steps_b.step()
+    steps_a.step()
+    one_other = steps_a.hold(one_other)
     steps_a.step()
     steps_a.step()
-    steps_a.step()
-    steps_b.step()
-    one_other = steps_a.hold(one_other)
-    steps_a.beside(steps_b)
-    steps_a.step()
-    down_other = steps_a.hold(down_other)
     steps_a.step()
     steps_a.beside(steps_b)
     share_b = steps_b.finish()

time: 217 us -> 212 us (0.977)
  waiting for transfers between devices: 78 us -> 73.5 us
    ppermute x54, waiting for transfers between devices: 75 us -> 69.6 us  [go(): return lax.ppermute(block, SEQ, route)]
  transfers between devices with their start and end apart: 63 -> 63, of which waited for: 29 -> 31; matrix products, arithmetic and copies ran while one was open for 13% -> 13% of each run, Pallas kernels for 15% -> 16%
where the time goes in v5:
time: 212 us; the launch traced here: 211 us
  waiting for transfers between devices  73.5 us (35%)
  starting transfers between devices  53.8 us (25%)
  Pallas kernels  46.2 us (22%)
  other arithmetic  23.1 us (11%)
  local copies, waits for them, and re-layouts  13 us (6%)
    ppermute x54, waiting for transfers between devices, go(): return lax.ppermute(block, SEQ, route)  69.6 us
    ppermute x54, starting transfers between devices, go(): return lax.ppermute(block, SEQ, route)  43 us
    pallas_call x4, Pallas kernels, call(): pl.pallas_call(kernel, in_specs=specs, out_specs=[VMEM] * len(outs), out_...  35 us
    pallas_call x2, Pallas kernels, weight_terms(): pl.pallas_call(functools.partial(weight_kernel, tail), grid_spec=pltpu.Pr...  11.1 us
    ppermute x6, starting transfers between devices, pair_swap(): return lax.ppermute(block, PAIR, [(0, 1), (1, 0)])  6.65 us
    convert_element_type x6, other arithmetic, scatter_sum(): downward = (at(self.half + step) + downward).astype(BF16)  6.6 us
  transfers between devices with their start and end apart: 63, of which 31 were waited for; matrix products, arithmetic and copies ran while one was open for 13% of the time, Pallas kernels for 16%

profile of v5, /device:TPU:0, one launch (start us, length us, event | category | flops | bytes accessed | tf_op | source)
XLA Modules:
  0.0 211.2 jit_solution(13560620313303312642)
XLA Ops:
  0.7 1.0 copy.48
  3.3 3.1 %collective-permute-start.1 = (bf16[64,2176]{1,0:T(8,128)(2,1)S(1)}, bf16[64,2176]{1,0:T(8,128)(2,1)}, u32[]{:S(2)}, u32[]{:S(2)}) collective-permute-start(bf16[64,2176]{1,0:T(8,128)(2,1)S(1)} %fusion.26.refs_0_), channel_id=1, source_target_pairs={{0,8},{2,10},{4,0},{6,2},{8,16},{10,18},{12,4},{14,6},{16,24},{18,... | collective-permute-start | bytes 835592 | tf_op jit(solution)/shard_map/gather_a_up_1/ppermute | solution.py:65
  7.4 1.3 collective-permute-start
  8.7 1.2 dynamic_slice.21
  10.0 1.3 compare_select_fusion.1
  14.6 3.6 %collective-permute-start.5 = (bf16[64,2176]{1,0:T(8,128)(2,1)}, bf16[64,2176]{1,0:T(8,128)(2,1)}, u32[]{:S(2)}, u32[]{:S(2)}) collective-permute-start(bf16[64,2176]{1,0:T(8,128)(2,1)} %collective-permute-done.1.refs_1_), channel_id=1, source_target_pairs={{0,8},{2,10},{4,0},{6,2},{8,16},{10,18},{12,4},{14,6},{16,24},{18,... | collective-permute-start | bytes 835592 | tf_op jit(solution)/shard_map/gather_a_up_2/ppermute | solution.py:65
  18.8 1.3 collective-permute-start.4
  20.4 4.0 %collective-permute-done.5.refs_3_ = bf16[64,2176]{1,0:T(8,128)(2,1)} collective-permute-done((bf16[64,2176]{1,0:T(8,128)(2,1)}, bf16[64,2176]{1,0:T(8,128)(2,1)}, u32[]{:S(2)}, u32[]{:S(2)}) %collective-permute-start.5) | collective-permute-done | bytes 278560 | tf_op jit(solution)/shard_map/gather_a_up_2/ppermute | solution.py:65
  24.4 3.2 %collective-permute-done.6.refs_4_ = bf16[64,2176]{1,0:T(8,128)(2,1)} collective-permute-done((bf16[64,2176]{1,0:T(8,128)(2,1)}, bf16[64,2176]{1,0:T(8,128)(2,1)}, u32[]{:S(2)}, u32[]{:S(2)}) %collective-permute-start.6) | collective-permute-done | bytes 278560 | tf_op jit(solution)/shard_map/gather_a_down_2/ppermute | solution.py:65
  27.9 1.7 collective-permute-start.9
  30.2 1.2 gather_fusion.1
  31.4 1.5 multiply_sine_fusion
  32.9 1.6 collective-permute-start.14
  34.9 1.3 collective-permute-done.10.refs_6_
  36.2 1.5 collective-permute-done.9.refs_5_
  40.1 1.8 collective-permute-start.11
  42.3 6.4 %collective-permute-done.14.refs_1_ = bf16[64,3968]{1,0:T(8,128)(2,1)} collective-permute-done((bf16[64,3968]{1,0:T(8,128)(2,1)S(1)}, bf16[64,3968]{1,0:T(8,128)(2,1)}, u32[]{:S(2)}, u32[]{:S(2)}) %collective-permute-start.14) | collective-permute-done | bytes 507936 | tf_op jit(solution)/shard_map/gather_b_up_1/ppermute | solution.py:65
  48.7 1.5 collective-permute-done.11.refs_7_
  50.8 1.5 collective-permute-start.21
  54.1 8.4 %shard_map.224 = (bf16[1024,2176]{1,0:T(8,128)(2,1)}, bf16[1024,512]{1,0:T(8,128)(2,1)}, f32[8,1024]{1,0:T(8,128)}, bf16[256,1024]{1,0:T(8,128)(2,1)}, bf16[256,...) custom-call(s32[18]{0:T(128)} %multiply_add_fusion.starts, ...), custom_call_target="tpu_custom_call" | custom-call | flops 805306368 | bytes 16777216 | tf_op jit(solution)/shard_map/pallas_call | solution.py:183
  62.5 2.5 %collective-permute-done.21.refs_3_ = bf16[64,3968]{1,0:T(8,128)(2,1)S(1)} collective-permute-done((bf16[64,3968]{1,0:T(8,128)(2,1)}, bf16[64,3968]{1,0:T(8,128)(2,1)S(1)}, u32[]{:S(2)}, u32[]{:S(2)}) %collective-permute-start.21) | collective-permute-done | bytes 507936 | tf_op jit(solution)/shard_map/gather_b_up_2/ppermute | solution.py:65
  65.0 1.3 collective-permute-done.22.refs_4_
  66.5 1.6 collective-permute-start.24
  69.0 10.0 %collective-permute-done.24.refs_5_ = bf16[64,3968]{1,0:T(8,128)(2,1)S(1)} collective-permute-done((bf16[64,3968]{1,0:T(8,128)(2,1)S(1)}, bf16[64,3968]{1,0:T(8,128)(2,1)S(1)}, u32[]{:S(2)}, u32[]{:S(2)}) %collective-permute-start.24) | collective-permute-done | bytes 507936 | tf_op jit(solution)/shard_map/gather_b_up_3/ppermute | solution.py:65
  79.1 1.3 collective-permute-done.25.refs_6_
  80.4 1.7 collective-permute-start.29
  83.2 3.5 %collective-permute-done.29.refs_7_ = bf16[32,3968]{1,0:T(8,128)(2,1)S(1)} collective-permute-done((bf16[32,3968]{1,0:T(8,128)(2,1)S(1)}, bf16[32,3968]{1,0:T(8,128)(2,1)S(1)}, u32[]{:S(2)}, u32[]{:S(2)}) %collective-permute-start.29) | collective-permute-done | bytes 253984 | tf_op jit(solution)/shard_map/gather_b_up_4/ppermute | solution.py:65
  86.7 1.9 collective-permute-done.30.refs_8_
  89.1 1.0 collective-permute-done.35.refs_16_
  92.3 12.8 %shard_map.225 = (f32[256,1024]{1,0:T(8,128)}, bf16[256,1024]{1,0:T(8,128)(2,1)}, bf16[256,1408]{1,0:T(8,128)(2,1)}, bf16[256,2688]{1,0:T(8,128)(2,1)}, bf16[256...) custom-call(s32[18]{0:T(128)} %multiply_add_fusion.starts, ...), custom_call_target="tpu_custom_call" | custom-call | flops 4127195136 | bytes 33554432 | tf_op jit(solution)/shard_map/pallas_call | solution.py:183
  105.4 1.8 collective-permute-start.38
  107.2 7.0 %shard_map.226 = (bf16[5,64,3968]{2,1,0:T(8,128)(2,1)}, bf16[5,64,3968]{2,1,0:T(8,128)(2,1)}) custom-call(s32[8]{0:T(128)} %gather_fusion.1, s32[1]{0:T(128)} %bitcast.8.core, bf16[256,1024]{1,0:T(8,128)(2,1)} %get-tuple-element.268.left_one, bf16[256,1024]{1,0:T(8,128)(2,1)} %pad_maximum_fusion.3.cot.left_two, ...), custom_call_target="tpu_custom_call" | custom-call | flops 1300234240 | bytes 7110656 | tf_op jit(solution)/shard_map/pallas_call | solution.py:501
  114.4 1.4 add_convert_fusion
  116.7 1.3 collective-permute-start.40
  118.0 1.9 collective-permute-done.38.grad_two_other
  120.0 7.0 %shard_map.227 = (f32[256,1024]{1,0:T(8,128)}, bf16[256,1024]{1,0:T(8,128)(2,1)}, f32[8,1024]{1,0:T(8,128)S(1)}, bf16[256,512]{1,0:T(8,128)(2,1)S(1)}, f32[256,1...) custom-call(s32[2]{0:T(128)S(1)} %copy-done.16, f32[256,1024]{1,0:T(8,128)S(1)} %copy-done, ...), custom_call_target="tpu_custom_call" | custom-call | flops 536870912 | bytes 25165824 | tf_op jit(solution)/shard_map/pallas_call | solution.py:183
  127.0 1.6 collective-permute-start.41
  128.6 1.3 collective-permute-start.42
  129.9 2.5 %fusion.5 = (bf16[64,3968]{1,0:T(8,128)(2,1)}, bf16[64,3968]{1,0:T(8,128)(2,1)}) fusion(bf16[3,64,3968]{2,1,0:T(8,128)(2,1)} %collective-permute-done.37, bf16[32,3968]{1,0:T(8,128)(2,1)S(1)} %collective-permute-done.40, bf16[3,64,3968]{2,1,0:T(8,128)(2,1)S(1)} %copy-done.22, bf16[32,3968]{1,0:T(8,128)(2,1)S(1)} %collective-permute-done.39), kind=kLoop, calls=%fused_computation.13 | loop fusion | flops 3047424 | bytes 3555328 | tf_op jit(solution)/shard_map/convert_element_type | solution.py:128
  132.5 5.6 %collective-permute-start.44 = (bf16[64,3968]{1,0:T(8,128)(2,1)}, bf16[64,3968]{1,0:T(8,128)(2,1)}, u32[]{:S(2)}, u32[]{:S(2)}) collective-permute-start(bf16[64,3968]{1,0:T(8,128)(2,1)} %get-tuple-element.309), channel_id=1, source_target_pairs={{0,8},{2,10},{4,0},{6,2},{8,16},{10,18},{12,4},{14,6},{16,24},{18,... | collective-permute-start | bytes 1523720 | tf_op jit(solution)/shard_map/sum_b_up_2/ppermute | solution.py:65
  139.8 6.9 %shard_map.228 = (bf16[256,1536]{1,0:T(8,128)(2,1)}, bf16[256,1024]{1,0:T(8,128)(2,1)}, bf16[1024,128]{1,0:T(8,128)(2,1)}, bf16[3,64,2176]{2,1,0:T(8,128)(2,1)}, bf16[3,64,2176]{2,1,0:T(8,128)(2,1)}) custom-call(s32[8]{0:T(128)} %gather_fusion.1, s32[1]{0:T(128)} %bitcast.8.core, bf16[256,512]{1,0:T(8,128)(2,1)} %copy-done.11, f32[256,1024]{1,0:T(8,128)} %copy-done.2, ...), custom_call_target="tpu_custom_call" | custom-call | flops 805306368 | bytes 16777216 | tf_op jit(solution)/shard_map/pallas_call | solution.py:183
  146.7 1.4 collective-permute-done.43
  148.7 2.2 %collective-permute-done.45 = bf16[64,3968]{1,0:T(8,128)(2,1)} collective-permute-done((bf16[64,3968]{1,0:T(8,128)(2,1)}, bf16[64,3968]{1,0:T(8,128)(2,1)}, u32[]{:S(2)}, u32[]{:S(2)}) %collective-permute-start.45) | collective-permute-done | bytes 507936 | tf_op jit(solution)/shard_map/sum_b_down_2/ppermute | solution.py:65
  152.8 1.9 fusion.3
  155.4 1.5 collective-permute-start.52
  157.6 1.5 collective-permute-start.49
  159.9 4.1 %shard_map.229 = (bf16[5,64,2176]{2,1,0:T(8,128)(2,1)}, bf16[5,64,2176]{2,1,0:T(8,128)(2,1)}) custom-call(s32[8]{0:T(128)S(1)} %copy-done.15, s32[1]{0:T(128)} %bitcast.8.core, bf16[256,1024]{1,0:T(8,128)(2,1)S(1)} %copy-done.7, bf16[256,1024]{1,0:T(8,128)(2,1)S(1)} %copy-done.8, bf16[256,1536]{1,0:T(8,128)(2,1)S(1)} %copy-done.17, ...), custom_call_target="tpu_custom_call" | custom-call | flops 713031680 | bytes 3899392 | tf_op jit(solution)/shard_map/pallas_call | solution.py:501
  164.0 5.2 %collective-permute-done.51 = bf16[64,3968]{1,0:T(8,128)(2,1)S(1)} collective-permute-done((bf16[64,3968]{1,0:T(8,128)(2,1)S(1)}, bf16[64,3968]{1,0:T(8,128)(2,1)S(1)}, u32[]{:S(2)}, u32[]{:S(2)}) %collective-permute-start.51) | collective-permute-done | bytes 507936 | tf_op jit(solution)/shard_map/sum_b_up_3/ppermute | solution.py:65
  169.8 1.7 collective-permute-done.48
  172.0 1.1 collective-permute-start.53
  173.1 1.0 collective-permute-start.54
  174.1 1.6 fusion.1
  175.7 1.1 collective-permute-start.58
  176.7 1.0 collective-permute-start.59
  177.8 3.9 %collective-permute-done.53 = bf16[64,2176]{1,0:T(8,128)(2,1)S(1)} collective-permute-done((bf16[64,2176]{1,0:T(8,128)(2,1)S(1)}, bf16[64,2176]{1,0:T(8,128)(2,1)S(1)}, u32[]{:S(2)}, u32[]{:S(2)}) %collective-permute-start.53) | collective-permute-done | bytes 278560 | tf_op jit(solution)/shard_map/sum_a_up_2/ppermute | solution.py:65
  181.7 1.0 collective-permute-done.54
  184.0 1.2 collective-permute-start.57
  185.3 1.0 fusion.23
  186.3 10.4 %collective-permute-done.56 = bf16[64,2176]{1,0:T(8,128)(2,1)S(1)} collective-permute-done((bf16[64,2176]{1,0:T(8,128)(2,1)S(1)}, bf16[64,2176]{1,0:T(8,128)(2,1)S(1)}, u32[]{:S(2)}, u32[]{:S(2)}) %collective-permute-start.56) | collective-permute-done | bytes 278560 | tf_op jit(solution)/shard_map/sum_a_up_3/ppermute | solution.py:65
  197.6 1.3 fusion
  199.6 1.4 collective-permute-start.61
  201.2 1.4 copy.44
  203.4 2.2 %collective-permute-done.60 = bf16[64,2176]{1,0:T(8,128)(2,1)S(1)} collective-permute-done((bf16[64,2176]{1,0:T(8,128)(2,1)S(1)}, bf16[64,2176]{1,0:T(8,128)(2,1)S(1)}, u32[]{:S(2)}, u32[]{:S(2)}) %collective-permute-start.60) | collective-permute-done | bytes 278560 | tf_op jit(solution)/shard_map/sum_a_up_4/ppermute | solution.py:65
  207.1 1.6 collective-permute-start.62
  (267 shorter events, 34.8 us)
Async XLA Ops:
  3.3 10.6 %collective-permute-start.1 = (bf16[64,2176]{1,0:T(8,128)(2,1)S(1)}, bf16[64,2176]{1,0:T(8,128)(2,1)}, u32[]{:S(2)}, u32[]{:S(2)}) collective-permute-start(bf16[64,2176]{1,0:T(8,128)(2,1)S(1)} %fusion.26.refs_0_), channel_id=1, source_target_pairs={{0,8},{2,10},{4,0},{6,2},{8,16},{10,18},{12,4},{14,6},{16,24},{18,... | collective-permute-start | bytes 835592 | tf_op jit(solution)/shard_map/gather_a_up_1/ppermute | solution.py:65
  6.4 8.2 %collective-permute-start.2 = (bf16[64,2176]{1,0:T(8,128)(2,1)S(1)}, bf16[64,2176]{1,0:T(8,128)(2,1)}, u32[]{:S(2)}, u32[]{:S(2)}) collective-permute-start(bf16[64,2176]{1,0:T(8,128)(2,1)S(1)} %fusion.26.refs_0_), channel_id=1, source_target_pairs={{0,4},{2,6},{4,12},{6,14},{8,0},{10,2},{12,20},{14,22},{16,8},{18,... | collective-permute-start | bytes 835592 | tf_op jit(solution)/shard_map/gather_a_down_1/ppermute | solution.py:65
  6.4 8.2 %collective-permute-start.3 = (bf16[64,2176]{1,0:T(8,128)(2,1)S(1)}, bf16[64,2176]{1,0:T(8,128)(2,1)S(1)}, u32[]{:S(2)}, u32[]{:S(2)}) collective-permute-start(bf16[64,2176]{1,0:T(8,128)(2,1)S(1)} %fusion.26.refs_0_), channel_id=1, source_target_pairs={{0,2},{2,0},{4,6},{6,4},{8,10},{10,8},{12,14},{14,12},{16,18},{18,... | collective-permute-start | bytes 835592 | tf_op jit(solution)/shard_map/gather_a_cores_0/ppermute | solution.py:65
  7.4 6.5 %collective-permute-start = (bf16[64,1024]{1,0:T(8,128)(2,1)S(1)}, bf16[64,1024]{1,0:T(8,128)(2,1)S(1)}, u32[]{:S(2)}, u32[]{:S(2)}) collective-permute-start(bf16[64,1024]{1,0:T(8,128)(2,1)S(1)} %slice_select_fusion), channel_id=1, source_target_pairs={{2,0},{4,2},{6,4},{8,6},{10,8},{12,10},{14,12},{16,14},{18,16},{20... | collective-permute-start | bytes 393224 | tf_op jit(solution)/shard_map/ppermute | solution.py:571
  14.6 9.8 %collective-permute-start.5 = (bf16[64,2176]{1,0:T(8,128)(2,1)}, bf16[64,2176]{1,0:T(8,128)(2,1)}, u32[]{:S(2)}, u32[]{:S(2)}) collective-permute-start(bf16[64,2176]{1,0:T(8,128)(2,1)} %collective-permute-done.1.refs_1_), channel_id=1, source_target_pairs={{0,8},{2,10},{4,0},{6,2},{8,16},{10,18},{12,4},{14,6},{16,24},{18,... | collective-permute-start | bytes 835592 | tf_op jit(solution)/shard_map/gather_a_up_2/ppermute | solution.py:65
  18.2 9.4 %collective-permute-start.7 = (bf16[64,2176]{1,0:T(8,128)(2,1)}, bf16[64,2176]{1,0:T(8,128)(2,1)}, u32[]{:S(2)}, u32[]{:S(2)}) collective-permute-start(bf16[64,2176]{1,0:T(8,128)(2,1)} %collective-permute-done.1.refs_1_), channel_id=1, source_target_pairs={{0,2},{2,0},{4,6},{6,4},{8,10},{10,8},{12,14},{14,12},{16,18},{18,... | collective-permute-start | bytes 835592 | tf_op jit(solution)/shard_map/gather_a_cores_-1/ppermute | solution.py:65
  18.2 9.4 %collective-permute-start.6 = (bf16[64,2176]{1,0:T(8,128)(2,1)}, bf16[64,2176]{1,0:T(8,128)(2,1)}, u32[]{:S(2)}, u32[]{:S(2)}) collective-permute-start(bf16[64,2176]{1,0:T(8,128)(2,1)} %collective-permute-done.2.refs_2_), channel_id=1, source_target_pairs={{0,4},{2,6},{4,12},{6,14},{8,0},{10,2},{12,20},{14,22},{16,8},{18,... | collective-permute-start | bytes 835592 | tf_op jit(solution)/shard_map/gather_a_down_2/ppermute | solution.py:65
  18.2 9.4 %collective-permute-start.8 = (bf16[64,2176]{1,0:T(8,128)(2,1)}, bf16[64,2176]{1,0:T(8,128)(2,1)}, u32[]{:S(2)}, u32[]{:S(2)}) collective-permute-start(bf16[64,2176]{1,0:T(8,128)(2,1)} %collective-permute-done.2.refs_2_), channel_id=1, source_target_pairs={{0,2},{2,0},{4,6},{6,4},{8,10},{10,8},{12,14},{14,12},{16,18},{18,... | collective-permute-start | bytes 835592 | tf_op jit(solution)/shard_map/gather_a_cores_1/ppermute | solution.py:65
  18.8 18.9 %collective-permute-start.4 = (bf16[320,1024]{1,0:T(8,128)(2,1)S(1)}, bf16[320,1024]{1,0:T(8,128)(2,1)S(1)}, u32[]{:S(2)}, u32[]{:S(2)}) collective-permute-start(bf16[320,1024]{1,0:T(8,128)(2,1)S(1)} %pad_maximum_fusion.1), channel_id=1, source_target_pairs={{0,1},{1,0},{2,3},{3,2},{4,5},{5,4},{6,7},{7,6},{8,9},{9,8},{10,11... | collective-permute-start | bytes 1966088 | tf_op jit(solution)/shard_map/ppermute | solution.py:32
  20.4 32.5 %copy-start.33 = (bf16[64,3968]{1,0:T(8,128)(2,1)}, bf16[64,3968]{1,0:T(8,128)(2,1)S(1)}, u32[]{:S(2)}) copy-start(bf16[64,3968]{1,0:T(8,128)(2,1)S(1)} %pad.37.refs_0_) | copy-start | bytes 1523716
  27.6 8.6 %collective-permute-start.10 = (bf16[64,2176]{1,0:T(8,128)(2,1)}, bf16[64,2176]{1,0:T(8,128)(2,1)S(1)}, u32[]{:S(2)}, u32[]{:S(2)}) collective-permute-start(bf16[64,2176]{1,0:T(8,128)(2,1)} %collective-permute-done.6.refs_4_), channel_id=1, source_target_pairs={{0,4},{2,6},{4,12},{6,14},{8,0},{10,2},{12,20},{14,22},{16,8},{18,... | collective-permute-start | bytes 835592 | tf_op jit(solution)/shard_map/gather_a_down_3/ppermute | solution.py:65
  27.9 9.8 %collective-permute-start.9 = (bf16[64,2176]{1,0:T(8,128)(2,1)}, bf16[64,2176]{1,0:T(8,128)(2,1)S(1)}, u32[]{:S(2)}, u32[]{:S(2)}) collective-permute-start(bf16[64,2176]{1,0:T(8,128)(2,1)} %collective-permute-done.5.refs_3_), channel_id=1, source_target_pairs={{0,8},{2,10},{4,0},{6,2},{8,16},{10,18},{12,4},{14,6},{16,24},{18,... | collective-permute-start | bytes 835592 | tf_op jit(solution)/shard_map/gather_a_up_3/ppermute | solution.py:65
  32.9 15.8 %collective-permute-start.14 = (bf16[64,3968]{1,0:T(8,128)(2,1)S(1)}, bf16[64,3968]{1,0:T(8,128)(2,1)}, u32[]{:S(2)}, u32[]{:S(2)}) collective-permute-start(bf16[64,3968]{1,0:T(8,128)(2,1)S(1)} %pad.37.refs_0_), channel_id=1, source_target_pairs={{0,8},{2,10},{4,0},{6,2},{8,16},{10,18},{12,4},{14,6},{16,24},{18,... | collective-permute-start | bytes 1523720 | tf_op jit(solution)/shard_map/gather_b_up_1/ppermute | solution.py:65
  34.4 14.2 %collective-permute-start.15 = (bf16[64,3968]{1,0:T(8,128)(2,1)S(1)}, bf16[64,3968]{1,0:T(8,128)(2,1)}, u32[]{:S(2)}, u32[]{:S(2)}) collective-permute-start(bf16[64,3968]{1,0:T(8,128)(2,1)S(1)} %pad.37.refs_0_), channel_id=1, source_target_pairs={{0,4},{2,6},{4,12},{6,14},{8,0},{10,2},{12,20},{14,22},{16,8},{18,... | collective-permute-start | bytes 1523720 | tf_op jit(solution)/shard_map/gather_b_down_1/ppermute | solution.py:65
  36.2 6.1 %collective-permute-start.13 = (bf16[64,2176]{1,0:T(8,128)(2,1)}, bf16[64,2176]{1,0:T(8,128)(2,1)S(1)}, u32[]{:S(2)}, u32[]{:S(2)}) collective-permute-start(bf16[64,2176]{1,0:T(8,128)(2,1)} %collective-permute-done.5.refs_3_), channel_id=1, source_target_pairs={{0,2},{2,0},{4,6},{6,4},{8,10},{10,8},{12,14},{14,12},{16,18},{18,... | collective-permute-start | bytes 835592 | tf_op jit(solution)/shard_map/gather_a_cores_-2/ppermute | solution.py:65
  40.1 10.0 %collective-permute-start.11 = (bf16[32,2176]{1,0:T(8,128)(2,1)S(1)}, bf16[32,2176]{1,0:T(8,128)(2,1)S(1)}, u32[]{:S(2)}, u32[]{:S(2)}) collective-permute-start(bf16[32,2176]{1,0:T(8,128)(2,1)S(1)} %slice.223), channel_id=1, source_target_pairs={{0,8},{2,10},{4,0},{6,2},{8,16},{10,18},{12,4},{14,6},{16,24},{18,... | collective-permute-start | bytes 417800 | tf_op jit(solution)/shard_map/gather_a_up_4/ppermute | solution.py:65
  41.9 8.2 %collective-permute-start.12 = (bf16[32,2176]{1,0:T(8,128)(2,1)S(1)}, bf16[32,2176]{1,0:T(8,128)(2,1)S(1)}, u32[]{:S(2)}, u32[]{:S(2)}) collective-permute-start(bf16[32,2176]{1,0:T(8,128)(2,1)S(1)} %slice.224), channel_id=1, source_target_pairs={{0,4},{2,6},{4,12},{6,14},{8,0},{10,2},{12,20},{14,22},{16,8},{18,... | collective-permute-start | bytes 417800 | tf_op jit(solution)/shard_map/gather_a_down_4/ppermute | solution.py:65
  42.3 8.6 %collective-permute-start.16 = (bf16[64,2176]{1,0:T(8,128)(2,1)}, bf16[64,2176]{1,0:T(8,128)(2,1)S(1)}, u32[]{:S(2)}, u32[]{:S(2)}) collective-permute-start(bf16[64,2176]{1,0:T(8,128)(2,1)} %collective-permute-done.6.refs_4_), channel_id=1, source_target_pairs={{0,2},{2,0},{4,6},{6,4},{8,10},{10,8},{12,14},{14,12},{16,18},{18,... | collective-permute-start | bytes 835592 | tf_op jit(solution)/shard_map/gather_a_cores_2/ppermute | solution.py:65
  48.6 4.3 %collective-permute-start.17 = (bf16[64,2176]{1,0:T(8,128)(2,1)S(1)}, bf16[64,2176]{1,0:T(8,128)(2,1)S(1)}, u32[]{:S(2)}, u32[]{:S(2)}) collective-permute-start(bf16[64,2176]{1,0:T(8,128)(2,1)S(1)} %collective-permute-done.9.refs_5_), channel_id=1, source_target_pairs={{0,2},{2,0},{4,6},{6,4},{8,10},{10,8},{12,14},{14,12},{16,18},{18,... | collective-permute-start | bytes 835592 | tf_op jit(solution)/shard_map/gather_a_cores_-3/ppermute | solution.py:65
  50.2 2.2 %collective-permute-start.19 = (bf16[32,2176]{1,0:T(8,128)(2,1)S(1)}, bf16[32,2176]{1,0:T(8,128)(2,1)S(1)}, u32[]{:S(2)}, u32[]{:S(2)}) collective-permute-start(bf16[32,2176]{1,0:T(8,128)(2,1)S(1)} %collective-permute-done.11.refs_7_), channel_id=1, source_target_pairs={{0,2},{2,0},{4,6},{6,4},{8,10},{10,8},{12,14},{14,12},{16,18},{18,... | collective-permute-start | bytes 417800 | tf_op jit(solution)/shard_map/gather_a_cores_-4/ppermute | solution.py:65
  50.2 2.6 %collective-permute-start.20 = (bf16[32,2176]{1,0:T(8,128)(2,1)S(1)}, bf16[32,2176]{1,0:T(8,128)(2,1)S(1)}, u32[]{:S(2)}, u32[]{:S(2)}) collective-permute-start(bf16[32,2176]{1,0:T(8,128)(2,1)S(1)} %collective-permute-done.12.refs_8_), channel_id=1, source_target_pairs={{0,2},{2,0},{4,6},{6,4},{8,10},{10,8},{12,14},{14,12},{16,18},{18,... | collective-permute-start | bytes 417800 | tf_op jit(solution)/shard_map/gather_a_cores_4/ppermute | solution.py:65
  50.7 2.7 %collective-permute-start.18 = (bf16[64,2176]{1,0:T(8,128)(2,1)S(1)}, bf16[64,2176]{1,0:T(8,128)(2,1)S(1)}, u32[]{:S(2)}, u32[]{:S(2)}) collective-permute-start(bf16[64,2176]{1,0:T(8,128)(2,1)S(1)} %collective-permute-done.10.refs_6_), channel_id=1, source_target_pairs={{0,2},{2,0},{4,6},{6,4},{8,10},{10,8},{12,14},{14,12},{16,18},{18,... | collective-permute-start | bytes 835592 | tf_op jit(solution)/shard_map/gather_a_cores_3/ppermute | solution.py:65
  50.8 14.1 %collective-permute-start.21 = (bf16[64,3968]{1,0:T(8,128)(2,1)}, bf16[64,3968]{1,0:T(8,128)(2,1)S(1)}, u32[]{:S(2)}, u32[]{:S(2)}) collective-permute-start(bf16[64,3968]{1,0:T(8,128)(2,1)} %collective-permute-done.14.refs_1_), channel_id=1, source_target_pairs={{0,8},{2,10},{4,0},{6,2},{8,16},{10,18},{12,4},{14,6},{16,24},{18,... | collective-permute-start | bytes 1523720 | tf_op jit(solution)/shard_map/gather_b_up_2/ppermute | solution.py:65
  52.4 13.9 %collective-permute-start.22 = (bf16[64,3968]{1,0:T(8,128)(2,1)}, bf16[64,3968]{1,0:T(8,128)(2,1)S(1)}, u32[]{:S(2)}, u32[]{:S(2)}) collective-permute-start(bf16[64,3968]{1,0:T(8,128)(2,1)} %collective-permute-done.15.refs_2_), channel_id=1, source_target_pairs={{0,4},{2,6},{4,12},{6,14},{8,0},{10,2},{12,20},{14,22},{16,8},{18,... | collective-permute-start | bytes 1523720 | tf_op jit(solution)/shard_map/gather_b_down_2/ppermute | solution.py:65
  52.9 15.2 %collective-permute-start.26 = (bf16[64,3968]{1,0:T(8,128)(2,1)S(1)}, bf16[64,3968]{1,0:T(8,128)(2,1)}, u32[]{:S(2)}, u32[]{:S(2)}) collective-permute-start(bf16[64,3968]{1,0:T(8,128)(2,1)S(1)} %pad.37.refs_0_), channel_id=1, source_target_pairs={{0,2},{2,0},{4,6},{6,4},{8,10},{10,8},{12,14},{14,12},{16,18},{18,... | collective-permute-start | bytes 1523720 | tf_op jit(solution)/shard_map/gather_b_cores_0/ppermute | solution.py:65
  53.0 15.5 %collective-permute-start.27 = (bf16[64,3968]{1,0:T(8,128)(2,1)}, bf16[64,3968]{1,0:T(8,128)(2,1)}, u32[]{:S(2)}, u32[]{:S(2)}) collective-permute-start(bf16[64,3968]{1,0:T(8,128)(2,1)} %collective-permute-done.14.refs_1_), channel_id=1, source_target_pairs={{0,2},{2,0},{4,6},{6,4},{8,10},{10,8},{12,14},{14,12},{16,18},{18,... | collective-permute-start | bytes 1523720 | tf_op jit(solution)/shard_map/gather_b_cores_-1/ppermute | solution.py:65
  53.5 15.1 %collective-permute-start.28 = (bf16[64,3968]{1,0:T(8,128)(2,1)}, bf16[64,3968]{1,0:T(8,128)(2,1)}, u32[]{:S(2)}, u32[]{:S(2)}) collective-permute-start(bf16[64,3968]{1,0:T(8,128)(2,1)} %collective-permute-done.15.refs_2_), channel_id=1, source_target_pairs={{0,2},{2,0},{4,6},{6,4},{8,10},{10,8},{12,14},{14,12},{16,18},{18,... | collective-permute-start | bytes 1523720 | tf_op jit(solution)/shard_map/gather_b_cores_1/ppermute | solution.py:65
  66.2 14.1 %collective-permute-start.23 = (bf16[256,1024]{1,0:T(8,128)(2,1)}, bf16[256,1024]{1,0:T(8,128)(2,1)S(1)}, u32[]{:S(2)}, u32[]{:S(2)}) collective-permute-start(bf16[256,1024]{1,0:T(8,128)(2,1)} %get-tuple-element.236.term), channel_id=1, source_target_pairs={{0,1},{1,0},{2,3},{3,2},{4,5},{5,4},{6,7},{7,6},{8,9},{9,8},{10,11... | collective-permute-start | bytes 1572872 | tf_op jit(solution)/shard_map/ppermute | solution.py:32
  66.5 12.6 %collective-permute-start.24 = (bf16[64,3968]{1,0:T(8,128)(2,1)S(1)}, bf16[64,3968]{1,0:T(8,128)(2,1)S(1)}, u32[]{:S(2)}, u32[]{:S(2)}) collective-permute-start(bf16[64,3968]{1,0:T(8,128)(2,1)S(1)} %collective-permute-done.21.refs_3_), channel_id=1, source_target_pairs={{0,8},{2,10},{4,0},{6,2},{8,16},{10,18},{12,4},{14,6},{16,24},{18,... | collective-permute-start | bytes 1523720 | tf_op jit(solution)/shard_map/gather_b_up_3/ppermute | solution.py:65
  68.1 12.3 %collective-permute-start.25 = (bf16[64,3968]{1,0:T(8,128)(2,1)S(1)}, bf16[64,3968]{1,0:T(8,128)(2,1)S(1)}, u32[]{:S(2)}, u32[]{:S(2)}) collective-permute-start(bf16[64,3968]{1,0:T(8,128)(2,1)S(1)} %collective-permute-done.22.refs_4_), channel_id=1, source_target_pairs={{0,4},{2,6},{4,12},{6,14},{8,0},{10,2},{12,20},{14,22},{16,8},{18,... | collective-permute-start | bytes 1523720 | tf_op jit(solution)/shard_map/gather_b_down_3/ppermute | solution.py:65
  68.5 14.2 %collective-permute-start.31 = (bf16[64,3968]{1,0:T(8,128)(2,1)S(1)}, bf16[64,3968]{1,0:T(8,128)(2,1)S(1)}, u32[]{:S(2)}, u32[]{:S(2)}) collective-permute-start(bf16[64,3968]{1,0:T(8,128)(2,1)S(1)} %collective-permute-done.21.refs_3_), channel_id=1, source_target_pairs={{0,2},{2,0},{4,6},{6,4},{8,10},{10,8},{12,14},{14,12},{16,18},{18,... | collective-permute-start | bytes 1523720 | tf_op jit(solution)/shard_map/gather_b_cores_-2/ppermute | solution.py:65
  68.5 14.7 %collective-permute-start.32 = (bf16[64,3968]{1,0:T(8,128)(2,1)S(1)}, bf16[64,3968]{1,0:T(8,128)(2,1)S(1)}, u32[]{:S(2)}, u32[]{:S(2)}) collective-permute-start(bf16[64,3968]{1,0:T(8,128)(2,1)S(1)} %collective-permute-done.22.refs_4_), channel_id=1, source_target_pairs={{0,2},{2,0},{4,6},{6,4},{8,10},{10,8},{12,14},{14,12},{16,18},{18,... | collective-permute-start | bytes 1523720 | tf_op jit(solution)/shard_map/gather_b_cores_2/ppermute | solution.py:65
  80.4 6.3 %collective-permute-start.29 = (bf16[32,3968]{1,0:T(8,128)(2,1)S(1)}, bf16[32,3968]{1,0:T(8,128)(2,1)S(1)}, u32[]{:S(2)}, u32[]{:S(2)}) collective-permute-start(bf16[32,3968]{1,0:T(8,128)(2,1)S(1)} %slice.225), channel_id=1, source_target_pairs={{0,8},{2,10},{4,0},{6,2},{8,16},{10,18},{12,4},{14,6},{16,24},{18,... | collective-permute-start | bytes 761864 | tf_op jit(solution)/shard_map/gather_b_up_4/ppermute | solution.py:65
  82.1 6.5 %collective-permute-start.30 = (bf16[32,3968]{1,0:T(8,128)(2,1)S(1)}, bf16[32,3968]{1,0:T(8,128)(2,1)S(1)}, u32[]{:S(2)}, u32[]{:S(2)}) collective-permute-start(bf16[32,3968]{1,0:T(8,128)(2,1)S(1)} %slice.226), channel_id=1, source_target_pairs={{0,4},{2,6},{4,12},{6,14},{8,0},{10,2},{12,20},{14,22},{16,8},{18,... | collective-permute-start | bytes 761864 | tf_op jit(solution)/shard_map/gather_b_down_4/ppermute | solution.py:65
  82.7 7.8 %collective-permute-start.33 = (bf16[64,3968]{1,0:T(8,128)(2,1)S(1)}, bf16[64,3968]{1,0:T(8,128)(2,1)S(1)}, u32[]{:S(2)}, u32[]{:S(2)}) collective-permute-start(bf16[64,3968]{1,0:T(8,128)(2,1)S(1)} %collective-permute-done.24.refs_5_), channel_id=1, source_target_pairs={{0,2},{2,0},{4,6},{6,4},{8,10},{10,8},{12,14},{14,12},{16,18},{18,... | collective-permute-start | bytes 1523720 | tf_op jit(solution)/shard_map/gather_b_cores_-3/ppermute | solution.py:65
  82.7 7.8 %collective-permute-start.34 = (bf16[64,3968]{1,0:T(8,128)(2,1)S(1)}, bf16[64,3968]{1,0:T(8,128)(2,1)S(1)}, u32[]{:S(2)}, u32[]{:S(2)}) collective-permute-start(bf16[64,3968]{1,0:T(8,128)(2,1)S(1)} %collective-permute-done.25.refs_6_), channel_id=1, source_target_pairs={{0,2},{2,0},{4,6},{6,4},{8,10},{10,8},{12,14},{14,12},{16,18},{18,... | collective-permute-start | bytes 1523720 | tf_op jit(solution)/shard_map/gather_b_cores_3/ppermute | solution.py:65
  88.6 1.5 collective-permute-start.35
  88.6 1.9 collective-permute-start.36
  105.1 9.3 %collective-permute-start.37 = (bf16[3,64,3968]{2,1,0:T(8,128)(2,1)}, bf16[3,64,3968]{2,1,0:T(8,128)(2,1)}, u32[]{:S(2)}, u32[]{:S(2)}) collective-permute-start(bf16[3,64,3968]{2,1,0:T(8,128)(2,1)} %get-tuple-element.274), channel_id=1, source_target_pairs={{0,2},{2,0},{4,6},{6,4},{8,10},{10,8},{12,14},{14,12},{16,18},{18,... | collective-permute-start | bytes 4571144 | tf_op jit(solution)/shard_map/sum_b_cores_early/ppermute | solution.py:65
  105.4 14.5 %collective-permute-start.38 = (bf16[256,1024]{1,0:T(8,128)(2,1)}, bf16[256,1024]{1,0:T(8,128)(2,1)S(1)}, u32[]{:S(2)}, u32[]{:S(2)}) collective-permute-start(bf16[256,1024]{1,0:T(8,128)(2,1)} %get-tuple-element.275.grad_two), channel_id=1, source_target_pairs={{0,1},{1,0},{2,3},{3,2},{4,5},{5,4},{6,7},{7,6},{8,9},{9,8},{10,11... | collective-permute-start | bytes 1572872 | tf_op jit(solution)/shard_map/ppermute | solution.py:32
  114.3 38.6 %collective-permute-start.50 = (bf16[5,64,3968]{2,1,0:T(8,128)(2,1)}, bf16[5,64,3968]{2,1,0:T(8,128)(2,1)}, u32[]{:S(2)}, u32[]{:S(2)}) collective-permute-start(bf16[5,64,3968]{2,1,0:T(8,128)(2,1)} %get-tuple-element.272), channel_id=1, source_target_pairs={{0,2},{2,0},{4,6},{6,4},{8,10},{10,8},{12,14},{14,12},{16,18},{18,... | collective-permute-start | bytes 7618568 | tf_op jit(solution)/shard_map/sum_b_cores_rest/ppermute | solution.py:65
  115.9 11.0 %collective-permute-start.39 = (bf16[32,3968]{1,0:T(8,128)(2,1)S(1)}, bf16[32,3968]{1,0:T(8,128)(2,1)S(1)}, u32[]{:S(2)}, u32[]{:S(2)}) collective-permute-start(bf16[32,3968]{1,0:T(8,128)(2,1)S(1)} %get-tuple-element.287), channel_id=1, source_target_pairs={{0,8},{2,10},{4,0},{6,2},{8,16},{10,18},{12,4},{14,6},{16,24},{18,... | collective-permute-start | bytes 761864 | tf_op jit(solution)/shard_map/sum_b_up_1/ppermute | solution.py:65
  116.7 10.3 %collective-permute-start.40 = (bf16[32,3968]{1,0:T(8,128)(2,1)S(1)}, bf16[32,3968]{1,0:T(8,128)(2,1)S(1)}, u32[]{:S(2)}, u32[]{:S(2)}) collective-permute-start(bf16[32,3968]{1,0:T(8,128)(2,1)S(1)} %get-tuple-element.288), channel_id=1, source_target_pairs={{0,4},{2,6},{4,12},{6,14},{8,0},{10,2},{12,20},{14,22},{16,8},{18,... | collective-permute-start | bytes 761864 | tf_op jit(solution)/shard_map/sum_b_down_1/ppermute | solution.py:65
  127.0 5.4 %collective-permute-start.41 = (bf16[64,1024]{1,0:T(8,128)(2,1)}, bf16[64,1024]{1,0:T(8,128)(2,1)S(1)}, u32[]{:S(2)}, u32[]{:S(2)}) collective-permute-start(bf16[64,1024]{1,0:T(8,128)(2,1)} %get-tuple-element.289), channel_id=1, source_target_pairs={{0,2},{2,4},{4,6},{6,8},{8,10},{10,12},{12,14},{14,16},{16,18},{18... | collective-permute-start | bytes 393224 | tf_op jit(solution)/shard_map/ppermute | solution.py:28
  128.6 4.0 %collective-permute-start.42 = (bf16[64,1024]{1,0:T(8,128)(2,1)}, bf16[64,1024]{1,0:T(8,128)(2,1)S(1)}, u32[]{:S(2)}, u32[]{:S(2)}) collective-permute-start(bf16[64,1024]{1,0:T(8,128)(2,1)} %get-tuple-element.290), channel_id=1, source_target_pairs={{2,0},{4,2},{6,4},{8,6},{10,8},{12,10},{14,12},{16,14},{18,16},{20... | collective-permute-start | bytes 393224 | tf_op jit(solution)/shard_map/ppermute | solution.py:28
  132.5 16.2 %collective-permute-start.44 = (bf16[64,3968]{1,0:T(8,128)(2,1)}, bf16[64,3968]{1,0:T(8,128)(2,1)}, u32[]{:S(2)}, u32[]{:S(2)}) collective-permute-start(bf16[64,3968]{1,0:T(8,128)(2,1)} %get-tuple-element.309), channel_id=1, source_target_pairs={{0,8},{2,10},{4,0},{6,2},{8,16},{10,18},{12,4},{14,6},{16,24},{18,... | collective-permute-start | bytes 1523720 | tf_op jit(solution)/shard_map/sum_b_up_2/ppermute | solution.py:65
  138.1 12.8 %collective-permute-start.45 = (bf16[64,3968]{1,0:T(8,128)(2,1)}, bf16[64,3968]{1,0:T(8,128)(2,1)}, u32[]{:S(2)}, u32[]{:S(2)}) collective-permute-start(bf16[64,3968]{1,0:T(8,128)(2,1)} %get-tuple-element.310), channel_id=1, source_target_pairs={{0,4},{2,6},{4,12},{6,14},{8,0},{10,2},{12,20},{14,22},{16,8},{18,... | collective-permute-start | bytes 1523720 | tf_op jit(solution)/shard_map/sum_b_down_2/ppermute | solution.py:65
  139.0 9.1 %collective-permute-start.43 = (bf16[128,1024]{1,0:T(8,128)(2,1)}, bf16[128,1024]{1,0:T(8,128)(2,1)S(1)}, u32[]{:S(2)}, u32[]{:S(2)}) collective-permute-start(bf16[128,1024]{1,0:T(8,128)(2,1)} %constant_dynamic-slice_fusion.1), channel_id=1, source_target_pairs={{0,1},{1,0},{2,3},{3,2},{4,5},{5,4},{6,7},{7,6},{8,9},{9,8},{10,11... | collective-permute-start | bytes 786440 | tf_op jit(solution)/shard_map/ppermute | solution.py:32
  150.9 6.0 %collective-permute-start.47 = (bf16[3,64,2176]{2,1,0:T(8,128)(2,1)}, bf16[3,64,2176]{2,1,0:T(8,128)(2,1)S(1)}, u32[]{:S(2)}, u32[]{:S(2)}) collective-permute-start(bf16[3,64,2176]{2,1,0:T(8,128)(2,1)} %get-tuple-element.315), channel_id=1, source_target_pairs={{0,2},{2,0},{4,6},{6,4},{8,10},{10,8},{12,14},{14,12},{16,18},{18,... | collective-permute-start | bytes 2506760 | tf_op jit(solution)/shard_map/sum_a_cores_early/ppermute | solution.py:65
  151.9 24.8 %collective-permute-start.46 = (bf16[128,1024]{1,0:T(8,128)(2,1)S(1)}, bf16[128,1024]{1,0:T(8,128)(2,1)S(1)}, u32[]{:S(2)}, u32[]{:S(2)}) collective-permute-start(bf16[128,1024]{1,0:T(8,128)(2,1)S(1)} %constant_dynamic-slice_fusion), channel_id=1, source_target_pairs={{0,1},{1,0},{2,3},{3,2},{4,5},{5,4},{6,7},{7,6},{8,9},{9,8},{10,11... | collective-permute-start | bytes 786440 | tf_op jit(solution)/shard_map/ppermute | solution.py:32
  154.8 14.5 %collective-permute-start.51 = (bf16[64,3968]{1,0:T(8,128)(2,1)S(1)}, bf16[64,3968]{1,0:T(8,128)(2,1)S(1)}, u32[]{:S(2)}, u32[]{:S(2)}) collective-permute-start(bf16[64,3968]{1,0:T(8,128)(2,1)S(1)} %get-tuple-element.325), channel_id=1, source_target_pairs={{0,8},{2,10},{4,0},{6,2},{8,16},{10,18},{12,4},{14,6},{16,24},{18,... | collective-permute-start | bytes 1523720 | tf_op jit(solution)/shard_map/sum_b_up_3/ppermute | solution.py:65
  155.4 14.4 %collective-permute-start.52 = (bf16[64,3968]{1,0:T(8,128)(2,1)S(1)}, bf16[64,3968]{1,0:T(8,128)(2,1)S(1)}, u32[]{:S(2)}, u32[]{:S(2)}) collective-permute-start(bf16[64,3968]{1,0:T(8,128)(2,1)S(1)} %get-tuple-element.326), channel_id=1, source_target_pairs={{0,4},{2,6},{4,12},{6,14},{8,0},{10,2},{12,20},{14,22},{16,8},{18,... | collective-permute-start | bytes 1523720 | tf_op jit(solution)/shard_map/sum_b_down_3/ppermute | solution.py:65
  157.0 14.6 %collective-permute-start.48 = (bf16[32,2176]{1,0:T(8,128)(2,1)S(1)}, bf16[32,2176]{1,0:T(8,128)(2,1)S(1)}, u32[]{:S(2)}, u32[]{:S(2)}) collective-permute-start(bf16[32,2176]{1,0:T(8,128)(2,1)S(1)} %get-tuple-element.316), channel_id=1, source_target_pairs={{0,8},{2,10},{4,0},{6,2},{8,16},{10,18},{12,4},{14,6},{16,24},{18,... | collective-permute-start | bytes 417800 | tf_op jit(solution)/shard_map/sum_a_up_1/ppermute | solution.py:65
  157.6 14.2 %collective-permute-start.49 = (bf16[32,2176]{1,0:T(8,128)(2,1)S(1)}, bf16[32,2176]{1,0:T(8,128)(2,1)S(1)}, u32[]{:S(2)}, u32[]{:S(2)}) collective-permute-start(bf16[32,2176]{1,0:T(8,128)(2,1)S(1)} %get-tuple-element.317), channel_id=1, source_target_pairs={{0,4},{2,6},{4,12},{6,14},{8,0},{10,2},{12,20},{14,22},{16,8},{18,... | collective-permute-start | bytes 417800 | tf_op jit(solution)/shard_map/sum_a_down_1/ppermute | solution.py:65
  169.3 13.7 %collective-permute-start.55 = (bf16[5,64,2176]{2,1,0:T(8,128)(2,1)}, bf16[5,64,2176]{2,1,0:T(8,128)(2,1)S(1)}, u32[]{:S(2)}, u32[]{:S(2)}) collective-permute-start(bf16[5,64,2176]{2,1,0:T(8,128)(2,1)} %get-tuple-element.337), channel_id=1, source_target_pairs={{0,2},{2,0},{4,6},{6,4},{8,10},{10,8},{12,14},{14,12},{16,18},{18,... | collective-permute-start | bytes 4177928 | tf_op jit(solution)/shard_map/sum_a_cores_rest/ppermute | solution.py:65
  172.0 9.6 %collective-permute-start.53 = (bf16[64,2176]{1,0:T(8,128)(2,1)S(1)}, bf16[64,2176]{1,0:T(8,128)(2,1)S(1)}, u32[]{:S(2)}, u32[]{:S(2)}) collective-permute-start(bf16[64,2176]{1,0:T(8,128)(2,1)S(1)} %get-tuple-element.331), channel_id=1, source_target_pairs={{0,8},{2,10},{4,0},{6,2},{8,16},{10,18},{12,4},{14,6},{16,24},{18,... | collective-permute-start | bytes 835592 | tf_op jit(solution)/shard_map/sum_a_up_2/ppermute | solution.py:65
  173.1 9.6 %collective-permute-start.54 = (bf16[64,2176]{1,0:T(8,128)(2,1)S(1)}, bf16[64,2176]{1,0:T(8,128)(2,1)S(1)}, u32[]{:S(2)}, u32[]{:S(2)}) collective-permute-start(bf16[64,2176]{1,0:T(8,128)(2,1)S(1)} %get-tuple-element.332), channel_id=1, source_target_pairs={{0,4},{2,6},{4,12},{6,14},{8,0},{10,2},{12,20},{14,22},{16,8},{18,... | collective-permute-start | bytes 835592 | tf_op jit(solution)/shard_map/sum_a_down_2/ppermute | solution.py:65
  175.7 21.9 %collective-permute-start.58 = (bf16[64,3968]{1,0:T(8,128)(2,1)S(1)}, bf16[64,3968]{1,0:T(8,128)(2,1)S(1)}, u32[]{:S(2)}, u32[]{:S(2)}) collective-permute-start(bf16[64,3968]{1,0:T(8,128)(2,1)S(1)} %get-tuple-element.350), channel_id=1, source_target_pairs={{0,8},{2,10},{4,0},{6,2},{8,16},{10,18},{12,4},{14,6},{16,24},{18,... | collective-permute-start | bytes 1523720 | tf_op jit(solution)/shard_map/sum_b_up_4/ppermute | solution.py:65
  176.7 20.8 %collective-permute-start.59 = (bf16[64,3968]{1,0:T(8,128)(2,1)S(1)}, bf16[64,3968]{1,0:T(8,128)(2,1)S(1)}, u32[]{:S(2)}, u32[]{:S(2)}) collective-permute-start(bf16[64,3968]{1,0:T(8,128)(2,1)S(1)} %get-tuple-element.351), channel_id=1, source_target_pairs={{0,4},{2,6},{4,12},{6,14},{8,0},{10,2},{12,20},{14,22},{16,8},{18,... | collective-permute-start | bytes 1523720 | tf_op jit(solution)/shard_map/sum_b_down_4/ppermute | solution.py:65
  183.2 13.5 %collective-permute-start.56 = (bf16[64,2176]{1,0:T(8,128)(2,1)S(1)}, bf16[64,2176]{1,0:T(8,128)(2,1)S(1)}, u32[]{:S(2)}, u32[]{:S(2)}) collective-permute-start(bf16[64,2176]{1,0:T(8,128)(2,1)S(1)} %get-tuple-element.342), channel_id=1, source_target_pairs={{0,8},{2,10},{4,0},{6,2},{8,16},{10,18},{12,4},{14,6},{16,24},{18,... | collective-permute-start | bytes 835592 | tf_op jit(solution)/shard_map/sum_a_up_3/ppermute | solution.py:65
  184.0 13.3 %collective-permute-start.57 = (bf16[64,2176]{1,0:T(8,128)(2,1)S(1)}, bf16[64,2176]{1,0:T(8,128)(2,1)S(1)}, u32[]{:S(2)}, u32[]{:S(2)}) collective-permute-start(bf16[64,2176]{1,0:T(8,128)(2,1)S(1)} %get-tuple-element.343), channel_id=1, source_target_pairs={{0,4},{2,6},{4,12},{6,14},{8,0},{10,2},{12,20},{14,22},{16,8},{18,... | collective-permute-start | bytes 835592 | tf_op jit(solution)/shard_map/sum_a_down_3/ppermute | solution.py:65
  199.0 6.6 %collective-permute-start.60 = (bf16[64,2176]{1,0:T(8,128)(2,1)S(1)}, bf16[64,2176]{1,0:T(8,128)(2,1)S(1)}, u32[]{:S(2)}, u32[]{:S(2)}) collective-permute-start(bf16[64,2176]{1,0:T(8,128)(2,1)S(1)} %get-tuple-element.354), channel_id=1, source_target_pairs={{0,8},{2,10},{4,0},{6,2},{8,16},{10,18},{12,4},{14,6},{16,24},{18,... | collective-permute-start | bytes 835592 | tf_op jit(solution)/shard_map/sum_a_up_4/ppermute | solution.py:65
  199.6 6.5 %collective-permute-start.61 = (bf16[64,2176]{1,0:T(8,128)(2,1)S(1)}, bf16[64,2176]{1,0:T(8,128)(2,1)S(1)}, u32[]{:S(2)}, u32[]{:S(2)}) collective-permute-start(bf16[64,2176]{1,0:T(8,128)(2,1)S(1)} %get-tuple-element.355), channel_id=1, source_target_pairs={{0,4},{2,6},{4,12},{6,14},{8,0},{10,2},{12,20},{14,22},{16,8},{18,... | collective-permute-start | bytes 835592 | tf_op jit(solution)/shard_map/sum_a_down_4/ppermute | solution.py:65
  207.1 3.5 %collective-permute-start.62 = (f32[64]{0:T(128)S(1)}, f32[64]{0:T(128)S(1)}, u32[]{:S(2)}, u32[]{:S(2)}) collective-permute-start(f32[64]{0:T(128)S(1)} %get-tuple-element.389), channel_id=1, source_target_pairs={{0,1},{1,0},{2,3},{3,2},{4,5},{5,4},{6,7},{7,6},{8,9},{9,8},{10,11... | collective-permute-start | bytes 776 | tf_op jit(solution)/shard_map/ppermute | solution.py:32
  (62 other events, 461.1 us)

commit v6 on v5

--- a/solution.py
+++ b/solution.py
@@ -50,6 +50,7 @@
         self.place = jnp.asarray(place, jnp.int32)[me // 2]
         self.order = jnp.asarray(order, jnp.int32)
         self.half = self.chips // 2
+        self.own = {}
         self.slots = [self.half]
         for step in range(1, self.half):
             self.slots += [self.half + step, self.half - step]
@@ -63,6 +64,11 @@
     def go(self, block, route, name):
         with jax.named_scope(name):
             return lax.ppermute(block, SEQ, route)
+
+    def go_across(self, block, route, name):
+        both = [(2 * i + side, 2 * j + 1 - side) for i, j in route for side in (0, 1)]
+        with jax.named_scope(name):
+            return lax.ppermute(block, (SEQ, PAIR), both)
 
     def gather(self, block, name, plan):
         if not self.short:
@@ -115,6 +121,8 @@
         far = at(self.half).astype(BF16)
         upward, downward = far[:middle], far[middle:]
         for step in range(1, self.half + 1):
+            if step == self.half:
+                self.own[name] = at(0)
             upward, downward = yield upward, downward
             upward = self.go(upward, self.up, f"{name}_up_{step}")
             downward = self.go(downward, self.down, f"{name}_down_{step}")
@@ -595,7 +603,7 @@
 def local(tokens, norm1_gain, w_qkv, w_attn_out, norm2_gain, w_in, w_down, cotangent):
     row_count, model_width = tokens.shape
     ring = Ring(model_width)
-    early = 3 if ring.short else 0
+    early, early_last = (2, 3) if ring.short else (0, 0)
     chips, core = ring.chips_at(ring.slots), ring.core.reshape(1)
     depth, _, width = w_qkv.shape
     units = w_down.shape[0]
@@ -721,7 +729,7 @@
     down_other = pair_swap(other_rows(down_term, row_count))
     from_prev, from_next = steps_b.ride((from_prev, from_next))
     last = call(
-        functools.partial(last_kernel, early),
+        functools.partial(last_kernel, early_last),
         (
             chips, core, grad_queries, grad_own, from_prev, from_next, cosine, sine, tokens_all,
             gain_two, work_one, grad_low, context, whole_a,
@@ -732,7 +740,7 @@
             shape_of(work_rows, model_width, BF16),
             shape_of(model_width, LANES, BF16),
         ]
-        + [pltpu.HBM((early, depth, blob_a.shape[1]), BF16)] * (2 if early else 0),
+        + [pltpu.HBM((early_last, depth, blob_a.shape[1]), BF16)] * (2 if early else 0),
         [
             pltpu.VMEM((work_rows, 2 * width), F32),
             pltpu.VMEM((model_width, 3 * width), BF16),
@@ -748,7 +756,7 @@
     grad_qkv = steps_b.ride(grad_qkv)
     factors = work_one, grad_qkv, grad_low, context, gain_columns
     if early:
-        rest_a = weight_terms(ring, chips, core, early, *factors)
+        rest_a = weight_terms(ring, chips, core, early_last, *factors)
         steps_a = Stepped(ring.scatter_sum(early_a, rest_a, "sum_a"))
     else:
         steps_a = Stepped(summed_terms(*factors))
@@ -760,6 +768,12 @@
     steps_a.step()
     steps_a.step()
     steps_a.step()
+    gain_parts = []
+    if early:
+        gain_parts.append(pair_swap(ring.own["sum_a"][:, 4 * width :]))
+        for block, route in zip(steps_a.state, (ring.up, ring.down)):
+            part = ring.go_across(block[:, 4 * width :], route, "gains_across")
+            gain_parts.append(part.astype(F32))
     steps_a.beside(steps_b)
     share_b = steps_b.finish()
     share_a = steps_a.finish()
@@ -784,7 +798,11 @@
 
     share_gains = share_a[:, 4 * width : 4 * width + 2] + share_a[:, 4 * width + 2 : 4 * width + 4]
     share_gain_one = share_gains[:, 0]
-    share_gain_one = share_gain_one + pair_swap(share_gain_one)
+    if early:
+        others = sum(gain_parts)
+        share_gain_one = share_gain_one + (others[:, 0] + others[:, 2])
+    else:
+        share_gain_one = share_gain_one + pair_swap(share_gain_one)
     return (
         output,
         grad_tokens,

time: 212 us -> 206 us (0.972)
  waiting for transfers between devices: 73.5 us -> 70.6 us
    ppermute x54, waiting for transfers between devices: 69.6 us -> 63.7 us  [go(): return lax.ppermute(block, SEQ, route)]
    ppermute x0 -> x2, starting transfers between devices: none -> 2.92 us  [go_across(): return lax.ppermute(block, (SEQ, PAIR), both)]
    convert_element_type x6, other arithmetic: 6.6 us -> 4.19 us  [scatter_sum(): downward = (at(self.half + step) + downward).astype(BF16)]
    ppermute x54, starting transfers between devices: 43 us -> 40.6 us  [go(): return lax.ppermute(block, SEQ, route)]
    ppermute x6, waiting for transfers between devices: 3.79 us -> 5.97 us  [pair_swap(): return lax.ppermute(block, PAIR, [(0, 1), (1, 0)])]
  transfers between devices with their start and end apart: 63 -> 65, of which waited for: 31 -> 30; matrix products, arithmetic and copies ran while one was open for 13% -> 13% of each run, Pallas kernels for 16% -> 17%
where the time goes in v6:
time: 206 us; the launch traced here: 205 us
  waiting for transfers between devices  70.6 us (34%)
  starting transfers between devices  53.4 us (26%)
  Pallas kernels  46.5 us (23%)
  other arithmetic  21.9 us (11%)
  local copies, waits for them, and re-layouts  11.3 us (5%)
    ppermute x54, waiting for transfers between devices, go(): return lax.ppermute(block, SEQ, route)  63.7 us
    ppermute x54, starting transfers between devices, go(): return lax.ppermute(block, SEQ, route)  40.6 us
    pallas_call x4, Pallas kernels, call(): pl.pallas_call(kernel, in_specs=specs, out_specs=[VMEM] * len(outs), out_...  34.3 us
    pallas_call x2, Pallas kernels, weight_terms(): pl.pallas_call(functools.partial(weight_kernel, tail), grid_spec=pltpu.Pr...  12.2 us
    ppermute x6, waiting for transfers between devices, pair_swap(): return lax.ppermute(block, PAIR, [(0, 1), (1, 0)])  5.97 us
    ppermute x6, starting transfers between devices, pair_swap(): return lax.ppermute(block, PAIR, [(0, 1), (1, 0)])  5.78 us
    convert_element_type x6, other arithmetic, scatter_sum(): downward = (at(self.half + step) + downward).astype(BF16)  4.19 us
  transfers between devices with their start and end apart: 65, of which 30 were waited for; matrix products, arithmetic and copies ran while one was open for 13% of the time, Pallas kernels for 17%

profile of v6, /device:TPU:0, one launch (start us, length us, event | category | flops | bytes accessed | tf_op | source)
XLA Modules:
  0.0 205.3 jit_solution(14628089003836799096)
XLA Ops:
  0.7 1.0 copy.48
  2.5 0.9 fusion.25.refs_0_
  3.3 3.1 %collective-permute-start.1 = (bf16[64,2176]{1,0:T(8,128)(2,1)S(1)}, bf16[64,2176]{1,0:T(8,128)(2,1)S(1)}, u32[]{:S(2)}, u32[]{:S(2)}) collective-permute-start(bf16[64,2176]{1,0:T(8,128)(2,1)S(1)} %fusion.25.refs_0_), channel_id=1, source_target_pairs={{0,8},{2,10},{4,0},{6,2},{8,16},{10,18},{12,4},{14,6},{16,24},{18,... | collective-permute-start | bytes 835592 | tf_op jit(solution)/shard_map/gather_a_up_1/ppermute | solution.py:66
  6.4 1.0 slice_select_fusion
  7.4 1.3 collective-permute-start
  13.0 1.6 collective-permute-done.2.refs_2_
  14.7 2.2 %collective-permute-start.5 = (bf16[64,2176]{1,0:T(8,128)(2,1)S(1)}, bf16[64,2176]{1,0:T(8,128)(2,1)}, u32[]{:S(2)}, u32[]{:S(2)}) collective-permute-start(bf16[64,2176]{1,0:T(8,128)(2,1)S(1)} %collective-permute-done.1.refs_1_), channel_id=1, source_target_pairs={{0,8},{2,10},{4,0},{6,2},{8,16},{10,18},{12,4},{14,6},{16,24},{18,... | collective-permute-start | bytes 835592 | tf_op jit(solution)/shard_map/gather_a_up_2/ppermute | solution.py:66
  17.5 2.1 %collective-permute-start.4 = (bf16[320,1024]{1,0:T(8,128)(2,1)S(1)}, bf16[320,1024]{1,0:T(8,128)(2,1)S(1)}, u32[]{:S(2)}, u32[]{:S(2)}) collective-permute-start(bf16[320,1024]{1,0:T(8,128)(2,1)S(1)} %pad_maximum_fusion.1), channel_id=1, source_target_pairs={{0,1},{1,0},{2,3},{3,2},{4,5},{5,4},{6,7},{7,6},{8,9},{9,8},{10,11... | collective-permute-start | bytes 1966088 | tf_op jit(solution)/shard_map/ppermute | solution.py:32
  20.7 3.6 %collective-permute-done.5.refs_3_ = bf16[64,2176]{1,0:T(8,128)(2,1)} collective-permute-done((bf16[64,2176]{1,0:T(8,128)(2,1)S(1)}, bf16[64,2176]{1,0:T(8,128)(2,1)}, u32[]{:S(2)}, u32[]{:S(2)}) %collective-permute-start.5) | collective-permute-done | bytes 278560 | tf_op jit(solution)/shard_map/gather_a_up_2/ppermute | solution.py:66
  24.2 2.0 collective-permute-done.6.refs_4_
  26.6 1.7 collective-permute-start.9
  28.9 1.2 gather_fusion.1
  30.0 1.5 multiply_sine_fusion
  31.5 1.6 collective-permute-start.14
  33.6 1.2 collective-permute-done.10.refs_6_
  34.8 1.3 collective-permute-done.9.refs_5_
  38.6 1.8 collective-permute-start.11
  40.7 6.2 %collective-permute-done.14.refs_1_ = bf16[64,3968]{1,0:T(8,128)(2,1)S(1)} collective-permute-done((bf16[64,3968]{1,0:T(8,128)(2,1)}, bf16[64,3968]{1,0:T(8,128)(2,1)S(1)}, u32[]{:S(2)}, u32[]{:S(2)}) %collective-permute-start.14) | collective-permute-done | bytes 507936 | tf_op jit(solution)/shard_map/gather_b_up_1/ppermute | solution.py:66
  47.3 1.4 collective-permute-done.11.refs_7_
  49.4 1.7 collective-permute-start.21
  52.7 8.3 %shard_map.224 = (bf16[1024,2176]{1,0:T(8,128)(2,1)}, bf16[1024,512]{1,0:T(8,128)(2,1)}, f32[8,1024]{1,0:T(8,128)}, bf16[256,1024]{1,0:T(8,128)(2,1)}, bf16[256,...) custom-call(s32[18]{0:T(128)} %multiply_add_fusion.starts, ...), custom_call_target="tpu_custom_call" | custom-call | flops 805306368 | bytes 16777216 | tf_op jit(solution)/shard_map/pallas_call | solution.py:191
  61.0 2.4 %collective-permute-done.21.refs_3_ = bf16[64,3968]{1,0:T(8,128)(2,1)} collective-permute-done((bf16[64,3968]{1,0:T(8,128)(2,1)S(1)}, bf16[64,3968]{1,0:T(8,128)(2,1)}, u32[]{:S(2)}, u32[]{:S(2)}) %collective-permute-start.21) | collective-permute-done | bytes 507936 | tf_op jit(solution)/shard_map/gather_b_up_2/ppermute | solution.py:66
  63.4 1.6 collective-permute-done.22.refs_4_
  65.0 2.1 collective-permute-start.23
  67.1 1.6 collective-permute-start.24
  69.6 10.2 %collective-permute-done.24.refs_5_ = bf16[64,3968]{1,0:T(8,128)(2,1)S(1)} collective-permute-done((bf16[64,3968]{1,0:T(8,128)(2,1)}, bf16[64,3968]{1,0:T(8,128)(2,1)S(1)}, u32[]{:S(2)}, u32[]{:S(2)}) %collective-permute-start.24) | collective-permute-done | bytes 507936 | tf_op jit(solution)/shard_map/gather_b_up_3/ppermute | solution.py:66
  79.8 1.3 collective-permute-done.25.refs_6_
  81.2 1.7 collective-permute-start.29
  84.0 3.5 %collective-permute-done.29.refs_7_ = bf16[32,3968]{1,0:T(8,128)(2,1)S(1)} collective-permute-done((bf16[32,3968]{1,0:T(8,128)(2,1)S(1)}, bf16[32,3968]{1,0:T(8,128)(2,1)S(1)}, u32[]{:S(2)}, u32[]{:S(2)}) %collective-permute-start.29) | collective-permute-done | bytes 253984 | tf_op jit(solution)/shard_map/gather_b_up_4/ppermute | solution.py:66
  87.5 1.9 collective-permute-done.30.refs_8_
  90.0 1.0 collective-permute-done.35.refs_16_
  92.9 12.2 %shard_map.225 = (f32[256,1024]{1,0:T(8,128)}, bf16[256,1024]{1,0:T(8,128)(2,1)}, bf16[256,1408]{1,0:T(8,128)(2,1)}, bf16[256,2688]{1,0:T(8,128)(2,1)}, bf16[256...) custom-call(s32[18]{0:T(128)} %multiply_add_fusion.starts, ...), custom_call_target="tpu_custom_call" | custom-call | flops 4127195136 | bytes 33554432 | tf_op jit(solution)/shard_map/pallas_call | solution.py:191
  105.8 8.0 %shard_map.226 = (bf16[6,64,3968]{2,1,0:T(8,128)(2,1)}, bf16[6,64,3968]{2,1,0:T(8,128)(2,1)}) custom-call(s32[8]{0:T(128)} %gather_fusion.1, s32[1]{0:T(128)} %bitcast.8.core, bf16[256,1024]{1,0:T(8,128)(2,1)} %get-tuple-element.268.left_one, bf16[256,1024]{1,0:T(8,128)(2,1)} %pad_maximum_fusion.3.cot.left_two, ...), custom_call_target="tpu_custom_call" | custom-call | flops 1560281088 | bytes 8126464 | tf_op jit(solution)/shard_map/pallas_call | solution.py:509
  114.0 1.4 add_convert_fusion
  116.3 1.3 collective-permute-start.40
  117.6 2.3 %collective-permute-done.38.grad_two_other = bf16[256,1024]{1,0:T(8,128)(2,1)S(1)} collective-permute-done((bf16[256,1024]{1,0:T(8,128)(2,1)}, bf16[256,1024]{1,0:T(8,128)(2,1)S(1)}, u32[]{:S(2)}, u32[]{:S(2)}) %collective-permute-start.38) | collective-permute-done | bytes 524320 | tf_op jit(solution)/shard_map/ppermute | solution.py:32
  120.0 7.0 %shard_map.227 = (f32[256,1024]{1,0:T(8,128)}, bf16[256,1024]{1,0:T(8,128)(2,1)}, f32[8,1024]{1,0:T(8,128)S(1)}, bf16[256,512]{1,0:T(8,128)(2,1)S(1)}, f32[256,1...) custom-call(s32[2]{0:T(128)S(1)} %copy-done.16, f32[256,1024]{1,0:T(8,128)S(1)} %copy-done, ...), custom_call_target="tpu_custom_call" | custom-call | flops 536870912 | bytes 25165824 | tf_op jit(solution)/shard_map/pallas_call | solution.py:191
  127.0 1.5 collective-permute-start.41
  128.5 1.3 collective-permute-start.42
  129.8 1.2 fusion.5
  131.0 1.6 fusion.6
  132.7 4.5 %collective-permute-start.45 = (bf16[64,3968]{1,0:T(8,128)(2,1)S(1)}, bf16[64,3968]{1,0:T(8,128)(2,1)S(1)}, u32[]{:S(2)}, u32[]{:S(2)}) collective-permute-start(bf16[64,3968]{1,0:T(8,128)(2,1)S(1)} %fusion.6), channel_id=1, source_target_pairs={{0,8},{2,10},{4,0},{6,2},{8,16},{10,18},{12,4},{14,6},{16,24},{18,... | collective-permute-start | bytes 1523720 | tf_op jit(solution)/shard_map/sum_b_up_2/ppermute | solution.py:66
  138.5 6.7 %shard_map.228 = (bf16[256,1536]{1,0:T(8,128)(2,1)}, bf16[256,1024]{1,0:T(8,128)(2,1)}, bf16[1024,128]{1,0:T(8,128)(2,1)}, bf16[3,64,2176]{2,1,0:T(8,128)(2,1)}, bf16[3,64,2176]{2,1,0:T(8,128)(2,1)}) custom-call(s32[8]{0:T(128)} %gather_fusion.1, s32[1]{0:T(128)} %bitcast.8.core, bf16[256,512]{1,0:T(8,128)(2,1)} %copy-done.11, f32[256,1024]{1,0:T(8,128)} %copy-done.2, ...), custom_call_target="tpu_custom_call" | custom-call | flops 805306368 | bytes 16777216 | tf_op jit(solution)/shard_map/pallas_call | solution.py:191
  145.2 2.2 %collective-permute-done.44 = bf16[128,1024]{1,0:T(8,128)(2,1)} collective-permute-done((bf16[128,1024]{1,0:T(8,128)(2,1)}, bf16[128,1024]{1,0:T(8,128)(2,1)}, u32[]{:S(2)}, u32[]{:S(2)}) %collective-permute-start.44) | collective-permute-done | bytes 262176 | tf_op jit(solution)/shard_map/ppermute | solution.py:32
  147.5 2.2 %collective-permute-done.46 = bf16[64,3968]{1,0:T(8,128)(2,1)S(1)} collective-permute-done((bf16[64,3968]{1,0:T(8,128)(2,1)S(1)}, bf16[64,3968]{1,0:T(8,128)(2,1)S(1)}, u32[]{:S(2)}, u32[]{:S(2)}) %collective-permute-start.46) | collective-permute-done | bytes 507936 | tf_op jit(solution)/shard_map/sum_b_down_2/ppermute | solution.py:66
  149.8 2.0 fusion.3
  152.3 1.6 collective-permute-start.52
  153.9 4.2 %shard_map.229 = (bf16[5,64,2176]{2,1,0:T(8,128)(2,1)}, bf16[5,64,2176]{2,1,0:T(8,128)(2,1)}) custom-call(s32[8]{0:T(128)S(1)} %copy-done.15, s32[1]{0:T(128)} %bitcast.8.core, bf16[256,1024]{1,0:T(8,128)(2,1)S(1)} %copy-done.7, bf16[256,1024]{1,0:T(8,128)(2,1)S(1)} %copy-done.8, bf16[256,1536]{1,0:T(8,128)(2,1)S(1)} %copy-done.17, ...), custom_call_target="tpu_custom_call" | custom-call | flops 713031680 | bytes 3899392 | tf_op jit(solution)/shard_map/pallas_call | solution.py:509
  158.7 1.6 collective-permute-start.50
  160.3 1.9 add_convert_fusion.2
  162.2 4.0 %collective-permute-done.51 = bf16[64,3968]{1,0:T(8,128)(2,1)S(1)} collective-permute-done((bf16[64,3968]{1,0:T(8,128)(2,1)S(1)}, bf16[64,3968]{1,0:T(8,128)(2,1)S(1)}, u32[]{:S(2)}, u32[]{:S(2)}) %collective-permute-start.51) | collective-permute-done | bytes 507936 | tf_op jit(solution)/shard_map/sum_b_up_3/ppermute | solution.py:66
  166.7 2.0 collective-permute-done.49
  169.5 1.6 collective-permute-start.54
  171.9 1.5 collective-permute-done.47
  173.4 1.5 collective-permute-start.59
  175.0 3.7 %collective-permute-done.53 = bf16[64,2176]{1,0:T(8,128)(2,1)S(1)} collective-permute-done((bf16[64,2176]{1,0:T(8,128)(2,1)S(1)}, bf16[64,2176]{1,0:T(8,128)(2,1)S(1)}, u32[]{:S(2)}, u32[]{:S(2)}) %collective-permute-start.53) | collective-permute-done | bytes 278560 | tf_op jit(solution)/shard_map/sum_a_up_2/ppermute | solution.py:66
  179.4 1.0 fusion.22
  180.6 1.6 collective-permute-start.56
  183.5 10.4 %collective-permute-done.56 = bf16[64,2176]{1,0:T(8,128)(2,1)S(1)} collective-permute-done((bf16[64,2176]{1,0:T(8,128)(2,1)S(1)}, bf16[64,2176]{1,0:T(8,128)(2,1)S(1)}, u32[]{:S(2)}, u32[]{:S(2)}) %collective-permute-start.56) | collective-permute-done | bytes 278560 | tf_op jit(solution)/shard_map/sum_a_up_3/ppermute | solution.py:66
  194.7 1.4 collective-permute-start.60
  196.8 1.4 collective-permute-start.63
  198.2 1.5 collective-permute-start.64
  200.6 1.4 copy.44
  202.0 0.9 collective-permute-done.64
  (280 shorter events, 30.8 us)
Async XLA Ops:
  3.3 9.7 %collective-permute-start.1 = (bf16[64,2176]{1,0:T(8,128)(2,1)S(1)}, bf16[64,2176]{1,0:T(8,128)(2,1)S(1)}, u32[]{:S(2)}, u32[]{:S(2)}) collective-permute-start(bf16[64,2176]{1,0:T(8,128)(2,1)S(1)} %fusion.25.refs_0_), channel_id=1, source_target_pairs={{0,8},{2,10},{4,0},{6,2},{8,16},{10,18},{12,4},{14,6},{16,24},{18,... | collective-permute-start | bytes 835592 | tf_op jit(solution)/shard_map/gather_a_up_1/ppermute | solution.py:66
  6.4 8.2 %collective-permute-start.2 = (bf16[64,2176]{1,0:T(8,128)(2,1)S(1)}, bf16[64,2176]{1,0:T(8,128)(2,1)}, u32[]{:S(2)}, u32[]{:S(2)}) collective-permute-start(bf16[64,2176]{1,0:T(8,128)(2,1)S(1)} %fusion.25.refs_0_), channel_id=1, source_target_pairs={{0,4},{2,6},{4,12},{6,14},{8,0},{10,2},{12,20},{14,22},{16,8},{18,... | collective-permute-start | bytes 835592 | tf_op jit(solution)/shard_map/gather_a_down_1/ppermute | solution.py:66
  6.4 8.2 %collective-permute-start.3 = (bf16[64,2176]{1,0:T(8,128)(2,1)S(1)}, bf16[64,2176]{1,0:T(8,128)(2,1)S(1)}, u32[]{:S(2)}, u32[]{:S(2)}) collective-permute-start(bf16[64,2176]{1,0:T(8,128)(2,1)S(1)} %fusion.25.refs_0_), channel_id=1, source_target_pairs={{0,2},{2,0},{4,6},{6,4},{8,10},{10,8},{12,14},{14,12},{16,18},{18,... | collective-permute-start | bytes 835592 | tf_op jit(solution)/shard_map/gather_a_cores_0/ppermute | solution.py:66
  7.4 5.2 %collective-permute-start = (bf16[64,1024]{1,0:T(8,128)(2,1)S(1)}, bf16[64,1024]{1,0:T(8,128)(2,1)S(1)}, u32[]{:S(2)}, u32[]{:S(2)}) collective-permute-start(bf16[64,1024]{1,0:T(8,128)(2,1)S(1)} %slice_select_fusion), channel_id=1, source_target_pairs={{2,0},{4,2},{6,4},{8,6},{10,8},{12,10},{14,12},{16,14},{18,16},{20... | collective-permute-start | bytes 393224 | tf_op jit(solution)/shard_map/ppermute | solution.py:579
  14.7 9.6 %collective-permute-start.5 = (bf16[64,2176]{1,0:T(8,128)(2,1)S(1)}, bf16[64,2176]{1,0:T(8,128)(2,1)}, u32[]{:S(2)}, u32[]{:S(2)}) collective-permute-start(bf16[64,2176]{1,0:T(8,128)(2,1)S(1)} %collective-permute-done.1.refs_1_), channel_id=1, source_target_pairs={{0,8},{2,10},{4,0},{6,2},{8,16},{10,18},{12,4},{14,6},{16,24},{18,... | collective-permute-start | bytes 835592 | tf_op jit(solution)/shard_map/gather_a_up_2/ppermute | solution.py:66
  16.9 9.4 %collective-permute-start.7 = (bf16[64,2176]{1,0:T(8,128)(2,1)S(1)}, bf16[64,2176]{1,0:T(8,128)(2,1)}, u32[]{:S(2)}, u32[]{:S(2)}) collective-permute-start(bf16[64,2176]{1,0:T(8,128)(2,1)S(1)} %collective-permute-done.1.refs_1_), channel_id=1, source_target_pairs={{0,2},{2,0},{4,6},{6,4},{8,10},{10,8},{12,14},{14,12},{16,18},{18,... | collective-permute-start | bytes 835592 | tf_op jit(solution)/shard_map/gather_a_cores_-1/ppermute | solution.py:66
  16.9 9.4 %collective-permute-start.6 = (bf16[64,2176]{1,0:T(8,128)(2,1)}, bf16[64,2176]{1,0:T(8,128)(2,1)}, u32[]{:S(2)}, u32[]{:S(2)}) collective-permute-start(bf16[64,2176]{1,0:T(8,128)(2,1)} %collective-permute-done.2.refs_2_), channel_id=1, source_target_pairs={{0,4},{2,6},{4,12},{6,14},{8,0},{10,2},{12,20},{14,22},{16,8},{18,... | collective-permute-start | bytes 835592 | tf_op jit(solution)/shard_map/gather_a_down_2/ppermute | solution.py:66
  17.4 8.9 %collective-permute-start.8 = (bf16[64,2176]{1,0:T(8,128)(2,1)}, bf16[64,2176]{1,0:T(8,128)(2,1)}, u32[]{:S(2)}, u32[]{:S(2)}) collective-permute-start(bf16[64,2176]{1,0:T(8,128)(2,1)} %collective-permute-done.2.refs_2_), channel_id=1, source_target_pairs={{0,2},{2,0},{4,6},{6,4},{8,10},{10,8},{12,14},{14,12},{16,18},{18,... | collective-permute-start | bytes 835592 | tf_op jit(solution)/shard_map/gather_a_cores_1/ppermute | solution.py:66
  17.5 18.6 %collective-permute-start.4 = (bf16[320,1024]{1,0:T(8,128)(2,1)S(1)}, bf16[320,1024]{1,0:T(8,128)(2,1)S(1)}, u32[]{:S(2)}, u32[]{:S(2)}) collective-permute-start(bf16[320,1024]{1,0:T(8,128)(2,1)S(1)} %pad_maximum_fusion.1), channel_id=1, source_target_pairs={{0,1},{1,0},{2,3},{3,2},{4,5},{5,4},{6,7},{7,6},{8,9},{9,8},{10,11... | collective-permute-start | bytes 1966088 | tf_op jit(solution)/shard_map/ppermute | solution.py:32
  26.3 8.5 %collective-permute-start.10 = (bf16[64,2176]{1,0:T(8,128)(2,1)}, bf16[64,2176]{1,0:T(8,128)(2,1)S(1)}, u32[]{:S(2)}, u32[]{:S(2)}) collective-permute-start(bf16[64,2176]{1,0:T(8,128)(2,1)} %collective-permute-done.6.refs_4_), channel_id=1, source_target_pairs={{0,4},{2,6},{4,12},{6,14},{8,0},{10,2},{12,20},{14,22},{16,8},{18,... | collective-permute-start | bytes 835592 | tf_op jit(solution)/shard_map/gather_a_down_3/ppermute | solution.py:66
  26.6 9.5 %collective-permute-start.9 = (bf16[64,2176]{1,0:T(8,128)(2,1)}, bf16[64,2176]{1,0:T(8,128)(2,1)S(1)}, u32[]{:S(2)}, u32[]{:S(2)}) collective-permute-start(bf16[64,2176]{1,0:T(8,128)(2,1)} %collective-permute-done.5.refs_3_), channel_id=1, source_target_pairs={{0,8},{2,10},{4,0},{6,2},{8,16},{10,18},{12,4},{14,6},{16,24},{18,... | collective-permute-start | bytes 835592 | tf_op jit(solution)/shard_map/gather_a_up_3/ppermute | solution.py:66
  31.5 15.4 %collective-permute-start.14 = (bf16[64,3968]{1,0:T(8,128)(2,1)}, bf16[64,3968]{1,0:T(8,128)(2,1)S(1)}, u32[]{:S(2)}, u32[]{:S(2)}) collective-permute-start(bf16[64,3968]{1,0:T(8,128)(2,1)} %pad.37.refs_0_), channel_id=1, source_target_pairs={{0,8},{2,10},{4,0},{6,2},{8,16},{10,18},{12,4},{14,6},{16,24},{18,... | collective-permute-start | bytes 1523720 | tf_op jit(solution)/shard_map/gather_b_up_1/ppermute | solution.py:66
  33.1 14.2 %collective-permute-start.15 = (bf16[64,3968]{1,0:T(8,128)(2,1)}, bf16[64,3968]{1,0:T(8,128)(2,1)}, u32[]{:S(2)}, u32[]{:S(2)}) collective-permute-start(bf16[64,3968]{1,0:T(8,128)(2,1)} %pad.37.refs_0_), channel_id=1, source_target_pairs={{0,4},{2,6},{4,12},{6,14},{8,0},{10,2},{12,20},{14,22},{16,8},{18,... | collective-permute-start | bytes 1523720 | tf_op jit(solution)/shard_map/gather_b_down_1/ppermute | solution.py:66
  34.8 6.0 %collective-permute-start.13 = (bf16[64,2176]{1,0:T(8,128)(2,1)}, bf16[64,2176]{1,0:T(8,128)(2,1)S(1)}, u32[]{:S(2)}, u32[]{:S(2)}) collective-permute-start(bf16[64,2176]{1,0:T(8,128)(2,1)} %collective-permute-done.5.refs_3_), channel_id=1, source_target_pairs={{0,2},{2,0},{4,6},{6,4},{8,10},{10,8},{12,14},{14,12},{16,18},{18,... | collective-permute-start | bytes 835592 | tf_op jit(solution)/shard_map/gather_a_cores_-2/ppermute | solution.py:66
  38.6 10.1 %collective-permute-start.11 = (bf16[32,2176]{1,0:T(8,128)(2,1)S(1)}, bf16[32,2176]{1,0:T(8,128)(2,1)S(1)}, u32[]{:S(2)}, u32[]{:S(2)}) collective-permute-start(bf16[32,2176]{1,0:T(8,128)(2,1)S(1)} %slice.240), channel_id=1, source_target_pairs={{0,8},{2,10},{4,0},{6,2},{8,16},{10,18},{12,4},{14,6},{16,24},{18,... | collective-permute-start | bytes 417800 | tf_op jit(solution)/shard_map/gather_a_up_4/ppermute | solution.py:66
  40.4 8.3 %collective-permute-start.12 = (bf16[32,2176]{1,0:T(8,128)(2,1)S(1)}, bf16[32,2176]{1,0:T(8,128)(2,1)S(1)}, u32[]{:S(2)}, u32[]{:S(2)}) collective-permute-start(bf16[32,2176]{1,0:T(8,128)(2,1)S(1)} %slice.241), channel_id=1, source_target_pairs={{0,4},{2,6},{4,12},{6,14},{8,0},{10,2},{12,20},{14,22},{16,8},{18,... | collective-permute-start | bytes 417800 | tf_op jit(solution)/shard_map/gather_a_down_4/ppermute | solution.py:66
  40.7 8.6 %collective-permute-start.16 = (bf16[64,2176]{1,0:T(8,128)(2,1)}, bf16[64,2176]{1,0:T(8,128)(2,1)S(1)}, u32[]{:S(2)}, u32[]{:S(2)}) collective-permute-start(bf16[64,2176]{1,0:T(8,128)(2,1)} %collective-permute-done.6.refs_4_), channel_id=1, source_target_pairs={{0,2},{2,0},{4,6},{6,4},{8,10},{10,8},{12,14},{14,12},{16,18},{18,... | collective-permute-start | bytes 835592 | tf_op jit(solution)/shard_map/gather_a_cores_2/ppermute | solution.py:66
  47.0 4.5 %collective-permute-start.17 = (bf16[64,2176]{1,0:T(8,128)(2,1)S(1)}, bf16[64,2176]{1,0:T(8,128)(2,1)S(1)}, u32[]{:S(2)}, u32[]{:S(2)}) collective-permute-start(bf16[64,2176]{1,0:T(8,128)(2,1)S(1)} %collective-permute-done.9.refs_5_), channel_id=1, source_target_pairs={{0,2},{2,0},{4,6},{6,4},{8,10},{10,8},{12,14},{14,12},{16,18},{18,... | collective-permute-start | bytes 835592 | tf_op jit(solution)/shard_map/gather_a_cores_-3/ppermute | solution.py:66
  48.7 2.3 %collective-permute-start.19 = (bf16[32,2176]{1,0:T(8,128)(2,1)S(1)}, bf16[32,2176]{1,0:T(8,128)(2,1)S(1)}, u32[]{:S(2)}, u32[]{:S(2)}) collective-permute-start(bf16[32,2176]{1,0:T(8,128)(2,1)S(1)} %collective-permute-done.11.refs_7_), channel_id=1, source_target_pairs={{0,2},{2,0},{4,6},{6,4},{8,10},{10,8},{12,14},{14,12},{16,18},{18,... | collective-permute-start | bytes 417800 | tf_op jit(solution)/shard_map/gather_a_cores_-4/ppermute | solution.py:66
  48.8 2.6 %collective-permute-start.20 = (bf16[32,2176]{1,0:T(8,128)(2,1)S(1)}, bf16[32,2176]{1,0:T(8,128)(2,1)S(1)}, u32[]{:S(2)}, u32[]{:S(2)}) collective-permute-start(bf16[32,2176]{1,0:T(8,128)(2,1)S(1)} %collective-permute-done.12.refs_8_), channel_id=1, source_target_pairs={{0,2},{2,0},{4,6},{6,4},{8,10},{10,8},{12,14},{14,12},{16,18},{18,... | collective-permute-start | bytes 417800 | tf_op jit(solution)/shard_map/gather_a_cores_4/ppermute | solution.py:66
  49.3 2.7 %collective-permute-start.18 = (bf16[64,2176]{1,0:T(8,128)(2,1)S(1)}, bf16[64,2176]{1,0:T(8,128)(2,1)S(1)}, u32[]{:S(2)}, u32[]{:S(2)}) collective-permute-start(bf16[64,2176]{1,0:T(8,128)(2,1)S(1)} %collective-permute-done.10.refs_6_), channel_id=1, source_target_pairs={{0,2},{2,0},{4,6},{6,4},{8,10},{10,8},{12,14},{14,12},{16,18},{18,... | collective-permute-start | bytes 835592 | tf_op jit(solution)/shard_map/gather_a_cores_3/ppermute | solution.py:66
  49.4 14.0 %collective-permute-start.21 = (bf16[64,3968]{1,0:T(8,128)(2,1)S(1)}, bf16[64,3968]{1,0:T(8,128)(2,1)}, u32[]{:S(2)}, u32[]{:S(2)}) collective-permute-start(bf16[64,3968]{1,0:T(8,128)(2,1)S(1)} %collective-permute-done.14.refs_1_), channel_id=1, source_target_pairs={{0,8},{2,10},{4,0},{6,2},{8,16},{10,18},{12,4},{14,6},{16,24},{18,... | collective-permute-start | bytes 1523720 | tf_op jit(solution)/shard_map/gather_b_up_2/ppermute | solution.py:66
  51.1 14.0 %collective-permute-start.22 = (bf16[64,3968]{1,0:T(8,128)(2,1)}, bf16[64,3968]{1,0:T(8,128)(2,1)}, u32[]{:S(2)}, u32[]{:S(2)}) collective-permute-start(bf16[64,3968]{1,0:T(8,128)(2,1)} %collective-permute-done.15.refs_2_), channel_id=1, source_target_pairs={{0,4},{2,6},{4,12},{6,14},{8,0},{10,2},{12,20},{14,22},{16,8},{18,... | collective-permute-start | bytes 1523720 | tf_op jit(solution)/shard_map/gather_b_down_2/ppermute | solution.py:66
  51.4 17.3 %collective-permute-start.26 = (bf16[64,3968]{1,0:T(8,128)(2,1)S(1)}, bf16[64,3968]{1,0:T(8,128)(2,1)}, u32[]{:S(2)}, u32[]{:S(2)}) collective-permute-start(bf16[64,3968]{1,0:T(8,128)(2,1)S(1)} %copy-done.34), channel_id=1, source_target_pairs={{0,2},{2,0},{4,6},{6,4},{8,10},{10,8},{12,14},{14,12},{16,18},{18,... | collective-permute-start | bytes 1523720 | tf_op jit(solution)/shard_map/gather_b_cores_0/ppermute | solution.py:66
  51.5 17.6 %collective-permute-start.27 = (bf16[64,3968]{1,0:T(8,128)(2,1)S(1)}, bf16[64,3968]{1,0:T(8,128)(2,1)}, u32[]{:S(2)}, u32[]{:S(2)}) collective-permute-start(bf16[64,3968]{1,0:T(8,128)(2,1)S(1)} %collective-permute-done.14.refs_1_), channel_id=1, source_target_pairs={{0,2},{2,0},{4,6},{6,4},{8,10},{10,8},{12,14},{14,12},{16,18},{18,... | collective-permute-start | bytes 1523720 | tf_op jit(solution)/shard_map/gather_b_cores_-1/ppermute | solution.py:66
  52.0 17.1 %collective-permute-start.28 = (bf16[64,3968]{1,0:T(8,128)(2,1)}, bf16[64,3968]{1,0:T(8,128)(2,1)}, u32[]{:S(2)}, u32[]{:S(2)}) collective-permute-start(bf16[64,3968]{1,0:T(8,128)(2,1)} %collective-permute-done.15.refs_2_), channel_id=1, source_target_pairs={{0,2},{2,0},{4,6},{6,4},{8,10},{10,8},{12,14},{14,12},{16,18},{18,... | collective-permute-start | bytes 1523720 | tf_op jit(solution)/shard_map/gather_b_cores_1/ppermute | solution.py:66
  65.0 16.1 %collective-permute-start.23 = (bf16[256,1024]{1,0:T(8,128)(2,1)}, bf16[256,1024]{1,0:T(8,128)(2,1)S(1)}, u32[]{:S(2)}, u32[]{:S(2)}) collective-permute-start(bf16[256,1024]{1,0:T(8,128)(2,1)} %get-tuple-element.236.term), channel_id=1, source_target_pairs={{0,1},{1,0},{2,3},{3,2},{4,5},{5,4},{6,7},{7,6},{8,9},{9,8},{10,11... | collective-permute-start | bytes 1572872 | tf_op jit(solution)/shard_map/ppermute | solution.py:32
  67.1 12.7 %collective-permute-start.24 = (bf16[64,3968]{1,0:T(8,128)(2,1)}, bf16[64,3968]{1,0:T(8,128)(2,1)S(1)}, u32[]{:S(2)}, u32[]{:S(2)}) collective-permute-start(bf16[64,3968]{1,0:T(8,128)(2,1)} %collective-permute-done.21.refs_3_), channel_id=1, source_target_pairs={{0,8},{2,10},{4,0},{6,2},{8,16},{10,18},{12,4},{14,6},{16,24},{18,... | collective-permute-start | bytes 1523720 | tf_op jit(solution)/shard_map/gather_b_up_3/ppermute | solution.py:66
  68.7 12.5 %collective-permute-start.25 = (bf16[64,3968]{1,0:T(8,128)(2,1)}, bf16[64,3968]{1,0:T(8,128)(2,1)S(1)}, u32[]{:S(2)}, u32[]{:S(2)}) collective-permute-start(bf16[64,3968]{1,0:T(8,128)(2,1)} %collective-permute-done.22.refs_4_), channel_id=1, source_target_pairs={{0,4},{2,6},{4,12},{6,14},{8,0},{10,2},{12,20},{14,22},{16,8},{18,... | collective-permute-start | bytes 1523720 | tf_op jit(solution)/shard_map/gather_b_down_3/ppermute | solution.py:66
  69.1 14.4 %collective-permute-start.31 = (bf16[64,3968]{1,0:T(8,128)(2,1)}, bf16[64,3968]{1,0:T(8,128)(2,1)S(1)}, u32[]{:S(2)}, u32[]{:S(2)}) collective-permute-start(bf16[64,3968]{1,0:T(8,128)(2,1)} %collective-permute-done.21.refs_3_), channel_id=1, source_target_pairs={{0,2},{2,0},{4,6},{6,4},{8,10},{10,8},{12,14},{14,12},{16,18},{18,... | collective-permute-start | bytes 1523720 | tf_op jit(solution)/shard_map/gather_b_cores_-2/ppermute | solution.py:66
  69.1 14.9 %collective-permute-start.32 = (bf16[64,3968]{1,0:T(8,128)(2,1)}, bf16[64,3968]{1,0:T(8,128)(2,1)S(1)}, u32[]{:S(2)}, u32[]{:S(2)}) collective-permute-start(bf16[64,3968]{1,0:T(8,128)(2,1)} %collective-permute-done.22.refs_4_), channel_id=1, source_target_pairs={{0,2},{2,0},{4,6},{6,4},{8,10},{10,8},{12,14},{14,12},{16,18},{18,... | collective-permute-start | bytes 1523720 | tf_op jit(solution)/shard_map/gather_b_cores_2/ppermute | solution.py:66
  81.2 6.3 %collective-permute-start.29 = (bf16[32,3968]{1,0:T(8,128)(2,1)S(1)}, bf16[32,3968]{1,0:T(8,128)(2,1)S(1)}, u32[]{:S(2)}, u32[]{:S(2)}) collective-permute-start(bf16[32,3968]{1,0:T(8,128)(2,1)S(1)} %slice.242), channel_id=1, source_target_pairs={{0,8},{2,10},{4,0},{6,2},{8,16},{10,18},{12,4},{14,6},{16,24},{18,... | collective-permute-start | bytes 761864 | tf_op jit(solution)/shard_map/gather_b_up_4/ppermute | solution.py:66
  82.9 6.5 %collective-permute-start.30 = (bf16[32,3968]{1,0:T(8,128)(2,1)S(1)}, bf16[32,3968]{1,0:T(8,128)(2,1)S(1)}, u32[]{:S(2)}, u32[]{:S(2)}) collective-permute-start(bf16[32,3968]{1,0:T(8,128)(2,1)S(1)} %slice.243), channel_id=1, source_target_pairs={{0,4},{2,6},{4,12},{6,14},{8,0},{10,2},{12,20},{14,22},{16,8},{18,... | collective-permute-start | bytes 761864 | tf_op jit(solution)/shard_map/gather_b_down_4/ppermute | solution.py:66
  83.5 7.8 %collective-permute-start.33 = (bf16[64,3968]{1,0:T(8,128)(2,1)S(1)}, bf16[64,3968]{1,0:T(8,128)(2,1)S(1)}, u32[]{:S(2)}, u32[]{:S(2)}) collective-permute-start(bf16[64,3968]{1,0:T(8,128)(2,1)S(1)} %collective-permute-done.24.refs_5_), channel_id=1, source_target_pairs={{0,2},{2,0},{4,6},{6,4},{8,10},{10,8},{12,14},{14,12},{16,18},{18,... | collective-permute-start | bytes 1523720 | tf_op jit(solution)/shard_map/gather_b_cores_-3/ppermute | solution.py:66
  83.5 7.8 %collective-permute-start.34 = (bf16[64,3968]{1,0:T(8,128)(2,1)S(1)}, bf16[64,3968]{1,0:T(8,128)(2,1)S(1)}, u32[]{:S(2)}, u32[]{:S(2)}) collective-permute-start(bf16[64,3968]{1,0:T(8,128)(2,1)S(1)} %collective-permute-done.25.refs_6_), channel_id=1, source_target_pairs={{0,2},{2,0},{4,6},{6,4},{8,10},{10,8},{12,14},{14,12},{16,18},{18,... | collective-permute-start | bytes 1523720 | tf_op jit(solution)/shard_map/gather_b_cores_3/ppermute | solution.py:66
  89.5 1.9 collective-permute-start.36
  105.1 8.9 %collective-permute-start.37 = (bf16[2,64,3968]{2,1,0:T(8,128)(2,1)}, bf16[2,64,3968]{2,1,0:T(8,128)(2,1)}, u32[]{:S(2)}, u32[]{:S(2)}) collective-permute-start(bf16[2,64,3968]{2,1,0:T(8,128)(2,1)} %get-tuple-element.274), channel_id=1, source_target_pairs={{0,2},{2,0},{4,6},{6,4},{8,10},{10,8},{12,14},{14,12},{16,18},{18,... | collective-permute-start | bytes 3047432 | tf_op jit(solution)/shard_map/sum_b_cores_early/ppermute | solution.py:66
  105.5 14.5 %collective-permute-start.38 = (bf16[256,1024]{1,0:T(8,128)(2,1)}, bf16[256,1024]{1,0:T(8,128)(2,1)S(1)}, u32[]{:S(2)}, u32[]{:S(2)}) collective-permute-start(bf16[256,1024]{1,0:T(8,128)(2,1)} %get-tuple-element.275.grad_two), channel_id=1, source_target_pairs={{0,1},{1,0},{2,3},{3,2},{4,5},{5,4},{6,7},{7,6},{8,9},{9,8},{10,11... | collective-permute-start | bytes 1572872 | tf_op jit(solution)/shard_map/ppermute | solution.py:32
  113.9 17.1 %collective-permute-start.43 = (bf16[6,64,3968]{2,1,0:T(8,128)(2,1)}, bf16[6,64,3968]{2,1,0:T(8,128)(2,1)S(1)}, u32[]{:S(2)}, u32[]{:S(2)}) collective-permute-start(bf16[6,64,3968]{2,1,0:T(8,128)(2,1)} %get-tuple-element.272), channel_id=1, source_target_pairs={{0,2},{2,0},{4,6},{6,4},{8,10},{10,8},{12,14},{14,12},{16,18},{18,... | collective-permute-start | bytes 9142280 | tf_op jit(solution)/shard_map/sum_b_cores_rest/ppermute | solution.py:66
  115.5 11.5 %collective-permute-start.39 = (bf16[32,3968]{1,0:T(8,128)(2,1)S(1)}, bf16[32,3968]{1,0:T(8,128)(2,1)S(1)}, u32[]{:S(2)}, u32[]{:S(2)}) collective-permute-start(bf16[32,3968]{1,0:T(8,128)(2,1)S(1)} %get-tuple-element.287), channel_id=1, source_target_pairs={{0,8},{2,10},{4,0},{6,2},{8,16},{10,18},{12,4},{14,6},{16,24},{18,... | collective-permute-start | bytes 761864 | tf_op jit(solution)/shard_map/sum_b_up_1/ppermute | solution.py:66
  116.3 10.7 %collective-permute-start.40 = (bf16[32,3968]{1,0:T(8,128)(2,1)S(1)}, bf16[32,3968]{1,0:T(8,128)(2,1)S(1)}, u32[]{:S(2)}, u32[]{:S(2)}) collective-permute-start(bf16[32,3968]{1,0:T(8,128)(2,1)S(1)} %get-tuple-element.288), channel_id=1, source_target_pairs={{0,4},{2,6},{4,12},{6,14},{8,0},{10,2},{12,20},{14,22},{16,8},{18,... | collective-permute-start | bytes 761864 | tf_op jit(solution)/shard_map/sum_b_down_1/ppermute | solution.py:66
  127.0 5.7 %collective-permute-start.41 = (bf16[64,1024]{1,0:T(8,128)(2,1)}, bf16[64,1024]{1,0:T(8,128)(2,1)S(1)}, u32[]{:S(2)}, u32[]{:S(2)}) collective-permute-start(bf16[64,1024]{1,0:T(8,128)(2,1)} %get-tuple-element.289), channel_id=1, source_target_pairs={{0,2},{2,4},{4,6},{6,8},{8,10},{10,12},{12,14},{14,16},{16,18},{18... | collective-permute-start | bytes 393224 | tf_op jit(solution)/shard_map/ppermute | solution.py:28
  128.5 4.3 %collective-permute-start.42 = (bf16[64,1024]{1,0:T(8,128)(2,1)}, bf16[64,1024]{1,0:T(8,128)(2,1)}, u32[]{:S(2)}, u32[]{:S(2)}) collective-permute-start(bf16[64,1024]{1,0:T(8,128)(2,1)} %get-tuple-element.290), channel_id=1, source_target_pairs={{2,0},{4,2},{6,4},{8,6},{10,8},{12,10},{14,12},{16,14},{18,16},{20... | collective-permute-start | bytes 393224 | tf_op jit(solution)/shard_map/ppermute | solution.py:28
  132.7 14.7 %collective-permute-start.45 = (bf16[64,3968]{1,0:T(8,128)(2,1)S(1)}, bf16[64,3968]{1,0:T(8,128)(2,1)S(1)}, u32[]{:S(2)}, u32[]{:S(2)}) collective-permute-start(bf16[64,3968]{1,0:T(8,128)(2,1)S(1)} %fusion.6), channel_id=1, source_target_pairs={{0,8},{2,10},{4,0},{6,2},{8,16},{10,18},{12,4},{14,6},{16,24},{18,... | collective-permute-start | bytes 1523720 | tf_op jit(solution)/shard_map/sum_b_up_2/ppermute | solution.py:66
  137.2 12.4 %collective-permute-start.46 = (bf16[64,3968]{1,0:T(8,128)(2,1)S(1)}, bf16[64,3968]{1,0:T(8,128)(2,1)S(1)}, u32[]{:S(2)}, u32[]{:S(2)}) collective-permute-start(bf16[64,3968]{1,0:T(8,128)(2,1)S(1)} %fusion.5), channel_id=1, source_target_pairs={{0,4},{2,6},{4,12},{6,14},{8,0},{10,2},{12,20},{14,22},{16,8},{18,... | collective-permute-start | bytes 1523720 | tf_op jit(solution)/shard_map/sum_b_down_2/ppermute | solution.py:66
  138.2 9.2 %collective-permute-start.44 = (bf16[128,1024]{1,0:T(8,128)(2,1)}, bf16[128,1024]{1,0:T(8,128)(2,1)}, u32[]{:S(2)}, u32[]{:S(2)}) collective-permute-start(bf16[128,1024]{1,0:T(8,128)(2,1)} %constant_dynamic-slice_fusion.1), channel_id=1, source_target_pairs={{0,1},{1,0},{2,3},{3,2},{4,5},{5,4},{6,7},{7,6},{8,9},{9,8},{10,11... | collective-permute-start | bytes 786440 | tf_op jit(solution)/shard_map/ppermute | solution.py:32
  149.7 8.4 %collective-permute-start.48 = (bf16[3,64,2176]{2,1,0:T(8,128)(2,1)}, bf16[3,64,2176]{2,1,0:T(8,128)(2,1)S(1)}, u32[]{:S(2)}, u32[]{:S(2)}) collective-permute-start(bf16[3,64,2176]{2,1,0:T(8,128)(2,1)} %get-tuple-element.315), channel_id=1, source_target_pairs={{0,2},{2,0},{4,6},{6,4},{8,10},{10,8},{12,14},{14,12},{16,18},{18,... | collective-permute-start | bytes 2506760 | tf_op jit(solution)/shard_map/sum_a_cores_early/ppermute | solution.py:66
  151.8 14.4 %collective-permute-start.51 = (bf16[64,3968]{1,0:T(8,128)(2,1)S(1)}, bf16[64,3968]{1,0:T(8,128)(2,1)S(1)}, u32[]{:S(2)}, u32[]{:S(2)}) collective-permute-start(bf16[64,3968]{1,0:T(8,128)(2,1)S(1)} %get-tuple-element.325), channel_id=1, source_target_pairs={{0,8},{2,10},{4,0},{6,2},{8,16},{10,18},{12,4},{14,6},{16,24},{18,... | collective-permute-start | bytes 1523720 | tf_op jit(solution)/shard_map/sum_b_up_3/ppermute | solution.py:66
  152.3 14.4 %collective-permute-start.52 = (bf16[64,3968]{1,0:T(8,128)(2,1)S(1)}, bf16[64,3968]{1,0:T(8,128)(2,1)S(1)}, u32[]{:S(2)}, u32[]{:S(2)}) collective-permute-start(bf16[64,3968]{1,0:T(8,128)(2,1)S(1)} %get-tuple-element.326), channel_id=1, source_target_pairs={{0,4},{2,6},{4,12},{6,14},{8,0},{10,2},{12,20},{14,22},{16,8},{18,... | collective-permute-start | bytes 1523720 | tf_op jit(solution)/shard_map/sum_b_down_3/ppermute | solution.py:66
  158.1 22.3 %collective-permute-start.55 = (bf16[5,64,2176]{2,1,0:T(8,128)(2,1)}, bf16[5,64,2176]{2,1,0:T(8,128)(2,1)S(1)}, u32[]{:S(2)}, u32[]{:S(2)}) collective-permute-start(bf16[5,64,2176]{2,1,0:T(8,128)(2,1)} %get-tuple-element.337), channel_id=1, source_target_pairs={{0,2},{2,0},{4,6},{6,4},{8,10},{10,8},{12,14},{14,12},{16,18},{18,... | collective-permute-start | bytes 4177928 | tf_op jit(solution)/shard_map/sum_a_cores_rest/ppermute | solution.py:66
  158.2 10.4 %collective-permute-start.49 = (bf16[32,2176]{1,0:T(8,128)(2,1)S(1)}, bf16[32,2176]{1,0:T(8,128)(2,1)S(1)}, u32[]{:S(2)}, u32[]{:S(2)}) collective-permute-start(bf16[32,2176]{1,0:T(8,128)(2,1)S(1)} %get-tuple-element.316), channel_id=1, source_target_pairs={{0,8},{2,10},{4,0},{6,2},{8,16},{10,18},{12,4},{14,6},{16,24},{18,... | collective-permute-start | bytes 417800 | tf_op jit(solution)/shard_map/sum_a_up_1/ppermute | solution.py:66
  158.7 10.1 %collective-permute-start.50 = (bf16[32,2176]{1,0:T(8,128)(2,1)S(1)}, bf16[32,2176]{1,0:T(8,128)(2,1)S(1)}, u32[]{:S(2)}, u32[]{:S(2)}) collective-permute-start(bf16[32,2176]{1,0:T(8,128)(2,1)S(1)} %get-tuple-element.317), channel_id=1, source_target_pairs={{0,4},{2,6},{4,12},{6,14},{8,0},{10,2},{12,20},{14,22},{16,8},{18,... | collective-permute-start | bytes 417800 | tf_op jit(solution)/shard_map/sum_a_down_1/ppermute | solution.py:66
  166.2 7.2 %collective-permute-start.47 = (bf16[128,1024]{1,0:T(8,128)(2,1)S(1)}, bf16[128,1024]{1,0:T(8,128)(2,1)S(1)}, u32[]{:S(2)}, u32[]{:S(2)}) collective-permute-start(bf16[128,1024]{1,0:T(8,128)(2,1)S(1)} %constant_dynamic-slice_fusion), channel_id=1, source_target_pairs={{0,1},{1,0},{2,3},{3,2},{4,5},{5,4},{6,7},{7,6},{8,9},{9,8},{10,11... | collective-permute-start | bytes 786440 | tf_op jit(solution)/shard_map/ppermute | solution.py:32
  169.0 9.6 %collective-permute-start.53 = (bf16[64,2176]{1,0:T(8,128)(2,1)S(1)}, bf16[64,2176]{1,0:T(8,128)(2,1)S(1)}, u32[]{:S(2)}, u32[]{:S(2)}) collective-permute-start(bf16[64,2176]{1,0:T(8,128)(2,1)S(1)} %get-tuple-element.331), channel_id=1, source_target_pairs={{0,8},{2,10},{4,0},{6,2},{8,16},{10,18},{12,4},{14,6},{16,24},{18,... | collective-permute-start | bytes 835592 | tf_op jit(solution)/shard_map/sum_a_up_2/ppermute | solution.py:66
  169.5 9.6 %collective-permute-start.54 = (bf16[64,2176]{1,0:T(8,128)(2,1)S(1)}, bf16[64,2176]{1,0:T(8,128)(2,1)S(1)}, u32[]{:S(2)}, u32[]{:S(2)}) collective-permute-start(bf16[64,2176]{1,0:T(8,128)(2,1)S(1)} %get-tuple-element.332), channel_id=1, source_target_pairs={{0,4},{2,6},{4,12},{6,14},{8,0},{10,2},{12,20},{14,22},{16,8},{18,... | collective-permute-start | bytes 835592 | tf_op jit(solution)/shard_map/sum_a_down_2/ppermute | solution.py:66
  171.5 22.8 %collective-permute-start.58 = (bf16[64,3968]{1,0:T(8,128)(2,1)S(1)}, bf16[64,3968]{1,0:T(8,128)(2,1)S(1)}, u32[]{:S(2)}, u32[]{:S(2)}) collective-permute-start(bf16[64,3968]{1,0:T(8,128)(2,1)S(1)} %get-tuple-element.350), channel_id=1, source_target_pairs={{0,8},{2,10},{4,0},{6,2},{8,16},{10,18},{12,4},{14,6},{16,24},{18,... | collective-permute-start | bytes 1523720 | tf_op jit(solution)/shard_map/sum_b_up_4/ppermute | solution.py:66
  173.4 20.8 %collective-permute-start.59 = (bf16[64,3968]{1,0:T(8,128)(2,1)S(1)}, bf16[64,3968]{1,0:T(8,128)(2,1)S(1)}, u32[]{:S(2)}, u32[]{:S(2)}) collective-permute-start(bf16[64,3968]{1,0:T(8,128)(2,1)S(1)} %get-tuple-element.351), channel_id=1, source_target_pairs={{0,4},{2,6},{4,12},{6,14},{8,0},{10,2},{12,20},{14,22},{16,8},{18,... | collective-permute-start | bytes 1523720 | tf_op jit(solution)/shard_map/sum_b_down_4/ppermute | solution.py:66
  180.6 13.3 %collective-permute-start.56 = (bf16[64,2176]{1,0:T(8,128)(2,1)S(1)}, bf16[64,2176]{1,0:T(8,128)(2,1)S(1)}, u32[]{:S(2)}, u32[]{:S(2)}) collective-permute-start(bf16[64,2176]{1,0:T(8,128)(2,1)S(1)} %get-tuple-element.342), channel_id=1, source_target_pairs={{0,8},{2,10},{4,0},{6,2},{8,16},{10,18},{12,4},{14,6},{16,24},{18,... | collective-permute-start | bytes 835592 | tf_op jit(solution)/shard_map/sum_a_up_3/ppermute | solution.py:66
  182.2 11.8 %collective-permute-start.57 = (bf16[64,2176]{1,0:T(8,128)(2,1)S(1)}, bf16[64,2176]{1,0:T(8,128)(2,1)S(1)}, u32[]{:S(2)}, u32[]{:S(2)}) collective-permute-start(bf16[64,2176]{1,0:T(8,128)(2,1)S(1)} %get-tuple-element.343), channel_id=1, source_target_pairs={{0,4},{2,6},{4,12},{6,14},{8,0},{10,2},{12,20},{14,22},{16,8},{18,... | collective-permute-start | bytes 835592 | tf_op jit(solution)/shard_map/sum_a_down_3/ppermute | solution.py:66
  182.7 19.2 %collective-permute-start.62 = (f32[64,128]{1,0:T(8,128)S(1)}, f32[64,128]{1,0:T(8,128)S(1)}, u32[]{:S(2)}, u32[]{:S(2)}) collective-permute-start(f32[64,128]{1,0:T(8,128)S(1)} %slice.334), channel_id=1, source_target_pairs={{0,1},{1,0},{2,3},{3,2},{4,5},{5,4},{6,7},{7,6},{8,9},{9,8},{10,11... | collective-permute-start | bytes 98312 | tf_op jit(solution)/shard_map/ppermute | solution.py:32
  194.7 8.2 %collective-permute-start.60 = (bf16[64,2176]{1,0:T(8,128)(2,1)S(1)}, bf16[64,2176]{1,0:T(8,128)(2,1)S(1)}, u32[]{:S(2)}, u32[]{:S(2)}) collective-permute-start(bf16[64,2176]{1,0:T(8,128)(2,1)S(1)} %get-tuple-element.354), channel_id=1, source_target_pairs={{0,8},{2,10},{4,0},{6,2},{8,16},{10,18},{12,4},{14,6},{16,24},{18,... | collective-permute-start | bytes 835592 | tf_op jit(solution)/shard_map/sum_a_up_4/ppermute | solution.py:66
  196.1 6.8 %collective-permute-start.61 = (bf16[64,2176]{1,0:T(8,128)(2,1)S(1)}, bf16[64,2176]{1,0:T(8,128)(2,1)S(1)}, u32[]{:S(2)}, u32[]{:S(2)}) collective-permute-start(bf16[64,2176]{1,0:T(8,128)(2,1)S(1)} %get-tuple-element.355), channel_id=1, source_target_pairs={{0,4},{2,6},{4,12},{6,14},{8,0},{10,2},{12,20},{14,22},{16,8},{18,... | collective-permute-start | bytes 835592 | tf_op jit(solution)/shard_map/sum_a_down_4/ppermute | solution.py:66
  196.8 5.2 %collective-permute-start.63 = (bf16[64,128]{1,0:T(8,128)(2,1)S(1)}, bf16[64,128]{1,0:T(8,128)(2,1)S(1)}, u32[]{:S(2)}, u32[]{:S(2)}) collective-permute-start(bf16[64,128]{1,0:T(8,128)(2,1)S(1)} %slice.335), channel_id=1, source_target_pairs={{0,9},{1,8},{2,11},{3,10},{4,1},{5,0},{6,3},{7,2},{8,17},{9,16},{1... | collective-permute-start | bytes 49160 | tf_op jit(solution)/shard_map/gains_across/ppermute | solution.py:71
  198.2 4.7 %collective-permute-start.64 = (bf16[64,128]{1,0:T(8,128)(2,1)S(1)}, bf16[64,128]{1,0:T(8,128)(2,1)S(1)}, u32[]{:S(2)}, u32[]{:S(2)}) collective-permute-start(bf16[64,128]{1,0:T(8,128)(2,1)S(1)} %slice.336), channel_id=1, source_target_pairs={{0,5},{1,4},{2,7},{3,6},{4,13},{5,12},{6,15},{7,14},{8,1},{9,0},{1... | collective-permute-start | bytes 49160 | tf_op jit(solution)/shard_map/gains_across/ppermute | solution.py:71
  (66 other events, 488.3 us)

commit v7 on v6

--- a/solution.py
+++ b/solution.py
@@ -748,7 +748,7 @@
         ],
         flops=6 * work_rows * model_width * width,
         moved=16 * MIB,
-        room=60,
+        room=28,
     )
     last, down_other = steps_b.ride((tuple(last), down_other))
     grad_qkv, grad_one, gain_columns, *early_a = last

time: 206 us -> 204 us (level)
  waiting for transfers between devices: 70.6 us -> 75.4 us
  other arithmetic: 21.9 us -> 17.6 us
  Pallas kernels: 46.5 us -> 43.9 us
    pallas_call x4, Pallas kernels: 34.3 us -> 31.7 us  [call(): pl.pallas_call(kernel, in_specs=specs, out_specs=[VMEM] * len(outs), out_...]
    ppermute x6, waiting for transfers between devices: 5.97 us -> 8.44 us  [pair_swap(): return lax.ppermute(block, PAIR, [(0, 1), (1, 0)])]
    ppermute x54, waiting for transfers between devices: 63.7 us -> 65.8 us  [go(): return lax.ppermute(block, SEQ, route)]
  transfers between devices with their start and end apart: 65 -> 65, of which waited for: 30 -> 33; matrix products, arithmetic and copies ran while one was open for 13% -> 11% of each run, Pallas kernels for 17% -> 16%
where the time goes in v7:
time: 204 us; the launch traced here: 203 us
  waiting for transfers between devices  75.4 us (37%)
  starting transfers between devices  52.9 us (26%)
  Pallas kernels  43.9 us (22%)
  other arithmetic  17.6 us (9%)
  local copies, waits for them, and re-layouts  11.6 us (6%)
    ppermute x54, waiting for transfers between devices, go(): return lax.ppermute(block, SEQ, route)  65.8 us
    ppermute x54, starting transfers between devices, go(): return lax.ppermute(block, SEQ, route)  40.1 us
    pallas_call x4, Pallas kernels, call(): pl.pallas_call(kernel, in_specs=specs, out_specs=[VMEM] * len(outs), out_...  31.7 us
    pallas_call x2, Pallas kernels, weight_terms(): pl.pallas_call(functools.partial(weight_kernel, tail), grid_spec=pltpu.Pr...  12.2 us
    ppermute x6, waiting for transfers between devices, pair_swap(): return lax.ppermute(block, PAIR, [(0, 1), (1, 0)])  8.44 us
    ppermute x6, starting transfers between devices, pair_swap(): return lax.ppermute(block, PAIR, [(0, 1), (1, 0)])  5.85 us
  transfers between devices with their start and end apart: 65, of which 33 were waited for; matrix products, arithmetic and copies ran while one was open for 11% of the time, Pallas kernels for 16%

profile of v7, /device:TPU:0, one launch (start us, length us, event | category | flops | bytes accessed | tf_op | source)
XLA Modules:
  0.0 203.0 jit_solution(4843065902371936913)
XLA Ops:
  0.7 1.0 copy.48
  2.5 0.9 fusion.25.refs_0_
  3.3 3.1 %collective-permute-start.1 = (bf16[64,2176]{1,0:T(8,128)(2,1)S(1)}, bf16[64,2176]{1,0:T(8,128)(2,1)S(1)}, u32[]{:S(2)}, u32[]{:S(2)}) collective-permute-start(bf16[64,2176]{1,0:T(8,128)(2,1)S(1)} %fusion.25.refs_0_), channel_id=1, source_target_pairs={{0,8},{2,10},{4,0},{6,2},{8,16},{10,18},{12,4},{14,6},{16,24},{18,... | collective-permute-start | bytes 835592 | tf_op jit(solution)/shard_map/gather_a_up_1/ppermute | solution.py:66
  6.4 1.0 slice_select_fusion
  7.4 1.3 collective-permute-start
  13.0 1.6 collective-permute-done.2.refs_2_
  14.7 2.2 %collective-permute-start.5 = (bf16[64,2176]{1,0:T(8,128)(2,1)S(1)}, bf16[64,2176]{1,0:T(8,128)(2,1)}, u32[]{:S(2)}, u32[]{:S(2)}) collective-permute-start(bf16[64,2176]{1,0:T(8,128)(2,1)S(1)} %collective-permute-done.1.refs_1_), channel_id=1, source_target_pairs={{0,8},{2,10},{4,0},{6,2},{8,16},{10,18},{12,4},{14,6},{16,24},{18,... | collective-permute-start | bytes 835592 | tf_op jit(solution)/shard_map/gather_a_up_2/ppermute | solution.py:66
  17.5 2.1 %collective-permute-start.4 = (bf16[320,1024]{1,0:T(8,128)(2,1)S(1)}, bf16[320,1024]{1,0:T(8,128)(2,1)S(1)}, u32[]{:S(2)}, u32[]{:S(2)}) collective-permute-start(bf16[320,1024]{1,0:T(8,128)(2,1)S(1)} %pad_maximum_fusion.1), channel_id=1, source_target_pairs={{0,1},{1,0},{2,3},{3,2},{4,5},{5,4},{6,7},{7,6},{8,9},{9,8},{10,11... | collective-permute-start | bytes 1966088 | tf_op jit(solution)/shard_map/ppermute | solution.py:32
  19.8 0.9 pad.37.refs_0_
  20.7 3.6 %collective-permute-done.5.refs_3_ = bf16[64,2176]{1,0:T(8,128)(2,1)} collective-permute-done((bf16[64,2176]{1,0:T(8,128)(2,1)S(1)}, bf16[64,2176]{1,0:T(8,128)(2,1)}, u32[]{:S(2)}, u32[]{:S(2)}) %collective-permute-start.5) | collective-permute-done | bytes 278560 | tf_op jit(solution)/shard_map/gather_a_up_2/ppermute | solution.py:66
  24.2 2.0 collective-permute-done.6.refs_4_
  26.5 1.7 collective-permute-start.9
  28.9 1.2 gather_fusion.1
  30.0 1.5 multiply_sine_fusion
  31.5 1.6 collective-permute-start.14
  33.6 1.2 collective-permute-done.10.refs_6_
  34.8 1.3 collective-permute-done.9.refs_5_
  36.2 0.8 pad_maximum_fusion.3.cot.left_two
  38.6 1.8 collective-permute-start.11
  40.7 6.2 %collective-permute-done.14.refs_1_ = bf16[64,3968]{1,0:T(8,128)(2,1)S(1)} collective-permute-done((bf16[64,3968]{1,0:T(8,128)(2,1)}, bf16[64,3968]{1,0:T(8,128)(2,1)S(1)}, u32[]{:S(2)}, u32[]{:S(2)}) %collective-permute-start.14) | collective-permute-done | bytes 507936 | tf_op jit(solution)/shard_map/gather_b_up_1/ppermute | solution.py:66
  47.3 1.4 collective-permute-done.11.refs_7_
  49.4 1.7 collective-permute-start.21
  52.7 8.3 %shard_map.224 = (bf16[1024,2176]{1,0:T(8,128)(2,1)}, bf16[1024,512]{1,0:T(8,128)(2,1)}, f32[8,1024]{1,0:T(8,128)}, bf16[256,1024]{1,0:T(8,128)(2,1)}, bf16[256,...) custom-call(s32[18]{0:T(128)} %multiply_add_fusion.starts, ...), custom_call_target="tpu_custom_call" | custom-call | flops 805306368 | bytes 16777216 | tf_op jit(solution)/shard_map/pallas_call | solution.py:191
  61.0 2.4 %collective-permute-done.21.refs_3_ = bf16[64,3968]{1,0:T(8,128)(2,1)} collective-permute-done((bf16[64,3968]{1,0:T(8,128)(2,1)S(1)}, bf16[64,3968]{1,0:T(8,128)(2,1)}, u32[]{:S(2)}, u32[]{:S(2)}) %collective-permute-start.21) | collective-permute-done | bytes 507936 | tf_op jit(solution)/shard_map/gather_b_up_2/ppermute | solution.py:66
  63.4 1.6 collective-permute-done.22.refs_4_
  65.0 2.1 %collective-permute-start.23 = (bf16[256,1024]{1,0:T(8,128)(2,1)}, bf16[256,1024]{1,0:T(8,128)(2,1)S(1)}, u32[]{:S(2)}, u32[]{:S(2)}) collective-permute-start(bf16[256,1024]{1,0:T(8,128)(2,1)} %get-tuple-element.236.term), channel_id=1, source_target_pairs={{0,1},{1,0},{2,3},{3,2},{4,5},{5,4},{6,7},{7,6},{8,9},{9,8},{10,11... | collective-permute-start | bytes 1572872 | tf_op jit(solution)/shard_map/ppermute | solution.py:32
  67.1 1.6 collective-permute-start.24
  69.6 10.2 %collective-permute-done.24.refs_5_ = bf16[64,3968]{1,0:T(8,128)(2,1)S(1)} collective-permute-done((bf16[64,3968]{1,0:T(8,128)(2,1)}, bf16[64,3968]{1,0:T(8,128)(2,1)S(1)}, u32[]{:S(2)}, u32[]{:S(2)}) %collective-permute-start.24) | collective-permute-done | bytes 507936 | tf_op jit(solution)/shard_map/gather_b_up_3/ppermute | solution.py:66
  79.8 1.3 collective-permute-done.25.refs_6_
  81.2 1.7 collective-permute-start.29
  84.0 3.5 %collective-permute-done.29.refs_7_ = bf16[32,3968]{1,0:T(8,128)(2,1)S(1)} collective-permute-done((bf16[32,3968]{1,0:T(8,128)(2,1)S(1)}, bf16[32,3968]{1,0:T(8,128)(2,1)S(1)}, u32[]{:S(2)}, u32[]{:S(2)}) %collective-permute-start.29) | collective-permute-done | bytes 253984 | tf_op jit(solution)/shard_map/gather_b_up_4/ppermute | solution.py:66
  87.5 1.9 collective-permute-done.30.refs_8_
  90.0 1.0 collective-permute-done.35.refs_16_
  92.9 12.2 %shard_map.225 = (f32[256,1024]{1,0:T(8,128)}, bf16[256,1024]{1,0:T(8,128)(2,1)}, bf16[256,1408]{1,0:T(8,128)(2,1)}, bf16[256,2688]{1,0:T(8,128)(2,1)}, bf16[256...) custom-call(s32[18]{0:T(128)} %multiply_add_fusion.starts, ...), custom_call_target="tpu_custom_call" | custom-call | flops 4127195136 | bytes 33554432 | tf_op jit(solution)/shard_map/pallas_call | solution.py:191
  105.9 8.0 %shard_map.226 = (bf16[6,64,3968]{2,1,0:T(8,128)(2,1)}, bf16[6,64,3968]{2,1,0:T(8,128)(2,1)}) custom-call(s32[8]{0:T(128)} %gather_fusion.1, s32[1]{0:T(128)} %bitcast.8.core, bf16[256,1024]{1,0:T(8,128)(2,1)} %get-tuple-element.268.left_one, bf16[256,1024]{1,0:T(8,128)(2,1)} %pad_maximum_fusion.3.cot.left_two, ...), custom_call_target="tpu_custom_call" | custom-call | flops 1560281088 | bytes 8126464 | tf_op jit(solution)/shard_map/pallas_call | solution.py:509
  114.1 1.3 add_convert_fusion
  116.2 1.3 collective-permute-start.40
  117.5 2.4 %collective-permute-done.38.grad_two_other = bf16[256,1024]{1,0:T(8,128)(2,1)S(1)} collective-permute-done((bf16[256,1024]{1,0:T(8,128)(2,1)}, bf16[256,1024]{1,0:T(8,128)(2,1)S(1)}, u32[]{:S(2)}, u32[]{:S(2)}) %collective-permute-start.38) | collective-permute-done | bytes 524320 | tf_op jit(solution)/shard_map/ppermute | solution.py:32
  120.0 7.0 %shard_map.227 = (f32[256,1024]{1,0:T(8,128)}, bf16[256,1024]{1,0:T(8,128)(2,1)}, f32[8,1024]{1,0:T(8,128)S(1)}, bf16[256,512]{1,0:T(8,128)(2,1)S(1)}, f32[256,1...) custom-call(s32[2]{0:T(128)S(1)} %copy-done.14, f32[256,1024]{1,0:T(8,128)S(1)} %copy-done.1, ...), custom_call_target="tpu_custom_call" | custom-call | flops 536870912 | bytes 25165824 | tf_op jit(solution)/shard_map/pallas_call | solution.py:191
  127.0 1.4 collective-permute-start.41
  128.5 1.3 collective-permute-start.42
  129.8 1.2 fusion.5
  131.2 1.1 collective-permute-done.42.from_after
  132.3 4.7 %collective-permute-start.45 = (bf16[64,3968]{1,0:T(8,128)(2,1)S(1)}, bf16[64,3968]{1,0:T(8,128)(2,1)S(1)}, u32[]{:S(2)}, u32[]{:S(2)}) collective-permute-start(bf16[64,3968]{1,0:T(8,128)(2,1)S(1)} %fusion.6), channel_id=1, source_target_pairs={{0,8},{2,10},{4,0},{6,2},{8,16},{10,18},{12,4},{14,6},{16,24},{18,... | collective-permute-start | bytes 1523720 | tf_op jit(solution)/shard_map/sum_b_up_2/ppermute | solution.py:66
  137.2 1.0 constant_dynamic-slice_fusion.1
  138.6 4.2 %shard_map.228 = (bf16[256,1536]{1,0:T(8,128)(2,1)S(1)}, bf16[256,1024]{1,0:T(8,128)(2,1)S(1)}, bf16[1024,128]{1,0:T(8,128)(2,1)S(1)}, bf16[3,64,2176]{2,1,0:T(8,128)(2,1)}, bf16[3,64,2176]{2,1,0:T(8,128)(2,1)}) custom-call(s32[8]{0:T(128)S(1)} %copy-done.13, s32[1]{0:T(128)} %bitcast.8.core, bf16[256,512]{1,0:T(8,128)(2,1)S(1)} %get-tuple-element.281.grad_queries, ...), custom_call_target="tpu_custom_call" | custom-call | flops 805306368 | bytes 16777216 | tf_op jit(solution)/shard_map/pallas_call | solution.py:191
  142.8 4.4 %collective-permute-done.44 = bf16[128,1024]{1,0:T(8,128)(2,1)S(1)} collective-permute-done((bf16[128,1024]{1,0:T(8,128)(2,1)S(1)}, bf16[128,1024]{1,0:T(8,128)(2,1)S(1)}, u32[]{:S(2)}, u32[]{:S(2)}) %collective-permute-start.44) | collective-permute-done | bytes 262176 | tf_op jit(solution)/shard_map/ppermute | solution.py:32
  147.3 2.2 %collective-permute-done.46 = bf16[64,3968]{1,0:T(8,128)(2,1)S(1)} collective-permute-done((bf16[64,3968]{1,0:T(8,128)(2,1)S(1)}, bf16[64,3968]{1,0:T(8,128)(2,1)S(1)}, u32[]{:S(2)}, u32[]{:S(2)}) %collective-permute-start.46) | collective-permute-done | bytes 507936 | tf_op jit(solution)/shard_map/sum_b_down_2/ppermute | solution.py:66
  150.4 1.6 collective-permute-start.52
  152.0 4.2 %shard_map.229 = (bf16[5,64,2176]{2,1,0:T(8,128)(2,1)}, bf16[5,64,2176]{2,1,0:T(8,128)(2,1)}) custom-call(s32[8]{0:T(128)S(1)} %copy-done.13, s32[1]{0:T(128)} %bitcast.8.core, bf16[256,1024]{1,0:T(8,128)(2,1)S(1)} %copy-done.7, bf16[256,1024]{1,0:T(8,128)(2,1)S(1)} %copy-done.8, bf16[256,1536]{1,0:T(8,128)(2,1)S(1)} %get-tuple-element.334.right_one, ...), custom_call_target="tpu_custom_call" | custom-call | flops 713031680 | bytes 3899392 | tf_op jit(solution)/shard_map/pallas_call | solution.py:509
  156.8 1.6 collective-permute-start.50
  159.2 5.2 %collective-permute-done.51 = bf16[64,3968]{1,0:T(8,128)(2,1)S(1)} collective-permute-done((bf16[64,3968]{1,0:T(8,128)(2,1)S(1)}, bf16[64,3968]{1,0:T(8,128)(2,1)S(1)}, u32[]{:S(2)}, u32[]{:S(2)}) %collective-permute-start.51) | collective-permute-done | bytes 507936 | tf_op jit(solution)/shard_map/sum_b_up_3/ppermute | solution.py:66
  164.8 2.1 %collective-permute-done.49 = bf16[32,2176]{1,0:T(8,128)(2,1)S(1)} collective-permute-done((bf16[32,2176]{1,0:T(8,128)(2,1)S(1)}, bf16[32,2176]{1,0:T(8,128)(2,1)S(1)}, u32[]{:S(2)}, u32[]{:S(2)}) %collective-permute-start.49) | collective-permute-done | bytes 139296 | tf_op jit(solution)/shard_map/sum_a_up_1/ppermute | solution.py:66
  167.8 1.6 collective-permute-start.54
  170.3 1.7 collective-permute-done.47
  171.9 0.9 collective-permute-start.59
  172.8 4.1 %collective-permute-done.53 = bf16[64,2176]{1,0:T(8,128)(2,1)S(1)} collective-permute-done((bf16[64,2176]{1,0:T(8,128)(2,1)S(1)}, bf16[64,2176]{1,0:T(8,128)(2,1)S(1)}, u32[]{:S(2)}, u32[]{:S(2)}) %collective-permute-start.53) | collective-permute-done | bytes 278560 | tf_op jit(solution)/shard_map/sum_a_up_2/ppermute | solution.py:66
  177.7 1.0 fusion.22
  178.9 1.1 collective-permute-start.56
  180.0 1.0 collective-permute-start.57
  181.7 10.6 %collective-permute-done.56 = bf16[64,2176]{1,0:T(8,128)(2,1)S(1)} collective-permute-done((bf16[64,2176]{1,0:T(8,128)(2,1)S(1)}, bf16[64,2176]{1,0:T(8,128)(2,1)S(1)}, u32[]{:S(2)}, u32[]{:S(2)}) %collective-permute-start.56) | collective-permute-done | bytes 278560 | tf_op jit(solution)/shard_map/sum_a_up_3/ppermute | solution.py:66
  193.6 1.6 collective-permute-start.61
  195.7 2.4 %collective-permute-start.64 = (bf16[64,128]{1,0:T(8,128)(2,1)S(1)}, bf16[64,128]{1,0:T(8,128)(2,1)S(1)}, u32[]{:S(2)}, u32[]{:S(2)}) collective-permute-start(bf16[64,128]{1,0:T(8,128)(2,1)S(1)} %slice.336), channel_id=1, source_target_pairs={{0,5},{1,4},{2,7},{3,6},{4,13},{5,12},{6,15},{7,14},{8,1},{9,0},{1... | collective-permute-start | bytes 49160 | tf_op jit(solution)/shard_map/gains_across/ppermute | solution.py:71
  199.0 1.4 copy.44
  (269 shorter events, 30.0 us)
Async XLA Ops:
  3.3 9.7 %collective-permute-start.1 = (bf16[64,2176]{1,0:T(8,128)(2,1)S(1)}, bf16[64,2176]{1,0:T(8,128)(2,1)S(1)}, u32[]{:S(2)}, u32[]{:S(2)}) collective-permute-start(bf16[64,2176]{1,0:T(8,128)(2,1)S(1)} %fusion.25.refs_0_), channel_id=1, source_target_pairs={{0,8},{2,10},{4,0},{6,2},{8,16},{10,18},{12,4},{14,6},{16,24},{18,... | collective-permute-start | bytes 835592 | tf_op jit(solution)/shard_map/gather_a_up_1/ppermute | solution.py:66
  6.4 8.2 %collective-permute-start.2 = (bf16[64,2176]{1,0:T(8,128)(2,1)S(1)}, bf16[64,2176]{1,0:T(8,128)(2,1)}, u32[]{:S(2)}, u32[]{:S(2)}) collective-permute-start(bf16[64,2176]{1,0:T(8,128)(2,1)S(1)} %fusion.25.refs_0_), channel_id=1, source_target_pairs={{0,4},{2,6},{4,12},{6,14},{8,0},{10,2},{12,20},{14,22},{16,8},{18,... | collective-permute-start | bytes 835592 | tf_op jit(solution)/shard_map/gather_a_down_1/ppermute | solution.py:66
  6.4 8.2 %collective-permute-start.3 = (bf16[64,2176]{1,0:T(8,128)(2,1)S(1)}, bf16[64,2176]{1,0:T(8,128)(2,1)S(1)}, u32[]{:S(2)}, u32[]{:S(2)}) collective-permute-start(bf16[64,2176]{1,0:T(8,128)(2,1)S(1)} %fusion.25.refs_0_), channel_id=1, source_target_pairs={{0,2},{2,0},{4,6},{6,4},{8,10},{10,8},{12,14},{14,12},{16,18},{18,... | collective-permute-start | bytes 835592 | tf_op jit(solution)/shard_map/gather_a_cores_0/ppermute | solution.py:66
  7.4 5.2 %collective-permute-start = (bf16[64,1024]{1,0:T(8,128)(2,1)S(1)}, bf16[64,1024]{1,0:T(8,128)(2,1)S(1)}, u32[]{:S(2)}, u32[]{:S(2)}) collective-permute-start(bf16[64,1024]{1,0:T(8,128)(2,1)S(1)} %slice_select_fusion), channel_id=1, source_target_pairs={{2,0},{4,2},{6,4},{8,6},{10,8},{12,10},{14,12},{16,14},{18,16},{20... | collective-permute-start | bytes 393224 | tf_op jit(solution)/shard_map/ppermute | solution.py:579
  14.7 9.6 %collective-permute-start.5 = (bf16[64,2176]{1,0:T(8,128)(2,1)S(1)}, bf16[64,2176]{1,0:T(8,128)(2,1)}, u32[]{:S(2)}, u32[]{:S(2)}) collective-permute-start(bf16[64,2176]{1,0:T(8,128)(2,1)S(1)} %collective-permute-done.1.refs_1_), channel_id=1, source_target_pairs={{0,8},{2,10},{4,0},{6,2},{8,16},{10,18},{12,4},{14,6},{16,24},{18,... | collective-permute-start | bytes 835592 | tf_op jit(solution)/shard_map/gather_a_up_2/ppermute | solution.py:66
  16.9 9.4 %collective-permute-start.7 = (bf16[64,2176]{1,0:T(8,128)(2,1)S(1)}, bf16[64,2176]{1,0:T(8,128)(2,1)}, u32[]{:S(2)}, u32[]{:S(2)}) collective-permute-start(bf16[64,2176]{1,0:T(8,128)(2,1)S(1)} %collective-permute-done.1.refs_1_), channel_id=1, source_target_pairs={{0,2},{2,0},{4,6},{6,4},{8,10},{10,8},{12,14},{14,12},{16,18},{18,... | collective-permute-start | bytes 835592 | tf_op jit(solution)/shard_map/gather_a_cores_-1/ppermute | solution.py:66
  16.9 9.4 %collective-permute-start.6 = (bf16[64,2176]{1,0:T(8,128)(2,1)}, bf16[64,2176]{1,0:T(8,128)(2,1)}, u32[]{:S(2)}, u32[]{:S(2)}) collective-permute-start(bf16[64,2176]{1,0:T(8,128)(2,1)} %collective-permute-done.2.refs_2_), channel_id=1, source_target_pairs={{0,4},{2,6},{4,12},{6,14},{8,0},{10,2},{12,20},{14,22},{16,8},{18,... | collective-permute-start | bytes 835592 | tf_op jit(solution)/shard_map/gather_a_down_2/ppermute | solution.py:66
  17.4 8.9 %collective-permute-start.8 = (bf16[64,2176]{1,0:T(8,128)(2,1)}, bf16[64,2176]{1,0:T(8,128)(2,1)}, u32[]{:S(2)}, u32[]{:S(2)}) collective-permute-start(bf16[64,2176]{1,0:T(8,128)(2,1)} %collective-permute-done.2.refs_2_), channel_id=1, source_target_pairs={{0,2},{2,0},{4,6},{6,4},{8,10},{10,8},{12,14},{14,12},{16,18},{18,... | collective-permute-start | bytes 835592 | tf_op jit(solution)/shard_map/gather_a_cores_1/ppermute | solution.py:66
  17.5 18.6 %collective-permute-start.4 = (bf16[320,1024]{1,0:T(8,128)(2,1)S(1)}, bf16[320,1024]{1,0:T(8,128)(2,1)S(1)}, u32[]{:S(2)}, u32[]{:S(2)}) collective-permute-start(bf16[320,1024]{1,0:T(8,128)(2,1)S(1)} %pad_maximum_fusion.1), channel_id=1, source_target_pairs={{0,1},{1,0},{2,3},{3,2},{4,5},{5,4},{6,7},{7,6},{8,9},{9,8},{10,11... | collective-permute-start | bytes 1966088 | tf_op jit(solution)/shard_map/ppermute | solution.py:32
  26.3 8.5 %collective-permute-start.10 = (bf16[64,2176]{1,0:T(8,128)(2,1)}, bf16[64,2176]{1,0:T(8,128)(2,1)S(1)}, u32[]{:S(2)}, u32[]{:S(2)}) collective-permute-start(bf16[64,2176]{1,0:T(8,128)(2,1)} %collective-permute-done.6.refs_4_), channel_id=1, source_target_pairs={{0,4},{2,6},{4,12},{6,14},{8,0},{10,2},{12,20},{14,22},{16,8},{18,... | collective-permute-start | bytes 835592 | tf_op jit(solution)/shard_map/gather_a_down_3/ppermute | solution.py:66
  26.5 9.5 %collective-permute-start.9 = (bf16[64,2176]{1,0:T(8,128)(2,1)}, bf16[64,2176]{1,0:T(8,128)(2,1)S(1)}, u32[]{:S(2)}, u32[]{:S(2)}) collective-permute-start(bf16[64,2176]{1,0:T(8,128)(2,1)} %collective-permute-done.5.refs_3_), channel_id=1, source_target_pairs={{0,8},{2,10},{4,0},{6,2},{8,16},{10,18},{12,4},{14,6},{16,24},{18,... | collective-permute-start | bytes 835592 | tf_op jit(solution)/shard_map/gather_a_up_3/ppermute | solution.py:66
  31.5 15.4 %collective-permute-start.14 = (bf16[64,3968]{1,0:T(8,128)(2,1)}, bf16[64,3968]{1,0:T(8,128)(2,1)S(1)}, u32[]{:S(2)}, u32[]{:S(2)}) collective-permute-start(bf16[64,3968]{1,0:T(8,128)(2,1)} %pad.37.refs_0_), channel_id=1, source_target_pairs={{0,8},{2,10},{4,0},{6,2},{8,16},{10,18},{12,4},{14,6},{16,24},{18,... | collective-permute-start | bytes 1523720 | tf_op jit(solution)/shard_map/gather_b_up_1/ppermute | solution.py:66
  33.1 14.2 %collective-permute-start.15 = (bf16[64,3968]{1,0:T(8,128)(2,1)}, bf16[64,3968]{1,0:T(8,128)(2,1)}, u32[]{:S(2)}, u32[]{:S(2)}) collective-permute-start(bf16[64,3968]{1,0:T(8,128)(2,1)} %pad.37.refs_0_), channel_id=1, source_target_pairs={{0,4},{2,6},{4,12},{6,14},{8,0},{10,2},{12,20},{14,22},{16,8},{18,... | collective-permute-start | bytes 1523720 | tf_op jit(solution)/shard_map/gather_b_down_1/ppermute | solution.py:66
  34.8 6.0 %collective-permute-start.13 = (bf16[64,2176]{1,0:T(8,128)(2,1)}, bf16[64,2176]{1,0:T(8,128)(2,1)S(1)}, u32[]{:S(2)}, u32[]{:S(2)}) collective-permute-start(bf16[64,2176]{1,0:T(8,128)(2,1)} %collective-permute-done.5.refs_3_), channel_id=1, source_target_pairs={{0,2},{2,0},{4,6},{6,4},{8,10},{10,8},{12,14},{14,12},{16,18},{18,... | collective-permute-start | bytes 835592 | tf_op jit(solution)/shard_map/gather_a_cores_-2/ppermute | solution.py:66
  38.6 10.1 %collective-permute-start.11 = (bf16[32,2176]{1,0:T(8,128)(2,1)S(1)}, bf16[32,2176]{1,0:T(8,128)(2,1)S(1)}, u32[]{:S(2)}, u32[]{:S(2)}) collective-permute-start(bf16[32,2176]{1,0:T(8,128)(2,1)S(1)} %slice.240), channel_id=1, source_target_pairs={{0,8},{2,10},{4,0},{6,2},{8,16},{10,18},{12,4},{14,6},{16,24},{18,... | collective-permute-start | bytes 417800 | tf_op jit(solution)/shard_map/gather_a_up_4/ppermute | solution.py:66
  40.4 8.3 %collective-permute-start.12 = (bf16[32,2176]{1,0:T(8,128)(2,1)S(1)}, bf16[32,2176]{1,0:T(8,128)(2,1)S(1)}, u32[]{:S(2)}, u32[]{:S(2)}) collective-permute-start(bf16[32,2176]{1,0:T(8,128)(2,1)S(1)} %slice.241), channel_id=1, source_target_pairs={{0,4},{2,6},{4,12},{6,14},{8,0},{10,2},{12,20},{14,22},{16,8},{18,... | collective-permute-start | bytes 417800 | tf_op jit(solution)/shard_map/gather_a_down_4/ppermute | solution.py:66
  40.7 8.6 %collective-permute-start.16 = (bf16[64,2176]{1,0:T(8,128)(2,1)}, bf16[64,2176]{1,0:T(8,128)(2,1)S(1)}, u32[]{:S(2)}, u32[]{:S(2)}) collective-permute-start(bf16[64,2176]{1,0:T(8,128)(2,1)} %collective-permute-done.6.refs_4_), channel_id=1, source_target_pairs={{0,2},{2,0},{4,6},{6,4},{8,10},{10,8},{12,14},{14,12},{16,18},{18,... | collective-permute-start | bytes 835592 | tf_op jit(solution)/shard_map/gather_a_cores_2/ppermute | solution.py:66
  47.0 4.5 %collective-permute-start.17 = (bf16[64,2176]{1,0:T(8,128)(2,1)S(1)}, bf16[64,2176]{1,0:T(8,128)(2,1)S(1)}, u32[]{:S(2)}, u32[]{:S(2)}) collective-permute-start(bf16[64,2176]{1,0:T(8,128)(2,1)S(1)} %collective-permute-done.9.refs_5_), channel_id=1, source_target_pairs={{0,2},{2,0},{4,6},{6,4},{8,10},{10,8},{12,14},{14,12},{16,18},{18,... | collective-permute-start | bytes 835592 | tf_op jit(solution)/shard_map/gather_a_cores_-3/ppermute | solution.py:66
  48.7 2.3 %collective-permute-start.19 = (bf16[32,2176]{1,0:T(8,128)(2,1)S(1)}, bf16[32,2176]{1,0:T(8,128)(2,1)S(1)}, u32[]{:S(2)}, u32[]{:S(2)}) collective-permute-start(bf16[32,2176]{1,0:T(8,128)(2,1)S(1)} %collective-permute-done.11.refs_7_), channel_id=1, source_target_pairs={{0,2},{2,0},{4,6},{6,4},{8,10},{10,8},{12,14},{14,12},{16,18},{18,... | collective-permute-start | bytes 417800 | tf_op jit(solution)/shard_map/gather_a_cores_-4/ppermute | solution.py:66
  48.8 2.6 %collective-permute-start.20 = (bf16[32,2176]{1,0:T(8,128)(2,1)S(1)}, bf16[32,2176]{1,0:T(8,128)(2,1)S(1)}, u32[]{:S(2)}, u32[]{:S(2)}) collective-permute-start(bf16[32,2176]{1,0:T(8,128)(2,1)S(1)} %collective-permute-done.12.refs_8_), channel_id=1, source_target_pairs={{0,2},{2,0},{4,6},{6,4},{8,10},{10,8},{12,14},{14,12},{16,18},{18,... | collective-permute-start | bytes 417800 | tf_op jit(solution)/shard_map/gather_a_cores_4/ppermute | solution.py:66
  49.3 2.7 %collective-permute-start.18 = (bf16[64,2176]{1,0:T(8,128)(2,1)S(1)}, bf16[64,2176]{1,0:T(8,128)(2,1)S(1)}, u32[]{:S(2)}, u32[]{:S(2)}) collective-permute-start(bf16[64,2176]{1,0:T(8,128)(2,1)S(1)} %collective-permute-done.10.refs_6_), channel_id=1, source_target_pairs={{0,2},{2,0},{4,6},{6,4},{8,10},{10,8},{12,14},{14,12},{16,18},{18,... | collective-permute-start | bytes 835592 | tf_op jit(solution)/shard_map/gather_a_cores_3/ppermute | solution.py:66
  49.4 14.0 %collective-permute-start.21 = (bf16[64,3968]{1,0:T(8,128)(2,1)S(1)}, bf16[64,3968]{1,0:T(8,128)(2,1)}, u32[]{:S(2)}, u32[]{:S(2)}) collective-permute-start(bf16[64,3968]{1,0:T(8,128)(2,1)S(1)} %collective-permute-done.14.refs_1_), channel_id=1, source_target_pairs={{0,8},{2,10},{4,0},{6,2},{8,16},{10,18},{12,4},{14,6},{16,24},{18,... | collective-permute-start | bytes 1523720 | tf_op jit(solution)/shard_map/gather_b_up_2/ppermute | solution.py:66
  51.0 14.0 %collective-permute-start.22 = (bf16[64,3968]{1,0:T(8,128)(2,1)}, bf16[64,3968]{1,0:T(8,128)(2,1)}, u32[]{:S(2)}, u32[]{:S(2)}) collective-permute-start(bf16[64,3968]{1,0:T(8,128)(2,1)} %collective-permute-done.15.refs_2_), channel_id=1, source_target_pairs={{0,4},{2,6},{4,12},{6,14},{8,0},{10,2},{12,20},{14,22},{16,8},{18,... | collective-permute-start | bytes 1523720 | tf_op jit(solution)/shard_map/gather_b_down_2/ppermute | solution.py:66
  51.4 17.3 %collective-permute-start.26 = (bf16[64,3968]{1,0:T(8,128)(2,1)S(1)}, bf16[64,3968]{1,0:T(8,128)(2,1)}, u32[]{:S(2)}, u32[]{:S(2)}) collective-permute-start(bf16[64,3968]{1,0:T(8,128)(2,1)S(1)} %copy-done.27), channel_id=1, source_target_pairs={{0,2},{2,0},{4,6},{6,4},{8,10},{10,8},{12,14},{14,12},{16,18},{18,... | collective-permute-start | bytes 1523720 | tf_op jit(solution)/shard_map/gather_b_cores_0/ppermute | solution.py:66
  51.5 17.6 %collective-permute-start.27 = (bf16[64,3968]{1,0:T(8,128)(2,1)S(1)}, bf16[64,3968]{1,0:T(8,128)(2,1)}, u32[]{:S(2)}, u32[]{:S(2)}) collective-permute-start(bf16[64,3968]{1,0:T(8,128)(2,1)S(1)} %collective-permute-done.14.refs_1_), channel_id=1, source_target_pairs={{0,2},{2,0},{4,6},{6,4},{8,10},{10,8},{12,14},{14,12},{16,18},{18,... | collective-permute-start | bytes 1523720 | tf_op jit(solution)/shard_map/gather_b_cores_-1/ppermute | solution.py:66
  52.0 17.1 %collective-permute-start.28 = (bf16[64,3968]{1,0:T(8,128)(2,1)}, bf16[64,3968]{1,0:T(8,128)(2,1)}, u32[]{:S(2)}, u32[]{:S(2)}) collective-permute-start(bf16[64,3968]{1,0:T(8,128)(2,1)} %collective-permute-done.15.refs_2_), channel_id=1, source_target_pairs={{0,2},{2,0},{4,6},{6,4},{8,10},{10,8},{12,14},{14,12},{16,18},{18,... | collective-permute-start | bytes 1523720 | tf_op jit(solution)/shard_map/gather_b_cores_1/ppermute | solution.py:66
  65.0 16.1 %collective-permute-start.23 = (bf16[256,1024]{1,0:T(8,128)(2,1)}, bf16[256,1024]{1,0:T(8,128)(2,1)S(1)}, u32[]{:S(2)}, u32[]{:S(2)}) collective-permute-start(bf16[256,1024]{1,0:T(8,128)(2,1)} %get-tuple-element.236.term), channel_id=1, source_target_pairs={{0,1},{1,0},{2,3},{3,2},{4,5},{5,4},{6,7},{7,6},{8,9},{9,8},{10,11... | collective-permute-start | bytes 1572872 | tf_op jit(solution)/shard_map/ppermute | solution.py:32
  67.1 12.7 %collective-permute-start.24 = (bf16[64,3968]{1,0:T(8,128)(2,1)}, bf16[64,3968]{1,0:T(8,128)(2,1)S(1)}, u32[]{:S(2)}, u32[]{:S(2)}) collective-permute-start(bf16[64,3968]{1,0:T(8,128)(2,1)} %collective-permute-done.21.refs_3_), channel_id=1, source_target_pairs={{0,8},{2,10},{4,0},{6,2},{8,16},{10,18},{12,4},{14,6},{16,24},{18,... | collective-permute-start | bytes 1523720 | tf_op jit(solution)/shard_map/gather_b_up_3/ppermute | solution.py:66
  68.7 12.5 %collective-permute-start.25 = (bf16[64,3968]{1,0:T(8,128)(2,1)}, bf16[64,3968]{1,0:T(8,128)(2,1)S(1)}, u32[]{:S(2)}, u32[]{:S(2)}) collective-permute-start(bf16[64,3968]{1,0:T(8,128)(2,1)} %collective-permute-done.22.refs_4_), channel_id=1, source_target_pairs={{0,4},{2,6},{4,12},{6,14},{8,0},{10,2},{12,20},{14,22},{16,8},{18,... | collective-permute-start | bytes 1523720 | tf_op jit(solution)/shard_map/gather_b_down_3/ppermute | solution.py:66
  69.1 14.4 %collective-permute-start.31 = (bf16[64,3968]{1,0:T(8,128)(2,1)}, bf16[64,3968]{1,0:T(8,128)(2,1)S(1)}, u32[]{:S(2)}, u32[]{:S(2)}) collective-permute-start(bf16[64,3968]{1,0:T(8,128)(2,1)} %collective-permute-done.21.refs_3_), channel_id=1, source_target_pairs={{0,2},{2,0},{4,6},{6,4},{8,10},{10,8},{12,14},{14,12},{16,18},{18,... | collective-permute-start | bytes 1523720 | tf_op jit(solution)/shard_map/gather_b_cores_-2/ppermute | solution.py:66
  69.1 14.9 %collective-permute-start.32 = (bf16[64,3968]{1,0:T(8,128)(2,1)}, bf16[64,3968]{1,0:T(8,128)(2,1)S(1)}, u32[]{:S(2)}, u32[]{:S(2)}) collective-permute-start(bf16[64,3968]{1,0:T(8,128)(2,1)} %collective-permute-done.22.refs_4_), channel_id=1, source_target_pairs={{0,2},{2,0},{4,6},{6,4},{8,10},{10,8},{12,14},{14,12},{16,18},{18,... | collective-permute-start | bytes 1523720 | tf_op jit(solution)/shard_map/gather_b_cores_2/ppermute | solution.py:66
  81.2 6.3 %collective-permute-start.29 = (bf16[32,3968]{1,0:T(8,128)(2,1)S(1)}, bf16[32,3968]{1,0:T(8,128)(2,1)S(1)}, u32[]{:S(2)}, u32[]{:S(2)}) collective-permute-start(bf16[32,3968]{1,0:T(8,128)(2,1)S(1)} %slice.242), channel_id=1, source_target_pairs={{0,8},{2,10},{4,0},{6,2},{8,16},{10,18},{12,4},{14,6},{16,24},{18,... | collective-permute-start | bytes 761864 | tf_op jit(solution)/shard_map/gather_b_up_4/ppermute | solution.py:66
  82.9 6.5 %collective-permute-start.30 = (bf16[32,3968]{1,0:T(8,128)(2,1)S(1)}, bf16[32,3968]{1,0:T(8,128)(2,1)S(1)}, u32[]{:S(2)}, u32[]{:S(2)}) collective-permute-start(bf16[32,3968]{1,0:T(8,128)(2,1)S(1)} %slice.243), channel_id=1, source_target_pairs={{0,4},{2,6},{4,12},{6,14},{8,0},{10,2},{12,20},{14,22},{16,8},{18,... | collective-permute-start | bytes 761864 | tf_op jit(solution)/shard_map/gather_b_down_4/ppermute | solution.py:66
  83.5 7.8 %collective-permute-start.33 = (bf16[64,3968]{1,0:T(8,128)(2,1)S(1)}, bf16[64,3968]{1,0:T(8,128)(2,1)S(1)}, u32[]{:S(2)}, u32[]{:S(2)}) collective-permute-start(bf16[64,3968]{1,0:T(8,128)(2,1)S(1)} %collective-permute-done.24.refs_5_), channel_id=1, source_target_pairs={{0,2},{2,0},{4,6},{6,4},{8,10},{10,8},{12,14},{14,12},{16,18},{18,... | collective-permute-start | bytes 1523720 | tf_op jit(solution)/shard_map/gather_b_cores_-3/ppermute | solution.py:66
  83.5 7.8 %collective-permute-start.34 = (bf16[64,3968]{1,0:T(8,128)(2,1)S(1)}, bf16[64,3968]{1,0:T(8,128)(2,1)S(1)}, u32[]{:S(2)}, u32[]{:S(2)}) collective-permute-start(bf16[64,3968]{1,0:T(8,128)(2,1)S(1)} %collective-permute-done.25.refs_6_), channel_id=1, source_target_pairs={{0,2},{2,0},{4,6},{6,4},{8,10},{10,8},{12,14},{14,12},{16,18},{18,... | collective-permute-start | bytes 1523720 | tf_op jit(solution)/shard_map/gather_b_cores_3/ppermute | solution.py:66
  89.5 1.9 collective-permute-start.36
  105.1 9.0 %collective-permute-start.37 = (bf16[2,64,3968]{2,1,0:T(8,128)(2,1)}, bf16[2,64,3968]{2,1,0:T(8,128)(2,1)}, u32[]{:S(2)}, u32[]{:S(2)}) collective-permute-start(bf16[2,64,3968]{2,1,0:T(8,128)(2,1)} %get-tuple-element.274), channel_id=1, source_target_pairs={{0,2},{2,0},{4,6},{6,4},{8,10},{10,8},{12,14},{14,12},{16,18},{18,... | collective-permute-start | bytes 3047432 | tf_op jit(solution)/shard_map/sum_b_cores_early/ppermute | solution.py:66
  105.5 14.5 %collective-permute-start.38 = (bf16[256,1024]{1,0:T(8,128)(2,1)}, bf16[256,1024]{1,0:T(8,128)(2,1)S(1)}, u32[]{:S(2)}, u32[]{:S(2)}) collective-permute-start(bf16[256,1024]{1,0:T(8,128)(2,1)} %get-tuple-element.275.grad_two), channel_id=1, source_target_pairs={{0,1},{1,0},{2,3},{3,2},{4,5},{5,4},{6,7},{7,6},{8,9},{9,8},{10,11... | collective-permute-start | bytes 1572872 | tf_op jit(solution)/shard_map/ppermute | solution.py:32
  113.9 17.1 %collective-permute-start.43 = (bf16[6,64,3968]{2,1,0:T(8,128)(2,1)}, bf16[6,64,3968]{2,1,0:T(8,128)(2,1)S(1)}, u32[]{:S(2)}, u32[]{:S(2)}) collective-permute-start(bf16[6,64,3968]{2,1,0:T(8,128)(2,1)} %get-tuple-element.272), channel_id=1, source_target_pairs={{0,2},{2,0},{4,6},{6,4},{8,10},{10,8},{12,14},{14,12},{16,18},{18,... | collective-permute-start | bytes 9142280 | tf_op jit(solution)/shard_map/sum_b_cores_rest/ppermute | solution.py:66
  115.4 11.6 %collective-permute-start.39 = (bf16[32,3968]{1,0:T(8,128)(2,1)S(1)}, bf16[32,3968]{1,0:T(8,128)(2,1)S(1)}, u32[]{:S(2)}, u32[]{:S(2)}) collective-permute-start(bf16[32,3968]{1,0:T(8,128)(2,1)S(1)} %get-tuple-element.287), channel_id=1, source_target_pairs={{0,8},{2,10},{4,0},{6,2},{8,16},{10,18},{12,4},{14,6},{16,24},{18,... | collective-permute-start | bytes 761864 | tf_op jit(solution)/shard_map/sum_b_up_1/ppermute | solution.py:66
  116.2 10.8 %collective-permute-start.40 = (bf16[32,3968]{1,0:T(8,128)(2,1)S(1)}, bf16[32,3968]{1,0:T(8,128)(2,1)S(1)}, u32[]{:S(2)}, u32[]{:S(2)}) collective-permute-start(bf16[32,3968]{1,0:T(8,128)(2,1)S(1)} %get-tuple-element.288), channel_id=1, source_target_pairs={{0,4},{2,6},{4,12},{6,14},{8,0},{10,2},{12,20},{14,22},{16,8},{18,... | collective-permute-start | bytes 761864 | tf_op jit(solution)/shard_map/sum_b_down_1/ppermute | solution.py:66
  127.0 4.2 %collective-permute-start.41 = (bf16[64,1024]{1,0:T(8,128)(2,1)}, bf16[64,1024]{1,0:T(8,128)(2,1)S(1)}, u32[]{:S(2)}, u32[]{:S(2)}) collective-permute-start(bf16[64,1024]{1,0:T(8,128)(2,1)} %get-tuple-element.289), channel_id=1, source_target_pairs={{0,2},{2,4},{4,6},{6,8},{8,10},{10,12},{12,14},{14,16},{16,18},{18... | collective-permute-start | bytes 393224 | tf_op jit(solution)/shard_map/ppermute | solution.py:28
  128.5 3.9 %collective-permute-start.42 = (bf16[64,1024]{1,0:T(8,128)(2,1)}, bf16[64,1024]{1,0:T(8,128)(2,1)S(1)}, u32[]{:S(2)}, u32[]{:S(2)}) collective-permute-start(bf16[64,1024]{1,0:T(8,128)(2,1)} %get-tuple-element.290), channel_id=1, source_target_pairs={{2,0},{4,2},{6,4},{8,6},{10,8},{12,10},{14,12},{16,14},{18,16},{20... | collective-permute-start | bytes 393224 | tf_op jit(solution)/shard_map/ppermute | solution.py:28
  132.3 15.0 %collective-permute-start.45 = (bf16[64,3968]{1,0:T(8,128)(2,1)S(1)}, bf16[64,3968]{1,0:T(8,128)(2,1)S(1)}, u32[]{:S(2)}, u32[]{:S(2)}) collective-permute-start(bf16[64,3968]{1,0:T(8,128)(2,1)S(1)} %fusion.6), channel_id=1, source_target_pairs={{0,8},{2,10},{4,0},{6,2},{8,16},{10,18},{12,4},{14,6},{16,24},{18,... | collective-permute-start | bytes 1523720 | tf_op jit(solution)/shard_map/sum_b_up_2/ppermute | solution.py:66
  137.0 12.5 %collective-permute-start.46 = (bf16[64,3968]{1,0:T(8,128)(2,1)S(1)}, bf16[64,3968]{1,0:T(8,128)(2,1)S(1)}, u32[]{:S(2)}, u32[]{:S(2)}) collective-permute-start(bf16[64,3968]{1,0:T(8,128)(2,1)S(1)} %fusion.5), channel_id=1, source_target_pairs={{0,4},{2,6},{4,12},{6,14},{8,0},{10,2},{12,20},{14,22},{16,8},{18,... | collective-permute-start | bytes 1523720 | tf_op jit(solution)/shard_map/sum_b_down_2/ppermute | solution.py:66
  138.2 9.0 %collective-permute-start.44 = (bf16[128,1024]{1,0:T(8,128)(2,1)S(1)}, bf16[128,1024]{1,0:T(8,128)(2,1)S(1)}, u32[]{:S(2)}, u32[]{:S(2)}) collective-permute-start(bf16[128,1024]{1,0:T(8,128)(2,1)S(1)} %constant_dynamic-slice_fusion.1), channel_id=1, source_target_pairs={{0,1},{1,0},{2,3},{3,2},{4,5},{5,4},{6,7},{7,6},{8,9},{9,8},{10,11... | collective-permute-start | bytes 786440 | tf_op jit(solution)/shard_map/ppermute | solution.py:32
  149.5 6.6 %collective-permute-start.48 = (bf16[3,64,2176]{2,1,0:T(8,128)(2,1)}, bf16[3,64,2176]{2,1,0:T(8,128)(2,1)S(1)}, u32[]{:S(2)}, u32[]{:S(2)}) collective-permute-start(bf16[3,64,2176]{2,1,0:T(8,128)(2,1)} %get-tuple-element.315), channel_id=1, source_target_pairs={{0,2},{2,0},{4,6},{6,4},{8,10},{10,8},{12,14},{14,12},{16,18},{18,... | collective-permute-start | bytes 2506760 | tf_op jit(solution)/shard_map/sum_a_cores_early/ppermute | solution.py:66
  149.9 14.4 %collective-permute-start.51 = (bf16[64,3968]{1,0:T(8,128)(2,1)S(1)}, bf16[64,3968]{1,0:T(8,128)(2,1)S(1)}, u32[]{:S(2)}, u32[]{:S(2)}) collective-permute-start(bf16[64,3968]{1,0:T(8,128)(2,1)S(1)} %get-tuple-element.325), channel_id=1, source_target_pairs={{0,8},{2,10},{4,0},{6,2},{8,16},{10,18},{12,4},{14,6},{16,24},{18,... | collective-permute-start | bytes 1523720 | tf_op jit(solution)/shard_map/sum_b_up_3/ppermute | solution.py:66
  150.4 14.4 %collective-permute-start.52 = (bf16[64,3968]{1,0:T(8,128)(2,1)S(1)}, bf16[64,3968]{1,0:T(8,128)(2,1)S(1)}, u32[]{:S(2)}, u32[]{:S(2)}) collective-permute-start(bf16[64,3968]{1,0:T(8,128)(2,1)S(1)} %get-tuple-element.326), channel_id=1, source_target_pairs={{0,4},{2,6},{4,12},{6,14},{8,0},{10,2},{12,20},{14,22},{16,8},{18,... | collective-permute-start | bytes 1523720 | tf_op jit(solution)/shard_map/sum_b_down_3/ppermute | solution.py:66
  156.2 22.5 %collective-permute-start.55 = (bf16[5,64,2176]{2,1,0:T(8,128)(2,1)}, bf16[5,64,2176]{2,1,0:T(8,128)(2,1)S(1)}, u32[]{:S(2)}, u32[]{:S(2)}) collective-permute-start(bf16[5,64,2176]{2,1,0:T(8,128)(2,1)} %get-tuple-element.337), channel_id=1, source_target_pairs={{0,2},{2,0},{4,6},{6,4},{8,10},{10,8},{12,14},{14,12},{16,18},{18,... | collective-permute-start | bytes 4177928 | tf_op jit(solution)/shard_map/sum_a_cores_rest/ppermute | solution.py:66
  156.3 10.7 %collective-permute-start.49 = (bf16[32,2176]{1,0:T(8,128)(2,1)S(1)}, bf16[32,2176]{1,0:T(8,128)(2,1)S(1)}, u32[]{:S(2)}, u32[]{:S(2)}) collective-permute-start(bf16[32,2176]{1,0:T(8,128)(2,1)S(1)} %get-tuple-element.316), channel_id=1, source_target_pairs={{0,8},{2,10},{4,0},{6,2},{8,16},{10,18},{12,4},{14,6},{16,24},{18,... | collective-permute-start | bytes 417800 | tf_op jit(solution)/shard_map/sum_a_up_1/ppermute | solution.py:66
  156.8 10.3 %collective-permute-start.50 = (bf16[32,2176]{1,0:T(8,128)(2,1)S(1)}, bf16[32,2176]{1,0:T(8,128)(2,1)S(1)}, u32[]{:S(2)}, u32[]{:S(2)}) collective-permute-start(bf16[32,2176]{1,0:T(8,128)(2,1)S(1)} %get-tuple-element.317), channel_id=1, source_target_pairs={{0,4},{2,6},{4,12},{6,14},{8,0},{10,2},{12,20},{14,22},{16,8},{18,... | collective-permute-start | bytes 417800 | tf_op jit(solution)/shard_map/sum_a_down_1/ppermute | solution.py:66
  164.4 7.6 %collective-permute-start.47 = (bf16[128,1024]{1,0:T(8,128)(2,1)S(1)}, bf16[128,1024]{1,0:T(8,128)(2,1)S(1)}, u32[]{:S(2)}, u32[]{:S(2)}) collective-permute-start(bf16[128,1024]{1,0:T(8,128)(2,1)S(1)} %constant_dynamic-slice_fusion), channel_id=1, source_target_pairs={{0,1},{1,0},{2,3},{3,2},{4,5},{5,4},{6,7},{7,6},{8,9},{9,8},{10,11... | collective-permute-start | bytes 786440 | tf_op jit(solution)/shard_map/ppermute | solution.py:32
  167.3 9.6 %collective-permute-start.53 = (bf16[64,2176]{1,0:T(8,128)(2,1)S(1)}, bf16[64,2176]{1,0:T(8,128)(2,1)S(1)}, u32[]{:S(2)}, u32[]{:S(2)}) collective-permute-start(bf16[64,2176]{1,0:T(8,128)(2,1)S(1)} %get-tuple-element.331), channel_id=1, source_target_pairs={{0,8},{2,10},{4,0},{6,2},{8,16},{10,18},{12,4},{14,6},{16,24},{18,... | collective-permute-start | bytes 835592 | tf_op jit(solution)/shard_map/sum_a_up_2/ppermute | solution.py:66
  167.8 9.6 %collective-permute-start.54 = (bf16[64,2176]{1,0:T(8,128)(2,1)S(1)}, bf16[64,2176]{1,0:T(8,128)(2,1)S(1)}, u32[]{:S(2)}, u32[]{:S(2)}) collective-permute-start(bf16[64,2176]{1,0:T(8,128)(2,1)S(1)} %get-tuple-element.332), channel_id=1, source_target_pairs={{0,4},{2,6},{4,12},{6,14},{8,0},{10,2},{12,20},{14,22},{16,8},{18,... | collective-permute-start | bytes 835592 | tf_op jit(solution)/shard_map/sum_a_down_2/ppermute | solution.py:66
  169.8 22.9 %collective-permute-start.58 = (bf16[64,3968]{1,0:T(8,128)(2,1)S(1)}, bf16[64,3968]{1,0:T(8,128)(2,1)S(1)}, u32[]{:S(2)}, u32[]{:S(2)}) collective-permute-start(bf16[64,3968]{1,0:T(8,128)(2,1)S(1)} %get-tuple-element.350), channel_id=1, source_target_pairs={{0,8},{2,10},{4,0},{6,2},{8,16},{10,18},{12,4},{14,6},{16,24},{18,... | collective-permute-start | bytes 1523720 | tf_op jit(solution)/shard_map/sum_b_up_4/ppermute | solution.py:66
  171.9 20.8 %collective-permute-start.59 = (bf16[64,3968]{1,0:T(8,128)(2,1)S(1)}, bf16[64,3968]{1,0:T(8,128)(2,1)S(1)}, u32[]{:S(2)}, u32[]{:S(2)}) collective-permute-start(bf16[64,3968]{1,0:T(8,128)(2,1)S(1)} %get-tuple-element.351), channel_id=1, source_target_pairs={{0,4},{2,6},{4,12},{6,14},{8,0},{10,2},{12,20},{14,22},{16,8},{18,... | collective-permute-start | bytes 1523720 | tf_op jit(solution)/shard_map/sum_b_down_4/ppermute | solution.py:66
  178.9 13.5 %collective-permute-start.56 = (bf16[64,2176]{1,0:T(8,128)(2,1)S(1)}, bf16[64,2176]{1,0:T(8,128)(2,1)S(1)}, u32[]{:S(2)}, u32[]{:S(2)}) collective-permute-start(bf16[64,2176]{1,0:T(8,128)(2,1)S(1)} %get-tuple-element.342), channel_id=1, source_target_pairs={{0,8},{2,10},{4,0},{6,2},{8,16},{10,18},{12,4},{14,6},{16,24},{18,... | collective-permute-start | bytes 835592 | tf_op jit(solution)/shard_map/sum_a_up_3/ppermute | solution.py:66
  180.0 12.5 %collective-permute-start.57 = (bf16[64,2176]{1,0:T(8,128)(2,1)S(1)}, bf16[64,2176]{1,0:T(8,128)(2,1)S(1)}, u32[]{:S(2)}, u32[]{:S(2)}) collective-permute-start(bf16[64,2176]{1,0:T(8,128)(2,1)S(1)} %get-tuple-element.343), channel_id=1, source_target_pairs={{0,4},{2,6},{4,12},{6,14},{8,0},{10,2},{12,20},{14,22},{16,8},{18,... | collective-permute-start | bytes 835592 | tf_op jit(solution)/shard_map/sum_a_down_3/ppermute | solution.py:66
  181.0 19.4 %collective-permute-start.62 = (f32[64,128]{1,0:T(8,128)S(1)}, f32[64,128]{1,0:T(8,128)S(1)}, u32[]{:S(2)}, u32[]{:S(2)}) collective-permute-start(f32[64,128]{1,0:T(8,128)S(1)} %slice.334), channel_id=1, source_target_pairs={{0,1},{1,0},{2,3},{3,2},{4,5},{5,4},{6,7},{7,6},{8,9},{9,8},{10,11... | collective-permute-start | bytes 98312 | tf_op jit(solution)/shard_map/ppermute | solution.py:32
  193.1 7.5 %collective-permute-start.60 = (bf16[64,2176]{1,0:T(8,128)(2,1)S(1)}, bf16[64,2176]{1,0:T(8,128)(2,1)S(1)}, u32[]{:S(2)}, u32[]{:S(2)}) collective-permute-start(bf16[64,2176]{1,0:T(8,128)(2,1)S(1)} %get-tuple-element.354), channel_id=1, source_target_pairs={{0,8},{2,10},{4,0},{6,2},{8,16},{10,18},{12,4},{14,6},{16,24},{18,... | collective-permute-start | bytes 835592 | tf_op jit(solution)/shard_map/sum_a_up_4/ppermute | solution.py:66
  193.6 7.0 %collective-permute-start.61 = (bf16[64,2176]{1,0:T(8,128)(2,1)S(1)}, bf16[64,2176]{1,0:T(8,128)(2,1)S(1)}, u32[]{:S(2)}, u32[]{:S(2)}) collective-permute-start(bf16[64,2176]{1,0:T(8,128)(2,1)S(1)} %get-tuple-element.355), channel_id=1, source_target_pairs={{0,4},{2,6},{4,12},{6,14},{8,0},{10,2},{12,20},{14,22},{16,8},{18,... | collective-permute-start | bytes 835592 | tf_op jit(solution)/shard_map/sum_a_down_4/ppermute | solution.py:66
  195.2 5.2 %collective-permute-start.63 = (bf16[64,128]{1,0:T(8,128)(2,1)S(1)}, bf16[64,128]{1,0:T(8,128)(2,1)S(1)}, u32[]{:S(2)}, u32[]{:S(2)}) collective-permute-start(bf16[64,128]{1,0:T(8,128)(2,1)S(1)} %slice.335), channel_id=1, source_target_pairs={{0,9},{1,8},{2,11},{3,10},{4,1},{5,0},{6,3},{7,2},{8,17},{9,16},{1... | collective-permute-start | bytes 49160 | tf_op jit(solution)/shard_map/gains_across/ppermute | solution.py:71
  195.7 4.8 %collective-permute-start.64 = (bf16[64,128]{1,0:T(8,128)(2,1)S(1)}, bf16[64,128]{1,0:T(8,128)(2,1)S(1)}, u32[]{:S(2)}, u32[]{:S(2)}) collective-permute-start(bf16[64,128]{1,0:T(8,128)(2,1)S(1)} %slice.336), channel_id=1, source_target_pairs={{0,5},{1,4},{2,7},{3,6},{4,13},{5,12},{6,15},{7,14},{8,1},{9,0},{1... | collective-permute-start | bytes 49160 | tf_op jit(solution)/shard_map/gains_across/ppermute | solution.py:71
  (60 other events, 487.2 us)
